TPU v7x, 32 devices: a whole 2x2x4 slice. The times are simulated.
32 devices in a mesh: seg: 8 (over z, y), col: 4 (over x, core).
Axes of the slice: x: 2, y: 2, z: 4, core: 2. Of those that a mesh axis runs over, the one named last changes fastest.
Arguments:
- model_mixing: float32 [16, 384, 384], P('seg', 'col'), may hold values from -0.07654656 to 0.07654656
- retention: float32 [16, 384], P('seg'), may hold values from 0.5 to 0.95
- forcing: float32 [16, 384], P('seg'), may hold values from -1.2 to 1.2
- observations: float32 [16, 1024], P('seg'), may hold values from -6 to 6
- model_noise: float32 [16, 384], P('seg'), may hold values from 0.01 to 0.1
- obs_noise: float32 [1024], replicated, may hold values from 0.5 to 2
- gain: float32 [384, 1024], replicated, may hold values from -0.01875 to 0.01875
- obs_operator_t: float32 [384, 1024], P('col'), may hold values from -0.30618623 to 0.30618623
- prior_mean: float32 [384], replicated, may hold values from -6 to 6
- prior_factor: float32 [384, 384], replicated, may hold values from -0.3125 to 0.3125
Outputs:
- means: float32 [16, 384], P('seg')
- covariances: float32 [16, 384, 384], P('seg', 'col')
All inputs are finite; a program needn't handle non-finite values.
Results may differ from a plain program's by a relative error of at most 0.00019.
Values sent between devices are 32-bit elements; how exact they have to be, the bound alone decides.
No kernel may reach another device: no remote copies, remote signals or barrier semaphores. Data moves between devices by JAX's collectives and lax.ppermute only.
A program may use at most 64 MiB of HBM per device.

v0:
```python
import jax
import jax.numpy as jnp
from jax import lax
from jax.sharding import PartitionSpec as P

precise = lax.Precision.HIGHEST


def passed_along(block, axis, distance):
    devices = range(lax.axis_size(axis))
    route = [(i - distance, i) for i in devices if i - distance in devices]
    return lax.ppermute(block, axis, route)


def product(left, right):
    return jnp.dot(left, right, precision=precise, preferred_element_type=jnp.float32)


def sandwich(row_block, step_full, offset_col, col_width):
    half_rows = product(row_block, step_full)
    half_full = lax.all_gather(half_rows, "col", axis=0, tiled=True)
    step_cols = lax.dynamic_slice_in_dim(step_full, offset_col, col_width, 1)
    return product(step_cols.T, half_full)


def advance_pair(element, mean_now, covar_now):
    step_total, offset_total, noise_total = element
    mean_next = product(mean_now, step_total) + offset_total
    covar_next = product(product(step_total.T, covar_now), step_total) + noise_total
    return (mean_next, covar_next)


def per_device(
    model_mixing,
    retention,
    forcing,
    observations,
    model_noise,
    obs_noise,
    gain,
    obs_operator_t,
    prior_mean,
    prior_factor,
):
    col_width = obs_operator_t.shape[0]
    states = gain.shape[0]
    offset_col = lax.axis_index("col") * col_width
    row_ids = lax.broadcasted_iota(jnp.int32, (col_width, states), 0) + offset_col
    col_ids = lax.broadcasted_iota(jnp.int32, (col_width, states), 1)
    eye_rows = (row_ids == col_ids).astype(jnp.float32)
    corr_rows = eye_rows - product(obs_operator_t, gain.T)
    corr_full = lax.all_gather(corr_rows, "col", axis=0, tiled=True)
    corr_cols = lax.dynamic_slice_in_dim(corr_full, offset_col, col_width, 1)
    gain_rows = lax.dynamic_slice_in_dim(gain, offset_col, col_width, 0)
    fixed_rows = product(gain_rows * obs_noise[None, :], gain.T)
    keep_cols = lax.dynamic_slice_in_dim(retention, offset_col, col_width, 1)
    step_rows = keep_cols[:, :, None] * corr_rows[None, :, :] + jnp.einsum(
        "swn,nm->swm",
        model_mixing,
        corr_full,
        precision=precise,
        preferred_element_type=jnp.float32,
    )
    scaled = corr_cols.T[None, :, :] * model_noise[:, None, :]
    noise_rows = (
        jnp.einsum(
            "swn,nm->swm", scaled, corr_full, precision=precise, preferred_element_type=jnp.float32
        )
        + fixed_rows[None, :, :]
    )
    offsets = product(forcing, corr_full) + product(observations, gain.T)
    step_full = lax.all_gather(step_rows, "col", axis=1, tiled=True)

    def compose(carried, inputs):
        acc_rows, acc_offset, acc_noise = carried
        step_now, offset_now, noise_now = inputs
        new_rows = product(acc_rows, step_now)
        new_offset = product(acc_offset, step_now) + offset_now
        new_noise = sandwich(acc_noise, step_now, offset_col, col_width) + noise_now
        return ((new_rows, new_offset, new_noise), None)

    start_pair = (
        eye_rows,
        jnp.zeros((states,), jnp.float32),
        jnp.zeros((col_width, states), jnp.float32),
    )
    totals, ignored = lax.scan(compose, start_pair, (step_full, offsets, noise_rows))
    total_rows, total_offset, total_noise = totals
    total_full, noise_full = (
        lax.all_gather(total_rows, "col", axis=0, tiled=True),
        lax.all_gather(total_noise, "col", axis=0, tiled=True),
    )
    prior_covar = product(prior_factor, prior_factor.T)
    element = (total_full, total_offset, noise_full)
    is_first = lax.axis_index("seg") == 0

    def turn(turn_index, carried):
        moved_mean, moved_covar = advance_pair(element, carried[0], carried[1])
        recv_mean, recv_covar = passed_along((moved_mean, moved_covar), "seg", 1)
        return (
            jnp.where(is_first, prior_mean, recv_mean),
            jnp.where(is_first, prior_covar, recv_covar),
        )

    entry_mean, entry_covar = lax.fori_loop(
        0, lax.axis_size("seg") - 1, turn, (prior_mean, prior_covar)
    )
    entry_rows = lax.dynamic_slice_in_dim(entry_covar, offset_col, col_width, 0)

    def rerun(carried, inputs):
        mean_now, covar_rows = carried
        step_now, offset_now, noise_now = inputs
        mean_next = product(mean_now, step_now) + offset_now
        covar_next = sandwich(covar_rows, step_now, offset_col, col_width) + noise_now
        return ((mean_next, covar_next), (mean_next, covar_next))

    final_pair, outputs = lax.scan(
        rerun, (entry_mean, entry_rows), (step_full, offsets, noise_rows)
    )
    return (outputs[0], outputs[1])


def solution(mesh):
    in_specs = (
        P("seg", "col", None),
        P("seg", None),
        P("seg", None),
        P("seg", None),
        P("seg", None),
        P(),
        P(),
        P("col", None),
        P(),
        P(),
    )
    out_specs = (P("seg", None), P("seg", "col", None))
    return jax.shard_map(
        per_device, mesh=mesh, in_specs=in_specs, out_specs=out_specs, check_vma=False
    )
```

profile of v0, /device:TPU:29, one launch (start us, length us, event | category | flops | bytes accessed | tf_op | source)
XLA Modules:
  0.0 249.5 jit_solution(7263817158387895197)
XLA Ops:
  7.3 3.1 %convolution_subtract_fusion = f32[96,384]{1,0:T(8,128)S(1)} fusion(f32[96,1024]{1,0:T(8,128)} %param.23, f32[384,1024]{1,0:T(8,128)} %param.22, s32[96]{0:T(128)S(1)} %iota_add_fusion), kind=kOutput, calls=%fused_computation.43 | convolution fusion | flops 453095424 | bytes 2113920 | tf_op jit(solution)/shard_map/dot_general | solution.py:16
  10.4 8.0 %all_gather.26 = f32[384,384]{1,0:T(8,128)S(1)} all-gather(f32[96,384]{1,0:T(8,128)S(1)} %convolution_subtract_fusion), channel_id=1, replica_groups=mesh['seg'=8,'col'=4] {'col'}, dimensions={0}, use_global_device_ids=true | all-gather | bytes 737280 | tf_op jit(solution)/shard_map/all_gather | solution.py:52
  19.2 1.5 fusion.25
  23.8 1.6 convolution_bitcast_fusion.4
  25.4 1.6 fusion.28
  27.0 1.5 convolution_add_fusion.3
  28.5 1.4 convolution_add_fusion.4
  29.9 8.9 %all-gather.2.cloned.1.call-done = f32[2,384,384]{2,1,0:T(8,128)} async-done(((f32[2,96,384]{2,1,0:T(8,128)}), f32[2,384,384]{2,1,0:T(8,128)}) %all-gather.2.cloned.1.call-update) | async-done | bytes 1179664 | tf_op jit(solution)/shard_map/all_gather | solution.py:72
  38.8 26.6 %while.51 = (s32[]{:T(128)}, f32[96,384]{1,0:T(8,128)}, f32[384]{0:T(512)S(1)}, f32[96,384]{1,0:T(8,128)S(1)}, f32[2,384,384]{2,1,0:T(8,128)}, /*index=5*/f32[2,...) while((s32[]{:T(128)}, f32[96,384]{1,0:T(8,128)}, f32[384]{0:T(512)S(1)}, ...), condition=%wide.region_1.2_spmd.clone, body=%wide.region_0.1_spmd.clone.sunk | while | flops 511451904 | bytes 10388716 | solution.py:87
  38.8 1.7 convolution_bitcast_fusion.10
  40.5 7.6 %all_gather.34 = f32[384,384]{1,0:T(8,128)S(1)} all-gather(f32[96,384]{1,0:T(8,128)S(1)} %convolution_bitcast_fusion.10), channel_id=1, replica_groups=mesh['seg'=8,'col'=4] {'col'}, dimensions={0}, use_global_device_ids=true | all-gather | bytes 737280 | tf_op jit(solution)/shard_map/while/body/eval_jaxpr/all_gather | solution.py:21
  48.1 2.3 convolution_add_fusion.8
  52.1 1.7 convolution_bitcast_fusion.10
  53.8 7.6 %all_gather.34 = f32[384,384]{1,0:T(8,128)S(1)} all-gather(f32[96,384]{1,0:T(8,128)S(1)} %convolution_bitcast_fusion.10), channel_id=1, replica_groups=mesh['seg'=8,'col'=4] {'col'}, dimensions={0}, use_global_device_ids=true | all-gather | bytes 737280 | tf_op jit(solution)/shard_map/while/body/eval_jaxpr/all_gather | solution.py:21
  61.5 2.3 convolution_add_fusion.8
  66.1 7.8 %all_gather.28 = f32[384,384]{1,0:T(8,128)S(1)} all-gather(f32[96,384]{1,0:T(8,128)} %get-tuple-element.345), channel_id=1, replica_groups=mesh['seg'=8,'col'=4] {'col'}, dimensions={0}, use_global_device_ids=true | all-gather | bytes 737280 | tf_op jit(solution)/shard_map/all_gather | solution.py:90
  74.0 8.9 %all_gather.29 = f32[384,384]{1,0:T(8,128)} all-gather(f32[96,384]{1,0:T(8,128)} %copy-done.10), channel_id=1, replica_groups=mesh['seg'=8,'col'=4] {'col'}, dimensions={0}, use_global_device_ids=true | all-gather | bytes 737280 | tf_op jit(solution)/shard_map/all_gather | solution.py:91
  82.8 133.9 %while.49 = (s32[]{:T(128)}, f32[384]{0:T(512)S(1)}, f32[384,384]{1,0:T(8,128)S(1)}, pred[]{:T(512)}, f32[384,384]{1,0:T(8,128)S(1)}, /*index=5*/f32[384]{0:T(51...) while((s32[]{:T(128)}, f32[384]{0:T(512)S(1)}, f32[384,384]{1,0:T(8,128)S(1)}, ...), condition=%wide.region_3.4_spmd, body=%wide.region_2.3_spmd.sunk | while | flops 1361019648 | bytes 11228371 | solution.py:105
  82.8 1.3 fusion.87
  88.5 13.8 %collective-permute-done = f32[384]{0:T(512)} collective-permute-done((f32[384]{0:T(512)S(1)}, f32[384]{0:T(512)}, u32[]{:S(2)}, u32[]{:S(2)}) %collective-permute-start) | collective-permute-done | bytes 1568 | tf_op jit(solution)/shard_map/while/body/eval_jaxpr/ppermute | solution.py:12
  104.1 1.3 fusion.87
  109.7 12.9 %collective-permute-done = f32[384]{0:T(512)} collective-permute-done((f32[384]{0:T(512)S(1)}, f32[384]{0:T(512)}, u32[]{:S(2)}, u32[]{:S(2)}) %collective-permute-start) | collective-permute-done | bytes 1568 | tf_op jit(solution)/shard_map/while/body/eval_jaxpr/ppermute | solution.py:12
  130.0 12.8 %collective-permute-done = f32[384]{0:T(512)} collective-permute-done((f32[384]{0:T(512)S(1)}, f32[384]{0:T(512)}, u32[]{:S(2)}, u32[]{:S(2)}) %collective-permute-start) | collective-permute-done | bytes 1568 | tf_op jit(solution)/shard_map/while/body/eval_jaxpr/ppermute | solution.py:12
  150.4 11.9 %collective-permute-done = f32[384]{0:T(512)} collective-permute-done((f32[384]{0:T(512)S(1)}, f32[384]{0:T(512)}, u32[]{:S(2)}, u32[]{:S(2)}) %collective-permute-start) | collective-permute-done | bytes 1568 | tf_op jit(solution)/shard_map/while/body/eval_jaxpr/ppermute | solution.py:12
  164.1 1.3 fusion.87
  169.7 11.0 %collective-permute-done = f32[384]{0:T(512)} collective-permute-done((f32[384]{0:T(512)S(1)}, f32[384]{0:T(512)}, u32[]{:S(2)}, u32[]{:S(2)}) %collective-permute-start) | collective-permute-done | bytes 1568 | tf_op jit(solution)/shard_map/while/body/eval_jaxpr/ppermute | solution.py:12
  188.2 10.1 %collective-permute-done = f32[384]{0:T(512)} collective-permute-done((f32[384]{0:T(512)S(1)}, f32[384]{0:T(512)}, u32[]{:S(2)}, u32[]{:S(2)}) %collective-permute-start) | collective-permute-done | bytes 1568 | tf_op jit(solution)/shard_map/while/body/eval_jaxpr/ppermute | solution.py:12
  200.1 1.3 fusion.87
  205.7 9.1 %collective-permute-done = f32[384]{0:T(512)} collective-permute-done((f32[384]{0:T(512)S(1)}, f32[384]{0:T(512)}, u32[]{:S(2)}, u32[]{:S(2)}) %collective-permute-start) | collective-permute-done | bytes 1568 | tf_op jit(solution)/shard_map/while/body/eval_jaxpr/ppermute | solution.py:12
  216.7 26.0 %while.50 = (s32[]{:T(128)}, f32[384]{0:T(512)S(1)}, f32[96,384]{1,0:T(8,128)S(1)}, f32[2,384]{1,0:T(2,128)}, f32[2,96,384]{2,1,0:T(8,128)}, /*index=5*/f32[2,38...) while((s32[]{:T(128)}, f32[384]{0:T(512)S(1)}, ...), condition=%wide.region_5.6_spmd, body=%wide.region_4.5_spmd.sunk | while | flops 341545344 | bytes 7024421 | solution.py:117
  217.3 13.6 %all_gather.33 = f32[384,384]{1,0:T(8,128)S(1)} all-gather(f32[96,384]{1,0:T(8,128)S(1)} %convolution_bitcast_fusion.8), channel_id=1, replica_groups=mesh['seg'=8,'col'=4] {'col'}, dimensions={0}, use_global_device_ids=true | all-gather | bytes 737280 | tf_op jit(solution)/shard_map/while/body/eval_jaxpr/all_gather | solution.py:21
  233.2 7.6 %all_gather.33 = f32[384,384]{1,0:T(8,128)S(1)} all-gather(f32[96,384]{1,0:T(8,128)S(1)} %convolution_bitcast_fusion.8), channel_id=1, replica_groups=mesh['seg'=8,'col'=4] {'col'}, dimensions={0}, use_global_device_ids=true | all-gather | bytes 737280 | tf_op jit(solution)/shard_map/while/body/eval_jaxpr/all_gather | solution.py:21
  (183 shorter events, 58.9 us)
Async XLA Ops:
  7.2 14.5 %copy-start = (f32[384,384]{1,0:T(8,128)S(1)}, f32[384,384]{1,0:T(8,128)}, u32[]{:S(2)}) copy-start(f32[384,384]{1,0:T(8,128)} %param.25) | copy-start | bytes 1769476
  7.2 31.6 %all-gather.2.cloned.1.call-start = ((), (), s32[]{:S(2)}) async-start(), calls=%async_computation | async-start | bytes 1474560 | tf_op jit(solution)/shard_map/all_gather | solution.py:72
  7.2 12.0 %copy-start.12 = (f32[2,96,384]{2,1,0:T(8,128)S(1)}, f32[2,96,384]{2,1,0:T(8,128)}, u32[]{:S(2)}) copy-start(f32[2,96,384]{2,1,0:T(8,128)} %param.16) | copy-start | bytes 884740
  18.4 3.3 %copy-start.5 = (f32[384,384]{1,0:T(8,128)}, f32[384,384]{1,0:T(8,128)S(1)}, u32[]{:S(2)}) copy-start(f32[384,384]{1,0:T(8,128)S(1)} %all_gather.26) | copy-start | bytes 1769476
  23.8 3.2 %copy-start.6 = (f32[384,384]{1,0:T(8,128)S(1)}, f32[384,384]{1,0:T(8,128)}, u32[]{:S(2)}) copy-start(f32[384,384]{1,0:T(8,128)} %copy-done.5) | copy-start | bytes 1769476
  23.8 3.2 %copy-start.11 = (f32[96,384]{1,0:T(8,128)S(1)}, f32[96,384]{1,0:T(8,128)}, u32[]{:S(2)}) copy-start(f32[96,384]{1,0:T(8,128)} %copy.13) | copy-start | bytes 442372
  23.8 3.2 %copy-start.17 = (f32[2,384]{1,0:T(2,128)S(1)}, f32[2,384]{1,0:T(2,128)}, u32[]{:S(2)}) copy-start(f32[2,384]{1,0:T(2,128)} %param.20) | copy-start | bytes 9220
  25.4 3.1 %copy-start.14 = (f32[2,1024]{1,0:T(2,128)S(1)}, f32[2,1024]{1,0:T(2,128)}, u32[]{:S(2)}) copy-start(f32[2,1024]{1,0:T(2,128)} %param.19) | copy-start | bytes 24580
  38.8 9.3 %copy-start.1 = (f32[2,384,384]{2,1,0:T(8,128)S(1)}, f32[2,384,384]{2,1,0:T(8,128)}, u32[]{:S(2)}) copy-start(f32[2,384,384]{2,1,0:T(8,128)} %get-tuple-element.620) | copy-start | bytes 3538948 | tf_op jit(solution)/shard_map/while
  48.1 2.8 %copy-start.8 = (f32[96,384]{1,0:T(8,128)S(1)}, f32[96,384]{1,0:T(8,128)}, u32[]{:S(2)}) copy-start(f32[96,384]{1,0:T(8,128)} %get-tuple-element.607) | copy-start | bytes 442372 | tf_op jit(solution)/shard_map/while
  52.1 9.3 %copy-start.1 = (f32[2,384,384]{2,1,0:T(8,128)S(1)}, f32[2,384,384]{2,1,0:T(8,128)}, u32[]{:S(2)}) copy-start(f32[2,384,384]{2,1,0:T(8,128)} %get-tuple-element.620) | copy-start | bytes 3538948 | tf_op jit(solution)/shard_map/while
  82.8 133.9 %copy-start.2 = (f32[2,384,384]{2,1,0:T(8,128)S(1)}, f32[2,384,384]{2,1,0:T(8,128)}, u32[]{:S(2)}) copy-start(f32[2,384,384]{2,1,0:T(8,128)} %get-tuple-element.691) | copy-start | bytes 3538948
  85.4 17.5 %collective-permute-start.1 = (f32[384,384]{1,0:T(8,128)S(1)}, f32[384,384]{1,0:T(8,128)}, u32[]{:S(2)}, u32[]{:S(2)}) collective-permute-start(f32[384,384]{1,0:T(8,128)S(1)} %convolution_add_fusion.7), channel_id=1, source_target_pairs={{0,4},{4,8},{8,12},{12,16},{16,20},{20,24},{24,28},{1,5},{5,9},{9,... | collective-permute-start | bytes 1769480 | tf_op jit(solution)/shard_map/while/body/eval_jaxpr/ppermute | solution.py:12
  87.2 15.1 %collective-permute-start = (f32[384]{0:T(512)S(1)}, f32[384]{0:T(512)}, u32[]{:S(2)}, u32[]{:S(2)}) collective-permute-start(f32[384]{0:T(512)S(1)} %add.134), channel_id=1, source_target_pairs={{0,4},{4,8},{8,12},{12,16},{16,20},{20,24},{24,28},{1,5},{5,9},{9,... | collective-permute-start | bytes 4616 | tf_op jit(solution)/shard_map/while/body/eval_jaxpr/ppermute | solution.py:12
  106.7 16.6 %collective-permute-start.1 = (f32[384,384]{1,0:T(8,128)S(1)}, f32[384,384]{1,0:T(8,128)}, u32[]{:S(2)}, u32[]{:S(2)}) collective-permute-start(f32[384,384]{1,0:T(8,128)S(1)} %convolution_add_fusion.7), channel_id=1, source_target_pairs={{0,4},{4,8},{8,12},{12,16},{16,20},{20,24},{24,28},{1,5},{5,9},{9,... | collective-permute-start | bytes 1769480 | tf_op jit(solution)/shard_map/while/body/eval_jaxpr/ppermute | solution.py:12
  108.4 14.2 %collective-permute-start = (f32[384]{0:T(512)S(1)}, f32[384]{0:T(512)}, u32[]{:S(2)}, u32[]{:S(2)}) collective-permute-start(f32[384]{0:T(512)S(1)} %add.134), channel_id=1, source_target_pairs={{0,4},{4,8},{8,12},{12,16},{16,20},{20,24},{24,28},{1,5},{5,9},{9,... | collective-permute-start | bytes 4616 | tf_op jit(solution)/shard_map/while/body/eval_jaxpr/ppermute | solution.py:12
  127.0 16.6 %collective-permute-start.1 = (f32[384,384]{1,0:T(8,128)S(1)}, f32[384,384]{1,0:T(8,128)}, u32[]{:S(2)}, u32[]{:S(2)}) collective-permute-start(f32[384,384]{1,0:T(8,128)S(1)} %convolution_add_fusion.7), channel_id=1, source_target_pairs={{0,4},{4,8},{8,12},{12,16},{16,20},{20,24},{24,28},{1,5},{5,9},{9,... | collective-permute-start | bytes 1769480 | tf_op jit(solution)/shard_map/while/body/eval_jaxpr/ppermute | solution.py:12
  128.7 14.1 %collective-permute-start = (f32[384]{0:T(512)S(1)}, f32[384]{0:T(512)}, u32[]{:S(2)}, u32[]{:S(2)}) collective-permute-start(f32[384]{0:T(512)S(1)} %add.134), channel_id=1, source_target_pairs={{0,4},{4,8},{8,12},{12,16},{16,20},{20,24},{24,28},{1,5},{5,9},{9,... | collective-permute-start | bytes 4616 | tf_op jit(solution)/shard_map/while/body/eval_jaxpr/ppermute | solution.py:12
  147.3 15.6 %collective-permute-start.1 = (f32[384,384]{1,0:T(8,128)S(1)}, f32[384,384]{1,0:T(8,128)}, u32[]{:S(2)}, u32[]{:S(2)}) collective-permute-start(f32[384,384]{1,0:T(8,128)S(1)} %convolution_add_fusion.7), channel_id=1, source_target_pairs={{0,4},{4,8},{8,12},{12,16},{16,20},{20,24},{24,28},{1,5},{5,9},{9,... | collective-permute-start | bytes 1769480 | tf_op jit(solution)/shard_map/while/body/eval_jaxpr/ppermute | solution.py:12
  149.1 13.2 %collective-permute-start = (f32[384]{0:T(512)S(1)}, f32[384]{0:T(512)}, u32[]{:S(2)}, u32[]{:S(2)}) collective-permute-start(f32[384]{0:T(512)S(1)} %add.134), channel_id=1, source_target_pairs={{0,4},{4,8},{8,12},{12,16},{16,20},{20,24},{24,28},{1,5},{5,9},{9,... | collective-permute-start | bytes 4616 | tf_op jit(solution)/shard_map/while/body/eval_jaxpr/ppermute | solution.py:12
  166.7 14.7 %collective-permute-start.1 = (f32[384,384]{1,0:T(8,128)S(1)}, f32[384,384]{1,0:T(8,128)}, u32[]{:S(2)}, u32[]{:S(2)}) collective-permute-start(f32[384,384]{1,0:T(8,128)S(1)} %convolution_add_fusion.7), channel_id=1, source_target_pairs={{0,4},{4,8},{8,12},{12,16},{16,20},{20,24},{24,28},{1,5},{5,9},{9,... | collective-permute-start | bytes 1769480 | tf_op jit(solution)/shard_map/while/body/eval_jaxpr/ppermute | solution.py:12
  168.4 12.3 %collective-permute-start = (f32[384]{0:T(512)S(1)}, f32[384]{0:T(512)}, u32[]{:S(2)}, u32[]{:S(2)}) collective-permute-start(f32[384]{0:T(512)S(1)} %add.134), channel_id=1, source_target_pairs={{0,4},{4,8},{8,12},{12,16},{16,20},{20,24},{24,28},{1,5},{5,9},{9,... | collective-permute-start | bytes 4616 | tf_op jit(solution)/shard_map/while/body/eval_jaxpr/ppermute | solution.py:12
  185.2 13.8 %collective-permute-start.1 = (f32[384,384]{1,0:T(8,128)S(1)}, f32[384,384]{1,0:T(8,128)}, u32[]{:S(2)}, u32[]{:S(2)}) collective-permute-start(f32[384,384]{1,0:T(8,128)S(1)} %convolution_add_fusion.7), channel_id=1, source_target_pairs={{0,4},{4,8},{8,12},{12,16},{16,20},{20,24},{24,28},{1,5},{5,9},{9,... | collective-permute-start | bytes 1769480 | tf_op jit(solution)/shard_map/while/body/eval_jaxpr/ppermute | solution.py:12
  186.9 11.4 %collective-permute-start = (f32[384]{0:T(512)S(1)}, f32[384]{0:T(512)}, u32[]{:S(2)}, u32[]{:S(2)}) collective-permute-start(f32[384]{0:T(512)S(1)} %add.134), channel_id=1, source_target_pairs={{0,4},{4,8},{8,12},{12,16},{16,20},{20,24},{24,28},{1,5},{5,9},{9,... | collective-permute-start | bytes 4616 | tf_op jit(solution)/shard_map/while/body/eval_jaxpr/ppermute | solution.py:12
  202.7 12.8 %collective-permute-start.1 = (f32[384,384]{1,0:T(8,128)S(1)}, f32[384,384]{1,0:T(8,128)}, u32[]{:S(2)}, u32[]{:S(2)}) collective-permute-start(f32[384,384]{1,0:T(8,128)S(1)} %convolution_add_fusion.7), channel_id=1, source_target_pairs={{0,4},{4,8},{8,12},{12,16},{16,20},{20,24},{24,28},{1,5},{5,9},{9,... | collective-permute-start | bytes 1769480 | tf_op jit(solution)/shard_map/while/body/eval_jaxpr/ppermute | solution.py:12
  204.4 10.4 %collective-permute-start = (f32[384]{0:T(512)S(1)}, f32[384]{0:T(512)}, u32[]{:S(2)}, u32[]{:S(2)}) collective-permute-start(f32[384]{0:T(512)S(1)} %add.134), channel_id=1, source_target_pairs={{0,4},{4,8},{8,12},{12,16},{16,20},{20,24},{24,28},{1,5},{5,9},{9,... | collective-permute-start | bytes 4616 | tf_op jit(solution)/shard_map/while/body/eval_jaxpr/ppermute | solution.py:12
  216.7 14.1 %copy-start.7 = (f32[2,96,384]{2,1,0:T(8,128)S(1)}, f32[2,96,384]{2,1,0:T(8,128)}, u32[]{:S(2)}) copy-start(f32[2,96,384]{2,1,0:T(8,128)} %get-tuple-element.686) | copy-start | bytes 884740 | tf_op jit(solution)/shard_map/while
  216.7 14.1 %copy-start.18 = (f32[2,96,384]{2,1,0:T(8,128)S(1)}, f32[2,96,384]{2,1,0:T(8,128)}, u32[]{:S(2)}) copy-start(f32[2,96,384]{2,1,0:T(8,128)} %get-tuple-element.671) | copy-start | bytes 884740 | tf_op jit(solution)/shard_map/while
  217.3 14.8 %copy-start.20 = (f32[2,384]{1,0:T(2,128)S(1)}, f32[2,384]{1,0:T(2,128)}, u32[]{:S(2)}) copy-start(f32[2,384]{1,0:T(2,128)} %get-tuple-element.670) | copy-start | bytes 9220 | tf_op jit(solution)/shard_map/while
  232.7 8.2 %copy-start.7 = (f32[2,96,384]{2,1,0:T(8,128)S(1)}, f32[2,96,384]{2,1,0:T(8,128)}, u32[]{:S(2)}) copy-start(f32[2,96,384]{2,1,0:T(8,128)} %get-tuple-element.686) | copy-start | bytes 884740 | tf_op jit(solution)/shard_map/while
  232.7 8.2 %copy-start.18 = (f32[2,96,384]{2,1,0:T(8,128)S(1)}, f32[2,96,384]{2,1,0:T(8,128)}, u32[]{:S(2)}) copy-start(f32[2,96,384]{2,1,0:T(8,128)} %get-tuple-element.671) | copy-start | bytes 884740 | tf_op jit(solution)/shard_map/while
  233.2 8.9 %copy-start.20 = (f32[2,384]{1,0:T(2,128)S(1)}, f32[2,384]{1,0:T(2,128)}, u32[]{:S(2)}) copy-start(f32[2,384]{1,0:T(2,128)} %get-tuple-element.670) | copy-start | bytes 9220 | tf_op jit(solution)/shard_map/while
  (19 other events, 27.1 us)
Sparse Core Ops, SparseCore 0:
  20.9 17.8 all-gather.1
where the time goes:
time: 253 us; the launch traced here: 250 us
  waiting for transfers between devices  90.6 us (36%)
  blocking collectives  61.3 us (24%)
  matrix products  47.1 us (19%)
  starting transfers between devices  18.1 us (7%)
  between operations  14.2 us (6%)
  other arithmetic  13.4 us (5%)
  local copies, waits for them, and re-layouts  3.97 us (2%)
    ppermute x14, waiting for transfers between devices, passed_along(): return lax.ppermute(block, axis, route)  81.6 us
    dot_general x40, matrix products, product(): jnp.dot(left, right, precision=precise, preferred_element_type=jnp.float32)  44.2 us
    all_gather x4, blocking collectives, sandwich(): half_full = lax.all_gather(half_rows, 'col', axis=0, tiled=True)  36.5 us
    ppermute x14, starting transfers between devices, passed_along(): return lax.ppermute(block, axis, route)  18.1 us
    all_gather x1, waiting for transfers between devices, per_device(): step_full = lax.all_gather(step_rows, 'col', axis=1, tiled=True)  8.94 us
    all_gather x1, blocking collectives, per_device(): lax.all_gather(total_noise, 'col', axis=0, tiled=True)  8.86 us
    all_gather x1, blocking collectives, per_device(): corr_full = lax.all_gather(corr_rows, 'col', axis=0, tiled=True)  8.05 us
    select_n x7, other arithmetic, turn(): jnp.where(is_first, prior_covar, recv_covar)  7.9 us
  transfers between devices with their start and end apart: 15, of which 8 were waited for; matrix products, arithmetic and copies ran while one was open for 7% of the time, Pallas kernels for 0%

commit v1 on v0

v1 whole, which is shorter than its diff:
```python
import jax
import jax.numpy as jnp
from jax import lax
from jax.sharding import PartitionSpec as P

three_pass = lax.Precision.HIGH


def dot_nn(left, right):
    return lax.dot_general(
        left,
        right,
        (((1,), (0,)), ((), ())),
        precision=three_pass,
        preferred_element_type=jnp.float32,
    )


def dot_nt(left, right):
    return lax.dot_general(
        left,
        right,
        (((1,), (1,)), ((), ())),
        precision=three_pass,
        preferred_element_type=jnp.float32,
    )


def sandwich(step, covar):
    return dot_nt(dot_nn(step, covar), step)


def swapped(block, axis, bit):
    return lax.ppermute(block, axis, [(i, i ^ bit) for i in range(lax.axis_size(axis))])


def shifted(block, axis, distance):
    size = lax.axis_size(axis)
    return lax.ppermute(block, axis, [(i, i + distance) for i in range(size - distance)])


def in_order(blocks, offsets, me):
    stacked = jnp.stack(blocks)
    inverse = {offset: at for at, offset in enumerate(offsets)}
    table = jnp.array([inverse[offset] for offset in range(len(offsets))])
    ordered = [
        lax.dynamic_index_in_dim(stacked, table[device ^ me], 0, keepdims=False)
        for device in range(len(offsets))
    ]
    return jnp.concatenate(ordered, axis=-2)


def per_device(
    model_mixing,
    retention,
    forcing,
    observations,
    model_noise,
    obs_noise,
    gain,
    obs_operator_t,
    prior_mean,
    prior_factor,
):
    steps, width, states = model_mixing.shape
    n_col, n_seg = lax.axis_size("col"), lax.axis_size("seg")
    col, seg = lax.axis_index("col"), lax.axis_index("seg")
    core = col % 2
    far_bits = []
    bit = n_col // 2
    while bit > 1:
        far_bits.append(bit)
        bit //= 2

    own = [model_mixing]
    for bit in far_bits:
        own = own + [swapped(b, "col", bit) for b in own]
    offsets = [0]
    for bit in far_bits:
        offsets = offsets + [o ^ bit for o in offsets]
    near = swapped(model_mixing, "seg", 1)
    vectors = jnp.concatenate([retention, model_noise, forcing, observations], axis=1)
    vectors_other = swapped(vectors, "seg", 1)

    row_ids = lax.broadcasted_iota(jnp.int32, (width, states), 0) + col * width
    col_ids = lax.broadcasted_iota(jnp.int32, (width, states), 1)
    corr_rows = (row_ids == col_ids).astype(jnp.float32) - dot_nt(obs_operator_t, gain)
    corr = [corr_rows]
    for bit in far_bits:
        corr = corr + [swapped(b, "col", bit) for b in corr]

    other_first = [near[:1]] + [swapped(b[:1], "seg", 1) for b in own[1:]]
    other_rest = [near[1:]]
    for bit in far_bits:
        other_rest = other_rest + [swapped(b, "col", bit) for b in other_rest]
    other = [jnp.concatenate(pair, axis=0) for pair in zip(other_first, other_rest)]

    def over_core(blocks):
        both = swapped(jnp.stack(blocks), "col", 1)
        return blocks + [both[i] for i in range(len(blocks))]

    offsets_all = offsets + [o ^ 1 for o in offsets]
    own_full = in_order(over_core(own), offsets_all, col)
    corr_t = in_order(over_core(corr), offsets_all, col)
    other_full = in_order(over_core(other), offsets_all, col)

    correction = corr_t.T
    fixed_noise = dot_nt(gain * obs_noise[None, :], gain)
    prior_covar = dot_nt(prior_factor, prior_factor)

    is_second = seg % 2 == 1
    is_first_group = seg < 2
    mixing_first = jnp.where(is_second, other_full, own_full)
    mixing_second = jnp.where(is_second, own_full, other_full)
    vectors_first = jnp.where(is_second, vectors_other, vectors)
    vectors_second = jnp.where(is_second, vectors, vectors_other)
    mixing = jnp.concatenate([mixing_first, mixing_second], axis=0)
    packed = jnp.concatenate([vectors_first, vectors_second], axis=0)
    keep, noise_var, push, seen = jnp.split(packed, [states, 2 * states, 3 * states], axis=1)
    eye = jnp.eye(states, dtype=jnp.float32)
    offset_each = dot_nt(push, correction) + dot_nt(seen, gain)

    total_covar = jnp.where(is_first_group, prior_covar, 0.0)
    total_mean = jnp.where(is_first_group, prior_mean, 0.0)[None, :]
    total_step = None
    marks = []
    for k in range(2 * steps):
        step = dot_nt(correction, mixing[k] + keep[k][:, None] * eye)
        noise = dot_nt(correction * noise_var[k][None, :], correction) + fixed_noise
        total_covar = sandwich(step, total_covar) + noise
        total_mean = dot_nt(total_mean, step) + offset_each[k][None, :]
        total_step = step if total_step is None else dot_nn(step, total_step)
        marks.append((total_step, total_mean, total_covar))

    half = states // 2
    pad = jnp.zeros((7, states), jnp.float32)

    def carried_along(matrix, vector, distance):
        part = lax.dynamic_slice_in_dim(matrix, core * half, half, 0)
        if vector is not None:
            part = jnp.concatenate([part, vector, pad], axis=0)
        came = shifted(part, "seg", distance)
        swap = swapped(came[:half], "col", 1)
        low = jnp.where(core == 0, came[:half], swap)
        high = jnp.where(core == 0, swap, came[:half])
        full = jnp.concatenate([low, high], axis=0)
        return full, (came[half : half + 1] if vector is not None else None)

    entry_covar, entry_mean = carried_along(total_covar, total_mean, 2)
    distance = 4
    entry_step = None
    if distance < n_seg:
        entry_step, ignored = carried_along(total_step, None, 2)
    while distance < n_seg:
        sent_covar = sandwich(total_step, entry_covar) + total_covar
        sent_mean = dot_nt(entry_mean, total_step) + total_mean
        came_covar, came_mean = carried_along(sent_covar, sent_mean, distance)
        if 2 * distance < n_seg:
            sent_step = dot_nn(total_step, entry_step)
            came_step, ignored = carried_along(sent_step, None, distance)
        entry_covar = sandwich(entry_step, came_covar) + entry_covar
        entry_mean = dot_nt(came_mean, entry_step) + entry_mean
        if 2 * distance < n_seg:
            entry_step = dot_nn(entry_step, came_step)
        distance *= 2

    means, covars = [], []
    for k in range(steps):
        step = jnp.where(is_second, marks[steps + k][0], marks[k][0])
        mean = jnp.where(is_second, marks[steps + k][1], marks[k][1])
        covar = jnp.where(is_second, marks[steps + k][2], marks[k][2])
        rows = lax.dynamic_slice_in_dim(step, col * width, width, 0)
        covar_rows = lax.dynamic_slice_in_dim(covar, col * width, width, 0)
        means.append(dot_nt(entry_mean, step) + mean)
        covars.append(dot_nt(dot_nn(rows, entry_covar), step) + covar_rows)
    return jnp.concatenate(means, axis=0), jnp.stack(covars)


def solution(mesh):
    in_specs = (
        P("seg", "col", None),
        P("seg", None),
        P("seg", None),
        P("seg", None),
        P("seg", None),
        P(),
        P(),
        P("col", None),
        P(),
        P(),
    )
    out_specs = (P("seg", None), P("seg", "col", None))
    return jax.shard_map(
        per_device, mesh=mesh, in_specs=in_specs, out_specs=out_specs, check_vma=False
    )
```

time: 253 us -> 98.3 us (0.39)
  waiting for transfers between devices: 90.6 us -> 25.7 us
  blocking collectives: 61.3 us -> 0 us
  matrix products: 47.1 us -> 32.9 us
  other arithmetic: 13.4 us -> 7.62 us
  between operations: 14.2 us -> 9.15 us
    all_gather x7 -> x0, blocking collectives: 61.3 us -> none  [the longest x4 36.5 us: sandwich(): half_full = lax.all_gather(half_rows, 'col', axis=0, tiled=True)]
    ppermute x14 -> x15, waiting for transfers between devices: 81.6 us -> 25.7 us  [the longest x3 25.7 us: shifted(): lax.ppermute(block, axis, [(i, i + distance) for i in range(size - distan...]
    dot_general x42 -> x40, matrix products: 47.1 us -> 32.9 us  [the longest x29 25.8 us: dot_nt(): lax.dot_general(left, right, (((1,), (1,)), ((), ())), precision=three_pa...]
    select_n x14 -> x6, other arithmetic: 12.6 us -> 3.16 us  [the longest x3 2.26 us: carried_along(): low = jnp.where(core == 0, came[:half], swap)]
    all_gather x1 -> x0, waiting for transfers between devices: 8.94 us -> none  [per_device(): step_full = lax.all_gather(step_rows, 'col', axis=1, tiled=True)]
    another operation x0 -> x8, other arithmetic: none -> 2.89 us  [the longest x4 1.13 us: in_order(): stacked = jnp.stack(blocks)]
    ppermute x14 -> x15, starting transfers between devices: 18.1 us -> 16.5 us  [the longest x12 12.5 us: swapped(): lax.ppermute(block, axis, [(i, i ^ bit) for i in range(lax.axis_size(axis...]
  transfers between devices with their start and end apart: 15 -> 15, of which waited for: 8 -> 3; matrix products, arithmetic and copies ran while one was open for 7% -> 26% of each run, Pallas kernels for 0% -> 0%
where the time goes in v1:
time: 98.3 us; the launch traced here: 96.6 us
  matrix products  32.9 us (33%)
  waiting for transfers between devices  25.7 us (26%)
  starting transfers between devices  16.5 us (17%)
  between operations  9.15 us (9%)
  other arithmetic  7.62 us (8%)
  local copies, waits for them, and re-layouts  4.63 us (5%)
    dot_general x29, matrix products, dot_nt(): lax.dot_general(left, right, (((1,), (1,)), ((), ())), precision=three_pa...  25.8 us
    ppermute x3, waiting for transfers between devices, shifted(): lax.ppermute(block, axis, [(i, i + distance) for i in range(size - distan...  25.7 us
    ppermute x12, starting transfers between devices, swapped(): lax.ppermute(block, axis, [(i, i ^ bit) for i in range(lax.axis_size(axis...  12.5 us
    dot_general x11, matrix products, dot_nn(): lax.dot_general(left, right, (((1,), (0,)), ((), ())), precision=three_pa...  7.11 us
    ppermute x3, starting transfers between devices, shifted(): lax.ppermute(block, axis, [(i, i + distance) for i in range(size - distan...  4.07 us
    select_n x3, other arithmetic, carried_along(): low = jnp.where(core == 0, came[:half], swap)  2.26 us
  transfers between devices with their start and end apart: 15, of which 3 were waited for; matrix products, arithmetic and copies ran while one was open for 26% of the time, Pallas kernels for 0%

profile of v1, /device:TPU:29, one launch (start us, length us, event | category | flops | bytes accessed | tf_op | source)
XLA Modules:
  0.0 96.6 jit_solution(3330410547445169971)
XLA Ops:
  0.7 1.3 %collective-permute-start.2 = (f32[2,96,384]{2,1,0:T(8,128)}, f32[2,96,384]{2,1,0:T(8,128)S(1)}, u32[]{:S(2)}, u32[]{:S(2)}) collective-permute-start(f32[2,96,384]{2,1,0:T(8,128)} %param.13), channel_id=1, source_target_pairs={{0,2},{1,3},{2,0},{3,1},{4,6},{5,7},{6,4},{7,5},{8,10},{9,11},{10,... | collective-permute-start | bytes 884744 | tf_op jit(solution)/shard_map/ppermute | solution.py:34
  2.2 2.4 %convolution_subtract_fusion = f32[96,384]{1,0:T(8,128)S(1)} fusion(f32[96,1024]{1,0:T(8,128)} %param.20, f32[384,1024]{1,0:T(8,128)} %param.19, s32[96]{0:T(128)S(1)} %iota_add_fusion), kind=kOutput, calls=%fused_computation.20 | convolution fusion | flops 226603008 | bytes 2113920 | tf_op jit(solution)/shard_map/dot_general | solution.py:20
  5.0 1.3 %collective-permute-start.8 = (f32[2,2176]{1,0:T(2,128)S(1)}, f32[2,2176]{1,0:T(2,128)}, u32[]{:S(2)}, u32[]{:S(2)}) collective-permute-start(f32[2,2176]{1,0:T(2,128)S(1)} %constant_dynamic-update-slice_fusion), channel_id=1, source_target_pairs={{0,4},{4,0},{8,12},{12,8},{16,20},{20,16},{24,28},{28,24},{1,5},{5... | collective-permute-start | bytes 52232 | tf_op jit(solution)/shard_map/ppermute | solution.py:34
  6.3 2.2 %fusion = f32[384,384]{1,0:T(8,128)} fusion(f32[384,1024]{1,0:T(8,128)S(1)} %copy-done.1, f32[1024]{0:T(1024)S(1)} %copy-done.21), kind=kOutput, calls=%fused_computation | convolution fusion | flops 906362880 | bytes 2166784 | tf_op jit(solution)/shard_map/dot_general | solution.py:20
  20.3 1.2 %collective-permute-start.6 = (f32[1,96,384]{2,1,0:T(8,128)S(1)}, f32[1,96,384]{2,1,0:T(8,128)S(1)}, u32[]{:S(2)}, u32[]{:S(2)}) collective-permute-start(f32[1,96,384]{2,1,0:T(8,128)S(1)} %slice.120), channel_id=1, source_target_pairs={{0,2},{1,3},{2,0},{3,1},{4,6},{5,7},{6,4},{7,5},{8,10},{9,11},{10,... | collective-permute-start | bytes 442376 | tf_op jit(solution)/shard_map/ppermute | solution.py:34
  21.6 0.9 pad_maximum_fusion.14
  22.5 2.4 %collective-permute-start.1 = (f32[2,96,384]{2,1,0:T(8,128)S(1)}, f32[2,96,384]{2,1,0:T(8,128)S(1)}, u32[]{:S(2)}, u32[]{:S(2)}) collective-permute-start(f32[2,96,384]{2,1,0:T(8,128)S(1)} %pad_maximum_fusion.14), channel_id=1, source_target_pairs={{0,1},{1,0},{2,3},{3,2},{4,5},{5,4},{6,7},{7,6},{8,9},{9,8},{10,11... | collective-permute-start | bytes 884744 | tf_op jit(solution)/shard_map/ppermute | solution.py:34
  25.2 2.6 %collective-permute-start.7 = (f32[2,2,96,384]{3,2,1,0:T(8,128)S(1)}, f32[2,2,96,384]{3,2,1,0:T(8,128)S(1)}, u32[]{:S(2)}, u32[]{:S(2)}) collective-permute-start(f32[2,2,96,384]{3,2,1,0:T(8,128)S(1)} %pad_maximum_fusion.7), channel_id=1, source_target_pairs={{0,1},{1,0},{2,3},{3,2},{4,5},{5,4},{6,7},{7,6},{8,9},{9,8},{10,11... | collective-permute-start | bytes 1769480 | tf_op jit(solution)/shard_map/ppermute | solution.py:34
  27.7 1.0 pad_maximum_fusion.4
  28.8 0.8 convolution_add_fusion.7
  29.6 0.8 convolution_add_fusion.5
  30.4 0.8 convolution_add_fusion.3
  31.6 0.8 convolution_add_fusion.1
  33.0 1.2 %fusion.13 = f32[384,384]{1,0:T(8,128)S(1)} fusion(f32[2,384,384]{2,1,0:T(8,128)S(1)} %get-tuple-element.10, f32[384]{0:T(512)S(1)} %get-tuple-element.41, f32[96,384]{1,0:T(8,128)S(1)} %get-tuple-element.27, f32[96,384]{1,0:T(8,128)S(1)} %get-tuple-element.28, f32[96,384]{1,0:T(8,128)S(1)} %get-tuple-element.29, f32[96,384]{1,0:T(8,128)S(1)} %get-tuple-element.26), kind=kOutput, calls=%fused_computation.36 | convolution fusion | flops 340623360 | bytes 1771520 | tf_op jit(solution)/shard_map/dot_general | solution.py:20
  34.2 1.2 %fusion.16 = f32[384,384]{1,0:T(8,128)S(1)} fusion(f32[2,384,384]{2,1,0:T(8,128)S(1)} %get-tuple-element.10, f32[384]{0:T(512)S(1)} %get-tuple-element.40, f32[96,384]{1,0:T(8,128)S(1)} %get-tuple-element.27, f32[96,384]{1,0:T(8,128)S(1)} %get-tuple-element.28, f32[96,384]{1,0:T(8,128)S(1)} %get-tuple-element.29, f32[96,384]{1,0:T(8,128)S(1)} %get-tuple-element.26), kind=kOutput, calls=%fused_computation.39 | convolution fusion | flops 340623360 | bytes 1771520 | tf_op jit(solution)/shard_map/dot_general | solution.py:20
  36.0 0.9 fusion.81
  38.4 1.2 %fusion.19 = f32[384,384]{1,0:T(8,128)S(1)} fusion(f32[2,384,384]{2,1,0:T(8,128)S(1)} %get-tuple-element.11, f32[384]{0:T(512)S(1)} %get-tuple-element.8, f32[96,384]{1,0:T(8,128)S(1)} %get-tuple-element.27, f32[96,384]{1,0:T(8,128)S(1)} %get-tuple-element.28, f32[96,384]{1,0:T(8,128)S(1)} %get-tuple-element.29, f32[96,384]{1,0:T(8,128)S(1)} %get-tuple-element.26), kind=kOutput, calls=%fused_computation.42 | convolution fusion | flops 340623360 | bytes 1771520 | tf_op jit(solution)/shard_map/dot_general | solution.py:20
  39.6 1.2 %fusion.22 = f32[384,384]{1,0:T(8,128)S(1)} fusion(f32[2,384,384]{2,1,0:T(8,128)S(1)} %get-tuple-element.11, f32[384]{0:T(512)S(1)} %get-tuple-element.9, f32[96,384]{1,0:T(8,128)S(1)} %get-tuple-element.27, f32[96,384]{1,0:T(8,128)S(1)} %get-tuple-element.28, f32[96,384]{1,0:T(8,128)S(1)} %get-tuple-element.29, f32[96,384]{1,0:T(8,128)S(1)} %get-tuple-element.26), kind=kOutput, calls=%fused_computation.45 | convolution fusion | flops 340623360 | bytes 1771520 | tf_op jit(solution)/shard_map/dot_general | solution.py:20
  46.1 1.3 %collective-permute-start.9 = (f32[200,384]{1,0:T(8,128)S(1)}, f32[200,384]{1,0:T(8,128)S(1)}, u32[]{:S(2)}, u32[]{:S(2)}) collective-permute-start(f32[200,384]{1,0:T(8,128)S(1)} %maximum_maximum_fusion), channel_id=1, source_target_pairs={{0,8},{4,12},{8,16},{12,20},{16,24},{20,28},{1,9},{5,13},{9,17},{1... | collective-permute-start | bytes 921608 | tf_op jit(solution)/shard_map/ppermute | solution.py:39
  49.6 1.5 %collective-permute-start.12 = (f32[192,384]{1,0:T(8,128)}, f32[192,384]{1,0:T(8,128)}, u32[]{:S(2)}, u32[]{:S(2)}) collective-permute-start(f32[192,384]{1,0:T(8,128)} %constant_dynamic-slice_fusion.1), channel_id=1, source_target_pairs={{0,8},{4,12},{8,16},{12,20},{16,24},{20,28},{1,9},{5,13},{9,17},{1... | collective-permute-start | bytes 884744 | tf_op jit(solution)/shard_map/ppermute | solution.py:39
  51.1 5.8 %collective-permute-done.9 = f32[200,384]{1,0:T(8,128)S(1)} collective-permute-done((f32[200,384]{1,0:T(8,128)S(1)}, f32[200,384]{1,0:T(8,128)S(1)}, u32[]{:S(2)}, u32[]{:S(2)}) %collective-permute-start.9) | collective-permute-done | bytes 307232 | tf_op jit(solution)/shard_map/ppermute | solution.py:39
  58.3 1.3 %collective-permute-start.10 = (f32[192,384]{1,0:T(8,128)}, f32[192,384]{1,0:T(8,128)}, u32[]{:S(2)}, u32[]{:S(2)}) collective-permute-start(f32[192,384]{1,0:T(8,128)} %slice.137), channel_id=1, source_target_pairs={{0,1},{1,0},{2,3},{3,2},{4,5},{5,4},{6,7},{7,6},{8,9},{9,8},{10,11... | collective-permute-start | bytes 884744 | tf_op jit(solution)/shard_map/ppermute | solution.py:34
  59.6 3.7 %collective-permute-done.12 = f32[192,384]{1,0:T(8,128)} collective-permute-done((f32[192,384]{1,0:T(8,128)}, f32[192,384]{1,0:T(8,128)}, u32[]{:S(2)}, u32[]{:S(2)}) %collective-permute-start.12) | collective-permute-done | bytes 294944 | tf_op jit(solution)/shard_map/ppermute | solution.py:39
  63.2 0.9 collective-permute-start.13
  64.1 1.1 %convolution_add_fusion.15 = f32[1,384]{1,0:T(1,128)S(1)} fusion(f32[1,384]{1,0:T(1,128)S(1)} %slice_add_fusion, f32[384,384]{1,0:T(8,128)S(1)} %get-tuple-element.37, f32[200,384]{1,0:T(8,128)} %copy-done.9), kind=kOutput, calls=%fused_computation.26 | convolution fusion | flops 885120 | bytes 594432 | tf_op jit(solution)/shard_map/dot_general | solution.py:20
  65.2 1.1 %broadcast_select_fusion.7 = (f32[192,384]{1,0:T(8,128)S(1)}, f32[192,384]{1,0:T(8,128)S(1)}) fusion(f32[192,384]{1,0:T(8,128)} %collective-permute-done.10, pred[]{:T(512)S(6)} %eq.29, f32[200,384]{1,0:T(8,128)} %copy-done.9), kind=kLoop, calls=%fused_computation.106 | loop fusion | flops 147456 | bytes 1179649 | tf_op jit(solution)/shard_map/jit(_where)/select_n | solution.py:144
  69.0 1.3 %collective-permute-start.11 = (f32[200,384]{1,0:T(8,128)}, f32[200,384]{1,0:T(8,128)S(1)}, u32[]{:S(2)}, u32[]{:S(2)}) collective-permute-start(f32[200,384]{1,0:T(8,128)} %maximum_maximum_fusion.1), channel_id=1, source_target_pairs={{0,16},{4,20},{8,24},{12,28},{1,17},{5,21},{9,25},{13,29},{2,18},{... | collective-permute-start | bytes 921608 | tf_op jit(solution)/shard_map/ppermute | solution.py:39
  70.3 1.1 %broadcast_select_fusion.5 = (f32[192,384]{1,0:T(8,128)S(1)}, f32[192,384]{1,0:T(8,128)S(1)}) fusion(f32[192,384]{1,0:T(8,128)} %collective-permute-done.12, f32[192,384]{1,0:T(8,128)} %collective-permute-done.13, pred[]{:T(512)S(6)} %eq.29), kind=kLoop, calls=%fused_computation.104 | loop fusion | flops 147456 | bytes 1179649 | tf_op jit(solution)/shard_map/jit(_where)/select_n | solution.py:144
  71.4 16.3 %collective-permute-done.11 = f32[200,384]{1,0:T(8,128)S(1)} collective-permute-done((f32[200,384]{1,0:T(8,128)}, f32[200,384]{1,0:T(8,128)S(1)}, u32[]{:S(2)}, u32[]{:S(2)}) %collective-permute-start.11) | collective-permute-done | bytes 307232 | tf_op jit(solution)/shard_map/ppermute | solution.py:39
  88.2 1.1 %fusion.4 = f32[384,1]{0,1:T(1,128)S(1)} fusion(f32[192,384]{1,0:T(8,128)S(1)} %get-tuple-element.25, f32[192,384]{1,0:T(8,128)S(1)} %get-tuple-element.24, f32[200,384]{1,0:T(8,128)S(1)} %collective-permute-done.11, f32[200,384]{1,0:T(8,128)} %copy-done.9), kind=kOutput, calls=%fused_computation.25 | convolution fusion | flops 1032576 | bytes 594432 | tf_op jit(solution)/shard_map/dot_general | solution.py:20
  93.2 1.3 %fusion.3 = f32[1,96,384]{2,1,0:T(8,128)S(1)} fusion(f32[96,384]{1,0:T(8,128)S(1)} %fusion.47, f32[384,384]{1,0:T(8,128)S(1)} %get-tuple-element.38, f32[384,384]{1,0:T(8,128)S(1)} %convolution_add_fusion.8, s32[]{:T(128)S(6)} %select_n.220, f32[384,384]{1,0:T(8,128)} %copy-done.2, pred[]{:T(512)S(6)} %eq.27), kind=kOutput, calls=%fused_computation.19 | convolution fusion | flops 85008384 | bytes 1179653 | tf_op jit(solution)/shard_map/dot_general | solution.py:20
  94.5 1.3 %fusion.2 = f32[1,96,384]{2,1,0:T(8,128)S(1)} fusion(f32[96,384]{1,0:T(8,128)S(1)} %fusion.45, f32[384,384]{1,0:T(8,128)S(1)} %get-tuple-element.36, f32[384,384]{1,0:T(8,128)S(1)} %convolution_add_fusion.6, s32[]{:T(128)S(6)} %select_n.220, f32[384,384]{1,0:T(8,128)} %copy-done.3, pred[]{:T(512)S(6)} %eq.27), kind=kOutput, calls=%fused_computation.17 | convolution fusion | flops 85008384 | bytes 1179653 | tf_op jit(solution)/shard_map/dot_general | solution.py:20
  (127 shorter events, 24.2 us)
Async XLA Ops:
  0.6 7.9 %copy-start = (f32[384,384]{1,0:T(8,128)S(1)}, f32[384,384]{1,0:T(8,128)}, u32[]{:S(2)}) copy-start(f32[384,384]{1,0:T(8,128)} %param.22) | copy-start | bytes 1769476
  0.6 5.6 %copy-start.1 = (f32[384,1024]{1,0:T(8,128)S(1)}, f32[384,1024]{1,0:T(8,128)}, u32[]{:S(2)}) copy-start(f32[384,1024]{1,0:T(8,128)} %param.19) | copy-start | bytes 4718596
  0.7 4.3 %copy-start.22 = (f32[2,384]{1,0:T(2,128)S(1)}, f32[2,384]{1,0:T(2,128)}, u32[]{:S(2)}) copy-start(f32[2,384]{1,0:T(2,128)} %param.14) | copy-start | bytes 9220
  0.7 4.3 %copy-start.23 = (f32[2,384]{1,0:T(2,128)S(1)}, f32[2,384]{1,0:T(2,128)}, u32[]{:S(2)}) copy-start(f32[2,384]{1,0:T(2,128)} %param.17) | copy-start | bytes 9220
  0.7 4.3 %copy-start.24 = (f32[2,384]{1,0:T(2,128)S(1)}, f32[2,384]{1,0:T(2,128)}, u32[]{:S(2)}) copy-start(f32[2,384]{1,0:T(2,128)} %param.15) | copy-start | bytes 9220
  0.7 4.3 %copy-start.19 = (f32[2,1024]{1,0:T(2,128)S(1)}, f32[2,1024]{1,0:T(2,128)}, u32[]{:S(2)}) copy-start(f32[2,1024]{1,0:T(2,128)} %param.16) | copy-start | bytes 24580
  0.7 5.6 %copy-start.21 = (f32[1024]{0:T(1024)S(1)}, f32[1024]{0:T(1024)}, u32[]{:S(2)}) copy-start(f32[1024]{0:T(1024)} %param.18) | copy-start | bytes 12292
  0.7 19.3 %collective-permute-start.2 = (f32[2,96,384]{2,1,0:T(8,128)}, f32[2,96,384]{2,1,0:T(8,128)S(1)}, u32[]{:S(2)}, u32[]{:S(2)}) collective-permute-start(f32[2,96,384]{2,1,0:T(8,128)} %param.13), channel_id=1, source_target_pairs={{0,2},{1,3},{2,0},{3,1},{4,6},{5,7},{6,4},{7,5},{8,10},{9,11},{10,... | collective-permute-start | bytes 884744 | tf_op jit(solution)/shard_map/ppermute | solution.py:34
  2.0 18.3 %collective-permute-start.4 = (f32[2,96,384]{2,1,0:T(8,128)}, f32[2,96,384]{2,1,0:T(8,128)S(1)}, u32[]{:S(2)}, u32[]{:S(2)}) collective-permute-start(f32[2,96,384]{2,1,0:T(8,128)} %param.13), channel_id=1, source_target_pairs={{0,4},{4,0},{8,12},{12,8},{16,20},{20,16},{24,28},{28,24},{1,5},{5... | collective-permute-start | bytes 884744 | tf_op jit(solution)/shard_map/ppermute | solution.py:34
  4.6 17.0 %collective-permute-start = (f32[96,384]{1,0:T(8,128)S(1)}, f32[96,384]{1,0:T(8,128)}, u32[]{:S(2)}, u32[]{:S(2)}) collective-permute-start(f32[96,384]{1,0:T(8,128)S(1)} %convolution_subtract_fusion), channel_id=1, source_target_pairs={{0,2},{1,3},{2,0},{3,1},{4,6},{5,7},{6,4},{7,5},{8,10},{9,11},{10,... | collective-permute-start | bytes 442376 | tf_op jit(solution)/shard_map/ppermute | solution.py:34
  5.0 13.4 %collective-permute-start.8 = (f32[2,2176]{1,0:T(2,128)S(1)}, f32[2,2176]{1,0:T(2,128)}, u32[]{:S(2)}, u32[]{:S(2)}) collective-permute-start(f32[2,2176]{1,0:T(2,128)S(1)} %constant_dynamic-update-slice_fusion), channel_id=1, source_target_pairs={{0,4},{4,0},{8,12},{12,8},{16,20},{20,16},{24,28},{28,24},{1,5},{5... | collective-permute-start | bytes 52232 | tf_op jit(solution)/shard_map/ppermute | solution.py:34
  18.4 27.6 %copy-start.16 = (f32[200]{0:T(256)}, f32[200]{0:T(256)S(1)}, u32[]{:S(2)}) copy-start(f32[200]{0:T(256)S(1)} %pad.15.clone) | copy-start | bytes 2404
  19.2 5.8 %copy-start.10 = (f32[2,96,384]{2,1,0:T(8,128)S(1)}, f32[2,96,384]{2,1,0:T(8,128)}, u32[]{:S(2)}) copy-start(f32[2,96,384]{2,1,0:T(8,128)} %param.13) | copy-start | bytes 884740
  20.0 5.1 %collective-permute-start.5 = (f32[1,96,384]{2,1,0:T(8,128)S(1)}, f32[1,96,384]{2,1,0:T(8,128)S(1)}, u32[]{:S(2)}, u32[]{:S(2)}) collective-permute-start(f32[1,96,384]{2,1,0:T(8,128)S(1)} %slice.119), channel_id=1, source_target_pairs={{0,4},{4,0},{8,12},{12,8},{16,20},{20,16},{24,28},{28,24},{1,5},{5... | collective-permute-start | bytes 442376 | tf_op jit(solution)/shard_map/ppermute | solution.py:34
  20.3 4.7 %collective-permute-start.6 = (f32[1,96,384]{2,1,0:T(8,128)S(1)}, f32[1,96,384]{2,1,0:T(8,128)S(1)}, u32[]{:S(2)}, u32[]{:S(2)}) collective-permute-start(f32[1,96,384]{2,1,0:T(8,128)S(1)} %slice.120), channel_id=1, source_target_pairs={{0,2},{1,3},{2,0},{3,1},{4,6},{5,7},{6,4},{7,5},{8,10},{9,11},{10,... | collective-permute-start | bytes 442376 | tf_op jit(solution)/shard_map/ppermute | solution.py:34
  22.5 5.2 %collective-permute-start.1 = (f32[2,96,384]{2,1,0:T(8,128)S(1)}, f32[2,96,384]{2,1,0:T(8,128)S(1)}, u32[]{:S(2)}, u32[]{:S(2)}) collective-permute-start(f32[2,96,384]{2,1,0:T(8,128)S(1)} %pad_maximum_fusion.14), channel_id=1, source_target_pairs={{0,1},{1,0},{2,3},{3,2},{4,5},{5,4},{6,7},{7,6},{8,9},{9,8},{10,11... | collective-permute-start | bytes 884744 | tf_op jit(solution)/shard_map/ppermute | solution.py:34
  25.0 7.4 %collective-permute-start.3 = (f32[2,2,96,384]{3,2,1,0:T(8,128)S(1)}, f32[2,2,96,384]{3,2,1,0:T(8,128)S(1)}, u32[]{:S(2)}, u32[]{:S(2)}) collective-permute-start(f32[2,2,96,384]{3,2,1,0:T(8,128)S(1)} %pad_maximum_fusion.6), channel_id=1, source_target_pairs={{0,1},{1,0},{2,3},{3,2},{4,5},{5,4},{6,7},{7,6},{8,9},{9,8},{10,11... | collective-permute-start | bytes 1769480 | tf_op jit(solution)/shard_map/ppermute | solution.py:34
  25.2 3.6 %copy-start.11 = (f32[384,384]{1,0:T(8,128)S(1)}, f32[384,384]{1,0:T(8,128)}, u32[]{:S(2)}) copy-start(f32[384,384]{1,0:T(8,128)} %fusion) | copy-start | bytes 1769476
  25.2 7.4 %collective-permute-start.7 = (f32[2,2,96,384]{3,2,1,0:T(8,128)S(1)}, f32[2,2,96,384]{3,2,1,0:T(8,128)S(1)}, u32[]{:S(2)}, u32[]{:S(2)}) collective-permute-start(f32[2,2,96,384]{3,2,1,0:T(8,128)S(1)} %pad_maximum_fusion.7), channel_id=1, source_target_pairs={{0,1},{1,0},{2,3},{3,2},{4,5},{5,4},{6,7},{7,6},{8,9},{9,8},{10,11... | collective-permute-start | bytes 1769480 | tf_op jit(solution)/shard_map/ppermute | solution.py:34
  39.6 1.2 %copy-start.20 = (f32[384,1]{0,1:T(1,128)S(1)}, f32[384,1]{0,1:T(1,128)}, u32[]{:S(2)}) copy-start(f32[384,1]{0,1:T(1,128)} %reshape.44) | copy-start | bytes 4612
  43.4 1.5 %copy-start.14 = (f32[1,384]{1,0:T(1,128)}, f32[1,384]{1,0:T(1,128)S(1)}, u32[]{:S(2)}) copy-start(f32[1,384]{1,0:T(1,128)S(1)} %slice_add_fusion.1) | copy-start | bytes 4612
  46.0 2.2 %copy-start.3 = (f32[384,384]{1,0:T(8,128)}, f32[384,384]{1,0:T(8,128)S(1)}, u32[]{:S(2)}) copy-start(f32[384,384]{1,0:T(8,128)S(1)} %convolution_add_fusion.2) | copy-start | bytes 1769476
  46.1 10.7 %collective-permute-start.9 = (f32[200,384]{1,0:T(8,128)S(1)}, f32[200,384]{1,0:T(8,128)S(1)}, u32[]{:S(2)}, u32[]{:S(2)}) collective-permute-start(f32[200,384]{1,0:T(8,128)S(1)} %maximum_maximum_fusion), channel_id=1, source_target_pairs={{0,8},{4,12},{8,16},{12,20},{16,24},{20,28},{1,9},{5,13},{9,17},{1... | collective-permute-start | bytes 921608 | tf_op jit(solution)/shard_map/ppermute | solution.py:39
  49.6 13.7 %collective-permute-start.12 = (f32[192,384]{1,0:T(8,128)}, f32[192,384]{1,0:T(8,128)}, u32[]{:S(2)}, u32[]{:S(2)}) collective-permute-start(f32[192,384]{1,0:T(8,128)} %constant_dynamic-slice_fusion.1), channel_id=1, source_target_pairs={{0,8},{4,12},{8,16},{12,20},{16,24},{20,28},{1,9},{5,13},{9,17},{1... | collective-permute-start | bytes 884744 | tf_op jit(solution)/shard_map/ppermute | solution.py:39
  58.3 6.9 %collective-permute-start.10 = (f32[192,384]{1,0:T(8,128)}, f32[192,384]{1,0:T(8,128)}, u32[]{:S(2)}, u32[]{:S(2)}) collective-permute-start(f32[192,384]{1,0:T(8,128)} %slice.137), channel_id=1, source_target_pairs={{0,1},{1,0},{2,3},{3,2},{4,5},{5,4},{6,7},{7,6},{8,9},{9,8},{10,11... | collective-permute-start | bytes 884744 | tf_op jit(solution)/shard_map/ppermute | solution.py:34
  63.2 7.0 %collective-permute-start.13 = (f32[192,384]{1,0:T(8,128)}, f32[192,384]{1,0:T(8,128)}, u32[]{:S(2)}, u32[]{:S(2)}) collective-permute-start(f32[192,384]{1,0:T(8,128)} %collective-permute-done.12), channel_id=1, source_target_pairs={{0,1},{1,0},{2,3},{3,2},{4,5},{5,4},{6,7},{7,6},{8,9},{9,8},{10,11... | collective-permute-start | bytes 884744 | tf_op jit(solution)/shard_map/ppermute | solution.py:34
  66.3 1.5 %copy-start.5 = (f32[192,384]{1,0:T(8,128)}, f32[192,384]{1,0:T(8,128)S(1)}, u32[]{:S(2)}) copy-start(f32[192,384]{1,0:T(8,128)S(1)} %get-tuple-element.22) | copy-start | bytes 884740
  66.3 1.5 %copy-start.7 = (f32[192,384]{1,0:T(8,128)}, f32[192,384]{1,0:T(8,128)S(1)}, u32[]{:S(2)}) copy-start(f32[192,384]{1,0:T(8,128)S(1)} %get-tuple-element.23) | copy-start | bytes 884740
  69.0 18.7 %collective-permute-start.11 = (f32[200,384]{1,0:T(8,128)}, f32[200,384]{1,0:T(8,128)S(1)}, u32[]{:S(2)}, u32[]{:S(2)}) collective-permute-start(f32[200,384]{1,0:T(8,128)} %maximum_maximum_fusion.1), channel_id=1, source_target_pairs={{0,16},{4,20},{8,24},{12,28},{1,17},{5,21},{9,25},{13,29},{2,18},{... | collective-permute-start | bytes 921608 | tf_op jit(solution)/shard_map/ppermute | solution.py:39
  70.3 19.0 %copy-start.15 = (f32[1,384]{1,0:T(1,128)S(1)}, f32[1,384]{1,0:T(1,128)}, u32[]{:S(2)}) copy-start(f32[1,384]{1,0:T(1,128)} %copy-done.14) | copy-start | bytes 4612
  71.4 18.3 %copy-start.13 = (f32[1,384]{1,0:T(1,128)S(1)}, f32[1,384]{1,0:T(1,128)}, u32[]{:S(2)}) copy-start(f32[1,384]{1,0:T(1,128)} %copy-done.12) | copy-start | bytes 4612
  87.7 3.0 %collective-permute-start.14 = (f32[192,384]{1,0:T(8,128)S(1)}, f32[192,384]{1,0:T(8,128)S(1)}, u32[]{:S(2)}, u32[]{:S(2)}) collective-permute-start(f32[192,384]{1,0:T(8,128)S(1)} %slice.140), channel_id=1, source_target_pairs={{0,1},{1,0},{2,3},{3,2},{4,5},{5,4},{6,7},{7,6},{8,9},{9,8},{10,11... | collective-permute-start | bytes 884744 | tf_op jit(solution)/shard_map/ppermute | solution.py:34
  (9 other events, 8.6 us)

commit v2 on v1

v2 whole, which is shorter than its diff:
```python
import functools

import jax
import jax.numpy as jnp
from jax import lax
from jax.experimental import pallas as pl
from jax.experimental.pallas import tpu as pltpu
from jax.sharding import PartitionSpec as P

F32, BF16 = jnp.float32, jnp.bfloat16
NN = (((1,), (0,)), ((), ()))
NT = (((1,), (1,)), ((), ()))
MEAN_ROWS = 16


def parts(x):
    high = x.astype(BF16)
    return high, (x - high.astype(F32)).astype(BF16)


def as_left(x):
    high, low = parts(x)
    return jnp.concatenate([high, high, low], axis=1)


def as_right(x, axis):
    high, low = parts(x)
    return jnp.concatenate([high, low, high], axis=axis)


def dot_nn(left, right):
    return lax.dot_general(as_left(left), as_right(right, 0), NN, preferred_element_type=F32)


def dot_nt(left, right):
    return lax.dot_general(as_left(left), as_right(right, 1), NT, preferred_element_type=F32)


def square(step, covar, mean):
    rows = covar.shape[0]
    both = dot_nt(jnp.concatenate([dot_nn(step, covar), mean], axis=0), step)
    return both[:rows], both[rows:]


def mean_block(row, states):
    return jnp.broadcast_to(row, (MEAN_ROWS, states))


def local_call(body, outs, *operands, scratch=(), products=1.0):
    states = outs[0][-1]
    shapes = [jax.ShapeDtypeStruct(shape, F32) for shape in outs]
    return pl.pallas_call(
        body,
        out_shape=shapes,
        scratch_shapes=[pltpu.VMEM(shape, F32) for shape in scratch],
        compiler_params=pltpu.CompilerParams(vmem_limit_bytes=36 * 2**20),
        cost_estimate=pl.CostEstimate(
            flops=int(products * 6 * 384**3), bytes_accessed=4 * states, transcendentals=0
        ),
    )(*operands)


def correction_rows(oper_ref, gain_ref, out_ref):
    width, states = out_ref.shape
    rows = lax.broadcasted_iota(jnp.int32, (width, states), 0) + lax.axis_index("col") * width
    cols = lax.broadcasted_iota(jnp.int32, (width, states), 1)
    out_ref[...] = (rows == cols).astype(F32) - dot_nt(oper_ref[...], gain_ref[...])


def fixed_parts(gain_ref, noise_ref, factor_ref, seen_ref, fixed_ref, prior_ref, pushed_ref):
    states = gain_ref.shape[0]
    gain = gain_ref[...]
    both = dot_nt(jnp.concatenate([gain * noise_ref[...], seen_ref[...]], axis=0), gain)
    fixed_ref[...] = both[:states]
    pushed_ref[...] = both[states:]
    first = (lax.axis_index("seg") < 2).astype(F32)
    prior_ref[...] = dot_nt(factor_ref[...], factor_ref[...]) * first


def place(pieces, offsets, out_ref, base):
    me = lax.axis_index("col")
    width = pieces[0].shape[-2]
    for piece, offset in zip(pieces, offsets):
        at = pl.multiple_of((me ^ offset) * width + base, 8)
        out_ref[pl.ds(at, width), :] = piece


def noises(offsets, vec_ref, pushed_ref, fixed_ref, *refs):
    pieces, (corr_ref, noise_ref, offset_ref, work_ref) = refs[:-4], refs[-4:]
    states = corr_ref.shape[0]
    every = vec_ref.shape[0]
    place([p[...] for p in pieces], offsets, work_ref, 0)
    corr = work_ref[...].T
    corr_ref[...] = corr
    right = as_right(corr, 1)
    push = jnp.concatenate(
        [vec_ref[:, 2 * states : 3 * states]] + [jnp.zeros((MEAN_ROWS - every, states), F32)], axis=0
    )
    left = [corr * vec_ref[k : k + 1, states : 2 * states] for k in range(every)] + [push]
    for k in range(every):
        noise = lax.dot_general(as_left(left[k]), right, NT, preferred_element_type=F32)
        noise_ref[k] = noise + fixed_ref[...]
    pushed = lax.dot_general(as_left(push), right, NT, preferred_element_type=F32) + pushed_ref[...]
    for k in range(every):
        offset_ref[k] = mean_block(pushed[k : k + 1], states)


def step_matrices(pieces, offsets, corr, keep_ref, base, work_ref):
    states = corr.shape[0]
    for k, of_step in enumerate(pieces):
        place(of_step, offsets, work_ref, k * states)
    mixed = dot_nt(corr, work_ref[...])
    return [
        mixed[:, k * states : (k + 1) * states] + corr * keep_ref[base + k : base + k + 1, :states]
        for k in range(len(pieces))
    ]


def own_segment(offsets, steps, vec_ref, corr_ref, noise_ref, offset_ref, prior_ref, start_ref, *refs):
    pieces, (psi_ref, covar_ref, mean_ref, work_ref) = refs[:-4], refs[-4:]
    states = corr_ref.shape[0]
    of_steps = [[p[k] for p in pieces] for k in range(steps)]
    matrices = step_matrices(of_steps, offsets, corr_ref[...], vec_ref, 0, work_ref)
    covar_ref[0] = noise_ref[0]
    mean_ref[0] = offset_ref[0]

    @pl.when(lax.axis_index("seg") == 0)
    def _():
        start = mean_block(start_ref[...], states)
        covar, mean = square(matrices[0], prior_ref[...], start)
        covar_ref[0] += covar
        mean_ref[0] += mean

    psi_ref[0] = matrices[0]
    for k in range(1, steps):
        covar, mean = square(matrices[k], covar_ref[k - 1], mean_ref[k - 1])
        covar_ref[k] = covar + noise_ref[k]
        mean_ref[k] = mean + offset_ref[k]
        psi_ref[k] = dot_nn(matrices[k], psi_ref[k - 1])


def put_packed(step_ref, covar, mean, blocks, out_ref):
    states = covar.shape[0]
    edge = states // 3
    core = lax.rem(lax.axis_index("col"), 2)

    @pl.when(core == 0)
    def _():
        rows = step_ref[: 2 * edge, :]
        low = dot_nt(dot_nn(rows, covar), rows)
        out_ref[:edge, :] = low[:edge, :edge] + blocks(0, 0)
        out_ref[edge : 2 * edge, :] = low[edge:, :edge] + blocks(1, 0)
        out_ref[2 * edge : 3 * edge, :] = low[edge:, edge:] + blocks(1, 1)
        out_ref[3 * edge :, :] = jnp.zeros((8, edge), F32)

    @pl.when(core == 1)
    def _():
        rows = step_ref[2 * edge :, :]
        both = dot_nt(jnp.concatenate([dot_nn(rows, covar), mean], axis=0), step_ref[...])
        out_ref[3 * edge :, :] = jnp.zeros((8, edge), F32)
        for j in range(3):
            at = slice(j * edge, (j + 1) * edge)
            out_ref[at, :] = both[:edge, at] + blocks(2, j)
            out_ref[3 * edge + j : 3 * edge + j + 1, :] = both[edge : edge + 1, at] + blocks(3, j)


def unpacked(mine_ref, mate_ref, covar_ref):
    states = covar_ref.shape[0]
    edge = states // 3
    is_low = lax.rem(lax.axis_index("col"), 2) == 0
    low = jnp.where(is_low, mine_ref[...], mate_ref[...])
    high = jnp.where(is_low, mate_ref[...], mine_ref[...])

    def put(i, j, block):
        covar_ref[i * edge : (i + 1) * edge, j * edge : (j + 1) * edge] = block
        if i != j:
            covar_ref[j * edge : (j + 1) * edge, i * edge : (i + 1) * edge] = block.T

    put(0, 0, low[:edge])
    put(1, 0, low[edge : 2 * edge])
    put(1, 1, low[2 * edge : 3 * edge])
    for j in range(3):
        put(2, j, high[j * edge : (j + 1) * edge])
    row = jnp.concatenate([high[3 * edge + j : 3 * edge + j + 1] for j in range(3)], axis=1)
    return mean_block(row, states)


def other_segment(
    offsets, steps, vec_ref, corr_ref, noise_ref, offset_ref, prior_ref, start_ref, psi_ref, covar_ref, mean_ref, *refs
):
    n_piece = len(offsets)
    firsts, rests = refs[:n_piece], refs[n_piece : 2 * n_piece]
    matrix_ref, psi_other_ref, covar_other_ref, mean_other_ref, out_ref, work_ref, after_ref = refs[2 * n_piece :]
    states = corr_ref.shape[0]
    is_second = lax.rem(lax.axis_index("seg"), 2) == 1
    of_steps = [[p[0] for p in firsts]] + [[p[k] for p in rests] for k in range(steps - 1)]
    matrices = step_matrices(of_steps, offsets, corr_ref[...], vec_ref, steps, work_ref)
    for k in range(steps):
        matrix_ref[k] = matrices[k]
    covar_other_ref[...] = noise_ref[steps]
    mean_other_ref[...] = offset_ref[steps]

    @pl.when(lax.axis_index("seg") == 1)
    def _():
        start = mean_block(start_ref[...], states)
        covar, mean = square(matrices[0], prior_ref[...], start)
        covar_other_ref[...] += covar
        mean_other_ref[...] += mean

    for k in range(1, steps):
        covar, mean = square(matrices[k], covar_other_ref[...], mean_other_ref[...])
        covar_other_ref[...] = covar + noise_ref[steps + k]
        mean_other_ref[...] = mean + offset_ref[steps + k]

    @pl.when(is_second)
    def _():
        after_ref[...] = psi_ref[steps - 1]

    @pl.when(jnp.logical_not(is_second))
    def _():
        psi_other_ref[...] = matrices[0]
        for k in range(1, steps):
            psi_other_ref[...] = dot_nn(matrices[k], psi_other_ref[...])
        after_ref[...] = psi_other_ref[...]

    edge = states // 3
    own_covar, own_mean = covar_ref[steps - 1], mean_ref[steps - 1]
    covar = jnp.where(is_second, covar_other_ref[...], own_covar)
    mean = jnp.where(is_second, mean_other_ref[...], own_mean)

    def blocks(i, j):
        at = slice(j * edge, (j + 1) * edge)
        if i == 3:
            return jnp.where(is_second, own_mean[:1, at], mean_other_ref[:1, at])
        rows = slice(i * edge, (i + 1) * edge)
        return jnp.where(is_second, covar_ref[steps - 1, rows, at], covar_other_ref[rows, at])

    put_packed(after_ref, covar, mean, blocks, out_ref)


def pair_elements(steps, width, psi_ref, covar_ref, mean_ref, matrix_ref, psi_other_ref, covar_other_ref, mean_other_ref, *refs):
    psi_out_ref, covar_out_ref, mean_out_ref, psi_all_ref, send_ref = refs
    states = psi_all_ref.shape[0]
    is_second = lax.rem(lax.axis_index("seg"), 2) == 1
    mine = pl.ds(pl.multiple_of(lax.axis_index("col") * width, 8), width)

    @pl.when(is_second)
    def _():
        before = matrix_ref[0]
        for k in range(1, steps):
            before = dot_nn(matrix_ref[k], before)
        covar, mean = covar_other_ref[...], mean_other_ref[...]
        for k in range(steps):
            psi_out_ref[k] = dot_nn(psi_ref[k], before)
            half = dot_nn(psi_ref[k, mine, :], covar)
            both = dot_nt(jnp.concatenate([half, mean], axis=0), psi_ref[k])
            covar_out_ref[k] = both[:width] + covar_ref[k, mine, :]
            mean_out_ref[k] = both[width:] + mean_ref[k]
        psi_all_ref[...] = psi_out_ref[steps - 1]

    @pl.when(jnp.logical_not(is_second))
    def _():
        for k in range(steps):
            psi_out_ref[k] = psi_ref[k]
            covar_out_ref[k] = covar_ref[k, mine, :]
            mean_out_ref[k] = mean_ref[k]
        psi_all_ref[...] = dot_nn(psi_other_ref[...], psi_ref[steps - 1])

    half = states // 2
    core = lax.rem(lax.axis_index("col"), 2)
    send_ref[...] = psi_all_ref[pl.ds(pl.multiple_of(core * half, 8), half), :]


def packed_blocks(ref, edge):
    def blocks(i, j):
        if i == 3:
            return ref[3 * edge + j : 3 * edge + j + 1, :]
        at = (i + j) if i < 2 else j
        return ref[at * edge : (at + 1) * edge, :]

    return blocks


def carried_on(step_ref, added_ref, mine_ref, mate_ref, out_ref, work_ref):
    mean = unpacked(mine_ref, mate_ref, work_ref)
    put_packed(step_ref, work_ref[...], mean, packed_blocks(added_ref, out_ref.shape[1]), out_ref)


def whole_matrix(mine_ref, mate_ref):
    is_low = lax.rem(lax.axis_index("col"), 2) == 0
    mine, mate = mine_ref[...], mate_ref[...]
    return jnp.concatenate([jnp.where(is_low, mine, mate), jnp.where(is_low, mate, mine)], axis=0)


def matrix_on(step_mine_ref, mine_ref, mate_ref, out_ref):
    out_ref[...] = dot_nn(step_mine_ref[...], whole_matrix(mine_ref, mate_ref))


def joined(mine_ref, mate_ref, out_ref):
    out_ref[...] = whole_matrix(mine_ref, mate_ref)


def entered(steps, width, psi_ref, covar_ref, mean_ref, mine_ref, mate_ref, step_mine_ref, step_mate_ref, *refs):
    psi_out_ref, covar_out_ref, mean_out_ref, work_ref = refs
    mine = pl.ds(pl.multiple_of(lax.axis_index("col") * width, 8), width)
    before = whole_matrix(step_mine_ref, step_mate_ref)
    mean = unpacked(mine_ref, mate_ref, work_ref)
    covar = work_ref[...]
    for k in range(steps):
        psi_out_ref[k] = dot_nn(psi_ref[k], before)
        half = dot_nn(psi_ref[k, mine, :], covar)
        both = dot_nt(jnp.concatenate([half, mean], axis=0), psi_ref[k])
        covar_out_ref[k] = both[:width] + covar_ref[k]
        mean_out_ref[k] = both[width:] + mean_ref[k]


def finished(steps, width, psi_ref, covar_ref, mean_ref, mine_ref, mate_ref, covar_out_ref, mean_out_ref, work_ref):
    mine = pl.ds(pl.multiple_of(lax.axis_index("col") * width, 8), width)
    mean = unpacked(mine_ref, mate_ref, work_ref)
    rows = jnp.concatenate([psi_ref[k, mine, :] for k in range(steps)], axis=0)
    half = dot_nn(rows, work_ref[...])
    for k in range(steps):
        part = half[k * width : (k + 1) * width]
        both = dot_nt(jnp.concatenate([part, mean], axis=0), psi_ref[k])
        covar_out_ref[k] = both[:width] + covar_ref[k]
        mean_out_ref[k : k + 1, :] = both[width : width + 1] + mean_ref[k, :1, :]


def swapped(block, axis, bit):
    return lax.ppermute(block, axis, [(i, i ^ bit) for i in range(lax.axis_size(axis))])


def shifted(block, distance):
    size = lax.axis_size("seg")
    return lax.ppermute(block, "seg", [(i, i + distance) for i in range(size - distance)])


def per_device(
    model_mixing,
    retention,
    forcing,
    observations,
    model_noise,
    obs_noise,
    gain,
    obs_operator_t,
    prior_mean,
    prior_factor,
):
    steps, width, states = model_mixing.shape
    n_col, n_seg = lax.axis_size("col"), lax.axis_size("seg")
    edge = states // 3
    far_bits = []
    bit = n_col // 2
    while bit > 1:
        far_bits.append(bit)
        bit //= 2
    offsets = [0]
    for bit in far_bits:
        offsets = offsets + [o ^ bit for o in offsets]
    offsets = offsets + [o ^ 1 for o in offsets]

    own = [model_mixing]
    for bit in far_bits:
        own = own + [swapped(b, "col", bit) for b in own]
    near = swapped(model_mixing, "seg", 1)
    vectors = jnp.concatenate([retention, model_noise, forcing, observations], axis=1)
    vectors_other = swapped(vectors, "seg", 1)

    (corr_mine,) = local_call(
        correction_rows, [(width, states)], obs_operator_t, gain, products=0.7
    )
    corr = [corr_mine]
    for bit in far_bits:
        corr = corr + [swapped(b, "col", bit) for b in corr]

    other_first = [near[:1]] + [swapped(b[:1], "seg", 1) for b in own[1:]]
    other_rest = [near[1:]]
    for bit in far_bits:
        other_rest = other_rest + [swapped(b, "col", bit) for b in other_rest]

    def over_core(blocks):
        return list(blocks) + [swapped(b, "col", 1) for b in blocks]

    own = over_core(own)
    corr = over_core(corr)
    other_first = over_core(other_first)
    other_rest = over_core(other_rest)

    all_vectors = jnp.concatenate([vectors, vectors_other], axis=0)
    seen = jnp.pad(all_vectors[:, 3 * states :], ((0, MEAN_ROWS - 2 * steps), (0, 0)))
    fixed, prior, pushed = local_call(
        fixed_parts,
        [(states, states), (states, states), (MEAN_ROWS, states)],
        gain,
        obs_noise[None, :],
        prior_factor,
        seen,
        products=4,
    )
    square_shape, mean_shape = (states, states), (MEAN_ROWS, states)
    correction, noise, offset = local_call(
        functools.partial(noises, offsets),
        [square_shape, (2 * steps,) + square_shape, (2 * steps,) + mean_shape],
        all_vectors,
        pushed,
        fixed,
        *corr,
        scratch=[square_shape],
        products=4,
    )
    start = prior_mean[None, :]
    psi, covar, mean = local_call(
        functools.partial(own_segment, offsets, steps),
        [(steps,) + square_shape, (steps,) + square_shape, (steps,) + mean_shape],
        all_vectors,
        correction,
        noise,
        offset,
        prior,
        start,
        *own,
        scratch=[(steps * states, states)],
        products=5,
    )
    share = (3 * edge + 8, edge)
    matrix, psi_other, covar_other, mean_other, total = local_call(
        functools.partial(other_segment, offsets, steps),
        [(steps,) + square_shape, square_shape, square_shape, mean_shape, share],
        all_vectors,
        correction,
        noise,
        offset,
        prior,
        start,
        psi,
        covar,
        mean,
        *other_first,
        *other_rest,
        scratch=[(steps * states, states), square_shape],
        products=7,
    )

    entry = shifted(total, 2)
    psi, covar, mean, psi_all, psi_half = local_call(
        functools.partial(pair_elements, steps, width),
        [(steps,) + square_shape, (steps, width, states), (steps,) + mean_shape, square_shape, (states // 2, states)],
        psi,
        covar,
        mean,
        matrix,
        psi_other,
        covar_other,
        mean_other,
        products=4,
    )
    entry = (entry, swapped(entry, "col", 1))
    distance = 4
    if distance < n_seg:
        step = shifted(psi_half, 2)
        step = (step, swapped(step, "col", 1))
    while distance < n_seg:
        more = 2 * distance < n_seg
        (sent,) = local_call(
            carried_on, [share], psi_all, total, *entry, scratch=[square_shape], products=1.5
        )
        came = shifted(sent, distance)
        if more:
            (sent,) = local_call(matrix_on, [(states // 2, states)], psi_half, *step)
            came_step = shifted(sent, distance)
            came_step = (came_step, swapped(came_step, "col", 1))
            came = (came, swapped(came, "col", 1))
            (whole,) = local_call(joined, [square_shape], *step)
            (entry_mine,) = local_call(
                carried_on, [share], whole, entry[0], *came, scratch=[square_shape], products=1.5
            )
            (step_mine,) = local_call(matrix_on, [(states // 2, states)], step[0], *came_step)
            entry = (entry_mine, swapped(entry_mine, "col", 1))
            step = (step_mine, swapped(step_mine, "col", 1))
        else:
            psi, covar, mean = local_call(
                functools.partial(entered, steps, width),
                [(steps,) + square_shape, (steps, width, states), (steps,) + mean_shape],
                psi,
                covar,
                mean,
                *entry,
                *step,
                scratch=[square_shape],
                products=4,
            )
            entry = (came, swapped(came, "col", 1))
        distance *= 2

    covars, means = local_call(
        functools.partial(finished, steps, width),
        [(steps, width, states), (steps, states)],
        psi,
        covar,
        mean,
        *entry,
        scratch=[square_shape],
        products=1.5,
    )
    return means, covars


def solution(mesh):
    in_specs = (
        P("seg", "col", None),
        P("seg", None),
        P("seg", None),
        P("seg", None),
        P("seg", None),
        P(),
        P(),
        P("col", None),
        P(),
        P(),
    )
    out_specs = (P("seg", None), P("seg", "col", None))
    return jax.shard_map(
        per_device, mesh=mesh, in_specs=in_specs, out_specs=out_specs, check_vma=False
    )
```

time: 98.3 us -> 71.5 us (0.73); the launches traced: 96.6 us -> 71.2 us
  matrix products: 32.9 us -> 0 us
  Pallas kernels: 0 us -> 19.5 us
  between operations: 9.15 us -> 0.82 us
  other arithmetic: 7.62 us -> 0.03 us
  starting transfers between devices: 16.5 us -> 18.6 us
  waiting for transfers between devices: 25.7 us -> 26.9 us
    dot_general x40 -> x0, matrix products: 32.9 us -> none  [the longest x29 25.8 us: dot_nt(): lax.dot_general(left, right, (((1,), (1,)), ((), ())), precision=three_pa...]
    pallas_call x0 -> x9, Pallas kernels: none -> 19.5 us  [local_call(): pl.pallas_call(body, out_shape=shapes, scratch_shapes=[pltpu.VMEM(shape,...]
    ppermute x12 -> x17, waiting for transfers between devices: 0.03 us -> 7.28 us  [swapped(): lax.ppermute(block, axis, [(i, i ^ bit) for i in range(lax.axis_size(axis...]
    ppermute x3, waiting for transfers between devices: 25.7 us -> 19.6 us  [shifted(): lax.ppermute(block, 'seg', [(i, i + distance) for i in range(size - dista...]
    select_n x6 -> x0, other arithmetic: 3.16 us -> none  [the longest x3 2.26 us: carried_along(): low = jnp.where(core == 0, came[:half], swap)]
    unnamed x55 -> x15, local copies, waits for them, and re-layouts: 1.47 us -> 4.49 us
    another operation x8 -> x0, other arithmetic: 2.89 us -> none  [the longest x4 1.13 us: in_order(): stacked = jnp.stack(blocks)]
    ppermute x12 -> x17, starting transfers between devices: 12.5 us -> 14.8 us  [swapped(): lax.ppermute(block, axis, [(i, i ^ bit) for i in range(lax.axis_size(axis...]
  transfers between devices with their start and end apart: 15 -> 20, of which waited for: 3 -> 5; matrix products, arithmetic and copies ran while one was open for 26% -> 0% of each run, Pallas kernels for 0% -> 20%
where the time goes in v2:
time: 71.5 us; the launch traced here: 71.2 us
  waiting for transfers between devices  26.9 us (38%)
  Pallas kernels  19.5 us (27%)
  starting transfers between devices  18.6 us (26%)
  local copies, waits for them, and re-layouts  5.23 us (7%)
  between operations  0.82 us (1%)
    ppermute x3, waiting for transfers between devices, shifted(): lax.ppermute(block, 'seg', [(i, i + distance) for i in range(size - dista...  19.6 us
    pallas_call x9, Pallas kernels, local_call(): pl.pallas_call(body, out_shape=shapes, scratch_shapes=[pltpu.VMEM(shape,...  19.5 us
    ppermute x17, starting transfers between devices, swapped(): lax.ppermute(block, axis, [(i, i ^ bit) for i in range(lax.axis_size(axis...  14.8 us
    ppermute x17, waiting for transfers between devices, swapped(): lax.ppermute(block, axis, [(i, i ^ bit) for i in range(lax.axis_size(axis...  7.28 us
    unnamed x15, local copies, waits for them, and re-layouts  4.49 us
    ppermute x3, starting transfers between devices, shifted(): lax.ppermute(block, 'seg', [(i, i + distance) for i in range(size - dista...  3.88 us
  transfers between devices with their start and end apart: 20, of which 5 were waited for; matrix products, arithmetic and copies ran while one was open for 0% of the time, Pallas kernels for 20%

profile of v2, /device:TPU:29, one launch (start us, length us, event | category | flops | bytes accessed | tf_op | source)
XLA Modules:
  0.0 71.2 jit_solution(17070644627346031336)
XLA Ops:
  0.6 0.7 constant_dynamic-update-slice_fusion.3
  1.3 0.7 constant_dynamic-update-slice_fusion.2
  2.7 0.7 constant_dynamic-update-slice_fusion
  3.6 1.4 %copy-done = f32[384,1024]{1,0:T(8,128)S(1)} copy-done((f32[384,1024]{1,0:T(8,128)S(1)}, f32[384,1024]{1,0:T(8,128)}, u32[]{:S(2)}) %copy-start) | copy-done | bytes 1572888
  5.1 1.0 %copy-done.1 = f32[96,1024]{1,0:T(8,128)S(1)} copy-done((f32[96,1024]{1,0:T(8,128)S(1)}, f32[96,1024]{1,0:T(8,128)}, u32[]{:S(2)}) %copy-start.1) | copy-done | bytes 393240
  6.1 0.8 %shard_map.114.refs_0_ = f32[96,384]{1,0:T(8,128)S(1)} custom-call(f32[96,1024]{1,0:T(8,128)S(1)} %copy-done.1, f32[384,1024]{1,0:T(8,128)S(1)} %copy-done), custom_call_target="tpu_custom_call" | custom-call | flops 237817040 | bytes 1536 | tf_op jit(solution)/shard_map/pallas_call | solution.py:52
  6.9 1.0 %collective-permute-start.2 = (f32[96,384]{1,0:T(8,128)S(1)}, f32[96,384]{1,0:T(8,128)S(1)}, u32[]{:S(2)}, u32[]{:S(2)}) collective-permute-start(f32[96,384]{1,0:T(8,128)S(1)} %shard_map.114.refs_0_), channel_id=1, source_target_pairs={{0,1},{1,0},{2,3},{3,2},{4,5},{5,4},{6,7},{7,6},{8,9},{9,8},{10,11... | collective-permute-start | bytes 442376 | tf_op jit(solution)/shard_map/ppermute | solution.py:330
  7.9 1.2 %collective-permute-start.1 = (f32[96,384]{1,0:T(8,128)S(1)}, f32[96,384]{1,0:T(8,128)S(1)}, u32[]{:S(2)}, u32[]{:S(2)}) collective-permute-start(f32[96,384]{1,0:T(8,128)S(1)} %shard_map.114.refs_0_), channel_id=1, source_target_pairs={{0,2},{1,3},{2,0},{3,1},{4,6},{5,7},{6,4},{7,5},{8,10},{9,11},{10,... | collective-permute-start | bytes 442376 | tf_op jit(solution)/shard_map/ppermute | solution.py:330
  9.8 1.3 %collective-permute-start.7 = (f32[2,96,384]{2,1,0:T(8,128)S(1)}, f32[2,96,384]{2,1,0:T(8,128)S(1)}, u32[]{:S(2)}, u32[]{:S(2)}) collective-permute-start(f32[2,96,384]{2,1,0:T(8,128)S(1)} %copy-done.3), channel_id=1, source_target_pairs={{0,4},{4,0},{8,12},{12,8},{16,20},{20,16},{24,28},{28,24},{1,5},{5... | collective-permute-start | bytes 884744 | tf_op jit(solution)/shard_map/ppermute | solution.py:330
  11.1 2.2 %collective-permute-done.1.refs_1_ = f32[96,384]{1,0:T(8,128)S(1)} collective-permute-done((f32[96,384]{1,0:T(8,128)S(1)}, f32[96,384]{1,0:T(8,128)S(1)}, u32[]{:S(2)}, u32[]{:S(2)}) %collective-permute-start.1) | collective-permute-done | bytes 147488 | tf_op jit(solution)/shard_map/ppermute | solution.py:330
  13.3 1.3 %collective-permute-start.3 = (f32[96,384]{1,0:T(8,128)S(1)}, f32[96,384]{1,0:T(8,128)S(1)}, u32[]{:S(2)}, u32[]{:S(2)}) collective-permute-start(f32[96,384]{1,0:T(8,128)S(1)} %collective-permute-done.1.refs_1_), channel_id=1, source_target_pairs={{0,1},{1,0},{2,3},{3,2},{4,5},{5,4},{6,7},{7,6},{8,9},{9,8},{10,11... | collective-permute-start | bytes 442376 | tf_op jit(solution)/shard_map/ppermute | solution.py:330
  14.6 5.0 %collective-permute-done.4.refs_1_ = f32[2,96,384]{2,1,0:T(8,128)S(1)} collective-permute-done((f32[2,96,384]{2,1,0:T(8,128)S(1)}, f32[2,96,384]{2,1,0:T(8,128)S(1)}, u32[]{:S(2)}, u32[]{:S(2)}) %collective-permute-start.4) | collective-permute-done | bytes 294944 | tf_op jit(solution)/shard_map/ppermute | solution.py:330
  19.7 1.3 %collective-permute-start.8 = (f32[1,96,384]{2,1,0:T(8,128)S(1)}, f32[1,96,384]{2,1,0:T(8,128)S(1)}, u32[]{:S(2)}, u32[]{:S(2)}) collective-permute-start(f32[1,96,384]{2,1,0:T(8,128)S(1)} %slice.19), channel_id=1, source_target_pairs={{0,4},{4,0},{8,12},{12,8},{16,20},{20,16},{24,28},{28,24},{1,5},{5... | collective-permute-start | bytes 442376 | tf_op jit(solution)/shard_map/ppermute | solution.py:330
  21.0 1.1 %collective-permute-start.6 = (f32[2,96,384]{2,1,0:T(8,128)S(1)}, f32[2,96,384]{2,1,0:T(8,128)S(1)}, u32[]{:S(2)}, u32[]{:S(2)}) collective-permute-start(f32[2,96,384]{2,1,0:T(8,128)S(1)} %collective-permute-done.4.refs_1_), channel_id=1, source_target_pairs={{0,1},{1,0},{2,3},{3,2},{4,5},{5,4},{6,7},{7,6},{8,9},{9,8},{10,11... | collective-permute-start | bytes 884744 | tf_op jit(solution)/shard_map/ppermute | solution.py:330
  22.1 1.3 %collective-permute-start.11 = (f32[1,96,384]{2,1,0:T(8,128)S(1)}, f32[1,96,384]{2,1,0:T(8,128)S(1)}, u32[]{:S(2)}, u32[]{:S(2)}) collective-permute-start(f32[1,96,384]{2,1,0:T(8,128)S(1)} %get-tuple-element.50.refs_4_), channel_id=1, source_target_pairs={{0,2},{1,3},{2,0},{3,1},{4,6},{5,7},{6,4},{7,5},{8,10},{9,11},{10,... | collective-permute-start | bytes 442376 | tf_op jit(solution)/shard_map/ppermute | solution.py:330
  23.4 1.9 %shard_map.113 = (f32[384,384]{1,0:T(8,128)S(1)}, f32[384,384]{1,0:T(8,128)S(1)}, f32[16,384]{1,0:T(8,128)S(1)}) custom-call(f32[384,1024]{1,0:T(8,128)S(1)} %copy-done, f32[1,1024]{1,0:T(1,128)S(1)} %bitcast.1, f32[384,384]{1,0:T(8,128)S(1)} %copy-done.2, f32[16,1024]{1,0:T(8,128)S(1)} %pad.4.seen_ref), custom_call_target="tpu_custom_call" | custom-call | flops 1358954496 | bytes 1536 | tf_op jit(solution)/shard_map/pallas_call | solution.py:52
  25.7 2.6 %shard_map.115 = (f32[384,384]{1,0:T(8,128)S(1)}, f32[4,384,384]{2,1,0:T(8,128)S(1)}, f32[4,16,384]{2,1,0:T(8,128)S(1)}) custom-call(f32[4,2176]{1,0:T(4,128)S(1)} %pad_maximum_fusion.vec_ref, f32[16,384]{1,0:T(8,128)S(1)} %get-tuple-element.26.pushed_ref, f32[384,384]{1,0:T(8,128)S(1)} %get-tuple-element.27.fixed_ref, f32[96,384]{1,0:T(8,128)S(1)} %shard_map.114.refs_0_, ...), custom_call_target="tpu_custom_call" | custom-call | flops 1358954496 | bytes 1536 | tf_op jit(solution)/shard_map/pallas_call | solution.py:52
  29.1 2.9 %shard_map.116 = (f32[2,384,384]{2,1,0:T(8,128)S(1)}, f32[2,384,384]{2,1,0:T(8,128)S(1)}, f32[2,16,384]{2,1,0:T(8,128)S(1)}) custom-call(f32[4,2176]{1,0:T(4,128)S(1)} %pad_maximum_fusion.vec_ref, f32[384,384]{1,0:T(8,128)S(1)} %get-tuple-element.28.corr_ref, f32[4,384,384]{2,1,0:T(8,128)S(1)} %get-tuple-element.29.noise_ref, ...), custom_call_target="tpu_custom_call" | custom-call | flops 1698693120 | bytes 1536 | tf_op jit(solution)/shard_map/pallas_call | solution.py:52
  32.1 3.4 %shard_map.117 = (f32[2,384,384]{2,1,0:T(8,128)S(1)}, f32[384,384]{1,0:T(8,128)S(1)}, f32[384,384]{1,0:T(8,128)S(1)}, f32[16,384]{1,0:T(8,128)S(1)}, f32[392,128]{1,0:T(8,128)S(1)}) custom-call(f32[4,2176]{1,0:T(4,128)S(1)} %pad_maximum_fusion.vec_ref, f32[384,384]{1,0:T(8,128)S(1)} %get-tuple-element.28.corr_ref, ...), custom_call_target="tpu_custom_call" | custom-call | flops 2378170368 | bytes 1536 | tf_op jit(solution)/shard_map/pallas_call | solution.py:52
  35.5 1.3 %collective-permute-start.14 = (f32[392,128]{1,0:T(8,128)S(1)}, f32[392,128]{1,0:T(8,128)S(1)}, u32[]{:S(2)}, u32[]{:S(2)}) collective-permute-start(f32[392,128]{1,0:T(8,128)S(1)} %get-tuple-element.42.added_ref), channel_id=1, source_target_pairs={{0,8},{4,12},{8,16},{12,20},{16,24},{20,28},{1,9},{5,13},{9,17},{1... | collective-permute-start | bytes 602120 | tf_op jit(solution)/shard_map/ppermute | solution.py:335
  36.8 2.9 %shard_map.118 = (f32[2,384,384]{2,1,0:T(8,128)S(1)}, f32[2,96,384]{2,1,0:T(8,128)S(1)}, f32[2,16,384]{2,1,0:T(8,128)S(1)}, f32[384,384]{1,0:T(8,128)S(1)}, f32[192,384]{1,0:T(8,128)S(1)}) custom-call(f32[2,384,384]{2,1,0:T(8,128)S(1)} %get-tuple-element.32.psi_ref, f32[2,384,384]{2,1,0:T(8,128)S(1)} %get-tuple-element.33.covar_ref, ...), custom_call_target="tpu_custom_call" | custom-call | flops 1358954496 | bytes 1536 | tf_op jit(solution)/shard_map/pallas_call | solution.py:52
  39.7 1.3 %collective-permute-start.16 = (f32[192,384]{1,0:T(8,128)S(1)}, f32[192,384]{1,0:T(8,128)S(1)}, u32[]{:S(2)}, u32[]{:S(2)}) collective-permute-start(f32[192,384]{1,0:T(8,128)S(1)} %get-tuple-element.43), channel_id=1, source_target_pairs={{0,8},{4,12},{8,16},{12,20},{16,24},{20,28},{1,9},{5,13},{9,17},{1... | collective-permute-start | bytes 884744 | tf_op jit(solution)/shard_map/ppermute | solution.py:335
  41.0 2.2 %collective-permute-done.14.mine_ref = f32[392,128]{1,0:T(8,128)S(1)} collective-permute-done((f32[392,128]{1,0:T(8,128)S(1)}, f32[392,128]{1,0:T(8,128)S(1)}, u32[]{:S(2)}, u32[]{:S(2)}) %collective-permute-start.14) | collective-permute-done | bytes 200736 | tf_op jit(solution)/shard_map/ppermute | solution.py:335
  43.3 1.5 %collective-permute-start.15 = (f32[392,128]{1,0:T(8,128)S(1)}, f32[392,128]{1,0:T(8,128)S(1)}, u32[]{:S(2)}, u32[]{:S(2)}) collective-permute-start(f32[392,128]{1,0:T(8,128)S(1)} %collective-permute-done.14.mine_ref), channel_id=1, source_target_pairs={{0,1},{1,0},{2,3},{3,2},{4,5},{5,4},{6,7},{7,6},{8,9},{9,8},{10,11... | collective-permute-start | bytes 602120 | tf_op jit(solution)/shard_map/ppermute | solution.py:330
  44.8 5.4 %collective-permute-done.16.step_mine_ref = f32[192,384]{1,0:T(8,128)S(1)} collective-permute-done((f32[192,384]{1,0:T(8,128)S(1)}, f32[192,384]{1,0:T(8,128)S(1)}, u32[]{:S(2)}, u32[]{:S(2)}) %collective-permute-start.16) | collective-permute-done | bytes 294944 | tf_op jit(solution)/shard_map/ppermute | solution.py:335
  50.2 1.5 %collective-permute-start.17 = (f32[192,384]{1,0:T(8,128)S(1)}, f32[192,384]{1,0:T(8,128)S(1)}, u32[]{:S(2)}, u32[]{:S(2)}) collective-permute-start(f32[192,384]{1,0:T(8,128)S(1)} %collective-permute-done.16.step_mine_ref), channel_id=1, source_target_pairs={{0,1},{1,0},{2,3},{3,2},{4,5},{5,4},{6,7},{7,6},{8,9},{9,8},{10,11... | collective-permute-start | bytes 884744 | tf_op jit(solution)/shard_map/ppermute | solution.py:330
  51.7 0.8 %shard_map.120 = f32[392,128]{1,0:T(8,128)S(1)} custom-call(f32[384,384]{1,0:T(8,128)S(1)} %get-tuple-element.47.step_ref, f32[392,128]{1,0:T(8,128)S(1)} %get-tuple-element.42.added_ref, f32[392,128]{1,0:T(8,128)S(1)} %collective-permute-done.14.mine_ref, f32[392,128]{1,0:T(8,128)S(1)} %collective-permute-done.15.mate_ref), custom_call_target="tpu_custom_call" | custom-call | flops 509607936 | bytes 512 | tf_op jit(solution)/shard_map/pallas_call | solution.py:52
  52.5 1.3 %collective-permute-start.18 = (f32[392,128]{1,0:T(8,128)S(1)}, f32[392,128]{1,0:T(8,128)S(1)}, u32[]{:S(2)}, u32[]{:S(2)}) collective-permute-start(f32[392,128]{1,0:T(8,128)S(1)} %shard_map.120), channel_id=1, source_target_pairs={{0,16},{4,20},{8,24},{12,28},{1,17},{5,21},{9,25},{13,29},{2,18},{... | collective-permute-start | bytes 602120 | tf_op jit(solution)/shard_map/ppermute | solution.py:335
  53.8 12.0 %collective-permute-done.18.mine_ref = f32[392,128]{1,0:T(8,128)S(1)} collective-permute-done((f32[392,128]{1,0:T(8,128)S(1)}, f32[392,128]{1,0:T(8,128)S(1)}, u32[]{:S(2)}, u32[]{:S(2)}) %collective-permute-start.18) | collective-permute-done | bytes 200736 | tf_op jit(solution)/shard_map/ppermute | solution.py:335
  65.8 1.2 %collective-permute-start.19 = (f32[392,128]{1,0:T(8,128)S(1)}, f32[392,128]{1,0:T(8,128)S(1)}, u32[]{:S(2)}, u32[]{:S(2)}) collective-permute-start(f32[392,128]{1,0:T(8,128)S(1)} %collective-permute-done.18.mine_ref), channel_id=1, source_target_pairs={{0,1},{1,0},{2,3},{3,2},{4,5},{5,4},{6,7},{7,6},{8,9},{9,8},{10,11... | collective-permute-start | bytes 602120 | tf_op jit(solution)/shard_map/ppermute | solution.py:330
  67.0 2.3 %shard_map.119 = (f32[2,384,384]{2,1,0:T(8,128)S(1)}, f32[2,96,384]{2,1,0:T(8,128)S(1)}, f32[2,16,384]{2,1,0:T(8,128)S(1)}) custom-call(f32[2,384,384]{2,1,0:T(8,128)S(1)} %get-tuple-element.39.psi_ref, f32[2,96,384]{2,1,0:T(8,128)S(1)} %get-tuple-element.40.covar_ref, f32[2,16,384]{2,1,0:T(8,128)S(1)} %get-tuple-element.41.mean_ref, ...), custom_call_target="tpu_custom_call" | custom-call | flops 1358954496 | bytes 1536 | tf_op jit(solution)/shard_map/pallas_call | solution.py:52
  69.3 1.9 %shard_map.121 = (f32[2,96,384]{2,1,0:T(8,128)}, f32[2,384]{1,0:T(2,128)}) custom-call(f32[2,384,384]{2,1,0:T(8,128)S(1)} %get-tuple-element.44.psi_ref, f32[2,96,384]{2,1,0:T(8,128)S(1)} %get-tuple-element.45.covar_ref, f32[2,16,384]{2,1,0:T(8,128)S(1)} %get-tuple-element.46.mean_ref, f32[392,128]{1,0:T(8,128)S(1)} %collective-permute-done.18.mine_ref, ...), custom_call_target="tpu_custom_call" | custom-call | flops 509607936 | bytes 1536 | tf_op jit(solution)/shard_map/pallas_call | solution.py:52
  (39 shorter events, 2.8 us)
Async XLA Ops:
  0.6 9.1 %copy-start.5 = (f32[384]{0:T(512)S(1)}, f32[384]{0:T(512)}, u32[]{:S(2)}) copy-start(f32[384]{0:T(512)} %param.18) | copy-start | bytes 4612
  3.4 6.3 %collective-permute-start = (f32[2,2176]{1,0:T(2,128)S(1)}, f32[2,2176]{1,0:T(2,128)S(1)}, u32[]{:S(2)}, u32[]{:S(2)}) collective-permute-start(f32[2,2176]{1,0:T(2,128)S(1)} %constant_dynamic-update-slice_fusion), channel_id=1, source_target_pairs={{0,4},{4,0},{8,12},{12,8},{16,20},{20,16},{24,28},{28,24},{1,5},{5... | collective-permute-start | bytes 52232 | tf_op jit(solution)/shard_map/ppermute | solution.py:330
  3.6 1.4 %copy-start = (f32[384,1024]{1,0:T(8,128)S(1)}, f32[384,1024]{1,0:T(8,128)}, u32[]{:S(2)}) copy-start(f32[384,1024]{1,0:T(8,128)} %gain_ref.3) | copy-start | bytes 4718596
  5.1 1.0 %copy-start.1 = (f32[96,1024]{1,0:T(8,128)S(1)}, f32[96,1024]{1,0:T(8,128)}, u32[]{:S(2)}) copy-start(f32[96,1024]{1,0:T(8,128)} %oper_ref.1) | copy-start | bytes 1179652
  6.0 3.1 %copy-start.3 = (f32[2,96,384]{2,1,0:T(8,128)S(1)}, f32[2,96,384]{2,1,0:T(8,128)}, u32[]{:S(2)}) copy-start(f32[2,96,384]{2,1,0:T(8,128)} %refs_0_.1) | copy-start | bytes 884740
  6.1 17.4 %copy-start.2 = (f32[384,384]{1,0:T(8,128)S(1)}, f32[384,384]{1,0:T(8,128)}, u32[]{:S(2)}) copy-start(f32[384,384]{1,0:T(8,128)} %factor_ref.1) | copy-start | bytes 1769476
  6.1 17.4 %copy-start.4 = (f32[1024]{0:T(1024)S(1)}, f32[1024]{0:T(1024)}, u32[]{:S(2)}) copy-start(f32[1024]{0:T(1024)} %param.15) | copy-start | bytes 12292
  6.9 15.3 %collective-permute-start.2 = (f32[96,384]{1,0:T(8,128)S(1)}, f32[96,384]{1,0:T(8,128)S(1)}, u32[]{:S(2)}, u32[]{:S(2)}) collective-permute-start(f32[96,384]{1,0:T(8,128)S(1)} %shard_map.114.refs_0_), channel_id=1, source_target_pairs={{0,1},{1,0},{2,3},{3,2},{4,5},{5,4},{6,7},{7,6},{8,9},{9,8},{10,11... | collective-permute-start | bytes 442376 | tf_op jit(solution)/shard_map/ppermute | solution.py:330
  7.9 5.4 %collective-permute-start.1 = (f32[96,384]{1,0:T(8,128)S(1)}, f32[96,384]{1,0:T(8,128)S(1)}, u32[]{:S(2)}, u32[]{:S(2)}) collective-permute-start(f32[96,384]{1,0:T(8,128)S(1)} %shard_map.114.refs_0_), channel_id=1, source_target_pairs={{0,2},{1,3},{2,0},{3,1},{4,6},{5,7},{6,4},{7,5},{8,10},{9,11},{10,... | collective-permute-start | bytes 442376 | tf_op jit(solution)/shard_map/ppermute | solution.py:330
  9.1 19.2 %collective-permute-start.5 = (f32[2,96,384]{2,1,0:T(8,128)S(1)}, f32[2,96,384]{2,1,0:T(8,128)S(1)}, u32[]{:S(2)}, u32[]{:S(2)}) collective-permute-start(f32[2,96,384]{2,1,0:T(8,128)S(1)} %copy-done.3), channel_id=1, source_target_pairs={{0,1},{1,0},{2,3},{3,2},{4,5},{5,4},{6,7},{7,6},{8,9},{9,8},{10,11... | collective-permute-start | bytes 884744 | tf_op jit(solution)/shard_map/ppermute | solution.py:330
  9.5 10.2 %collective-permute-start.4 = (f32[2,96,384]{2,1,0:T(8,128)S(1)}, f32[2,96,384]{2,1,0:T(8,128)S(1)}, u32[]{:S(2)}, u32[]{:S(2)}) collective-permute-start(f32[2,96,384]{2,1,0:T(8,128)S(1)} %copy-done.3), channel_id=1, source_target_pairs={{0,2},{1,3},{2,0},{3,1},{4,6},{5,7},{6,4},{7,5},{8,10},{9,11},{10,... | collective-permute-start | bytes 884744 | tf_op jit(solution)/shard_map/ppermute | solution.py:330
  9.8 11.2 %collective-permute-start.7 = (f32[2,96,384]{2,1,0:T(8,128)S(1)}, f32[2,96,384]{2,1,0:T(8,128)S(1)}, u32[]{:S(2)}, u32[]{:S(2)}) collective-permute-start(f32[2,96,384]{2,1,0:T(8,128)S(1)} %copy-done.3), channel_id=1, source_target_pairs={{0,4},{4,0},{8,12},{12,8},{16,20},{20,16},{24,28},{28,24},{1,5},{5... | collective-permute-start | bytes 884744 | tf_op jit(solution)/shard_map/ppermute | solution.py:330
  13.3 12.0 %collective-permute-start.3 = (f32[96,384]{1,0:T(8,128)S(1)}, f32[96,384]{1,0:T(8,128)S(1)}, u32[]{:S(2)}, u32[]{:S(2)}) collective-permute-start(f32[96,384]{1,0:T(8,128)S(1)} %collective-permute-done.1.refs_1_), channel_id=1, source_target_pairs={{0,1},{1,0},{2,3},{3,2},{4,5},{5,4},{6,7},{7,6},{8,9},{9,8},{10,11... | collective-permute-start | bytes 442376 | tf_op jit(solution)/shard_map/ppermute | solution.py:330
  19.7 8.9 %collective-permute-start.8 = (f32[1,96,384]{2,1,0:T(8,128)S(1)}, f32[1,96,384]{2,1,0:T(8,128)S(1)}, u32[]{:S(2)}, u32[]{:S(2)}) collective-permute-start(f32[1,96,384]{2,1,0:T(8,128)S(1)} %slice.19), channel_id=1, source_target_pairs={{0,4},{4,0},{8,12},{12,8},{16,20},{20,16},{24,28},{28,24},{1,5},{5... | collective-permute-start | bytes 442376 | tf_op jit(solution)/shard_map/ppermute | solution.py:330
  21.0 8.2 %collective-permute-start.6 = (f32[2,96,384]{2,1,0:T(8,128)S(1)}, f32[2,96,384]{2,1,0:T(8,128)S(1)}, u32[]{:S(2)}, u32[]{:S(2)}) collective-permute-start(f32[2,96,384]{2,1,0:T(8,128)S(1)} %collective-permute-done.4.refs_1_), channel_id=1, source_target_pairs={{0,1},{1,0},{2,3},{3,2},{4,5},{5,4},{6,7},{7,6},{8,9},{9,8},{10,11... | collective-permute-start | bytes 884744 | tf_op jit(solution)/shard_map/ppermute | solution.py:330
  22.1 6.8 %collective-permute-start.11 = (f32[1,96,384]{2,1,0:T(8,128)S(1)}, f32[1,96,384]{2,1,0:T(8,128)S(1)}, u32[]{:S(2)}, u32[]{:S(2)}) collective-permute-start(f32[1,96,384]{2,1,0:T(8,128)S(1)} %get-tuple-element.50.refs_4_), channel_id=1, source_target_pairs={{0,2},{1,3},{2,0},{3,1},{4,6},{5,7},{6,4},{7,5},{8,10},{9,11},{10,... | collective-permute-start | bytes 442376 | tf_op jit(solution)/shard_map/ppermute | solution.py:330
  25.4 6.7 %collective-permute-start.12 = (f32[1,96,384]{2,1,0:T(8,128)S(1)}, f32[1,96,384]{2,1,0:T(8,128)S(1)}, u32[]{:S(2)}, u32[]{:S(2)}) collective-permute-start(f32[1,96,384]{2,1,0:T(8,128)S(1)} %get-tuple-element.50.refs_4_), channel_id=1, source_target_pairs={{0,1},{1,0},{2,3},{3,2},{4,5},{5,4},{6,7},{7,6},{8,9},{9,8},{10,11... | collective-permute-start | bytes 442376 | tf_op jit(solution)/shard_map/ppermute | solution.py:330
  28.3 3.7 %collective-permute-start.9 = (f32[1,96,384]{2,1,0:T(8,128)S(1)}, f32[1,96,384]{2,1,0:T(8,128)S(1)}, u32[]{:S(2)}, u32[]{:S(2)}) collective-permute-start(f32[1,96,384]{2,1,0:T(8,128)S(1)} %get-tuple-element.51.refs_0_), channel_id=1, source_target_pairs={{0,1},{1,0},{2,3},{3,2},{4,5},{5,4},{6,7},{7,6},{8,9},{9,8},{10,11... | collective-permute-start | bytes 442376 | tf_op jit(solution)/shard_map/ppermute | solution.py:330
  28.6 3.5 %collective-permute-start.10 = (f32[1,96,384]{2,1,0:T(8,128)S(1)}, f32[1,96,384]{2,1,0:T(8,128)S(1)}, u32[]{:S(2)}, u32[]{:S(2)}) collective-permute-start(f32[1,96,384]{2,1,0:T(8,128)S(1)} %collective-permute-done.8.refs_1_), channel_id=1, source_target_pairs={{0,1},{1,0},{2,3},{3,2},{4,5},{5,4},{6,7},{7,6},{8,9},{9,8},{10,11... | collective-permute-start | bytes 442376 | tf_op jit(solution)/shard_map/ppermute | solution.py:330
  28.9 3.2 %collective-permute-start.13 = (f32[1,96,384]{2,1,0:T(8,128)S(1)}, f32[1,96,384]{2,1,0:T(8,128)S(1)}, u32[]{:S(2)}, u32[]{:S(2)}) collective-permute-start(f32[1,96,384]{2,1,0:T(8,128)S(1)} %collective-permute-done.11.refs_5_), channel_id=1, source_target_pairs={{0,1},{1,0},{2,3},{3,2},{4,5},{5,4},{6,7},{7,6},{8,9},{9,8},{10,11... | collective-permute-start | bytes 442376 | tf_op jit(solution)/shard_map/ppermute | solution.py:330
  35.5 7.8 %collective-permute-start.14 = (f32[392,128]{1,0:T(8,128)S(1)}, f32[392,128]{1,0:T(8,128)S(1)}, u32[]{:S(2)}, u32[]{:S(2)}) collective-permute-start(f32[392,128]{1,0:T(8,128)S(1)} %get-tuple-element.42.added_ref), channel_id=1, source_target_pairs={{0,8},{4,12},{8,16},{12,20},{16,24},{20,28},{1,9},{5,13},{9,17},{1... | collective-permute-start | bytes 602120 | tf_op jit(solution)/shard_map/ppermute | solution.py:335
  39.7 10.4 %collective-permute-start.16 = (f32[192,384]{1,0:T(8,128)S(1)}, f32[192,384]{1,0:T(8,128)S(1)}, u32[]{:S(2)}, u32[]{:S(2)}) collective-permute-start(f32[192,384]{1,0:T(8,128)S(1)} %get-tuple-element.43), channel_id=1, source_target_pairs={{0,8},{4,12},{8,16},{12,20},{16,24},{20,28},{1,9},{5,13},{9,17},{1... | collective-permute-start | bytes 884744 | tf_op jit(solution)/shard_map/ppermute | solution.py:335
  43.3 8.4 %collective-permute-start.15 = (f32[392,128]{1,0:T(8,128)S(1)}, f32[392,128]{1,0:T(8,128)S(1)}, u32[]{:S(2)}, u32[]{:S(2)}) collective-permute-start(f32[392,128]{1,0:T(8,128)S(1)} %collective-permute-done.14.mine_ref), channel_id=1, source_target_pairs={{0,1},{1,0},{2,3},{3,2},{4,5},{5,4},{6,7},{7,6},{8,9},{9,8},{10,11... | collective-permute-start | bytes 602120 | tf_op jit(solution)/shard_map/ppermute | solution.py:330
  50.2 16.9 %collective-permute-start.17 = (f32[192,384]{1,0:T(8,128)S(1)}, f32[192,384]{1,0:T(8,128)S(1)}, u32[]{:S(2)}, u32[]{:S(2)}) collective-permute-start(f32[192,384]{1,0:T(8,128)S(1)} %collective-permute-done.16.step_mine_ref), channel_id=1, source_target_pairs={{0,1},{1,0},{2,3},{3,2},{4,5},{5,4},{6,7},{7,6},{8,9},{9,8},{10,11... | collective-permute-start | bytes 884744 | tf_op jit(solution)/shard_map/ppermute | solution.py:330
  52.5 13.3 %collective-permute-start.18 = (f32[392,128]{1,0:T(8,128)S(1)}, f32[392,128]{1,0:T(8,128)S(1)}, u32[]{:S(2)}, u32[]{:S(2)}) collective-permute-start(f32[392,128]{1,0:T(8,128)S(1)} %shard_map.120), channel_id=1, source_target_pairs={{0,16},{4,20},{8,24},{12,28},{1,17},{5,21},{9,25},{13,29},{2,18},{... | collective-permute-start | bytes 602120 | tf_op jit(solution)/shard_map/ppermute | solution.py:335
  65.8 3.5 %collective-permute-start.19 = (f32[392,128]{1,0:T(8,128)S(1)}, f32[392,128]{1,0:T(8,128)S(1)}, u32[]{:S(2)}, u32[]{:S(2)}) collective-permute-start(f32[392,128]{1,0:T(8,128)S(1)} %collective-permute-done.18.mine_ref), channel_id=1, source_target_pairs={{0,1},{1,0},{2,3},{3,2},{4,5},{5,4},{6,7},{7,6},{8,9},{9,8},{10,11... | collective-permute-start | bytes 602120 | tf_op jit(solution)/shard_map/ppermute | solution.py:330

commit v3 on v2

v3 whole, which is shorter than its diff:
```python
import functools

import jax
import jax.numpy as jnp
from jax import lax
from jax.experimental import pallas as pl
from jax.experimental.pallas import tpu as pltpu
from jax.sharding import PartitionSpec as P

F32, BF16 = jnp.float32, jnp.bfloat16
NN = (((1,), (0,)), ((), ()))
NT = (((1,), (1,)), ((), ()))
MEAN_ROWS = 16
COST = 7 * 10**8


def parts(x):
    high = x.astype(BF16)
    return high, (x - high.astype(F32)).astype(BF16)


def as_left(x):
    high, low = parts(x)
    return jnp.concatenate([high, high, low], axis=1)


def as_right(x, axis):
    high, low = parts(x)
    return jnp.concatenate([high, low, high], axis=axis)


def dot_nn(left, right):
    return lax.dot_general(as_left(left), as_right(right, 0), NN, preferred_element_type=F32)


def dot_nt(left, right):
    return lax.dot_general(as_left(left), as_right(right, 1), NT, preferred_element_type=F32)


def square(step, covar, mean):
    rows = covar.shape[0]
    both = dot_nt(jnp.concatenate([dot_nn(step, covar), mean], axis=0), step)
    return both[:rows], both[rows:]


def mean_block(row, states):
    return jnp.broadcast_to(row, (MEAN_ROWS, states))


def local_call(body, outs, *operands, scratch=(), copied=False, cost=0):
    shapes = [jax.ShapeDtypeStruct(shape, F32) for shape in outs]
    return pl.pallas_call(
        body,
        out_shape=shapes,
        name=getattr(body, "func", body).__name__,
        in_specs=[pl.BlockSpec(memory_space=pltpu.HBM if copied else pltpu.VMEM)] * len(operands),
        scratch_shapes=[pltpu.VMEM(o.shape, F32) for o in operands if copied]
        + [pltpu.SemaphoreType.DMA((len(operands),))] * copied
        + [pltpu.VMEM(shape, F32) for shape in scratch],
        compiler_params=pltpu.CompilerParams(vmem_limit_bytes=(58 if copied else 36) * 2**20),
        cost_estimate=pl.CostEstimate(
            flops=cost * COST, bytes_accessed=4096, transcendentals=0
        ),
    )(*operands)


def by_gain(left, right):
    return lax.dot_general(as_left(left), right, NT, preferred_element_type=F32)


def correction_rows(
    gain_hbm, oper_hbm, seen_hbm, keep_hbm, push_hbm, var_hbm, corr_ref, vec_ref,
    gain_ref, oper_ref, seen_ref, keep_ref, push_ref, var_ref, sems,
):
    moves = [
        pltpu.make_async_copy(source, target, sems.at[i])
        for i, (source, target) in enumerate(
            [
                (gain_hbm, gain_ref),
                (oper_hbm, oper_ref),
                (seen_hbm, seen_ref),
                (keep_hbm, keep_ref),
                (push_hbm, push_ref),
                (var_hbm, var_ref),
            ]
        )
    ]
    for move in moves:
        move.start()
    width, states = corr_ref.shape
    steps = keep_ref.shape[0]
    rows = lax.broadcasted_iota(jnp.int32, (width, states), 0) + lax.axis_index("col") * width
    cols = lax.broadcasted_iota(jnp.int32, (width, states), 1)
    for move in moves:
        move.wait()
    blank = jnp.zeros((MEAN_ROWS - steps, gain_ref.shape[1]), F32)
    left = jnp.concatenate([oper_ref[...], seen_ref[...], blank], axis=0)
    both = by_gain(left, as_right(gain_ref[...], 1))
    corr_ref[...] = (rows == cols).astype(F32) - both[:width]
    for k in range(steps):
        here = slice(k, k + 1)
        vec_ref[k, 0:1, :] = keep_ref[here, :]
        vec_ref[k, 1:2, :] = var_ref[here, :]
        vec_ref[k, 2:3, :] = push_ref[here, :]
        vec_ref[k, 3:4, :] = both[width + k : width + k + 1]


def fixed_parts(gain_ref, noise_ref, factor_ref, fixed_ref, prior_ref):
    gain = gain_ref[...]
    fixed_ref[...] = by_gain(gain * noise_ref[...], as_right(gain, 1))

    @pl.when(lax.axis_index("seg") < 2)
    def _():
        prior_ref[...] = dot_nt(factor_ref[...], factor_ref[...])


def place(pieces, offsets, out_ref, base):
    me = lax.axis_index("col")
    width = pieces[0].shape[-2]
    for piece, offset in zip(pieces, offsets):
        at = pl.multiple_of((me ^ offset) * width + base, 8)
        out_ref[pl.ds(at, width), :] = piece


def noises(offsets, vec_ref, vec_other_ref, fixed_ref, *refs):
    pieces, (corr_ref, noise_ref, offset_ref, work_ref) = refs[:-4], refs[-4:]
    states = corr_ref.shape[0]
    steps = vec_ref.shape[0]
    place([p[...] for p in pieces], offsets, work_ref, 0)
    corr = work_ref[...].T
    corr_ref[...] = corr
    right = as_right(corr, 1)
    vectors = [vec_ref[k] for k in range(steps)] + [vec_other_ref[k] for k in range(steps)]
    push = [v[2:3] for v in vectors] + [jnp.zeros((MEAN_ROWS - 2 * steps, states), F32)]
    left = jnp.concatenate([corr * v[1:2] for v in vectors] + push, axis=0)
    both = lax.dot_general(as_left(left), right, NT, preferred_element_type=F32)
    base = 2 * steps * states
    for k in range(2 * steps):
        noise_ref[k] = both[k * states : (k + 1) * states] + fixed_ref[...]
        offset_ref[k] = mean_block(both[base + k : base + k + 1] + vectors[k][3:4], states)


def mixed_rows(steps_of, corr_ref, *refs):
    pieces, (out_ref,) = refs[:-1], refs[-1:]
    width = pieces[0].shape[1]
    blocks = [(k, piece[i]) for piece, of in zip(pieces, steps_of) for i, k in enumerate(of)]
    mixed = dot_nt(jnp.concatenate([block for _, block in blocks], axis=0), corr_ref[...])
    filled = [0] * out_ref.shape[0]
    for i, (k, _) in enumerate(blocks):
        out_ref[k, filled[k] : filled[k] + width, :] = mixed[i * width : (i + 1) * width]
        filled[k] += width


def matrices_of(offsets, vec_ref, corr, mine_ref, mate_ref, work_ref, out_ref):
    steps, half, states = mine_ref.shape
    width = half // len(offsets)
    for k in range(steps):
        for ref, bit in ((mine_ref, 0), (mate_ref, 1)):
            blocks = [ref[k, i * width : (i + 1) * width, :] for i in range(len(offsets))]
            place(blocks, [o ^ bit for o in offsets], work_ref, 0)
        out_ref[k] = work_ref[...].T + corr * vec_ref[k, 0:1, :]


def all_matrices(
    offsets, vec_ref, vec_other_ref, corr_ref, mine_ref, mate_ref, mine_other_ref, mate_other_ref,
    matrix_ref, psi_ref, matrix_other_ref, psi_other_ref, psi_half_ref, work_ref, work_other_ref,
):
    steps, half, states = mine_ref.shape
    seg = lax.axis_index("seg")
    is_second = lax.rem(seg, 2) == 1
    corr = corr_ref[...]
    matrices_of(offsets, vec_ref, corr, mine_ref, mate_ref, work_ref, matrix_ref)
    matrices_of(offsets, vec_other_ref, corr, mine_other_ref, mate_other_ref, work_other_ref, matrix_other_ref)
    mine = pl.ds(pl.multiple_of(lax.rem(lax.axis_index("col"), 2) * half, 8), half)
    psi_ref[0] = matrix_ref[0]
    for k in range(1, steps):
        psi_ref[k] = dot_nn(matrix_ref[k], psi_ref[k - 1])

    @pl.when(seg >= 2)
    def _():
        psi_other_ref[...] = matrix_other_ref[0]
        for k in range(1, steps):
            psi_other_ref[...] = dot_nn(matrix_other_ref[k], psi_other_ref[...])

        @pl.when(is_second)
        def _():
            psi_half_ref[...] = dot_nn(psi_ref[steps - 1, mine, :], psi_other_ref[...])

        @pl.when(jnp.logical_not(is_second))
        def _():
            psi_half_ref[...] = dot_nn(psi_other_ref[mine, :], psi_ref[steps - 1])


def put_packed(step_ref, covar, mean, blocks, out_ref):
    states = covar.shape[0]
    edge = states // 3
    core = lax.rem(lax.axis_index("col"), 2)

    @pl.when(core == 0)
    def _():
        rows = step_ref[: 2 * edge, :]
        low = dot_nt(dot_nn(rows, covar), rows)
        out_ref[:edge, :] = low[:edge, :edge] + blocks(0, 0)
        out_ref[edge : 2 * edge, :] = low[edge:, :edge] + blocks(1, 0)
        out_ref[2 * edge : 3 * edge, :] = low[edge:, edge:] + blocks(1, 1)
        out_ref[3 * edge :, :] = jnp.zeros((8, edge), F32)

    @pl.when(core == 1)
    def _():
        rows = step_ref[2 * edge :, :]
        both = dot_nt(jnp.concatenate([dot_nn(rows, covar), mean], axis=0), step_ref[...])
        out_ref[3 * edge :, :] = jnp.zeros((8, edge), F32)
        for j in range(3):
            at = slice(j * edge, (j + 1) * edge)
            out_ref[at, :] = both[:edge, at] + blocks(2, j)
            out_ref[3 * edge + j : 3 * edge + j + 1, :] = both[edge : edge + 1, at] + blocks(3, j)


def unpacked(mine_ref, mate_ref, covar_ref):
    states = covar_ref.shape[0]
    edge = states // 3
    is_low = lax.rem(lax.axis_index("col"), 2) == 0
    low = jnp.where(is_low, mine_ref[...], mate_ref[...])
    high = jnp.where(is_low, mate_ref[...], mine_ref[...])

    def put(i, j, block):
        covar_ref[i * edge : (i + 1) * edge, j * edge : (j + 1) * edge] = block
        if i != j:
            covar_ref[j * edge : (j + 1) * edge, i * edge : (i + 1) * edge] = block.T

    put(0, 0, low[:edge])
    put(1, 0, low[edge : 2 * edge])
    put(1, 1, low[2 * edge : 3 * edge])
    for j in range(3):
        put(2, j, high[j * edge : (j + 1) * edge])
    row = jnp.concatenate([high[3 * edge + j : 3 * edge + j + 1] for j in range(3)], axis=1)
    return mean_block(row, states)


def pair_covariance(
    steps, noise_ref, offset_ref, prior_ref, start_ref, matrix_ref, psi_ref, matrix_other_ref,
    covar_ref, mean_ref, covar_other_ref, mean_other_ref, out_ref, step_ref,
):
    states = prior_ref.shape[0]
    edge = states // 3
    seg = lax.axis_index("seg")
    is_second = lax.rem(seg, 2) == 1
    last = steps - 1
    covar_ref[0] = noise_ref[0]
    mean_ref[0] = offset_ref[0]

    def with_prior(step):
        return square(step, prior_ref[...], mean_block(start_ref[...], states))

    @pl.when(seg == 0)
    def _():
        covar, mean = with_prior(matrix_ref[0])
        covar_ref[0] += covar
        mean_ref[0] += mean

    for k in range(1, steps):
        covar, mean = square(matrix_ref[k], covar_ref[k - 1], mean_ref[k - 1])
        covar_ref[k] = covar + noise_ref[k]
        mean_ref[k] = mean + offset_ref[k]

    @pl.when(is_second)
    def _():
        covar_other_ref[...] = noise_ref[steps]
        mean_other_ref[...] = offset_ref[steps]
        step_ref[...] = psi_ref[last]

        @pl.when(seg == 1)
        def _():
            covar, mean = with_prior(matrix_other_ref[0])
            covar_other_ref[...] += covar
            mean_other_ref[...] += mean

    @pl.when(jnp.logical_not(is_second))
    def _():
        covar_other_ref[...] = covar_ref[last]
        mean_other_ref[...] = mean_ref[last]
        step_ref[...] = matrix_other_ref[last]

    def one_step(k):
        covar, mean = square(matrix_other_ref[k], covar_other_ref[...], mean_other_ref[...])
        covar_other_ref[...] = covar + noise_ref[steps + k]
        mean_other_ref[...] = mean + offset_ref[steps + k]

    for k in range(last):
        one_step(k + is_second.astype(jnp.int32))

    def blocks(i, j):
        at = slice(j * edge, (j + 1) * edge)
        if i == 3:
            return jnp.where(is_second, mean_ref[last, :1, at], offset_ref[steps + last, :1, at])
        rows = slice(i * edge, (i + 1) * edge)
        return jnp.where(is_second, covar_ref[last, rows, at], noise_ref[steps + last, rows, at])

    put_packed(step_ref, covar_other_ref[...], mean_other_ref[...], blocks, out_ref)


def pair_elements(steps, width, psi_ref, covar_ref, mean_ref, psi_other_ref, covar_other_ref, mean_other_ref, *refs):
    psi_out_ref, covar_out_ref, mean_out_ref, psi_all_ref = refs
    seg = lax.axis_index("seg")
    is_second = lax.rem(seg, 2) == 1
    mine = pl.ds(pl.multiple_of(lax.axis_index("col") * width, 8), width)

    @pl.when(seg < 2)
    def _():
        psi_out_ref[...] = jnp.zeros_like(psi_out_ref)

    @pl.when(seg >= 2)
    def _():
        for k in range(steps):

            @pl.when(is_second)
            def _():
                psi_out_ref[k] = dot_nn(psi_ref[k], psi_other_ref[...])

            @pl.when(jnp.logical_not(is_second))
            def _():
                psi_out_ref[k] = psi_ref[k]

        @pl.when(is_second)
        def _():
            psi_all_ref[...] = psi_out_ref[steps - 1]

        @pl.when(jnp.logical_not(is_second))
        def _():
            psi_all_ref[...] = dot_nn(psi_other_ref[...], psi_ref[steps - 1])

    @pl.when(is_second)
    def _():
        covar, mean = covar_other_ref[...], mean_other_ref[...]
        for k in range(steps):
            half = dot_nn(psi_ref[k, mine, :], covar)
            both = dot_nt(jnp.concatenate([half, mean], axis=0), psi_ref[k])
            covar_out_ref[k] = both[:width] + covar_ref[k, mine, :]
            mean_out_ref[k] = both[width:] + mean_ref[k]

    @pl.when(jnp.logical_not(is_second))
    def _():
        for k in range(steps):
            covar_out_ref[k] = covar_ref[k, mine, :]
            mean_out_ref[k] = mean_ref[k]


def packed_blocks(ref, edge):
    def blocks(i, j):
        if i == 3:
            return ref[3 * edge + j : 3 * edge + j + 1, :]
        at = (i + j) if i < 2 else j
        return ref[at * edge : (at + 1) * edge, :]

    return blocks


def carried_on(distance, step_ref, added_ref, mine_ref, mate_ref, out_ref, work_ref):
    @pl.when(lax.axis_index("seg") < lax.axis_size("seg") - distance)
    def _():
        mean = unpacked(mine_ref, mate_ref, work_ref)
        put_packed(step_ref, work_ref[...], mean, packed_blocks(added_ref, out_ref.shape[1]), out_ref)


def whole_matrix(mine_ref, mate_ref):
    is_low = lax.rem(lax.axis_index("col"), 2) == 0
    mine, mate = mine_ref[...], mate_ref[...]
    return jnp.concatenate([jnp.where(is_low, mine, mate), jnp.where(is_low, mate, mine)], axis=0)


def matrix_on(step_mine_ref, mine_ref, mate_ref, out_ref):
    out_ref[...] = dot_nn(step_mine_ref[...], whole_matrix(mine_ref, mate_ref))


def joined(mine_ref, mate_ref, out_ref):
    out_ref[...] = whole_matrix(mine_ref, mate_ref)


def entered(steps, width, psi_ref, covar_ref, mean_ref, mine_ref, mate_ref, step_mine_ref, step_mate_ref, *refs):
    psi_out_ref, covar_out_ref, mean_out_ref, work_ref = refs
    mine = pl.ds(pl.multiple_of(lax.axis_index("col") * width, 8), width)
    before = whole_matrix(step_mine_ref, step_mate_ref)
    mean = unpacked(mine_ref, mate_ref, work_ref)
    covar = work_ref[...]
    for k in range(steps):
        psi_out_ref[k] = dot_nn(psi_ref[k], before)
        half = dot_nn(psi_ref[k, mine, :], covar)
        both = dot_nt(jnp.concatenate([half, mean], axis=0), psi_ref[k])
        covar_out_ref[k] = both[:width] + covar_ref[k]
        mean_out_ref[k] = both[width:] + mean_ref[k]


def finished(steps, width, psi_ref, covar_ref, mean_ref, *refs):
    shares, (covar_out_ref, mean_out_ref, mine_ref, mate_ref, work_ref) = refs[:-5], refs[-5:]
    mine_ref[...] = sum(r[...] for r in shares[0::2])
    mate_ref[...] = sum(r[...] for r in shares[1::2])
    mine = pl.ds(pl.multiple_of(lax.axis_index("col") * width, 8), width)
    mean = unpacked(mine_ref, mate_ref, work_ref)
    rows = jnp.concatenate([psi_ref[k, mine, :] for k in range(steps)], axis=0)
    half = dot_nn(rows, work_ref[...])
    for k in range(steps):
        part = half[k * width : (k + 1) * width]
        both = dot_nt(jnp.concatenate([part, mean], axis=0), psi_ref[k])
        covar_out_ref[k] = both[:width] + covar_ref[k]
        mean_out_ref[k : k + 1, :] = both[width : width + 1] + mean_ref[k, :1, :]


def swapped(block, axis, bit):
    return lax.ppermute(block, axis, [(i, i ^ bit) for i in range(lax.axis_size(axis))])


def shifted(block, distance, start=0, stop=None):
    size = lax.axis_size("seg")
    stop = size - distance if stop is None else stop
    return lax.ppermute(block, "seg", [(i, i + distance) for i in range(start, stop)])


def with_mate(share):
    return (share, swapped(share, "col", 1))


def per_device(
    model_mixing,
    retention,
    forcing,
    observations,
    model_noise,
    obs_noise,
    gain,
    obs_operator_t,
    prior_mean,
    prior_factor,
):
    steps, width, states = model_mixing.shape
    n_col, n_seg = lax.axis_size("col"), lax.axis_size("seg")
    edge = states // 3
    square_shape, mean_shape = (states, states), (MEAN_ROWS, states)
    share_shape, half_shape = (3 * edge + 8, edge), (states // 2, states)
    far_bits = []
    bit = n_col // 2
    while bit > 1:
        far_bits.append(bit)
        bit //= 2
    offsets = [0]
    for bit in far_bits:
        offsets = offsets + [o ^ bit for o in offsets]

    own = [model_mixing]
    for bit in far_bits:
        own = own + [swapped(b, "col", bit) for b in own]
    near = swapped(model_mixing, "seg", 1)
    corr_mine, vectors = local_call(
        correction_rows,
        [(width, states), (steps, 4, states)],
        gain,
        obs_operator_t,
        observations,
        retention,
        forcing,
        model_noise,
        copied=True,
        cost=3,
    )
    corr = [corr_mine]
    for bit in far_bits:
        corr = corr + [swapped(b, "col", bit) for b in corr]
    vectors_other = swapped(vectors, "seg", 1)
    fixed, prior = local_call(
        fixed_parts, [square_shape, square_shape], gain, obs_noise[None, :], prior_factor
    )
    own, near, fixed = lax.optimization_barrier((own, near, fixed))
    other_first = [near[:1]] + [swapped(b[:1], "seg", 1) for b in own[1:]]
    other_rest = [near[1:]]
    for bit in far_bits:
        other_rest = other_rest + [swapped(b, "col", bit) for b in other_rest]
    corr, vectors_other, fixed = lax.optimization_barrier((corr, vectors_other, fixed))
    corr = corr + [swapped(b, "col", 1) for b in corr]

    correction, noise, offset = local_call(
        functools.partial(noises, offsets + [o ^ 1 for o in offsets]),
        [square_shape, (2 * steps,) + square_shape, (2 * steps,) + mean_shape],
        vectors,
        vectors_other,
        fixed,
        *corr,
        scratch=[square_shape],
    )
    rows_shape = (steps,) + half_shape
    every = list(range(steps))
    (rows,) = local_call(
        functools.partial(mixed_rows, [every] * len(own)), [rows_shape], correction, *own
    )
    other_first, other_rest, correction, noise, rows = lax.optimization_barrier(
        (other_first, other_rest, correction, noise, rows)
    )
    (rows_other,) = local_call(
        functools.partial(mixed_rows, [every[:1]] * len(own) + [every[1:]] * len(own)),
        [rows_shape],
        correction,
        *other_first,
        *other_rest,
    )
    matrix, psi, matrix_other, psi_other, psi_half = local_call(
        functools.partial(all_matrices, offsets),
        [(steps,) + square_shape, (steps,) + square_shape, (steps,) + square_shape, square_shape, half_shape],
        vectors,
        vectors_other,
        correction,
        *with_mate(rows),
        *with_mate(rows_other),
        scratch=[square_shape, square_shape],
    )
    if n_seg > 4:
        step = shifted(psi_half, 2, 2)
    covar, mean, covar_other, mean_other, total = local_call(
        functools.partial(pair_covariance, steps),
        [(steps,) + square_shape, (steps,) + mean_shape, square_shape, mean_shape, share_shape],
        noise,
        offset,
        prior,
        prior_mean[None, :],
        matrix,
        psi,
        matrix_other,
        scratch=[square_shape],
    )
    entry = shifted(total, 2)
    psi, covar, mean, psi_all = local_call(
        functools.partial(pair_elements, steps, width),
        [(steps,) + square_shape, (steps, width, states), (steps,) + mean_shape, square_shape],
        psi,
        covar,
        mean,
        psi_other,
        covar_other,
        mean_other,
    )
    if n_seg > 4:
        entry, psi_all, step = lax.optimization_barrier((entry, psi_all, step))
    entry = with_mate(entry)
    entries = [entry]
    distance = 4
    while distance < n_seg:
        more = 2 * distance < n_seg
        (sent,) = local_call(
            functools.partial(carried_on, distance), [share_shape], psi_all, total, *entry, scratch=[square_shape]
        )
        step, sent = lax.optimization_barrier((step, sent))
        step = with_mate(step)
        if more:
            came = with_mate(shifted(sent, distance))
            (sent,) = local_call(matrix_on, [half_shape], psi_half, *step)
            came_step = with_mate(shifted(sent, distance))
            (whole,) = local_call(joined, [square_shape], *step)
            (entry,) = local_call(
                functools.partial(carried_on, 0), [share_shape], whole, entry[0], *came, scratch=[square_shape]
            )
            entry = with_mate(entry)
            (step,) = local_call(matrix_on, [half_shape], step[0], *came_step)
        else:
            early = shifted(total, distance, 0, 2)
            came = shifted(sent, distance, 2)
            psi, covar, mean = local_call(
                functools.partial(entered, steps, width),
                [(steps,) + square_shape, (steps, width, states), (steps,) + mean_shape],
                psi,
                covar,
                mean,
                *entry,
                *step,
                scratch=[square_shape],
            )
            came, psi = lax.optimization_barrier((came, psi))
            entries = [with_mate(early), with_mate(came)]
        distance *= 2

    covars, means = local_call(
        functools.partial(finished, steps, width),
        [(steps, width, states), (steps, states)],
        psi,
        covar,
        mean,
        *[share for pair in entries for share in pair],
        scratch=[share_shape, share_shape, square_shape],
    )
    return means, covars


def solution(mesh):
    in_specs = (
        P("seg", "col", None),
        P("seg", None),
        P("seg", None),
        P("seg", None),
        P("seg", None),
        P(),
        P(),
        P("col", None),
        P(),
        P(),
    )
    out_specs = (P("seg", None), P("seg", "col", None))
    return jax.shard_map(
        per_device, mesh=mesh, in_specs=in_specs, out_specs=out_specs, check_vma=False
    )
```

time: 71.5 us -> 61.5 us (0.86)
  local copies, waits for them, and re-layouts: 5.23 us -> 0.07 us
  starting transfers between devices: 18.6 us -> 14.8 us
  waiting for transfers between devices: 26.9 us -> 25.1 us
  Pallas kernels: 19.5 us -> 20.5 us
    ppermute x17 -> x14, starting transfers between devices: 14.8 us -> 10.3 us  [swapped(): lax.ppermute(block, axis, [(i, i ^ bit) for i in range(lax.axis_size(axis...]
    unnamed x15 -> x14, local copies, waits for them, and re-layouts: 4.49 us -> 0.04 us
    ppermute x3 -> x4, waiting for transfers between devices: 19.6 us -> 15.6 us  [shifted(): lax.ppermute(block, 'seg', [(i, i + distance) for i in range(start, stop)])]
    ppermute x17 -> x14, waiting for transfers between devices: 7.28 us -> 9.44 us  [swapped(): lax.ppermute(block, axis, [(i, i ^ bit) for i in range(lax.axis_size(axis...]
    pallas_call x9 -> x11, Pallas kernels: 19.5 us -> 20.5 us  [local_call(): pl.pallas_call(body, out_shape=shapes, name=getattr(body, 'func', body)._...]
    ppermute x3 -> x4, starting transfers between devices: 3.88 us -> 4.54 us  [shifted(): lax.ppermute(block, 'seg', [(i, i + distance) for i in range(start, stop)])]
  transfers between devices with their start and end apart: 20 -> 18, of which waited for: 5 -> 12; matrix products, arithmetic and copies ran while one was open for 0% -> 0% of each run, Pallas kernels for 20% -> 26%
where the time goes in v3:
time: 61.5 us; the launch traced here: 61.3 us
  waiting for transfers between devices  25.1 us (41%)
  Pallas kernels  20.5 us (33%)
  starting transfers between devices  14.8 us (24%)
  between operations  0.84 us (1%)
    pallas_call x11, Pallas kernels, local_call(): pl.pallas_call(body, out_shape=shapes, name=getattr(body, 'func', body)._...  20.5 us
    ppermute x4, waiting for transfers between devices, shifted(): lax.ppermute(block, 'seg', [(i, i + distance) for i in range(start, stop)])  15.6 us
    ppermute x14, starting transfers between devices, swapped(): lax.ppermute(block, axis, [(i, i ^ bit) for i in range(lax.axis_size(axis...  10.3 us
    ppermute x14, waiting for transfers between devices, swapped(): lax.ppermute(block, axis, [(i, i ^ bit) for i in range(lax.axis_size(axis...  9.44 us
    ppermute x4, starting transfers between devices, shifted(): lax.ppermute(block, 'seg', [(i, i + distance) for i in range(start, stop)])  4.54 us
  transfers between devices with their start and end apart: 18, of which 12 were waited for; matrix products, arithmetic and copies ran while one was open for 0% of the time, Pallas kernels for 26%

profile of v3, /device:TPU:29, one launch (start us, length us, event | category | flops | bytes accessed | tf_op | source)
XLA Modules:
  0.0 61.3 jit_solution(1112741203722621834)
XLA Ops:
  0.7 1.3 %collective-permute-start = (f32[2,96,384]{2,1,0:T(8,128)}, f32[2,96,384]{2,1,0:T(8,128)S(1)}, u32[]{:S(2)}, u32[]{:S(2)}) collective-permute-start(f32[2,96,384]{2,1,0:T(8,128)} %refs_0_), channel_id=1, source_target_pairs={{0,2},{1,3},{2,0},{3,1},{4,6},{5,7},{6,4},{7,5},{8,10},{9,11},{10,... | collective-permute-start | bytes 884744 | tf_op jit(solution)/shard_map/ppermute | solution.py:409
  2.2 3.0 %correction_rows.1 = (f32[96,384]{1,0:T(8,128)}, f32[2,4,384]{2,1,0:T(4,128)}) custom-call(f32[384,1024]{1,0:T(8,128)} %gain_hbm.1, f32[96,1024]{1,0:T(8,128)} %oper_hbm.1, f32[2,1024]{1,0:T(2,128)} %seen_hbm.1, f32[2,384]{1,0:T(2,128)} %keep_hbm.1, f32[2,384]{1,0:T(2,128)} %push_hbm.1, f32[2,384]{1,0:T(2,128)} %var_hbm.1), custom_call_target="tpu_custom_call" | custom-call | flops 2100000000 | bytes 4096 | tf_op jit(solution)/shard_map/correction_rows/pallas_call | solution.py:52
  5.2 0.4 collective-permute-start.4
  5.6 1.2 %collective-permute-start.5 = (f32[2,4,384]{2,1,0:T(4,128)}, f32[2,4,384]{2,1,0:T(4,128)S(1)}, u32[]{:S(2)}, u32[]{:S(2)}) collective-permute-start(f32[2,4,384]{2,1,0:T(4,128)} %get-tuple-element.53.vec_ref), channel_id=1, source_target_pairs={{0,4},{4,0},{8,12},{12,8},{16,20},{20,16},{24,28},{28,24},{1,5},{5... | collective-permute-start | bytes 36872 | tf_op jit(solution)/shard_map/ppermute | solution.py:409
  6.8 1.4 %fixed_parts.1 = (f32[384,384]{1,0:T(8,128)S(1)}, f32[384,384]{1,0:T(8,128)S(1)}) custom-call(f32[384,1024]{1,0:T(8,128)S(1)} %copy-done, f32[1,1024]{1,0:T(1,128)S(1)} %bitcast.1, f32[384,384]{1,0:T(8,128)S(1)} %copy-done.1), custom_call_target="tpu_custom_call" | custom-call | bytes 4096 | tf_op jit(solution)/shard_map/fixed_parts/pallas_call | solution.py:52
  8.2 0.6 collective-permute-done.refs_1_
  8.8 0.9 %collective-permute-done.1 = f32[2,96,384]{2,1,0:T(8,128)S(1)} collective-permute-done((f32[2,96,384]{2,1,0:T(8,128)}, f32[2,96,384]{2,1,0:T(8,128)S(1)}, u32[]{:S(2)}, u32[]{:S(2)}) %collective-permute-start.1) | collective-permute-done | bytes 294944 | tf_op jit(solution)/shard_map/ppermute | solution.py:409
  10.0 2.0 %collective-permute-done.4.refs_1_ = f32[96,384]{1,0:T(8,128)S(1)} collective-permute-done((f32[96,384]{1,0:T(8,128)}, f32[96,384]{1,0:T(8,128)S(1)}, u32[]{:S(2)}, u32[]{:S(2)}) %collective-permute-start.4) | collective-permute-done | bytes 147488 | tf_op jit(solution)/shard_map/ppermute | solution.py:409
  12.0 1.5 %collective-permute-start.6 = (f32[96,384]{1,0:T(8,128)S(1)}, f32[96,384]{1,0:T(8,128)S(1)}, u32[]{:S(2)}, u32[]{:S(2)}) collective-permute-start(f32[96,384]{1,0:T(8,128)S(1)} %copy-done.3), channel_id=1, source_target_pairs={{0,1},{1,0},{2,3},{3,2},{4,5},{5,4},{6,7},{7,6},{8,9},{9,8},{10,11... | collective-permute-start | bytes 442376 | tf_op jit(solution)/shard_map/ppermute | solution.py:409
  13.6 1.3 %collective-permute-start.3 = (f32[1,96,384]{2,1,0:T(8,128)S(1)}, f32[1,96,384]{2,1,0:T(8,128)S(1)}, u32[]{:S(2)}, u32[]{:S(2)}) collective-permute-start(f32[1,96,384]{2,1,0:T(8,128)S(1)} %get-tuple-element.70.refs_2_), channel_id=1, source_target_pairs={{0,2},{1,3},{2,0},{3,1},{4,6},{5,7},{6,4},{7,5},{8,10},{9,11},{10,... | collective-permute-start | bytes 442376 | tf_op jit(solution)/shard_map/ppermute | solution.py:409
  15.1 2.5 %noises.1 = (f32[384,384]{1,0:T(8,128)S(1)}, f32[4,384,384]{2,1,0:T(8,128)S(1)}, f32[4,16,384]{2,1,0:T(8,128)S(1)}) custom-call(f32[2,4,384]{2,1,0:T(4,128)S(1)} %copy-done.4, f32[2,4,384]{2,1,0:T(4,128)S(1)} %collective-permute-done.5.vec_other_ref, f32[384,384]{1,0:T(8,128)S(1)} %get-tuple-element.57.fixed_ref, f32[96,384]{1,0:T(8,128)S(1)} %copy-done.3, ...), custom_call_target="tpu_custom_call" | custom-call | bytes 4096 | tf_op jit(solution)/shard_map/noises/pallas_call | solution.py:52
  17.7 0.7 %mixed_rows.2.mine_ref = f32[2,192,384]{2,1,0:T(8,128)S(1)} custom-call(f32[384,384]{1,0:T(8,128)S(1)} %get-tuple-element.66.corr_ref, f32[2,96,384]{2,1,0:T(8,128)S(1)} %copy-done.2, f32[2,96,384]{2,1,0:T(8,128)S(1)} %collective-permute-done.refs_1_), custom_call_target="tpu_custom_call" | custom-call | bytes 4096 | tf_op jit(solution)/shard_map/mixed_rows/pallas_call | solution.py:52
  18.5 1.0 %collective-permute-done.2.refs_1_ = f32[1,96,384]{2,1,0:T(8,128)S(1)} collective-permute-done((f32[1,96,384]{2,1,0:T(8,128)S(1)}, f32[1,96,384]{2,1,0:T(8,128)S(1)}, u32[]{:S(2)}, u32[]{:S(2)}) %collective-permute-start.2) | collective-permute-done | bytes 147488 | tf_op jit(solution)/shard_map/ppermute | solution.py:409
  19.5 0.7 %mixed_rows.3.mine_other_ref = f32[2,192,384]{2,1,0:T(8,128)S(1)} custom-call(f32[384,384]{1,0:T(8,128)S(1)} %get-tuple-element.66.corr_ref, f32[1,96,384]{2,1,0:T(8,128)S(1)} %get-tuple-element.68.refs_0_, f32[1,96,384]{2,1,0:T(8,128)S(1)} %collective-permute-done.2.refs_1_, f32[1,96,384]{2,1,0:T(8,128)S(1)} %get-tuple-element.70.refs_2_, ...), custom_call_target="tpu_custom_call" | custom-call | bytes 4096 | tf_op jit(solution)/shard_map/mixed_rows/pallas_call | solution.py:52
  20.2 1.7 %collective-permute-start.9 = (f32[2,192,384]{2,1,0:T(8,128)S(1)}, f32[2,192,384]{2,1,0:T(8,128)S(1)}, u32[]{:S(2)}, u32[]{:S(2)}) collective-permute-start(f32[2,192,384]{2,1,0:T(8,128)S(1)} %mixed_rows.3.mine_other_ref), channel_id=1, source_target_pairs={{0,1},{1,0},{2,3},{3,2},{4,5},{5,4},{6,7},{7,6},{8,9},{9,8},{10,11... | collective-permute-start | bytes 1769480 | tf_op jit(solution)/shard_map/ppermute | solution.py:409
  22.0 1.6 %collective-permute-done.9.mate_other_ref = f32[2,192,384]{2,1,0:T(8,128)S(1)} collective-permute-done((f32[2,192,384]{2,1,0:T(8,128)S(1)}, f32[2,192,384]{2,1,0:T(8,128)S(1)}, u32[]{:S(2)}, u32[]{:S(2)}) %collective-permute-start.9) | collective-permute-done | bytes 589856 | tf_op jit(solution)/shard_map/ppermute | solution.py:409
  23.6 0.8 %collective-permute-done.8.mate_ref = f32[2,192,384]{2,1,0:T(8,128)S(1)} collective-permute-done((f32[2,192,384]{2,1,0:T(8,128)S(1)}, f32[2,192,384]{2,1,0:T(8,128)S(1)}, u32[]{:S(2)}, u32[]{:S(2)}) %collective-permute-start.8) | collective-permute-done | bytes 589856 | tf_op jit(solution)/shard_map/ppermute | solution.py:409
  24.4 2.1 %all_matrices.1 = (f32[2,384,384]{2,1,0:T(8,128)S(1)}, f32[2,384,384]{2,1,0:T(8,128)S(1)}, f32[2,384,384]{2,1,0:T(8,128)S(1)}, f32[384,384]{1,0:T(8,128)S(1)}, f32[192,384]{1,0:T(8,128)S(1)}) custom-call(f32[2,4,384]{2,1,0:T(4,128)S(1)} %copy-done.4, f32[2,4,384]{2,1,0:T(4,128)S(1)} %collective-permute-done.5.vec_other_ref, ...), custom_call_target="tpu_custom_call" | custom-call | bytes 4096 | tf_op jit(solution)/shard_map/all_matrices/pallas_call | solution.py:52
  26.5 1.3 %collective-permute-start.11 = (f32[192,384]{1,0:T(8,128)S(1)}, f32[192,384]{1,0:T(8,128)S(1)}, u32[]{:S(2)}, u32[]{:S(2)}) collective-permute-start(f32[192,384]{1,0:T(8,128)S(1)} %get-tuple-element.82), channel_id=1, source_target_pairs={{8,16},{12,20},{16,24},{20,28},{9,17},{13,21},{17,25},{21,29},{10,... | collective-permute-start | bytes 884744 | tf_op jit(solution)/shard_map/ppermute | solution.py:415
  27.8 3.5 %pair_covariance.1 = (f32[2,384,384]{2,1,0:T(8,128)S(1)}, f32[2,16,384]{2,1,0:T(8,128)S(1)}, f32[384,384]{1,0:T(8,128)S(1)}, f32[16,384]{1,0:T(8,128)S(1)}, f32[392,128]{1,0:T(8,128)S(1)}) custom-call(f32[4,384,384]{2,1,0:T(8,128)S(1)} %get-tuple-element.63.noise_ref, f32[4,16,384]{2,1,0:T(8,128)S(1)} %get-tuple-element.64.offset_ref, ...), custom_call_target="tpu_custom_call" | custom-call | bytes 4096 | tf_op jit(solution)/shard_map/pair_covariance/pallas_call | solution.py:52
  31.4 1.3 %collective-permute-start.10 = (f32[392,128]{1,0:T(8,128)S(1)}, f32[392,128]{1,0:T(8,128)S(1)}, u32[]{:S(2)}, u32[]{:S(2)}) collective-permute-start(f32[392,128]{1,0:T(8,128)S(1)} %get-tuple-element.75.added_ref), channel_id=1, source_target_pairs={{0,8},{4,12},{8,16},{12,20},{16,24},{20,28},{1,9},{5,13},{9,17},{1... | collective-permute-start | bytes 602120 | tf_op jit(solution)/shard_map/ppermute | solution.py:415
  32.7 2.5 %pair_elements.1 = (f32[2,384,384]{2,1,0:T(8,128)S(1)}, f32[2,96,384]{2,1,0:T(8,128)S(1)}, f32[2,16,384]{2,1,0:T(8,128)S(1)}, f32[384,384]{1,0:T(8,128)S(1)}) custom-call(f32[2,384,384]{2,1,0:T(8,128)S(1)} %get-tuple-element.73.psi_ref, f32[2,384,384]{2,1,0:T(8,128)S(1)} %get-tuple-element.76.covar_ref, f32[2,16,384]{2,1,0:T(8,128)S(1)} %get-tuple-element.77.mean_ref, ...), custom_call_target="tpu_custom_call" | custom-call | bytes 4096 | tf_op jit(solution)/shard_map/pair_elements/pallas_call | solution.py:52
  35.2 5.7 %collective-permute-done.10.mine_ref = f32[392,128]{1,0:T(8,128)S(1)} collective-permute-done((f32[392,128]{1,0:T(8,128)S(1)}, f32[392,128]{1,0:T(8,128)S(1)}, u32[]{:S(2)}, u32[]{:S(2)}) %collective-permute-start.10) | collective-permute-done | bytes 200736 | tf_op jit(solution)/shard_map/ppermute | solution.py:415
  40.9 1.2 %collective-permute-start.12 = (f32[392,128]{1,0:T(8,128)S(1)}, f32[392,128]{1,0:T(8,128)S(1)}, u32[]{:S(2)}, u32[]{:S(2)}) collective-permute-start(f32[392,128]{1,0:T(8,128)S(1)} %collective-permute-done.10.mine_ref), channel_id=1, source_target_pairs={{0,1},{1,0},{2,3},{3,2},{4,5},{5,4},{6,7},{7,6},{8,9},{9,8},{10,11... | collective-permute-start | bytes 602120 | tf_op jit(solution)/shard_map/ppermute | solution.py:409
  42.1 1.1 %collective-permute-done.12.mate_ref = f32[392,128]{1,0:T(8,128)S(1)} collective-permute-done((f32[392,128]{1,0:T(8,128)S(1)}, f32[392,128]{1,0:T(8,128)S(1)}, u32[]{:S(2)}, u32[]{:S(2)}) %collective-permute-start.12) | collective-permute-done | bytes 200736 | tf_op jit(solution)/shard_map/ppermute | solution.py:409
  43.6 0.7 %collective-permute-start.15 = (f32[392,128]{1,0:T(8,128)S(1)}, f32[392,128]{1,0:T(8,128)S(1)}, u32[]{:S(2)}, u32[]{:S(2)}) collective-permute-start(f32[392,128]{1,0:T(8,128)S(1)} %get-tuple-element.75.added_ref), channel_id=1, source_target_pairs={{0,16},{4,20},{1,17},{5,21},{2,18},{6,22},{3,19},{7,23}} | collective-permute-start | bytes 602120 | tf_op jit(solution)/shard_map/ppermute | solution.py:415
  44.2 1.3 %collective-permute-start.13 = (f32[392,128]{1,0:T(8,128)S(1)}, f32[392,128]{1,0:T(8,128)S(1)}, u32[]{:S(2)}, u32[]{:S(2)}) collective-permute-start(f32[392,128]{1,0:T(8,128)S(1)} %carried_on.1), channel_id=1, source_target_pairs={{8,24},{12,28},{9,25},{13,29},{10,26},{14,30},{11,27},{15,31}} | collective-permute-start | bytes 602120 | tf_op jit(solution)/shard_map/ppermute | solution.py:415
  45.8 2.3 %entered.1 = (f32[2,384,384]{2,1,0:T(8,128)S(1)}, f32[2,96,384]{2,1,0:T(8,128)S(1)}, f32[2,16,384]{2,1,0:T(8,128)S(1)}) custom-call(f32[2,384,384]{2,1,0:T(8,128)S(1)} %get-tuple-element.87.psi_ref, f32[2,96,384]{2,1,0:T(8,128)S(1)} %get-tuple-element.88.covar_ref, f32[2,16,384]{2,1,0:T(8,128)S(1)} %get-tuple-element.89.mean_ref, ...), custom_call_target="tpu_custom_call" | custom-call | bytes 4096 | tf_op jit(solution)/shard_map/entered/pallas_call | solution.py:52
  48.0 9.9 %collective-permute-done.13.refs_2_ = f32[392,128]{1,0:T(8,128)S(1)} collective-permute-done((f32[392,128]{1,0:T(8,128)S(1)}, f32[392,128]{1,0:T(8,128)S(1)}, u32[]{:S(2)}, u32[]{:S(2)}) %collective-permute-start.13) | collective-permute-done | bytes 200736 | tf_op jit(solution)/shard_map/ppermute | solution.py:415
  57.9 0.5 collective-permute-start.17
  58.4 1.1 %collective-permute-done.17.refs_3_ = f32[392,128]{1,0:T(8,128)S(1)} collective-permute-done((f32[392,128]{1,0:T(8,128)S(1)}, f32[392,128]{1,0:T(8,128)S(1)}, u32[]{:S(2)}, u32[]{:S(2)}) %collective-permute-start.17) | collective-permute-done | bytes 200736 | tf_op jit(solution)/shard_map/ppermute | solution.py:409
  59.5 1.8 %finished.1 = (f32[2,96,384]{2,1,0:T(8,128)}, f32[2,384]{1,0:T(2,128)}) custom-call(f32[2,384,384]{2,1,0:T(8,128)S(1)} %get-tuple-element.92.psi_ref, f32[2,96,384]{2,1,0:T(8,128)S(1)} %get-tuple-element.93.covar_ref, f32[2,16,384]{2,1,0:T(8,128)S(1)} %get-tuple-element.94.mean_ref, f32[392,128]{1,0:T(8,128)S(1)} %collective-permute-done.15.refs_0_, ...), custom_call_target="tpu_custom_call" | custom-call | bytes 4096 | tf_op jit(solution)/shard_map/finished/pallas_call | solution.py:52
  (32 shorter events, 1.7 us)
Async XLA Ops:
  0.6 6.1 %copy-start = (f32[384,1024]{1,0:T(8,128)S(1)}, f32[384,1024]{1,0:T(8,128)}, u32[]{:S(2)}) copy-start(f32[384,1024]{1,0:T(8,128)} %gain_hbm.1) | copy-start | bytes 4718596
  0.6 6.1 %copy-start.5 = (f32[1024]{0:T(1024)S(1)}, f32[1024]{0:T(1024)}, u32[]{:S(2)}) copy-start(f32[1024]{0:T(1024)} %param.15) | copy-start | bytes 12292
  0.7 6.1 %copy-start.1 = (f32[384,384]{1,0:T(8,128)S(1)}, f32[384,384]{1,0:T(8,128)}, u32[]{:S(2)}) copy-start(f32[384,384]{1,0:T(8,128)} %factor_ref.1) | copy-start | bytes 1769476
  0.7 8.2 %collective-permute-start = (f32[2,96,384]{2,1,0:T(8,128)}, f32[2,96,384]{2,1,0:T(8,128)S(1)}, u32[]{:S(2)}, u32[]{:S(2)}) collective-permute-start(f32[2,96,384]{2,1,0:T(8,128)} %refs_0_), channel_id=1, source_target_pairs={{0,2},{1,3},{2,0},{3,1},{4,6},{5,7},{6,4},{7,5},{8,10},{9,11},{10,... | collective-permute-start | bytes 884744 | tf_op jit(solution)/shard_map/ppermute | solution.py:409
  1.9 7.8 %collective-permute-start.1 = (f32[2,96,384]{2,1,0:T(8,128)}, f32[2,96,384]{2,1,0:T(8,128)S(1)}, u32[]{:S(2)}, u32[]{:S(2)}) collective-permute-start(f32[2,96,384]{2,1,0:T(8,128)} %refs_0_), channel_id=1, source_target_pairs={{0,4},{4,0},{8,12},{12,8},{16,20},{20,16},{24,28},{28,24},{1,5},{5... | collective-permute-start | bytes 884744 | tf_op jit(solution)/shard_map/ppermute | solution.py:409
  5.2 6.8 %copy-start.3 = (f32[96,384]{1,0:T(8,128)S(1)}, f32[96,384]{1,0:T(8,128)}, u32[]{:S(2)}) copy-start(f32[96,384]{1,0:T(8,128)} %get-tuple-element.58.refs_0_) | copy-start | bytes 442372
  5.2 6.8 %collective-permute-start.4 = (f32[96,384]{1,0:T(8,128)}, f32[96,384]{1,0:T(8,128)S(1)}, u32[]{:S(2)}, u32[]{:S(2)}) collective-permute-start(f32[96,384]{1,0:T(8,128)} %get-tuple-element.58.refs_0_), channel_id=1, source_target_pairs={{0,2},{1,3},{2,0},{3,1},{4,6},{5,7},{6,4},{7,5},{8,10},{9,11},{10,... | collective-permute-start | bytes 442376 | tf_op jit(solution)/shard_map/ppermute | solution.py:409
  5.6 4.4 %collective-permute-start.5 = (f32[2,4,384]{2,1,0:T(4,128)}, f32[2,4,384]{2,1,0:T(4,128)S(1)}, u32[]{:S(2)}, u32[]{:S(2)}) collective-permute-start(f32[2,4,384]{2,1,0:T(4,128)} %get-tuple-element.53.vec_ref), channel_id=1, source_target_pairs={{0,4},{4,0},{8,12},{12,8},{16,20},{20,16},{24,28},{28,24},{1,5},{5... | collective-permute-start | bytes 36872 | tf_op jit(solution)/shard_map/ppermute | solution.py:409
  6.8 8.4 %copy-start.4 = (f32[2,4,384]{2,1,0:T(4,128)S(1)}, f32[2,4,384]{2,1,0:T(4,128)}, u32[]{:S(2)}) copy-start(f32[2,4,384]{2,1,0:T(4,128)} %get-tuple-element.53.vec_ref) | copy-start | bytes 36868
  8.2 9.5 %copy-start.2 = (f32[2,96,384]{2,1,0:T(8,128)S(1)}, f32[2,96,384]{2,1,0:T(8,128)}, u32[]{:S(2)}) copy-start(f32[2,96,384]{2,1,0:T(8,128)} %refs_0_) | copy-start | bytes 884740
  12.0 3.2 %collective-permute-start.6 = (f32[96,384]{1,0:T(8,128)S(1)}, f32[96,384]{1,0:T(8,128)S(1)}, u32[]{:S(2)}, u32[]{:S(2)}) collective-permute-start(f32[96,384]{1,0:T(8,128)S(1)} %copy-done.3), channel_id=1, source_target_pairs={{0,1},{1,0},{2,3},{3,2},{4,5},{5,4},{6,7},{7,6},{8,9},{9,8},{10,11... | collective-permute-start | bytes 442376 | tf_op jit(solution)/shard_map/ppermute | solution.py:409
  13.5 1.6 %collective-permute-start.7 = (f32[96,384]{1,0:T(8,128)S(1)}, f32[96,384]{1,0:T(8,128)S(1)}, u32[]{:S(2)}, u32[]{:S(2)}) collective-permute-start(f32[96,384]{1,0:T(8,128)S(1)} %collective-permute-done.4.refs_1_), channel_id=1, source_target_pairs={{0,1},{1,0},{2,3},{3,2},{4,5},{5,4},{6,7},{7,6},{8,9},{9,8},{10,11... | collective-permute-start | bytes 442376 | tf_op jit(solution)/shard_map/ppermute | solution.py:409
  13.6 5.0 %collective-permute-start.3 = (f32[1,96,384]{2,1,0:T(8,128)S(1)}, f32[1,96,384]{2,1,0:T(8,128)S(1)}, u32[]{:S(2)}, u32[]{:S(2)}) collective-permute-start(f32[1,96,384]{2,1,0:T(8,128)S(1)} %get-tuple-element.70.refs_2_), channel_id=1, source_target_pairs={{0,2},{1,3},{2,0},{3,1},{4,6},{5,7},{6,4},{7,5},{8,10},{9,11},{10,... | collective-permute-start | bytes 442376 | tf_op jit(solution)/shard_map/ppermute | solution.py:409
  14.8 4.7 %collective-permute-start.2 = (f32[1,96,384]{2,1,0:T(8,128)S(1)}, f32[1,96,384]{2,1,0:T(8,128)S(1)}, u32[]{:S(2)}, u32[]{:S(2)}) collective-permute-start(f32[1,96,384]{2,1,0:T(8,128)S(1)} %slice.10), channel_id=1, source_target_pairs={{0,4},{4,0},{8,12},{12,8},{16,20},{20,16},{24,28},{28,24},{1,5},{5... | collective-permute-start | bytes 442376 | tf_op jit(solution)/shard_map/ppermute | solution.py:409
  20.2 7.6 %copy-start.6 = (f32[384]{0:T(512)S(1)}, f32[384]{0:T(512)}, u32[]{:S(2)}) copy-start(f32[384]{0:T(512)} %param.18) | copy-start | bytes 4612
  20.2 3.4 %collective-permute-start.9 = (f32[2,192,384]{2,1,0:T(8,128)S(1)}, f32[2,192,384]{2,1,0:T(8,128)S(1)}, u32[]{:S(2)}, u32[]{:S(2)}) collective-permute-start(f32[2,192,384]{2,1,0:T(8,128)S(1)} %mixed_rows.3.mine_other_ref), channel_id=1, source_target_pairs={{0,1},{1,0},{2,3},{3,2},{4,5},{5,4},{6,7},{7,6},{8,9},{9,8},{10,11... | collective-permute-start | bytes 1769480 | tf_op jit(solution)/shard_map/ppermute | solution.py:409
  21.9 2.5 %collective-permute-start.8 = (f32[2,192,384]{2,1,0:T(8,128)S(1)}, f32[2,192,384]{2,1,0:T(8,128)S(1)}, u32[]{:S(2)}, u32[]{:S(2)}) collective-permute-start(f32[2,192,384]{2,1,0:T(8,128)S(1)} %mixed_rows.2.mine_ref), channel_id=1, source_target_pairs={{0,1},{1,0},{2,3},{3,2},{4,5},{5,4},{6,7},{7,6},{8,9},{9,8},{10,11... | collective-permute-start | bytes 1769480 | tf_op jit(solution)/shard_map/ppermute | solution.py:409
  26.5 14.4 %collective-permute-start.11 = (f32[192,384]{1,0:T(8,128)S(1)}, f32[192,384]{1,0:T(8,128)S(1)}, u32[]{:S(2)}, u32[]{:S(2)}) collective-permute-start(f32[192,384]{1,0:T(8,128)S(1)} %get-tuple-element.82), channel_id=1, source_target_pairs={{8,16},{12,20},{16,24},{20,28},{9,17},{13,21},{17,25},{21,29},{10,... | collective-permute-start | bytes 884744 | tf_op jit(solution)/shard_map/ppermute | solution.py:415
  31.4 9.5 %collective-permute-start.10 = (f32[392,128]{1,0:T(8,128)S(1)}, f32[392,128]{1,0:T(8,128)S(1)}, u32[]{:S(2)}, u32[]{:S(2)}) collective-permute-start(f32[392,128]{1,0:T(8,128)S(1)} %get-tuple-element.75.added_ref), channel_id=1, source_target_pairs={{0,8},{4,12},{8,16},{12,20},{16,24},{20,28},{1,9},{5,13},{9,17},{1... | collective-permute-start | bytes 602120 | tf_op jit(solution)/shard_map/ppermute | solution.py:415
  40.9 2.3 %collective-permute-start.12 = (f32[392,128]{1,0:T(8,128)S(1)}, f32[392,128]{1,0:T(8,128)S(1)}, u32[]{:S(2)}, u32[]{:S(2)}) collective-permute-start(f32[392,128]{1,0:T(8,128)S(1)} %collective-permute-done.10.mine_ref), channel_id=1, source_target_pairs={{0,1},{1,0},{2,3},{3,2},{4,5},{5,4},{6,7},{7,6},{8,9},{9,8},{10,11... | collective-permute-start | bytes 602120 | tf_op jit(solution)/shard_map/ppermute | solution.py:409
  43.2 2.6 %collective-permute-start.14 = (f32[192,384]{1,0:T(8,128)S(1)}, f32[192,384]{1,0:T(8,128)S(1)}, u32[]{:S(2)}, u32[]{:S(2)}) collective-permute-start(f32[192,384]{1,0:T(8,128)S(1)} %collective-permute-done.11.step_mine_ref), channel_id=1, source_target_pairs={{0,1},{1,0},{2,3},{3,2},{4,5},{5,4},{6,7},{7,6},{8,9},{9,8},{10,11... | collective-permute-start | bytes 884744 | tf_op jit(solution)/shard_map/ppermute | solution.py:409
  43.6 2.0 %collective-permute-start.15 = (f32[392,128]{1,0:T(8,128)S(1)}, f32[392,128]{1,0:T(8,128)S(1)}, u32[]{:S(2)}, u32[]{:S(2)}) collective-permute-start(f32[392,128]{1,0:T(8,128)S(1)} %get-tuple-element.75.added_ref), channel_id=1, source_target_pairs={{0,16},{4,20},{1,17},{5,21},{2,18},{6,22},{3,19},{7,23}} | collective-permute-start | bytes 602120 | tf_op jit(solution)/shard_map/ppermute | solution.py:415
  44.2 13.7 %collective-permute-start.13 = (f32[392,128]{1,0:T(8,128)S(1)}, f32[392,128]{1,0:T(8,128)S(1)}, u32[]{:S(2)}, u32[]{:S(2)}) collective-permute-start(f32[392,128]{1,0:T(8,128)S(1)} %carried_on.1), channel_id=1, source_target_pairs={{8,24},{12,28},{9,25},{13,29},{10,26},{14,30},{11,27},{15,31}} | collective-permute-start | bytes 602120 | tf_op jit(solution)/shard_map/ppermute | solution.py:415
  45.5 12.9 %collective-permute-start.16 = (f32[392,128]{1,0:T(8,128)S(1)}, f32[392,128]{1,0:T(8,128)S(1)}, u32[]{:S(2)}, u32[]{:S(2)}) collective-permute-start(f32[392,128]{1,0:T(8,128)S(1)} %collective-permute-done.15.refs_0_), channel_id=1, source_target_pairs={{0,1},{1,0},{2,3},{3,2},{4,5},{5,4},{6,7},{7,6},{8,9},{9,8},{10,11... | collective-permute-start | bytes 602120 | tf_op jit(solution)/shard_map/ppermute | solution.py:409
  57.9 1.5 %collective-permute-start.17 = (f32[392,128]{1,0:T(8,128)S(1)}, f32[392,128]{1,0:T(8,128)S(1)}, u32[]{:S(2)}, u32[]{:S(2)}) collective-permute-start(f32[392,128]{1,0:T(8,128)S(1)} %collective-permute-done.13.refs_2_), channel_id=1, source_target_pairs={{0,1},{1,0},{2,3},{3,2},{4,5},{5,4},{6,7},{7,6},{8,9},{9,8},{10,11... | collective-permute-start | bytes 602120 | tf_op jit(solution)/shard_map/ppermute | solution.py:409

commit v4 on v3

--- a/solution.py
+++ b/solution.py
@@ -122,33 +122,39 @@
         out_ref[pl.ds(at, width), :] = piece
 
 
-def noises(offsets, vec_ref, vec_other_ref, fixed_ref, *refs):
-    pieces, (corr_ref, noise_ref, offset_ref, work_ref) = refs[:-4], refs[-4:]
+def noises(vec_ref, vec_other_ref, fixed_ref, corr_ref, noise_ref, offset_ref):
     states = corr_ref.shape[0]
     steps = vec_ref.shape[0]
-    place([p[...] for p in pieces], offsets, work_ref, 0)
-    corr = work_ref[...].T
-    corr_ref[...] = corr
-    right = as_right(corr, 1)
+    corr = corr_ref[...]
     vectors = [vec_ref[k] for k in range(steps)] + [vec_other_ref[k] for k in range(steps)]
     push = [v[2:3] for v in vectors] + [jnp.zeros((MEAN_ROWS - 2 * steps, states), F32)]
     left = jnp.concatenate([corr * v[1:2] for v in vectors] + push, axis=0)
-    both = lax.dot_general(as_left(left), right, NT, preferred_element_type=F32)
+    both = dot_nt(left, corr)
     base = 2 * steps * states
     for k in range(2 * steps):
         noise_ref[k] = both[k * states : (k + 1) * states] + fixed_ref[...]
         offset_ref[k] = mean_block(both[base + k : base + k + 1] + vectors[k][3:4], states)
 
 
-def mixed_rows(steps_of, corr_ref, *refs):
-    pieces, (out_ref,) = refs[:-1], refs[-1:]
-    width = pieces[0].shape[1]
-    blocks = [(k, piece[i]) for piece, of in zip(pieces, steps_of) for i, k in enumerate(of)]
-    mixed = dot_nt(jnp.concatenate([block for _, block in blocks], axis=0), corr_ref[...])
-    filled = [0] * out_ref.shape[0]
-    for i, (k, _) in enumerate(blocks):
-        out_ref[k, filled[k] : filled[k] + width, :] = mixed[i * width : (i + 1) * width]
-        filled[k] += width
+def mixed_rows(out_ref, pieces, corr):
+    steps, width = pieces[0].shape[:2]
+    rows = jnp.concatenate([piece[k] for k in range(steps) for piece in pieces], axis=0)
+    mixed = dot_nt(rows, corr)
+    half = width * len(pieces)
+    for k in range(steps):
+        out_ref[k] = mixed[k * half : (k + 1) * half]
+
+
+def own_rows(offsets, *refs):
+    n_piece = len(offsets)
+    pieces, own, (corr_ref, out_ref, work_ref) = refs[:n_piece], refs[n_piece:-3], refs[-3:]
+    place([p[...] for p in pieces], offsets, work_ref, 0)
+    corr_ref[...] = work_ref[...].T
+    mixed_rows(out_ref, own, corr_ref[...])
+
+
+def other_rows(corr_ref, *refs):
+    mixed_rows(refs[-1], refs[:-1], corr_ref[...])
 
 
 def matrices_of(offsets, vec_ref, corr, mine_ref, mate_ref, work_ref, out_ref):
@@ -161,26 +167,31 @@
         out_ref[k] = work_ref[...].T + corr * vec_ref[k, 0:1, :]
 
 
-def all_matrices(
-    offsets, vec_ref, vec_other_ref, corr_ref, mine_ref, mate_ref, mine_other_ref, mate_other_ref,
-    matrix_ref, psi_ref, matrix_other_ref, psi_other_ref, psi_half_ref, work_ref, work_other_ref,
+def own_matrices(offsets, vec_ref, corr_ref, mine_ref, mate_ref, matrix_ref, psi_ref, work_ref):
+    matrices_of(offsets, vec_ref, corr_ref[...], mine_ref, mate_ref, work_ref, matrix_ref)
+    psi_ref[0] = matrix_ref[0]
+    for k in range(1, matrix_ref.shape[0]):
+        psi_ref[k] = dot_nn(matrix_ref[k], psi_ref[k - 1])
+
+
+def other_matrices(
+    offsets, vec_ref, corr_ref, mine_ref, mate_ref, psi_ref, matrix_ref, psi_other_ref, psi_half_ref, work_ref
 ):
     steps, half, states = mine_ref.shape
     seg = lax.axis_index("seg")
     is_second = lax.rem(seg, 2) == 1
-    corr = corr_ref[...]
-    matrices_of(offsets, vec_ref, corr, mine_ref, mate_ref, work_ref, matrix_ref)
-    matrices_of(offsets, vec_other_ref, corr, mine_other_ref, mate_other_ref, work_other_ref, matrix_other_ref)
+    matrices_of(offsets, vec_ref, corr_ref[...], mine_ref, mate_ref, work_ref, matrix_ref)
     mine = pl.ds(pl.multiple_of(lax.rem(lax.axis_index("col"), 2) * half, 8), half)
-    psi_ref[0] = matrix_ref[0]
-    for k in range(1, steps):
-        psi_ref[k] = dot_nn(matrix_ref[k], psi_ref[k - 1])
+
+    @pl.when(seg < 2)
+    def _():
+        psi_half_ref[...] = jnp.zeros_like(psi_half_ref)
 
     @pl.when(seg >= 2)
     def _():
-        psi_other_ref[...] = matrix_other_ref[0]
+        psi_other_ref[...] = matrix_ref[0]
         for k in range(1, steps):
-            psi_other_ref[...] = dot_nn(matrix_other_ref[k], psi_other_ref[...])
+            psi_other_ref[...] = dot_nn(matrix_ref[k], psi_other_ref[...])
 
         @pl.when(is_second)
         def _():
@@ -308,6 +319,7 @@
     @pl.when(seg < 2)
     def _():
         psi_out_ref[...] = jnp.zeros_like(psi_out_ref)
+        psi_all_ref[...] = jnp.zeros_like(psi_all_ref)
 
     @pl.when(seg >= 2)
     def _():
@@ -355,64 +367,85 @@
     return blocks
 
 
-def carried_on(distance, step_ref, added_ref, mine_ref, mate_ref, out_ref, work_ref):
-    @pl.when(lax.axis_index("seg") < lax.axis_size("seg") - distance)
-    def _():
-        mean = unpacked(mine_ref, mate_ref, work_ref)
-        put_packed(step_ref, work_ref[...], mean, packed_blocks(added_ref, out_ref.shape[1]), out_ref)
-
-
 def whole_matrix(mine_ref, mate_ref):
     is_low = lax.rem(lax.axis_index("col"), 2) == 0
     mine, mate = mine_ref[...], mate_ref[...]
     return jnp.concatenate([jnp.where(is_low, mine, mate), jnp.where(is_low, mate, mine)], axis=0)
 
 
-def matrix_on(step_mine_ref, mine_ref, mate_ref, out_ref):
-    out_ref[...] = dot_nn(step_mine_ref[...], whole_matrix(mine_ref, mate_ref))
-
-
-def joined(mine_ref, mate_ref, out_ref):
-    out_ref[...] = whole_matrix(mine_ref, mate_ref)
-
-
-def entered(steps, width, psi_ref, covar_ref, mean_ref, mine_ref, mate_ref, step_mine_ref, step_mate_ref, *refs):
+def is_upper(bit):
+    return lax.rem(lax.div(lax.axis_index("seg"), bit), 2) == 1
+
+
+def joined_covariance(
+    bit, last, psi_ref, mine_ref, mate_ref, step_mine_ref, step_mate_ref, came_mine_ref, came_mate_ref, out_ref,
+    step_ref, first_mine_ref, first_mate_ref, added_ref, work_ref,
+):
+    @pl.when(jnp.logical_not(last) | jnp.logical_not(is_upper(2 * bit)))
+    def _():
+        upper = is_upper(bit)
+        step_ref[...] = jnp.where(upper, psi_ref[...], whole_matrix(step_mine_ref, step_mate_ref))
+        first_mine_ref[...] = jnp.where(upper, came_mine_ref[...], mine_ref[...])
+        first_mate_ref[...] = jnp.where(upper, came_mate_ref[...], mate_ref[...])
+        added_ref[...] = jnp.where(upper, mine_ref[...], came_mine_ref[...])
+        mean = unpacked(first_mine_ref, first_mate_ref, work_ref)
+        put_packed(step_ref, work_ref[...], mean, packed_blocks(added_ref, out_ref.shape[1]), out_ref)
+
+
+def joined_matrix(bit, psi_ref, step_mine_ref, step_mate_ref, out_ref):
+    came = whole_matrix(step_mine_ref, step_mate_ref)
+    upper = is_upper(bit)
+    out_ref[...] = dot_nn(jnp.where(upper, psi_ref[...], came), jnp.where(upper, came, psi_ref[...]))
+
+
+def entered(bit, psi_ref, covar_ref, mean_ref, step_mine_ref, step_mate_ref, mine_ref, mate_ref, *refs):
     psi_out_ref, covar_out_ref, mean_out_ref, work_ref = refs
+    steps, width, states = covar_ref.shape
     mine = pl.ds(pl.multiple_of(lax.axis_index("col") * width, 8), width)
-    before = whole_matrix(step_mine_ref, step_mate_ref)
-    mean = unpacked(mine_ref, mate_ref, work_ref)
-    covar = work_ref[...]
-    for k in range(steps):
-        psi_out_ref[k] = dot_nn(psi_ref[k], before)
-        half = dot_nn(psi_ref[k, mine, :], covar)
-        both = dot_nt(jnp.concatenate([half, mean], axis=0), psi_ref[k])
-        covar_out_ref[k] = both[:width] + covar_ref[k]
-        mean_out_ref[k] = both[width:] + mean_ref[k]
-
-
-def finished(steps, width, psi_ref, covar_ref, mean_ref, *refs):
-    shares, (covar_out_ref, mean_out_ref, mine_ref, mate_ref, work_ref) = refs[:-5], refs[-5:]
-    mine_ref[...] = sum(r[...] for r in shares[0::2])
-    mate_ref[...] = sum(r[...] for r in shares[1::2])
+
+    @pl.when(is_upper(bit))
+    def _():
+        before = whole_matrix(step_mine_ref, step_mate_ref)
+        mean = unpacked(mine_ref, mate_ref, work_ref)
+        covar = work_ref[...]
+        for k in range(steps):
+            psi_out_ref[k] = dot_nn(psi_ref[k], before)
+            half = dot_nn(psi_ref[k, mine, :], covar)
+            both = dot_nt(jnp.concatenate([half, mean], axis=0), psi_ref[k])
+            covar_out_ref[k] = both[:width] + covar_ref[k]
+            mean_out_ref[k] = both[width:] + mean_ref[k]
+
+    @pl.when(jnp.logical_not(is_upper(bit)))
+    def _():
+        psi_out_ref[...] = psi_ref[...]
+        covar_out_ref[...] = covar_ref[...]
+        mean_out_ref[...] = mean_ref[...]
+
+
+def finished(bit, psi_ref, covar_ref, mean_ref, mine_ref, mate_ref, covar_out_ref, mean_out_ref, work_ref):
+    steps, width, states = covar_ref.shape
     mine = pl.ds(pl.multiple_of(lax.axis_index("col") * width, 8), width)
-    mean = unpacked(mine_ref, mate_ref, work_ref)
-    rows = jnp.concatenate([psi_ref[k, mine, :] for k in range(steps)], axis=0)
-    half = dot_nn(rows, work_ref[...])
-    for k in range(steps):
-        part = half[k * width : (k + 1) * width]
-        both = dot_nt(jnp.concatenate([part, mean], axis=0), psi_ref[k])
-        covar_out_ref[k] = both[:width] + covar_ref[k]
-        mean_out_ref[k : k + 1, :] = both[width : width + 1] + mean_ref[k, :1, :]
+
+    @pl.when(is_upper(bit))
+    def _():
+        mean = unpacked(mine_ref, mate_ref, work_ref)
+        rows = jnp.concatenate([psi_ref[k, mine, :] for k in range(steps)], axis=0)
+        half = dot_nn(rows, work_ref[...])
+        for k in range(steps):
+            part = half[k * width : (k + 1) * width]
+            both = dot_nt(jnp.concatenate([part, mean], axis=0), psi_ref[k])
+            covar_out_ref[k] = both[:width] + covar_ref[k]
+            mean_out_ref[k : k + 1, :] = both[width : width + 1] + mean_ref[k, :1, :]
+
+    @pl.when(jnp.logical_not(is_upper(bit)))
+    def _():
+        covar_out_ref[...] = covar_ref[...]
+        for k in range(steps):
+            mean_out_ref[k : k + 1, :] = mean_ref[k, :1, :]
 
 
 def swapped(block, axis, bit):
     return lax.ppermute(block, axis, [(i, i ^ bit) for i in range(lax.axis_size(axis))])
-
-
-def shifted(block, distance, start=0, stop=None):
-    size = lax.axis_size("seg")
-    stop = size - distance if stop is None else stop
-    return lax.ppermute(block, "seg", [(i, i + distance) for i in range(start, stop)])
 
 
 def with_mate(share):
@@ -433,6 +466,7 @@
 ):
     steps, width, states = model_mixing.shape
     n_col, n_seg = lax.axis_size("col"), lax.axis_size("seg")
+    col = lax.axis_index("col")
     edge = states // 3
     square_shape, mean_shape = (states, states), (MEAN_ROWS, states)
     share_shape, half_shape = (3 * edge + 8, edge), (states // 2, states)
@@ -468,50 +502,52 @@
     fixed, prior = local_call(
         fixed_parts, [square_shape, square_shape], gain, obs_noise[None, :], prior_factor
     )
-    own, near, fixed = lax.optimization_barrier((own, near, fixed))
-    other_first = [near[:1]] + [swapped(b[:1], "seg", 1) for b in own[1:]]
-    other_rest = [near[1:]]
-    for bit in far_bits:
-        other_rest = other_rest + [swapped(b, "col", bit) for b in other_rest]
+    own, near, fixed, vectors_other = lax.optimization_barrier((own, near, fixed, vectors_other))
+    other = [near] + [swapped(b, "seg", 1) for b in own[1:]]
     corr, vectors_other, fixed = lax.optimization_barrier((corr, vectors_other, fixed))
     corr = corr + [swapped(b, "col", 1) for b in corr]
 
-    correction, noise, offset = local_call(
-        functools.partial(noises, offsets + [o ^ 1 for o in offsets]),
-        [square_shape, (2 * steps,) + square_shape, (2 * steps,) + mean_shape],
+    rows_shape = (steps,) + half_shape
+    correction, rows = local_call(
+        functools.partial(own_rows, offsets + [o ^ 1 for o in offsets]),
+        [square_shape, rows_shape],
+        *corr,
+        *own,
+        scratch=[square_shape],
+    )
+    noise, offset = local_call(
+        noises,
+        [(2 * steps,) + square_shape, (2 * steps,) + mean_shape],
         vectors,
         vectors_other,
         fixed,
-        *corr,
+        correction,
+    )
+    other, correction, noise = lax.optimization_barrier((other, correction, noise))
+    rows = with_mate(rows)
+    (rows_other,) = local_call(other_rows, [rows_shape], correction, *other, cost=1)
+    matrix, psi = local_call(
+        functools.partial(own_matrices, offsets),
+        [(steps,) + square_shape, (steps,) + square_shape],
+        vectors,
+        correction,
+        *rows,
         scratch=[square_shape],
-    )
-    rows_shape = (steps,) + half_shape
-    every = list(range(steps))
-    (rows,) = local_call(
-        functools.partial(mixed_rows, [every] * len(own)), [rows_shape], correction, *own
-    )
-    other_first, other_rest, correction, noise, rows = lax.optimization_barrier(
-        (other_first, other_rest, correction, noise, rows)
-    )
-    (rows_other,) = local_call(
-        functools.partial(mixed_rows, [every[:1]] * len(own) + [every[1:]] * len(own)),
-        [rows_shape],
-        correction,
-        *other_first,
-        *other_rest,
-    )
-    matrix, psi, matrix_other, psi_other, psi_half = local_call(
-        functools.partial(all_matrices, offsets),
-        [(steps,) + square_shape, (steps,) + square_shape, (steps,) + square_shape, square_shape, half_shape],
-        vectors,
+        cost=1,
+    )
+    matrix_other, psi_other, psi_half = local_call(
+        functools.partial(other_matrices, offsets),
+        [(steps,) + square_shape, square_shape, half_shape],
         vectors_other,
         correction,
-        *with_mate(rows),
         *with_mate(rows_other),
-        scratch=[square_shape, square_shape],
-    )
-    if n_seg > 4:
-        step = shifted(psi_half, 2, 2)
+        psi,
+        scratch=[square_shape],
+    )
+    bit = 2
+    more = 2 * bit < n_seg
+    if more:
+        step = swapped(psi_half, "seg", bit)
     covar, mean, covar_other, mean_other, total = local_call(
         functools.partial(pair_covariance, steps),
         [(steps,) + square_shape, (steps,) + mean_shape, square_shape, mean_shape, share_shape],
@@ -524,7 +560,7 @@
         matrix_other,
         scratch=[square_shape],
     )
-    entry = shifted(total, 2)
+    came = swapped(total, "seg", bit)
     psi, covar, mean, psi_all = local_call(
         functools.partial(pair_elements, steps, width),
         [(steps,) + square_shape, (steps, width, states), (steps,) + mean_shape, square_shape],
@@ -535,53 +571,47 @@
         covar_other,
         mean_other,
     )
-    if n_seg > 4:
-        entry, psi_all, step = lax.optimization_barrier((entry, psi_all, step))
-    entry = with_mate(entry)
-    entries = [entry]
-    distance = 4
-    while distance < n_seg:
-        more = 2 * distance < n_seg
-        (sent,) = local_call(
-            functools.partial(carried_on, distance), [share_shape], psi_all, total, *entry, scratch=[square_shape]
+    while more:
+        total = with_mate(total)
+        came, step, psi_all, psi = lax.optimization_barrier((came, step, psi_all, psi))
+        came, step = with_mate(came), with_mate(step)
+        last = 4 * bit >= n_seg
+        (total_next,) = local_call(
+            functools.partial(joined_covariance, bit, last),
+            [share_shape],
+            psi_all,
+            *total,
+            *step,
+            *came,
+            scratch=[square_shape, share_shape, share_shape, share_shape, square_shape],
         )
-        step, sent = lax.optimization_barrier((step, sent))
-        step = with_mate(step)
-        if more:
-            came = with_mate(shifted(sent, distance))
-            (sent,) = local_call(matrix_on, [half_shape], psi_half, *step)
-            came_step = with_mate(shifted(sent, distance))
-            (whole,) = local_call(joined, [square_shape], *step)
-            (entry,) = local_call(
-                functools.partial(carried_on, 0), [share_shape], whole, entry[0], *came, scratch=[square_shape]
-            )
-            entry = with_mate(entry)
-            (step,) = local_call(matrix_on, [half_shape], step[0], *came_step)
-        else:
-            early = shifted(total, distance, 0, 2)
-            came = shifted(sent, distance, 2)
-            psi, covar, mean = local_call(
-                functools.partial(entered, steps, width),
-                [(steps,) + square_shape, (steps, width, states), (steps,) + mean_shape],
-                psi,
-                covar,
-                mean,
-                *entry,
-                *step,
-                scratch=[square_shape],
-            )
-            came, psi = lax.optimization_barrier((came, psi))
-            entries = [with_mate(early), with_mate(came)]
-        distance *= 2
-
+        came_next = swapped(total_next, "seg", 2 * bit)
+        psi, covar, mean = local_call(
+            functools.partial(entered, bit),
+            [(steps,) + square_shape, (steps, width, states), (steps,) + mean_shape],
+            psi,
+            covar,
+            mean,
+            *step,
+            *came,
+            scratch=[square_shape],
+        )
+        if not last:
+            (psi_all,) = local_call(functools.partial(joined_matrix, bit), [square_shape], psi_all, *step)
+            psi_half = lax.dynamic_slice_in_dim(psi_all, col % 2 * (states // 2), states // 2, 0)
+            step = swapped(psi_half, "seg", 2 * bit)
+        total, came = total_next, came_next
+        bit *= 2
+        more = not last
+    came, psi = lax.optimization_barrier((came, psi))
     covars, means = local_call(
-        functools.partial(finished, steps, width),
+        functools.partial(finished, bit),
         [(steps, width, states), (steps, states)],
         psi,
         covar,
         mean,
-        *[share for pair in entries for share in pair],
-        scratch=[share_shape, share_shape, square_shape],
+        *with_mate(came),
+        scratch=[square_shape],
     )
     return means, covars
 

time: 61.5 us -> 55.5 us (0.902)
  the two profiles are of different devices: /device:TPU:29 before, /device:TPU:0 now
where the time goes in v4:
time: 55.5 us; the launch traced here: 55.4 us
  waiting for transfers between devices  24.4 us (44%)
  Pallas kernels  17.8 us (32%)
  starting transfers between devices  12.3 us (22%)
  between operations  0.8 us (1%)
    ppermute x16, waiting for transfers between devices, swapped(): lax.ppermute(block, axis, [(i, i ^ bit) for i in range(lax.axis_size(axis...  24.4 us
    pallas_call x12, Pallas kernels, local_call(): pl.pallas_call(body, out_shape=shapes, name=getattr(body, 'func', body)._...  17.8 us
    ppermute x16, starting transfers between devices, swapped(): lax.ppermute(block, axis, [(i, i ^ bit) for i in range(lax.axis_size(axis...  12.3 us
  transfers between devices with their start and end apart: 16, of which 10 were waited for; matrix products, arithmetic and copies ran while one was open for 0% of the time, Pallas kernels for 28%

profile of v4, /device:TPU:0, one launch (start us, length us, event | category | flops | bytes accessed | tf_op | source)
XLA Modules:
  0.0 55.4 jit_solution(4340605518216219073)
XLA Ops:
  0.7 3.0 %collective-permute-start = (f32[2,96,384]{2,1,0:T(8,128)}, f32[2,96,384]{2,1,0:T(8,128)S(1)}, u32[]{:S(2)}, u32[]{:S(2)}) collective-permute-start(f32[2,96,384]{2,1,0:T(8,128)} %refs_4_), channel_id=1, source_target_pairs={{0,2},{1,3},{2,0},{3,1},{4,6},{5,7},{6,4},{7,5},{8,10},{9,11},{10,... | collective-permute-start | bytes 884744 | tf_op jit(solution)/shard_map/ppermute | solution.py:448
  3.7 1.5 %collective-permute-start.1 = (f32[2,96,384]{2,1,0:T(8,128)}, f32[2,96,384]{2,1,0:T(8,128)S(1)}, u32[]{:S(2)}, u32[]{:S(2)}) collective-permute-start(f32[2,96,384]{2,1,0:T(8,128)} %refs_4_), channel_id=1, source_target_pairs={{0,4},{4,0},{8,12},{12,8},{16,20},{20,16},{24,28},{28,24},{1,5},{5... | collective-permute-start | bytes 884744 | tf_op jit(solution)/shard_map/ppermute | solution.py:448
  5.2 3.0 %correction_rows.1 = (f32[96,384]{1,0:T(8,128)}, f32[2,4,384]{2,1,0:T(4,128)}) custom-call(f32[384,1024]{1,0:T(8,128)} %gain_hbm.1, f32[96,1024]{1,0:T(8,128)} %oper_hbm.1, f32[2,1024]{1,0:T(2,128)} %seen_hbm.1, f32[2,384]{1,0:T(2,128)} %keep_hbm.1, f32[2,384]{1,0:T(2,128)} %push_hbm.1, f32[2,384]{1,0:T(2,128)} %var_hbm.1), custom_call_target="tpu_custom_call" | custom-call | flops 2100000000 | bytes 4096 | tf_op jit(solution)/shard_map/correction_rows/pallas_call | solution.py:52
  8.2 0.6 %collective-permute-start.2 = (f32[2,4,384]{2,1,0:T(4,128)}, f32[2,4,384]{2,1,0:T(4,128)S(1)}, u32[]{:S(2)}, u32[]{:S(2)}) collective-permute-start(f32[2,4,384]{2,1,0:T(4,128)} %get-tuple-element.49.vec_ref), channel_id=1, source_target_pairs={{0,4},{4,0},{8,12},{12,8},{16,20},{20,16},{24,28},{28,24},{1,5},{5... | collective-permute-start | bytes 36872 | tf_op jit(solution)/shard_map/ppermute | solution.py:448
  8.8 0.1 collective-permute-start.4
  8.9 2.1 %fixed_parts.1 = (f32[384,384]{1,0:T(8,128)S(1)}, f32[384,384]{1,0:T(8,128)S(1)}) custom-call(f32[384,1024]{1,0:T(8,128)S(1)} %copy-done, f32[1,1024]{1,0:T(1,128)S(1)} %bitcast.1, f32[384,384]{1,0:T(8,128)S(1)} %copy-done.1), custom_call_target="tpu_custom_call" | custom-call | bytes 4096 | tf_op jit(solution)/shard_map/fixed_parts/pallas_call | solution.py:52
  11.0 1.6 %collective-permute-done.2.vec_other_ref.vec_ref = f32[2,4,384]{2,1,0:T(4,128)S(1)} collective-permute-done((f32[2,4,384]{2,1,0:T(4,128)}, f32[2,4,384]{2,1,0:T(4,128)S(1)}, u32[]{:S(2)}, u32[]{:S(2)}) %collective-permute-start.2) | collective-permute-done | bytes 12320 | tf_op jit(solution)/shard_map/ppermute | solution.py:448
  12.6 1.5 %collective-permute-start.3 = (f32[2,96,384]{2,1,0:T(8,128)S(1)}, f32[2,96,384]{2,1,0:T(8,128)S(1)}, u32[]{:S(2)}, u32[]{:S(2)}) collective-permute-start(f32[2,96,384]{2,1,0:T(8,128)S(1)} %collective-permute-done.refs_5_), channel_id=1, source_target_pairs={{0,4},{4,0},{8,12},{12,8},{16,20},{20,16},{24,28},{28,24},{1,5},{5... | collective-permute-start | bytes 884744 | tf_op jit(solution)/shard_map/ppermute | solution.py:448
  14.2 0.5 collective-permute-start.6
  14.7 0.9 %collective-permute-done.5.refs_2_ = f32[96,384]{1,0:T(8,128)S(1)} collective-permute-done((f32[96,384]{1,0:T(8,128)S(1)}, f32[96,384]{1,0:T(8,128)S(1)}, u32[]{:S(2)}, u32[]{:S(2)}) %collective-permute-start.5) | collective-permute-done | bytes 147488 | tf_op jit(solution)/shard_map/ppermute | solution.py:448
  15.5 0.2 collective-permute-done.6.refs_3_
  15.8 0.8 %own_rows.1 = (f32[384,384]{1,0:T(8,128)S(1)}, f32[2,192,384]{2,1,0:T(8,128)S(1)}) custom-call(f32[96,384]{1,0:T(8,128)S(1)} %copy-done.3, f32[96,384]{1,0:T(8,128)S(1)} %collective-permute-done.4.refs_1_, f32[96,384]{1,0:T(8,128)S(1)} %collective-permute-done.5.refs_2_, f32[96,384]{1,0:T(8,128)S(1)} %collective-permute-done.6.refs_3_, ...), custom_call_target="tpu_custom_call" | custom-call | bytes 4096 | tf_op jit(solution)/shard_map/own_rows/pallas_call | solution.py:52
  16.6 0.4 collective-permute-start.7
  17.0 2.3 %noises.1 = (f32[4,384,384]{2,1,0:T(8,128)S(1)}, f32[4,16,384]{2,1,0:T(8,128)S(1)}) custom-call(f32[2,4,384]{2,1,0:T(4,128)S(1)} %copy-done.4, f32[2,4,384]{2,1,0:T(4,128)S(1)} %collective-permute-done.2.vec_other_ref.vec_ref, f32[384,384]{1,0:T(8,128)S(1)} %get-tuple-element.60.fixed_ref, f32[384,384]{1,0:T(8,128)S(1)} %get-tuple-element.65.corr_ref), custom_call_target="tpu_custom_call" | custom-call | bytes 4096 | tf_op jit(solution)/shard_map/noises/pallas_call | solution.py:52
  19.3 0.9 %collective-permute-done.3.refs_1_ = f32[2,96,384]{2,1,0:T(8,128)S(1)} collective-permute-done((f32[2,96,384]{2,1,0:T(8,128)S(1)}, f32[2,96,384]{2,1,0:T(8,128)S(1)}, u32[]{:S(2)}, u32[]{:S(2)}) %collective-permute-start.3) | collective-permute-done | bytes 294944 | tf_op jit(solution)/shard_map/ppermute | solution.py:448
  20.2 0.7 %other_rows.1.mine_ref = f32[2,192,384]{2,1,0:T(8,128)S(1)} custom-call(f32[384,384]{1,0:T(8,128)S(1)} %get-tuple-element.65.corr_ref, f32[2,96,384]{2,1,0:T(8,128)S(1)} %collective-permute-done.1.refs_0_, f32[2,96,384]{2,1,0:T(8,128)S(1)} %collective-permute-done.3.refs_1_), custom_call_target="tpu_custom_call" | custom-call | flops 700000000 | bytes 4096 | tf_op jit(solution)/shard_map/other_rows/pallas_call | solution.py:52
  20.9 1.0 %own_matrices.1 = (f32[2,384,384]{2,1,0:T(8,128)S(1)}, f32[2,384,384]{2,1,0:T(8,128)S(1)}) custom-call(f32[2,4,384]{2,1,0:T(4,128)S(1)} %copy-done.4, f32[384,384]{1,0:T(8,128)S(1)} %get-tuple-element.65.corr_ref, f32[2,192,384]{2,1,0:T(8,128)S(1)} %get-tuple-element.66.mine_ref, f32[2,192,384]{2,1,0:T(8,128)S(1)} %collective-permute-done.7.mate_ref), custom_call_target="tpu_custom_call" | custom-call | flops 700000000 | bytes 4096 | tf_op jit(solution)/shard_map/own_matrices/pallas_call | solution.py:52
  21.9 1.0 %collective-permute-done.8.mate_ref = f32[2,192,384]{2,1,0:T(8,128)S(1)} collective-permute-done((f32[2,192,384]{2,1,0:T(8,128)S(1)}, f32[2,192,384]{2,1,0:T(8,128)S(1)}, u32[]{:S(2)}, u32[]{:S(2)}) %collective-permute-start.8) | collective-permute-done | bytes 589856 | tf_op jit(solution)/shard_map/ppermute | solution.py:448
  22.9 0.5 other_matrices.1
  23.4 2.7 %collective-permute-start.10 = (f32[192,384]{1,0:T(8,128)S(1)}, f32[192,384]{1,0:T(8,128)S(1)}, u32[]{:S(2)}, u32[]{:S(2)}) collective-permute-start(f32[192,384]{1,0:T(8,128)S(1)} %get-tuple-element.73), channel_id=1, source_target_pairs={{0,8},{4,12},{8,0},{12,4},{16,24},{20,28},{24,16},{28,20},{1,9},{5... | collective-permute-start | bytes 884744 | tf_op jit(solution)/shard_map/ppermute | solution.py:448
  26.1 5.2 %pair_covariance.1 = (f32[2,384,384]{2,1,0:T(8,128)S(1)}, f32[2,16,384]{2,1,0:T(8,128)S(1)}, f32[384,384]{1,0:T(8,128)S(1)}, f32[16,384]{1,0:T(8,128)S(1)}, f32[392,128]{1,0:T(8,128)S(1)}) custom-call(f32[4,384,384]{2,1,0:T(8,128)S(1)} %get-tuple-element.62.noise_ref, f32[4,16,384]{2,1,0:T(8,128)S(1)} %get-tuple-element.63.offset_ref, ...), custom_call_target="tpu_custom_call" | custom-call | bytes 4096 | tf_op jit(solution)/shard_map/pair_covariance/pallas_call | solution.py:52
  31.4 0.2 pair_elements.1
  31.6 6.2 %collective-permute-done.9.came_mine_ref.mine_ref = f32[392,128]{1,0:T(8,128)S(1)} collective-permute-done((f32[392,128]{1,0:T(8,128)S(1)}, f32[392,128]{1,0:T(8,128)S(1)}, u32[]{:S(2)}, u32[]{:S(2)}) %collective-permute-start.9) | collective-permute-done | bytes 200736 | tf_op jit(solution)/shard_map/ppermute | solution.py:448
  37.8 0.5 collective-permute-start.11
  38.3 1.4 %collective-permute-done.11.mate_ref = f32[392,128]{1,0:T(8,128)S(1)} collective-permute-done((f32[392,128]{1,0:T(8,128)S(1)}, f32[392,128]{1,0:T(8,128)S(1)}, u32[]{:S(2)}, u32[]{:S(2)}) %collective-permute-start.11) | collective-permute-done | bytes 200736 | tf_op jit(solution)/shard_map/ppermute | solution.py:448
  39.6 0.3 collective-permute-done.13.came_mate_ref.mate_ref
  39.9 1.3 %joined_covariance.1 = f32[392,128]{1,0:T(8,128)S(1)} custom-call(f32[384,384]{1,0:T(8,128)S(1)} %get-tuple-element.81.psi_ref, f32[392,128]{1,0:T(8,128)S(1)} %get-tuple-element.72.mine_ref, f32[392,128]{1,0:T(8,128)S(1)} %collective-permute-done.11.mate_ref, f32[192,384]{1,0:T(8,128)S(1)} %collective-permute-done.10.step_mine_ref, ...), custom_call_target="tpu_custom_call" | custom-call | bytes 4096 | tf_op jit(solution)/shard_map/joined_covariance/pallas_call | solution.py:52
  41.2 1.4 %collective-permute-start.14 = (f32[392,128]{1,0:T(8,128)S(1)}, f32[392,128]{1,0:T(8,128)S(1)}, u32[]{:S(2)}, u32[]{:S(2)}) collective-permute-start(f32[392,128]{1,0:T(8,128)S(1)} %joined_covariance.1), channel_id=1, source_target_pairs={{0,16},{4,20},{8,24},{12,28},{16,0},{20,4},{24,8},{28,12},{1,17},{... | collective-permute-start | bytes 602120 | tf_op jit(solution)/shard_map/ppermute | solution.py:448
  42.6 0.1 entered.1
  42.7 10.5 %collective-permute-done.14.mine_ref = f32[392,128]{1,0:T(8,128)S(1)} collective-permute-done((f32[392,128]{1,0:T(8,128)S(1)}, f32[392,128]{1,0:T(8,128)S(1)}, u32[]{:S(2)}, u32[]{:S(2)}) %collective-permute-start.14) | collective-permute-done | bytes 200736 | tf_op jit(solution)/shard_map/ppermute | solution.py:448
  53.2 1.4 %collective-permute-done.15.mate_ref = f32[392,128]{1,0:T(8,128)S(1)} collective-permute-done((f32[392,128]{1,0:T(8,128)S(1)}, f32[392,128]{1,0:T(8,128)S(1)}, u32[]{:S(2)}, u32[]{:S(2)}) %collective-permute-start.15) | collective-permute-done | bytes 200736 | tf_op jit(solution)/shard_map/ppermute | solution.py:448
  54.6 0.7 %finished.1 = (f32[2,96,384]{2,1,0:T(8,128)}, f32[2,384]{1,0:T(2,128)}) custom-call(f32[2,384,384]{2,1,0:T(8,128)S(1)} %get-tuple-element.88.psi_ref, f32[2,96,384]{2,1,0:T(8,128)S(1)} %get-tuple-element.89.covar_ref, f32[2,16,384]{2,1,0:T(8,128)S(1)} %get-tuple-element.90.mean_ref, f32[392,128]{1,0:T(8,128)S(1)} %collective-permute-done.14.mine_ref, ...), custom_call_target="tpu_custom_call" | custom-call | bytes 4096 | tf_op jit(solution)/shard_map/finished/pallas_call | solution.py:52
  (27 shorter events, 0.2 us)
Async XLA Ops:
  0.6 8.3 %copy-start = (f32[384,1024]{1,0:T(8,128)S(1)}, f32[384,1024]{1,0:T(8,128)}, u32[]{:S(2)}) copy-start(f32[384,1024]{1,0:T(8,128)} %gain_hbm.1) | copy-start | bytes 4718596
  0.6 8.3 %copy-start.1 = (f32[384,384]{1,0:T(8,128)S(1)}, f32[384,384]{1,0:T(8,128)}, u32[]{:S(2)}) copy-start(f32[384,384]{1,0:T(8,128)} %factor_ref.1) | copy-start | bytes 1769476
  0.7 8.3 %copy-start.5 = (f32[1024]{0:T(1024)S(1)}, f32[1024]{0:T(1024)}, u32[]{:S(2)}) copy-start(f32[1024]{0:T(1024)} %param.15) | copy-start | bytes 12292
  0.7 11.9 %collective-permute-start = (f32[2,96,384]{2,1,0:T(8,128)}, f32[2,96,384]{2,1,0:T(8,128)S(1)}, u32[]{:S(2)}, u32[]{:S(2)}) collective-permute-start(f32[2,96,384]{2,1,0:T(8,128)} %refs_4_), channel_id=1, source_target_pairs={{0,2},{1,3},{2,0},{3,1},{4,6},{5,7},{6,4},{7,5},{8,10},{9,11},{10,... | collective-permute-start | bytes 884744 | tf_op jit(solution)/shard_map/ppermute | solution.py:448
  3.7 8.9 %collective-permute-start.1 = (f32[2,96,384]{2,1,0:T(8,128)}, f32[2,96,384]{2,1,0:T(8,128)S(1)}, u32[]{:S(2)}, u32[]{:S(2)}) collective-permute-start(f32[2,96,384]{2,1,0:T(8,128)} %refs_4_), channel_id=1, source_target_pairs={{0,4},{4,0},{8,12},{12,8},{16,20},{20,16},{24,28},{28,24},{1,5},{5... | collective-permute-start | bytes 884744 | tf_op jit(solution)/shard_map/ppermute | solution.py:448
  8.2 6.0 %copy-start.3 = (f32[96,384]{1,0:T(8,128)S(1)}, f32[96,384]{1,0:T(8,128)}, u32[]{:S(2)}) copy-start(f32[96,384]{1,0:T(8,128)} %get-tuple-element.55.refs_0_) | copy-start | bytes 442372
  8.2 7.5 %copy-start.2 = (f32[2,96,384]{2,1,0:T(8,128)S(1)}, f32[2,96,384]{2,1,0:T(8,128)}, u32[]{:S(2)}) copy-start(f32[2,96,384]{2,1,0:T(8,128)} %refs_4_) | copy-start | bytes 884740
  8.2 4.4 %collective-permute-start.2 = (f32[2,4,384]{2,1,0:T(4,128)}, f32[2,4,384]{2,1,0:T(4,128)S(1)}, u32[]{:S(2)}, u32[]{:S(2)}) collective-permute-start(f32[2,4,384]{2,1,0:T(4,128)} %get-tuple-element.49.vec_ref), channel_id=1, source_target_pairs={{0,4},{4,0},{8,12},{12,8},{16,20},{20,16},{24,28},{28,24},{1,5},{5... | collective-permute-start | bytes 36872 | tf_op jit(solution)/shard_map/ppermute | solution.py:448
  8.8 5.4 %collective-permute-start.4 = (f32[96,384]{1,0:T(8,128)}, f32[96,384]{1,0:T(8,128)S(1)}, u32[]{:S(2)}, u32[]{:S(2)}) collective-permute-start(f32[96,384]{1,0:T(8,128)} %get-tuple-element.55.refs_0_), channel_id=1, source_target_pairs={{0,2},{1,3},{2,0},{3,1},{4,6},{5,7},{6,4},{7,5},{8,10},{9,11},{10,... | collective-permute-start | bytes 442376 | tf_op jit(solution)/shard_map/ppermute | solution.py:448
  8.9 8.0 %copy-start.4 = (f32[2,4,384]{2,1,0:T(4,128)S(1)}, f32[2,4,384]{2,1,0:T(4,128)}, u32[]{:S(2)}) copy-start(f32[2,4,384]{2,1,0:T(4,128)} %get-tuple-element.49.vec_ref) | copy-start | bytes 36868
  12.6 7.6 %collective-permute-start.3 = (f32[2,96,384]{2,1,0:T(8,128)S(1)}, f32[2,96,384]{2,1,0:T(8,128)S(1)}, u32[]{:S(2)}, u32[]{:S(2)}) collective-permute-start(f32[2,96,384]{2,1,0:T(8,128)S(1)} %collective-permute-done.refs_5_), channel_id=1, source_target_pairs={{0,4},{4,0},{8,12},{12,8},{16,20},{20,16},{24,28},{28,24},{1,5},{5... | collective-permute-start | bytes 884744 | tf_op jit(solution)/shard_map/ppermute | solution.py:448
  14.2 1.4 %collective-permute-start.5 = (f32[96,384]{1,0:T(8,128)S(1)}, f32[96,384]{1,0:T(8,128)S(1)}, u32[]{:S(2)}, u32[]{:S(2)}) collective-permute-start(f32[96,384]{1,0:T(8,128)S(1)} %copy-done.3), channel_id=1, source_target_pairs={{0,1},{1,0},{2,3},{3,2},{4,5},{5,4},{6,7},{7,6},{8,9},{9,8},{10,11... | collective-permute-start | bytes 442376 | tf_op jit(solution)/shard_map/ppermute | solution.py:448
  14.2 1.6 %collective-permute-start.6 = (f32[96,384]{1,0:T(8,128)S(1)}, f32[96,384]{1,0:T(8,128)S(1)}, u32[]{:S(2)}, u32[]{:S(2)}) collective-permute-start(f32[96,384]{1,0:T(8,128)S(1)} %collective-permute-done.4.refs_1_), channel_id=1, source_target_pairs={{0,1},{1,0},{2,3},{3,2},{4,5},{5,4},{6,7},{7,6},{8,9},{9,8},{10,11... | collective-permute-start | bytes 442376 | tf_op jit(solution)/shard_map/ppermute | solution.py:448
  16.6 4.3 %collective-permute-start.7 = (f32[2,192,384]{2,1,0:T(8,128)S(1)}, f32[2,192,384]{2,1,0:T(8,128)S(1)}, u32[]{:S(2)}, u32[]{:S(2)}) collective-permute-start(f32[2,192,384]{2,1,0:T(8,128)S(1)} %get-tuple-element.66.mine_ref), channel_id=1, source_target_pairs={{0,1},{1,0},{2,3},{3,2},{4,5},{5,4},{6,7},{7,6},{8,9},{9,8},{10,11... | collective-permute-start | bytes 1769480 | tf_op jit(solution)/shard_map/ppermute | solution.py:448
  20.9 2.1 %collective-permute-start.8 = (f32[2,192,384]{2,1,0:T(8,128)S(1)}, f32[2,192,384]{2,1,0:T(8,128)S(1)}, u32[]{:S(2)}, u32[]{:S(2)}) collective-permute-start(f32[2,192,384]{2,1,0:T(8,128)S(1)} %other_rows.1.mine_ref), channel_id=1, source_target_pairs={{0,1},{1,0},{2,3},{3,2},{4,5},{5,4},{6,7},{7,6},{8,9},{9,8},{10,11... | collective-permute-start | bytes 1769480 | tf_op jit(solution)/shard_map/ppermute | solution.py:448
  22.9 3.2 %copy-start.6 = (f32[384]{0:T(512)S(1)}, f32[384]{0:T(512)}, u32[]{:S(2)}) copy-start(f32[384]{0:T(512)} %param.18) | copy-start | bytes 4612
  23.4 14.4 %collective-permute-start.10 = (f32[192,384]{1,0:T(8,128)S(1)}, f32[192,384]{1,0:T(8,128)S(1)}, u32[]{:S(2)}, u32[]{:S(2)}) collective-permute-start(f32[192,384]{1,0:T(8,128)S(1)} %get-tuple-element.73), channel_id=1, source_target_pairs={{0,8},{4,12},{8,0},{12,4},{16,24},{20,28},{24,16},{28,20},{1,9},{5... | collective-permute-start | bytes 884744 | tf_op jit(solution)/shard_map/ppermute | solution.py:448
  31.3 6.5 %collective-permute-start.9 = (f32[392,128]{1,0:T(8,128)S(1)}, f32[392,128]{1,0:T(8,128)S(1)}, u32[]{:S(2)}, u32[]{:S(2)}) collective-permute-start(f32[392,128]{1,0:T(8,128)S(1)} %get-tuple-element.72.mine_ref), channel_id=1, source_target_pairs={{0,8},{4,12},{8,0},{12,4},{16,24},{20,28},{24,16},{28,20},{1,9},{5... | collective-permute-start | bytes 602120 | tf_op jit(solution)/shard_map/ppermute | solution.py:448
  37.8 2.2 %collective-permute-start.12 = (f32[192,384]{1,0:T(8,128)S(1)}, f32[192,384]{1,0:T(8,128)S(1)}, u32[]{:S(2)}, u32[]{:S(2)}) collective-permute-start(f32[192,384]{1,0:T(8,128)S(1)} %collective-permute-done.10.step_mine_ref), channel_id=1, source_target_pairs={{0,1},{1,0},{2,3},{3,2},{4,5},{5,4},{6,7},{7,6},{8,9},{9,8},{10,11... | collective-permute-start | bytes 884744 | tf_op jit(solution)/shard_map/ppermute | solution.py:448
  37.8 1.9 %collective-permute-start.11 = (f32[392,128]{1,0:T(8,128)S(1)}, f32[392,128]{1,0:T(8,128)S(1)}, u32[]{:S(2)}, u32[]{:S(2)}) collective-permute-start(f32[392,128]{1,0:T(8,128)S(1)} %get-tuple-element.72.mine_ref), channel_id=1, source_target_pairs={{0,1},{1,0},{2,3},{3,2},{4,5},{5,4},{6,7},{7,6},{8,9},{9,8},{10,11... | collective-permute-start | bytes 602120 | tf_op jit(solution)/shard_map/ppermute | solution.py:448
  38.3 1.6 %collective-permute-start.13 = (f32[392,128]{1,0:T(8,128)S(1)}, f32[392,128]{1,0:T(8,128)S(1)}, u32[]{:S(2)}, u32[]{:S(2)}) collective-permute-start(f32[392,128]{1,0:T(8,128)S(1)} %collective-permute-done.9.came_mine_ref.mine_ref), channel_id=1, source_target_pairs={{0,1},{1,0},{2,3},{3,2},{4,5},{5,4},{6,7},{7,6},{8,9},{9,8},{10,11... | collective-permute-start | bytes 602120 | tf_op jit(solution)/shard_map/ppermute | solution.py:448
  41.2 11.9 %collective-permute-start.14 = (f32[392,128]{1,0:T(8,128)S(1)}, f32[392,128]{1,0:T(8,128)S(1)}, u32[]{:S(2)}, u32[]{:S(2)}) collective-permute-start(f32[392,128]{1,0:T(8,128)S(1)} %joined_covariance.1), channel_id=1, source_target_pairs={{0,16},{4,20},{8,24},{12,28},{16,0},{20,4},{24,8},{28,12},{1,17},{... | collective-permute-start | bytes 602120 | tf_op jit(solution)/shard_map/ppermute | solution.py:448
  53.2 1.4 %collective-permute-start.15 = (f32[392,128]{1,0:T(8,128)S(1)}, f32[392,128]{1,0:T(8,128)S(1)}, u32[]{:S(2)}, u32[]{:S(2)}) collective-permute-start(f32[392,128]{1,0:T(8,128)S(1)} %collective-permute-done.14.mine_ref), channel_id=1, source_target_pairs={{0,1},{1,0},{2,3},{3,2},{4,5},{5,4},{6,7},{7,6},{8,9},{9,8},{10,11... | collective-permute-start | bytes 602120 | tf_op jit(solution)/shard_map/ppermute | solution.py:448

commit v5 on v4

--- a/solution.py
+++ b/solution.py
@@ -11,6 +11,7 @@
 NN = (((1,), (0,)), ((), ()))
 NT = (((1,), (1,)), ((), ()))
 MEAN_ROWS = 16
+CHUNKS = 4
 COST = 7 * 10**8
 
 
@@ -55,7 +56,7 @@
         name=getattr(body, "func", body).__name__,
         in_specs=[pl.BlockSpec(memory_space=pltpu.HBM if copied else pltpu.VMEM)] * len(operands),
         scratch_shapes=[pltpu.VMEM(o.shape, F32) for o in operands if copied]
-        + [pltpu.SemaphoreType.DMA((len(operands),))] * copied
+        + [pltpu.SemaphoreType.DMA((len(operands) + CHUNKS,))] * copied
         + [pltpu.VMEM(shape, F32) for shape in scratch],
         compiler_params=pltpu.CompilerParams(vmem_limit_bytes=(58 if copied else 36) * 2**20),
         cost_estimate=pl.CostEstimate(
@@ -72,31 +73,39 @@
     gain_hbm, oper_hbm, seen_hbm, keep_hbm, push_hbm, var_hbm, corr_ref, vec_ref,
     gain_ref, oper_ref, seen_ref, keep_ref, push_ref, var_ref, sems,
 ):
-    moves = [
-        pltpu.make_async_copy(source, target, sems.at[i])
-        for i, (source, target) in enumerate(
-            [
-                (gain_hbm, gain_ref),
-                (oper_hbm, oper_ref),
-                (seen_hbm, seen_ref),
-                (keep_hbm, keep_ref),
-                (push_hbm, push_ref),
-                (var_hbm, var_ref),
-            ]
-        )
-    ]
-    for move in moves:
-        move.start()
     width, states = corr_ref.shape
     steps = keep_ref.shape[0]
+    observed = gain_hbm.shape[1]
+    chunk = observed // CHUNKS
+    pairs = [
+        (oper_hbm, oper_ref),
+        (seen_hbm, seen_ref),
+        (keep_hbm, keep_ref),
+        (push_hbm, push_ref),
+        (var_hbm, var_ref),
+    ]
+    small = [pltpu.make_async_copy(a, b, sems.at[i]) for i, (a, b) in enumerate(pairs)]
+    large = []
+    for i in range(CHUNKS):
+        at = pl.ds(i * chunk, chunk)
+        large.append(pltpu.make_async_copy(gain_hbm.at[:, at], gain_ref.at[:, at], sems.at[len(pairs) + i]))
+    for move in small[:2] + large + small[2:]:
+        move.start()
     rows = lax.broadcasted_iota(jnp.int32, (width, states), 0) + lax.axis_index("col") * width
     cols = lax.broadcasted_iota(jnp.int32, (width, states), 1)
-    for move in moves:
+    small[0].wait()
+    small[1].wait()
+    blank = jnp.zeros((MEAN_ROWS - steps, observed), F32)
+    left = jnp.concatenate([oper_ref[...], seen_ref[...], blank], axis=0)
+    both = None
+    for i in range(CHUNKS):
+        at = slice(i * chunk, (i + 1) * chunk)
+        large[i].wait()
+        part = dot_nt(left[:, at], gain_ref[:, at])
+        both = part if both is None else both + part
+    corr_ref[...] = (rows == cols).astype(F32) - both[:width]
+    for move in small[2:]:
         move.wait()
-    blank = jnp.zeros((MEAN_ROWS - steps, gain_ref.shape[1]), F32)
-    left = jnp.concatenate([oper_ref[...], seen_ref[...], blank], axis=0)
-    both = by_gain(left, as_right(gain_ref[...], 1))
-    corr_ref[...] = (rows == cols).astype(F32) - both[:width]
     for k in range(steps):
         here = slice(k, k + 1)
         vec_ref[k, 0:1, :] = keep_ref[here, :]
@@ -122,16 +131,15 @@
         out_ref[pl.ds(at, width), :] = piece
 
 
-def noises(vec_ref, vec_other_ref, fixed_ref, corr_ref, noise_ref, offset_ref):
-    states = corr_ref.shape[0]
-    steps = vec_ref.shape[0]
+def noises(vec_ref, fixed_ref, corr_ref, noise_ref, offset_ref):
+    steps, states = vec_ref.shape[0], corr_ref.shape[0]
     corr = corr_ref[...]
-    vectors = [vec_ref[k] for k in range(steps)] + [vec_other_ref[k] for k in range(steps)]
-    push = [v[2:3] for v in vectors] + [jnp.zeros((MEAN_ROWS - 2 * steps, states), F32)]
+    vectors = [vec_ref[k] for k in range(steps)]
+    push = [v[2:3] for v in vectors] + [jnp.zeros((MEAN_ROWS - steps, states), F32)]
     left = jnp.concatenate([corr * v[1:2] for v in vectors] + push, axis=0)
     both = dot_nt(left, corr)
-    base = 2 * steps * states
-    for k in range(2 * steps):
+    base = steps * states
+    for k in range(steps):
         noise_ref[k] = both[k * states : (k + 1) * states] + fixed_ref[...]
         offset_ref[k] = mean_block(both[base + k : base + k + 1] + vectors[k][3:4], states)
 
@@ -167,21 +175,48 @@
         out_ref[k] = work_ref[...].T + corr * vec_ref[k, 0:1, :]
 
 
-def own_matrices(offsets, vec_ref, corr_ref, mine_ref, mate_ref, matrix_ref, psi_ref, work_ref):
+def add_prior(step_ref, prior_ref, start_ref, covar_ref, mean_ref):
+    covar, mean = square(step_ref[0], prior_ref[...], mean_block(start_ref[...], prior_ref.shape[0]))
+    covar_ref[...] += covar
+    mean_ref[...] += mean
+
+
+def own_segment(
+    offsets, vec_ref, corr_ref, mine_ref, mate_ref, noise_ref, offset_ref, prior_ref, start_ref,
+    matrix_ref, psi_ref, covar_ref, mean_ref, work_ref,
+):
+    steps = matrix_ref.shape[0]
     matrices_of(offsets, vec_ref, corr_ref[...], mine_ref, mate_ref, work_ref, matrix_ref)
+    covar_ref[0] = noise_ref[0]
+    mean_ref[0] = offset_ref[0]
+
+    @pl.when(lax.axis_index("seg") == 0)
+    def _():
+        add_prior(matrix_ref, prior_ref, start_ref, covar_ref.at[0], mean_ref.at[0])
+
     psi_ref[0] = matrix_ref[0]
-    for k in range(1, matrix_ref.shape[0]):
+    for k in range(1, steps):
         psi_ref[k] = dot_nn(matrix_ref[k], psi_ref[k - 1])
+        covar, mean = square(matrix_ref[k], covar_ref[k - 1], mean_ref[k - 1])
+        covar_ref[k] = covar + noise_ref[k]
+        mean_ref[k] = mean + offset_ref[k]
 
 
 def other_matrices(
-    offsets, vec_ref, corr_ref, mine_ref, mate_ref, psi_ref, matrix_ref, psi_other_ref, psi_half_ref, work_ref
+    offsets, vec_ref, corr_ref, mine_ref, mate_ref, psi_ref, prior_ref, start_ref,
+    matrix_ref, psi_other_ref, psi_half_ref, covar_ref, mean_ref, work_ref,
 ):
     steps, half, states = mine_ref.shape
     seg = lax.axis_index("seg")
     is_second = lax.rem(seg, 2) == 1
     matrices_of(offsets, vec_ref, corr_ref[...], mine_ref, mate_ref, work_ref, matrix_ref)
     mine = pl.ds(pl.multiple_of(lax.rem(lax.axis_index("col"), 2) * half, 8), half)
+    covar_ref[...] = jnp.zeros_like(covar_ref)
+    mean_ref[...] = jnp.zeros_like(mean_ref)
+
+    @pl.when(seg == 1)
+    def _():
+        add_prior(matrix_ref, prior_ref, start_ref, covar_ref, mean_ref)
 
     @pl.when(seg < 2)
     def _():
@@ -249,42 +284,19 @@
 
 
 def pair_covariance(
-    steps, noise_ref, offset_ref, prior_ref, start_ref, matrix_ref, psi_ref, matrix_other_ref,
-    covar_ref, mean_ref, covar_other_ref, mean_other_ref, out_ref, step_ref,
+    steps, psi_ref, covar_ref, mean_ref, noise_other_ref, offset_other_ref, matrix_other_ref, first_other_ref,
+    first_mean_other_ref, covar_other_ref, mean_other_ref, out_ref, step_ref,
 ):
-    states = prior_ref.shape[0]
+    states = first_other_ref.shape[0]
     edge = states // 3
-    seg = lax.axis_index("seg")
-    is_second = lax.rem(seg, 2) == 1
+    is_second = lax.rem(lax.axis_index("seg"), 2) == 1
     last = steps - 1
-    covar_ref[0] = noise_ref[0]
-    mean_ref[0] = offset_ref[0]
-
-    def with_prior(step):
-        return square(step, prior_ref[...], mean_block(start_ref[...], states))
-
-    @pl.when(seg == 0)
-    def _():
-        covar, mean = with_prior(matrix_ref[0])
-        covar_ref[0] += covar
-        mean_ref[0] += mean
-
-    for k in range(1, steps):
-        covar, mean = square(matrix_ref[k], covar_ref[k - 1], mean_ref[k - 1])
-        covar_ref[k] = covar + noise_ref[k]
-        mean_ref[k] = mean + offset_ref[k]
 
     @pl.when(is_second)
     def _():
-        covar_other_ref[...] = noise_ref[steps]
-        mean_other_ref[...] = offset_ref[steps]
+        covar_other_ref[...] = noise_other_ref[0] + first_other_ref[...]
+        mean_other_ref[...] = offset_other_ref[0] + first_mean_other_ref[...]
         step_ref[...] = psi_ref[last]
-
-        @pl.when(seg == 1)
-        def _():
-            covar, mean = with_prior(matrix_other_ref[0])
-            covar_other_ref[...] += covar
-            mean_other_ref[...] += mean
 
     @pl.when(jnp.logical_not(is_second))
     def _():
@@ -292,20 +304,18 @@
         mean_other_ref[...] = mean_ref[last]
         step_ref[...] = matrix_other_ref[last]
 
-    def one_step(k):
-        covar, mean = square(matrix_other_ref[k], covar_other_ref[...], mean_other_ref[...])
-        covar_other_ref[...] = covar + noise_ref[steps + k]
-        mean_other_ref[...] = mean + offset_ref[steps + k]
-
     for k in range(last):
-        one_step(k + is_second.astype(jnp.int32))
+        at = k + is_second.astype(jnp.int32)
+        covar, mean = square(matrix_other_ref[at], covar_other_ref[...], mean_other_ref[...])
+        covar_other_ref[...] = covar + noise_other_ref[at]
+        mean_other_ref[...] = mean + offset_other_ref[at]
 
     def blocks(i, j):
         at = slice(j * edge, (j + 1) * edge)
         if i == 3:
-            return jnp.where(is_second, mean_ref[last, :1, at], offset_ref[steps + last, :1, at])
+            return jnp.where(is_second, mean_ref[last, :1, at], offset_other_ref[last, :1, at])
         rows = slice(i * edge, (i + 1) * edge)
-        return jnp.where(is_second, covar_ref[last, rows, at], noise_ref[steps + last, rows, at])
+        return jnp.where(is_second, covar_ref[last, rows, at], noise_other_ref[last, rows, at])
 
     put_packed(step_ref, covar_other_ref[...], mean_other_ref[...], blocks, out_ref)
 
@@ -373,43 +383,57 @@
     return jnp.concatenate([jnp.where(is_low, mine, mate), jnp.where(is_low, mate, mine)], axis=0)
 
 
+def place_in(bit):
+    return lax.div(lax.rem(lax.axis_index("seg"), 2 * bit) - bit, 2) - (lax.rem(lax.axis_index("seg"), 2 * bit) < bit)
+
+
 def is_upper(bit):
-    return lax.rem(lax.div(lax.axis_index("seg"), bit), 2) == 1
-
-
-def joined_covariance(
-    bit, last, psi_ref, mine_ref, mate_ref, step_mine_ref, step_mate_ref, came_mine_ref, came_mate_ref, out_ref,
-    step_ref, first_mine_ref, first_mate_ref, added_ref, work_ref,
-):
-    @pl.when(jnp.logical_not(last) | jnp.logical_not(is_upper(2 * bit)))
-    def _():
-        upper = is_upper(bit)
-        step_ref[...] = jnp.where(upper, psi_ref[...], whole_matrix(step_mine_ref, step_mate_ref))
-        first_mine_ref[...] = jnp.where(upper, came_mine_ref[...], mine_ref[...])
-        first_mate_ref[...] = jnp.where(upper, came_mate_ref[...], mate_ref[...])
-        added_ref[...] = jnp.where(upper, mine_ref[...], came_mine_ref[...])
-        mean = unpacked(first_mine_ref, first_mate_ref, work_ref)
-        put_packed(step_ref, work_ref[...], mean, packed_blocks(added_ref, out_ref.shape[1]), out_ref)
-
-
-def joined_matrix(bit, psi_ref, step_mine_ref, step_mate_ref, out_ref):
-    came = whole_matrix(step_mine_ref, step_mate_ref)
-    upper = is_upper(bit)
-    out_ref[...] = dot_nn(jnp.where(upper, psi_ref[...], came), jnp.where(upper, came, psi_ref[...]))
-
-
-def entered(bit, psi_ref, covar_ref, mean_ref, step_mine_ref, step_mate_ref, mine_ref, mate_ref, *refs):
-    psi_out_ref, covar_out_ref, mean_out_ref, work_ref = refs
+    return lax.rem(lax.axis_index("seg"), 2 * bit) >= bit
+
+
+def chosen(refs, bit):
+    at = place_in(bit)
+    value = refs[0][...]
+    for i, ref in enumerate(refs[1:]):
+        value = jnp.where(at == i + 1, ref[...], value)
+    return value
+
+
+def joined_covariance(bit, psi_ref, total_ref, *refs):
+    n_group = bit // 2
+    mines, mates = refs[:n_group], refs[n_group : 2 * n_group]
+    out_ref, mine_ref, mate_ref, work_ref = refs[2 * n_group :]
+
+    @pl.when(lax.rem(lax.axis_index("seg"), 2 * bit) >= 2 * bit - 2)
+    def _():
+        mine_ref[...] = chosen(mines, bit)
+        mate_ref[...] = chosen(mates, bit)
+        mean = unpacked(mine_ref, mate_ref, work_ref)
+        put_packed(psi_ref, work_ref[...], mean, packed_blocks(total_ref, out_ref.shape[1]), out_ref)
+
+
+def joined_matrix(bit, psi_ref, *refs):
+    n_group = bit // 2
+    psi_ref_out, mine_ref, mate_ref = refs[2 * n_group :]
+    mine_ref[...] = chosen(refs[:n_group], bit)
+    mate_ref[...] = chosen(refs[n_group : 2 * n_group], bit)
+    psi_ref_out[...] = dot_nn(psi_ref[...], whole_matrix(mine_ref, mate_ref))
+
+
+def entered(bit, psi_ref, covar_ref, mean_ref, *refs):
+    n_group = bit // 2
+    mines, mates = refs[:n_group], refs[n_group : 2 * n_group]
+    covar_out_ref, mean_out_ref, mine_ref, mate_ref, work_ref = refs[2 * n_group :]
     steps, width, states = covar_ref.shape
     mine = pl.ds(pl.multiple_of(lax.axis_index("col") * width, 8), width)
 
     @pl.when(is_upper(bit))
     def _():
-        before = whole_matrix(step_mine_ref, step_mate_ref)
+        mine_ref[...] = chosen(mines, bit)
+        mate_ref[...] = chosen(mates, bit)
         mean = unpacked(mine_ref, mate_ref, work_ref)
         covar = work_ref[...]
         for k in range(steps):
-            psi_out_ref[k] = dot_nn(psi_ref[k], before)
             half = dot_nn(psi_ref[k, mine, :], covar)
             both = dot_nt(jnp.concatenate([half, mean], axis=0), psi_ref[k])
             covar_out_ref[k] = both[:width] + covar_ref[k]
@@ -417,23 +441,65 @@
 
     @pl.when(jnp.logical_not(is_upper(bit)))
     def _():
-        psi_out_ref[...] = psi_ref[...]
         covar_out_ref[...] = covar_ref[...]
         mean_out_ref[...] = mean_ref[...]
 
 
-def finished(bit, psi_ref, covar_ref, mean_ref, mine_ref, mate_ref, covar_out_ref, mean_out_ref, work_ref):
+def takes_matrix(bit):
+    return is_upper(bit) & (lax.axis_index("seg") >= 2 * bit)
+
+
+def matrices_entered(bit, psi_ref, *refs):
+    n_group = bit // 2
+    psi_out_ref, mine_ref, mate_ref = refs[2 * n_group :]
+    psi_out_ref[...] = psi_ref[...]
+
+    @pl.when(takes_matrix(bit))
+    def _():
+        mine_ref[...] = chosen(refs[:n_group], bit)
+        mate_ref[...] = chosen(refs[n_group : 2 * n_group], bit)
+        before = whole_matrix(mine_ref, mate_ref)
+        for k in range(psi_ref.shape[0]):
+            psi_out_ref[k] = dot_nn(psi_ref[k], before)
+
+
+def finished(bit, n_step, psi_ref, covar_ref, mean_ref, *refs):
+    n_group = bit // 2
+    step_refs, refs = refs[: 2 * n_step], refs[2 * n_step :]
+    mines, mates = refs[:n_group], refs[n_group : 2 * n_group]
+    covar_out_ref, mean_out_ref, mine_ref, mate_ref, work_ref, half_ref, other_half_ref, rows_ref, enter_ref = refs[2 * n_group :]
     steps, width, states = covar_ref.shape
     mine = pl.ds(pl.multiple_of(lax.axis_index("col") * width, 8), width)
 
     @pl.when(is_upper(bit))
     def _():
+        mine_ref[...] = chosen(mines, bit)
+        mate_ref[...] = chosen(mates, bit)
         mean = unpacked(mine_ref, mate_ref, work_ref)
-        rows = jnp.concatenate([psi_ref[k, mine, :] for k in range(steps)], axis=0)
-        half = dot_nn(rows, work_ref[...])
         for k in range(steps):
-            part = half[k * width : (k + 1) * width]
-            both = dot_nt(jnp.concatenate([part, mean], axis=0), psi_ref[k])
+            rows_ref[k * width : (k + 1) * width, :] = psi_ref[k, mine, :]
+        n_row = steps * width
+
+        def through(rows):
+            return jnp.concatenate([dot_nn(rows, work_ref[...]), mean], axis=0)
+
+        if n_step:
+
+            @pl.when(takes_matrix(bit // 2))
+            def _():
+                half_ref[...] = chosen(step_refs[:n_step], bit // 2)
+                other_half_ref[...] = chosen(step_refs[n_step:], bit // 2)
+                before = whole_matrix(half_ref, other_half_ref)
+                enter_ref[...] = dot_nt(through(dot_nn(rows_ref[...], before)), before)
+
+            @pl.when(jnp.logical_not(takes_matrix(bit // 2)))
+            def _():
+                enter_ref[...] = through(rows_ref[...])
+        else:
+            enter_ref[...] = through(rows_ref[...])
+        for k in range(steps):
+            part = jnp.concatenate([enter_ref[k * width : (k + 1) * width, :], enter_ref[n_row:, :]], axis=0)
+            both = dot_nt(part, psi_ref[k])
             covar_out_ref[k] = both[:width] + covar_ref[k]
             mean_out_ref[k : k + 1, :] = both[width : width + 1] + mean_ref[k, :1, :]
 
@@ -446,6 +512,20 @@
 
 def swapped(block, axis, bit):
     return lax.ppermute(block, axis, [(i, i ^ bit) for i in range(lax.axis_size(axis))])
+
+
+def handed_up(block, bit, first=0):
+    n_seg, n_col = lax.axis_size("seg"), lax.axis_size("col")
+    came = []
+    for group in range(bit // 2):
+        aside = n_col // 2 if group % 2 == 0 else n_col
+        to = {i: i ^ aside for i in range(n_seg * n_col)}
+        for low in range(first * 2 * bit, n_seg, 2 * bit):
+            for i in range((low + bit - 2) * n_col, (low + bit) * n_col):
+                j = i + (2 + 2 * group) * n_col
+                to[i], to[j] = j, i
+        came.append(lax.ppermute(block, ("seg", "col"), sorted(to.items())))
+    return came
 
 
 def with_mate(share):
@@ -495,19 +575,19 @@
         copied=True,
         cost=3,
     )
+    corr_mine, gain = lax.optimization_barrier((corr_mine, gain))
+    fixed, prior = local_call(
+        fixed_parts, [square_shape, square_shape], gain, obs_noise[None, :], prior_factor
+    )
     corr = [corr_mine]
     for bit in far_bits:
         corr = corr + [swapped(b, "col", bit) for b in corr]
     vectors_other = swapped(vectors, "seg", 1)
-    fixed, prior = local_call(
-        fixed_parts, [square_shape, square_shape], gain, obs_noise[None, :], prior_factor
-    )
     own, near, fixed, vectors_other = lax.optimization_barrier((own, near, fixed, vectors_other))
     other = [near] + [swapped(b, "seg", 1) for b in own[1:]]
-    corr, vectors_other, fixed = lax.optimization_barrier((corr, vectors_other, fixed))
     corr = corr + [swapped(b, "col", 1) for b in corr]
-
     rows_shape = (steps,) + half_shape
+    noise_shapes = [(steps,) + square_shape, (steps,) + mean_shape]
     correction, rows = local_call(
         functools.partial(own_rows, offsets + [o ^ 1 for o in offsets]),
         [square_shape, rows_shape],
@@ -515,52 +595,55 @@
         *own,
         scratch=[square_shape],
     )
-    noise, offset = local_call(
-        noises,
-        [(2 * steps,) + square_shape, (2 * steps,) + mean_shape],
-        vectors,
-        vectors_other,
-        fixed,
-        correction,
-    )
-    other, correction, noise = lax.optimization_barrier((other, correction, noise))
-    rows = with_mate(rows)
-    (rows_other,) = local_call(other_rows, [rows_shape], correction, *other, cost=1)
-    matrix, psi = local_call(
-        functools.partial(own_matrices, offsets),
-        [(steps,) + square_shape, (steps,) + square_shape],
+    noise, offset = local_call(noises, noise_shapes, vectors, fixed, correction)
+    start = prior_mean[None, :]
+    noise_other, offset_other = local_call(noises, noise_shapes, vectors_other, fixed, correction)
+    other, correction, noise, noise_other = lax.optimization_barrier((other, correction, noise, noise_other))
+    (rows_other,) = local_call(other_rows, [rows_shape], correction, *other)
+    matrix, psi, covar, mean = local_call(
+        functools.partial(own_segment, offsets),
+        [(steps,) + square_shape, (steps,) + square_shape, (steps,) + square_shape, (steps,) + mean_shape],
         vectors,
         correction,
-        *rows,
+        *with_mate(rows),
+        noise,
+        offset,
+        prior,
+        start,
         scratch=[square_shape],
         cost=1,
     )
-    matrix_other, psi_other, psi_half = local_call(
+    matrix_other, psi_other, psi_half, first_other, first_mean_other = local_call(
         functools.partial(other_matrices, offsets),
-        [(steps,) + square_shape, square_shape, half_shape],
+        [(steps,) + square_shape, square_shape, half_shape, square_shape, mean_shape],
         vectors_other,
         correction,
         *with_mate(rows_other),
         psi,
+        prior,
+        start,
         scratch=[square_shape],
     )
     bit = 2
     more = 2 * bit < n_seg
+    covar_other, mean_other, total = local_call(
+        functools.partial(pair_covariance, steps),
+        [square_shape, mean_shape, share_shape],
+        psi,
+        covar,
+        mean,
+        noise_other,
+        offset_other,
+        matrix_other,
+        first_other,
+        first_mean_other,
+        scratch=[square_shape],
+    )
+    total, psi_half = lax.optimization_barrier((total, psi_half))
+    came = handed_up(total, bit)
+    step = []
     if more:
-        step = swapped(psi_half, "seg", bit)
-    covar, mean, covar_other, mean_other, total = local_call(
-        functools.partial(pair_covariance, steps),
-        [(steps,) + square_shape, (steps,) + mean_shape, square_shape, mean_shape, share_shape],
-        noise,
-        offset,
-        prior,
-        prior_mean[None, :],
-        matrix,
-        psi,
-        matrix_other,
-        scratch=[square_shape],
-    )
-    came = swapped(total, "seg", bit)
+        step = handed_up(psi_half, bit, 1)
     psi, covar, mean, psi_all = local_call(
         functools.partial(pair_elements, steps, width),
         [(steps,) + square_shape, (steps, width, states), (steps,) + mean_shape, square_shape],
@@ -571,47 +654,58 @@
         covar_other,
         mean_other,
     )
+    def over_core(blocks):
+        return list(blocks) + [swapped(b, "col", 1) for b in blocks]
+
     while more:
-        total = with_mate(total)
-        came, step, psi_all, psi = lax.optimization_barrier((came, step, psi_all, psi))
-        came, step = with_mate(came), with_mate(step)
-        last = 4 * bit >= n_seg
-        (total_next,) = local_call(
-            functools.partial(joined_covariance, bit, last),
+        more = 4 * bit < n_seg
+        came, psi_all, psi = lax.optimization_barrier((came, psi_all, psi))
+        came = over_core(came)
+        (total,) = local_call(
+            functools.partial(joined_covariance, bit),
             [share_shape],
             psi_all,
-            *total,
-            *step,
+            total,
             *came,
-            scratch=[square_shape, share_shape, share_shape, share_shape, square_shape],
+            scratch=[share_shape, share_shape, square_shape],
         )
-        came_next = swapped(total_next, "seg", 2 * bit)
-        psi, covar, mean = local_call(
+        came_next = handed_up(total, 2 * bit)
+        covar, mean = local_call(
             functools.partial(entered, bit),
-            [(steps,) + square_shape, (steps, width, states), (steps,) + mean_shape],
+            [(steps, width, states), (steps,) + mean_shape],
             psi,
             covar,
             mean,
-            *step,
             *came,
-            scratch=[square_shape],
+            scratch=[share_shape, share_shape, square_shape],
         )
-        if not last:
-            (psi_all,) = local_call(functools.partial(joined_matrix, bit), [square_shape], psi_all, *step)
+        if more:
+            step = over_core(step)
+            (psi,) = local_call(
+                functools.partial(matrices_entered, bit),
+                [(steps,) + square_shape],
+                psi,
+                *step,
+                scratch=[half_shape, half_shape],
+            )
+            (psi_all,) = local_call(
+                functools.partial(joined_matrix, bit), [square_shape], psi_all, *step, scratch=[half_shape, half_shape]
+            )
             psi_half = lax.dynamic_slice_in_dim(psi_all, col % 2 * (states // 2), states // 2, 0)
-            step = swapped(psi_half, "seg", 2 * bit)
-        total, came = total_next, came_next
+            step = handed_up(psi_half, 2 * bit, 1)
+        came = came_next
         bit *= 2
-        more = not last
-    came, psi = lax.optimization_barrier((came, psi))
+    came, covar, step = lax.optimization_barrier((came, covar, step))
     covars, means = local_call(
-        functools.partial(finished, bit),
+        functools.partial(finished, bit, len(step)),
         [(steps, width, states), (steps, states)],
         psi,
         covar,
         mean,
-        *with_mate(came),
-        scratch=[square_shape],
+        *over_core(step),
+        *over_core(came),
+        scratch=[share_shape, share_shape, square_shape, half_shape, half_shape]
+        + [(steps * width, states), (steps * width + MEAN_ROWS, states)],
     )
     return means, covars
 

time: 55.5 us -> 52.1 us (0.939)
  the two profiles are of different devices: /device:TPU:0 before, /device:TPU:29 now
where the time goes in v5:
time: 52.1 us; the launch traced here: 51.9 us
  Pallas kernels  21.8 us (42%)
  waiting for transfers between devices  17.5 us (34%)
  starting transfers between devices  11.8 us (23%)
  between operations  0.8 us (2%)
    pallas_call x13, Pallas kernels, local_call(): pl.pallas_call(body, out_shape=shapes, name=getattr(body, 'func', body)._...  21.8 us
    ppermute x4, waiting for transfers between devices, handed_up(): came.append(lax.ppermute(block, ('seg', 'col'), sorted(to.items())))  12.5 us
    ppermute x13, starting transfers between devices, swapped(): lax.ppermute(block, axis, [(i, i ^ bit) for i in range(lax.axis_size(axis...  10.7 us
    ppermute x13, waiting for transfers between devices, swapped(): lax.ppermute(block, axis, [(i, i ^ bit) for i in range(lax.axis_size(axis...  4.91 us
    ppermute x4, starting transfers between devices, handed_up(): came.append(lax.ppermute(block, ('seg', 'col'), sorted(to.items())))  1.13 us
  transfers between devices with their start and end apart: 17, of which 7 were waited for; matrix products, arithmetic and copies ran while one was open for 0% of the time, Pallas kernels for 29%

profile of v5, /device:TPU:29, one launch (start us, length us, event | category | flops | bytes accessed | tf_op | source)
XLA Modules:
  0.0 51.9 jit_solution(13117249516226412374)
XLA Ops:
  0.7 1.3 %collective-permute-start = (f32[2,96,384]{2,1,0:T(8,128)}, f32[2,96,384]{2,1,0:T(8,128)S(1)}, u32[]{:S(2)}, u32[]{:S(2)}) collective-permute-start(f32[2,96,384]{2,1,0:T(8,128)} %refs_4_), channel_id=1, source_target_pairs={{0,2},{1,3},{2,0},{3,1},{4,6},{5,7},{6,4},{7,5},{8,10},{9,11},{10,... | collective-permute-start | bytes 884744 | tf_op jit(solution)/shard_map/ppermute | solution.py:514
  2.2 3.1 %correction_rows.1 = (f32[96,384]{1,0:T(8,128)}, f32[2,4,384]{2,1,0:T(4,128)}) custom-call(f32[384,1024]{1,0:T(8,128)} %gain_ref, f32[96,1024]{1,0:T(8,128)} %oper_hbm.1, f32[2,1024]{1,0:T(2,128)} %seen_hbm.1, f32[2,384]{1,0:T(2,128)} %keep_hbm.1, f32[2,384]{1,0:T(2,128)} %push_hbm.1, f32[2,384]{1,0:T(2,128)} %var_hbm.1), custom_call_target="tpu_custom_call" | custom-call | flops 2100000000 | bytes 4096 | tf_op jit(solution)/shard_map/correction_rows/pallas_call | solution.py:53
  5.3 0.4 collective-permute-start.4
  5.7 1.2 %collective-permute-start.2 = (f32[2,4,384]{2,1,0:T(4,128)}, f32[2,4,384]{2,1,0:T(4,128)S(1)}, u32[]{:S(2)}, u32[]{:S(2)}) collective-permute-start(f32[2,4,384]{2,1,0:T(4,128)} %get-tuple-element.52.vec_ref), channel_id=1, source_target_pairs={{0,4},{4,0},{8,12},{12,8},{16,20},{20,16},{24,28},{28,24},{1,5},{5... | collective-permute-start | bytes 36872 | tf_op jit(solution)/shard_map/ppermute | solution.py:514
  6.9 1.4 %fixed_parts.1 = (f32[384,384]{1,0:T(8,128)S(1)}, f32[384,384]{1,0:T(8,128)S(1)}) custom-call(f32[384,1024]{1,0:T(8,128)S(1)} %copy-done, f32[1,1024]{1,0:T(1,128)S(1)} %bitcast.1, f32[384,384]{1,0:T(8,128)S(1)} %copy-done.1), custom_call_target="tpu_custom_call" | custom-call | bytes 4096 | tf_op jit(solution)/shard_map/fixed_parts/pallas_call | solution.py:53
  8.3 1.7 %collective-permute-done.2.vec_ref = f32[2,4,384]{2,1,0:T(4,128)S(1)} collective-permute-done((f32[2,4,384]{2,1,0:T(4,128)}, f32[2,4,384]{2,1,0:T(4,128)S(1)}, u32[]{:S(2)}, u32[]{:S(2)}) %collective-permute-start.2) | collective-permute-done | bytes 12320 | tf_op jit(solution)/shard_map/ppermute | solution.py:514
  10.2 2.3 %collective-permute-start.5 = (f32[96,384]{1,0:T(8,128)S(1)}, f32[96,384]{1,0:T(8,128)S(1)}, u32[]{:S(2)}, u32[]{:S(2)}) collective-permute-start(f32[96,384]{1,0:T(8,128)S(1)} %copy-done.3), channel_id=1, source_target_pairs={{0,1},{1,0},{2,3},{3,2},{4,5},{5,4},{6,7},{7,6},{8,9},{9,8},{10,11... | collective-permute-start | bytes 442376 | tf_op jit(solution)/shard_map/ppermute | solution.py:514
  12.6 1.0 %collective-permute-start.6 = (f32[96,384]{1,0:T(8,128)S(1)}, f32[96,384]{1,0:T(8,128)S(1)}, u32[]{:S(2)}, u32[]{:S(2)}) collective-permute-start(f32[96,384]{1,0:T(8,128)S(1)} %collective-permute-done.4.refs_1_), channel_id=1, source_target_pairs={{0,1},{1,0},{2,3},{3,2},{4,5},{5,4},{6,7},{7,6},{8,9},{9,8},{10,11... | collective-permute-start | bytes 442376 | tf_op jit(solution)/shard_map/ppermute | solution.py:514
  13.6 1.0 %collective-permute-done.6.refs_3_ = f32[96,384]{1,0:T(8,128)S(1)} collective-permute-done((f32[96,384]{1,0:T(8,128)S(1)}, f32[96,384]{1,0:T(8,128)S(1)}, u32[]{:S(2)}, u32[]{:S(2)}) %collective-permute-start.6) | collective-permute-done | bytes 147488 | tf_op jit(solution)/shard_map/ppermute | solution.py:514
  14.5 0.8 %own_rows.1 = (f32[384,384]{1,0:T(8,128)S(1)}, f32[2,192,384]{2,1,0:T(8,128)S(1)}) custom-call(f32[96,384]{1,0:T(8,128)S(1)} %copy-done.3, f32[96,384]{1,0:T(8,128)S(1)} %collective-permute-done.4.refs_1_, f32[96,384]{1,0:T(8,128)S(1)} %collective-permute-done.5.refs_2_, f32[96,384]{1,0:T(8,128)S(1)} %collective-permute-done.6.refs_3_, ...), custom_call_target="tpu_custom_call" | custom-call | bytes 4096 | tf_op jit(solution)/shard_map/own_rows/pallas_call | solution.py:53
  15.4 0.4 collective-permute-start.7
  15.8 1.3 %noises.2 = (f32[2,384,384]{2,1,0:T(8,128)S(1)}, f32[2,16,384]{2,1,0:T(8,128)S(1)}) custom-call(f32[2,4,384]{2,1,0:T(4,128)S(1)} %copy-done.4, f32[384,384]{1,0:T(8,128)S(1)} %get-tuple-element.61.fixed_ref, f32[384,384]{1,0:T(8,128)S(1)} %get-tuple-element.65.corr_ref), custom_call_target="tpu_custom_call" | custom-call | bytes 4096 | tf_op jit(solution)/shard_map/noises/pallas_call | solution.py:53
  17.1 1.3 %noises.3 = (f32[2,384,384]{2,1,0:T(8,128)S(1)}, f32[2,16,384]{2,1,0:T(8,128)S(1)}) custom-call(f32[2,4,384]{2,1,0:T(4,128)S(1)} %collective-permute-done.2.vec_ref, f32[384,384]{1,0:T(8,128)S(1)} %get-tuple-element.61.fixed_ref, f32[384,384]{1,0:T(8,128)S(1)} %get-tuple-element.65.corr_ref), custom_call_target="tpu_custom_call" | custom-call | bytes 4096 | tf_op jit(solution)/shard_map/noises/pallas_call | solution.py:53
  18.4 0.7 %other_rows.1.mine_ref = f32[2,192,384]{2,1,0:T(8,128)S(1)} custom-call(f32[384,384]{1,0:T(8,128)S(1)} %get-tuple-element.65.corr_ref, f32[2,96,384]{2,1,0:T(8,128)S(1)} %collective-permute-done.1.refs_0_, f32[2,96,384]{2,1,0:T(8,128)S(1)} %collective-permute-done.3.refs_1_), custom_call_target="tpu_custom_call" | custom-call | bytes 4096 | tf_op jit(solution)/shard_map/other_rows/pallas_call | solution.py:53
  19.0 1.1 %collective-permute-start.8 = (f32[2,192,384]{2,1,0:T(8,128)S(1)}, f32[2,192,384]{2,1,0:T(8,128)S(1)}, u32[]{:S(2)}, u32[]{:S(2)}) collective-permute-start(f32[2,192,384]{2,1,0:T(8,128)S(1)} %other_rows.1.mine_ref), channel_id=1, source_target_pairs={{0,1},{1,0},{2,3},{3,2},{4,5},{5,4},{6,7},{7,6},{8,9},{9,8},{10,11... | collective-permute-start | bytes 1769480 | tf_op jit(solution)/shard_map/ppermute | solution.py:514
  20.2 2.2 %own_segment.1 = (f32[2,384,384]{2,1,0:T(8,128)}, f32[2,384,384]{2,1,0:T(8,128)S(1)}, f32[2,384,384]{2,1,0:T(8,128)S(1)}, f32[2,16,384]{2,1,0:T(8,128)S(1)}) custom-call(f32[2,4,384]{2,1,0:T(4,128)S(1)} %copy-done.4, f32[384,384]{1,0:T(8,128)S(1)} %get-tuple-element.65.corr_ref, f32[2,192,384]{2,1,0:T(8,128)S(1)} %get-tuple-element.66.mine_ref, ...), custom_call_target="tpu_custom_call" | custom-call | flops 700000000 | bytes 4096 | tf_op jit(solution)/shard_map/own_segment/pallas_call | solution.py:53
  22.4 1.7 %other_matrices.1 = (f32[2,384,384]{2,1,0:T(8,128)S(1)}, f32[384,384]{1,0:T(8,128)S(1)}, f32[192,384]{1,0:T(8,128)S(1)}, f32[384,384]{1,0:T(8,128)S(1)}, f32[16,384]{1,0:T(8,128)S(1)}) custom-call(f32[2,4,384]{2,1,0:T(4,128)S(1)} %collective-permute-done.2.vec_ref, f32[384,384]{1,0:T(8,128)S(1)} %get-tuple-element.65.corr_ref, ...), custom_call_target="tpu_custom_call" | custom-call | bytes 4096 | tf_op jit(solution)/shard_map/other_matrices/pallas_call | solution.py:53
  24.0 2.1 %pair_covariance.1 = (f32[384,384]{1,0:T(8,128)S(1)}, f32[16,384]{1,0:T(8,128)S(1)}, f32[392,128]{1,0:T(8,128)S(1)}) custom-call(f32[2,384,384]{2,1,0:T(8,128)S(1)} %get-tuple-element.70.psi_ref, f32[2,384,384]{2,1,0:T(8,128)S(1)} %get-tuple-element.71.covar_ref, f32[2,16,384]{2,1,0:T(8,128)S(1)} %get-tuple-element.72.mean_ref, ...), custom_call_target="tpu_custom_call" | custom-call | bytes 4096 | tf_op jit(solution)/shard_map/pair_covariance/pallas_call | solution.py:53
  26.4 2.5 %pair_elements.1 = (f32[2,384,384]{2,1,0:T(8,128)S(1)}, f32[2,96,384]{2,1,0:T(8,128)S(1)}, f32[2,16,384]{2,1,0:T(8,128)S(1)}, f32[384,384]{1,0:T(8,128)S(1)}) custom-call(f32[2,384,384]{2,1,0:T(8,128)S(1)} %get-tuple-element.70.psi_ref, f32[2,384,384]{2,1,0:T(8,128)S(1)} %get-tuple-element.71.covar_ref, f32[2,16,384]{2,1,0:T(8,128)S(1)} %get-tuple-element.72.mean_ref, ...), custom_call_target="tpu_custom_call" | custom-call | bytes 4096 | tf_op jit(solution)/shard_map/pair_elements/pallas_call | solution.py:53
  28.9 3.5 %collective-permute-done.9.refs_0_ = f32[392,128]{1,0:T(8,128)S(1)} collective-permute-done((f32[392,128]{1,0:T(8,128)S(1)}, f32[392,128]{1,0:T(8,128)S(1)}, u32[]{:S(2)}, u32[]{:S(2)}) %collective-permute-start.9) | collective-permute-done | bytes 200736 | tf_op jit(solution)/shard_map/ppermute | solution.py:527
  32.4 1.2 %collective-permute-start.10 = (f32[392,128]{1,0:T(8,128)S(1)}, f32[392,128]{1,0:T(8,128)S(1)}, u32[]{:S(2)}, u32[]{:S(2)}) collective-permute-start(f32[392,128]{1,0:T(8,128)S(1)} %collective-permute-done.9.refs_0_), channel_id=1, source_target_pairs={{0,1},{1,0},{2,3},{3,2},{4,5},{5,4},{6,7},{7,6},{8,9},{9,8},{10,11... | collective-permute-start | bytes 602120 | tf_op jit(solution)/shard_map/ppermute | solution.py:514
  33.8 0.9 %collective-permute-done.10.refs_1_ = f32[392,128]{1,0:T(8,128)S(1)} collective-permute-done((f32[392,128]{1,0:T(8,128)S(1)}, f32[392,128]{1,0:T(8,128)S(1)}, u32[]{:S(2)}, u32[]{:S(2)}) %collective-permute-start.10) | collective-permute-done | bytes 200736 | tf_op jit(solution)/shard_map/ppermute | solution.py:514
  34.7 0.8 %joined_covariance.1 = f32[392,128]{1,0:T(8,128)S(1)} custom-call(f32[384,384]{1,0:T(8,128)S(1)} %get-tuple-element.89.psi_ref, f32[392,128]{1,0:T(8,128)S(1)} %get-tuple-element.82.total_ref, f32[392,128]{1,0:T(8,128)S(1)} %collective-permute-done.9.refs_0_, f32[392,128]{1,0:T(8,128)S(1)} %collective-permute-done.10.refs_1_), custom_call_target="tpu_custom_call" | custom-call | bytes 4096 | tf_op jit(solution)/shard_map/joined_covariance/pallas_call | solution.py:53
  35.5 0.4 collective-permute-start.11
  35.9 0.4 collective-permute-start.12
  36.3 1.2 %entered.1 = (f32[2,96,384]{2,1,0:T(8,128)S(1)}, f32[2,16,384]{2,1,0:T(8,128)S(1)}) custom-call(f32[2,384,384]{2,1,0:T(8,128)S(1)} %get-tuple-element.88.psi_ref, f32[2,96,384]{2,1,0:T(8,128)S(1)} %get-tuple-element.91.covar_ref, f32[2,16,384]{2,1,0:T(8,128)S(1)} %get-tuple-element.92.mean_ref, f32[392,128]{1,0:T(8,128)S(1)} %collective-permute-done.9.refs_0_, ...), custom_call_target="tpu_custom_call" | custom-call | bytes 4096 | tf_op jit(solution)/shard_map/entered/pallas_call | solution.py:53
  37.5 9.0 %collective-permute-done.13.refs_0_ = f32[192,384]{1,0:T(8,128)S(1)} collective-permute-done((f32[192,384]{1,0:T(8,128)S(1)}, f32[192,384]{1,0:T(8,128)S(1)}, u32[]{:S(2)}, u32[]{:S(2)}) %collective-permute-start.13) | collective-permute-done | bytes 294944 | tf_op jit(solution)/shard_map/ppermute | solution.py:527
  46.6 0.8 %collective-permute-start.14 = (f32[192,384]{1,0:T(8,128)S(1)}, f32[192,384]{1,0:T(8,128)S(1)}, u32[]{:S(2)}, u32[]{:S(2)}) collective-permute-start(f32[192,384]{1,0:T(8,128)S(1)} %collective-permute-done.13.refs_0_), channel_id=1, source_target_pairs={{0,1},{1,0},{2,3},{3,2},{4,5},{5,4},{6,7},{7,6},{8,9},{9,8},{10,11... | collective-permute-start | bytes 884744 | tf_op jit(solution)/shard_map/ppermute | solution.py:514
  47.4 0.4 collective-permute-start.16
  47.9 1.0 %collective-permute-done.15.refs_4_ = f32[392,128]{1,0:T(8,128)S(1)} collective-permute-done((f32[392,128]{1,0:T(8,128)S(1)}, f32[392,128]{1,0:T(8,128)S(1)}, u32[]{:S(2)}, u32[]{:S(2)}) %collective-permute-start.15) | collective-permute-done | bytes 200736 | tf_op jit(solution)/shard_map/ppermute | solution.py:514
  48.8 0.3 collective-permute-done.16.refs_5_
  49.1 2.8 %finished.1 = (f32[2,96,384]{2,1,0:T(8,128)}, f32[2,384]{1,0:T(2,128)}) custom-call(f32[2,384,384]{2,1,0:T(8,128)S(1)} %get-tuple-element.88.psi_ref, f32[2,96,384]{2,1,0:T(8,128)S(1)} %get-tuple-element.95.covar_ref, f32[2,16,384]{2,1,0:T(8,128)S(1)} %get-tuple-element.96.mean_ref, f32[192,384]{1,0:T(8,128)S(1)} %collective-permute-done.13.refs_0_, ...), custom_call_target="tpu_custom_call" | custom-call | bytes 4096 | tf_op jit(solution)/shard_map/finished/pallas_call | solution.py:53
  (30 shorter events, 1.0 us)
Async XLA Ops:
  0.6 6.2 %copy-start = (f32[384,1024]{1,0:T(8,128)S(1)}, f32[384,1024]{1,0:T(8,128)}, u32[]{:S(2)}) copy-start(f32[384,1024]{1,0:T(8,128)} %gain_ref) | copy-start | bytes 4718596
  0.6 6.2 %copy-start.5 = (f32[1024]{0:T(1024)S(1)}, f32[1024]{0:T(1024)}, u32[]{:S(2)}) copy-start(f32[1024]{0:T(1024)} %param.15) | copy-start | bytes 12292
  0.7 6.2 %copy-start.1 = (f32[384,384]{1,0:T(8,128)S(1)}, f32[384,384]{1,0:T(8,128)}, u32[]{:S(2)}) copy-start(f32[384,384]{1,0:T(8,128)} %factor_ref.1) | copy-start | bytes 1769476
  0.7 9.3 %collective-permute-start = (f32[2,96,384]{2,1,0:T(8,128)}, f32[2,96,384]{2,1,0:T(8,128)S(1)}, u32[]{:S(2)}, u32[]{:S(2)}) collective-permute-start(f32[2,96,384]{2,1,0:T(8,128)} %refs_4_), channel_id=1, source_target_pairs={{0,2},{1,3},{2,0},{3,1},{4,6},{5,7},{6,4},{7,5},{8,10},{9,11},{10,... | collective-permute-start | bytes 884744 | tf_op jit(solution)/shard_map/ppermute | solution.py:514
  1.9 8.0 %collective-permute-start.1 = (f32[2,96,384]{2,1,0:T(8,128)}, f32[2,96,384]{2,1,0:T(8,128)S(1)}, u32[]{:S(2)}, u32[]{:S(2)}) collective-permute-start(f32[2,96,384]{2,1,0:T(8,128)} %refs_4_), channel_id=1, source_target_pairs={{0,4},{4,0},{8,12},{12,8},{16,20},{20,16},{24,28},{28,24},{1,5},{5... | collective-permute-start | bytes 884744 | tf_op jit(solution)/shard_map/ppermute | solution.py:514
  5.3 5.0 %copy-start.3 = (f32[96,384]{1,0:T(8,128)S(1)}, f32[96,384]{1,0:T(8,128)}, u32[]{:S(2)}) copy-start(f32[96,384]{1,0:T(8,128)} %get-tuple-element.58.refs_0_) | copy-start | bytes 442372
  5.3 9.3 %copy-start.2 = (f32[2,96,384]{2,1,0:T(8,128)S(1)}, f32[2,96,384]{2,1,0:T(8,128)}, u32[]{:S(2)}) copy-start(f32[2,96,384]{2,1,0:T(8,128)} %refs_4_) | copy-start | bytes 884740
  5.3 7.3 %collective-permute-start.4 = (f32[96,384]{1,0:T(8,128)}, f32[96,384]{1,0:T(8,128)S(1)}, u32[]{:S(2)}, u32[]{:S(2)}) collective-permute-start(f32[96,384]{1,0:T(8,128)} %get-tuple-element.58.refs_0_), channel_id=1, source_target_pairs={{0,2},{1,3},{2,0},{3,1},{4,6},{5,7},{6,4},{7,5},{8,10},{9,11},{10,... | collective-permute-start | bytes 442376 | tf_op jit(solution)/shard_map/ppermute | solution.py:514
  5.7 4.3 %collective-permute-start.2 = (f32[2,4,384]{2,1,0:T(4,128)}, f32[2,4,384]{2,1,0:T(4,128)S(1)}, u32[]{:S(2)}, u32[]{:S(2)}) collective-permute-start(f32[2,4,384]{2,1,0:T(4,128)} %get-tuple-element.52.vec_ref), channel_id=1, source_target_pairs={{0,4},{4,0},{8,12},{12,8},{16,20},{20,16},{24,28},{28,24},{1,5},{5... | collective-permute-start | bytes 36872 | tf_op jit(solution)/shard_map/ppermute | solution.py:514
  6.9 9.0 %copy-start.4 = (f32[2,4,384]{2,1,0:T(4,128)S(1)}, f32[2,4,384]{2,1,0:T(4,128)}, u32[]{:S(2)}) copy-start(f32[2,4,384]{2,1,0:T(4,128)} %get-tuple-element.52.vec_ref) | copy-start | bytes 36868
  10.0 8.4 %collective-permute-start.3 = (f32[2,96,384]{2,1,0:T(8,128)S(1)}, f32[2,96,384]{2,1,0:T(8,128)S(1)}, u32[]{:S(2)}, u32[]{:S(2)}) collective-permute-start(f32[2,96,384]{2,1,0:T(8,128)S(1)} %collective-permute-done.refs_5_), channel_id=1, source_target_pairs={{0,4},{4,0},{8,12},{12,8},{16,20},{20,16},{24,28},{28,24},{1,5},{5... | collective-permute-start | bytes 884744 | tf_op jit(solution)/shard_map/ppermute | solution.py:514
  10.2 3.3 %collective-permute-start.5 = (f32[96,384]{1,0:T(8,128)S(1)}, f32[96,384]{1,0:T(8,128)S(1)}, u32[]{:S(2)}, u32[]{:S(2)}) collective-permute-start(f32[96,384]{1,0:T(8,128)S(1)} %copy-done.3), channel_id=1, source_target_pairs={{0,1},{1,0},{2,3},{3,2},{4,5},{5,4},{6,7},{7,6},{8,9},{9,8},{10,11... | collective-permute-start | bytes 442376 | tf_op jit(solution)/shard_map/ppermute | solution.py:514
  12.6 2.0 %collective-permute-start.6 = (f32[96,384]{1,0:T(8,128)S(1)}, f32[96,384]{1,0:T(8,128)S(1)}, u32[]{:S(2)}, u32[]{:S(2)}) collective-permute-start(f32[96,384]{1,0:T(8,128)S(1)} %collective-permute-done.4.refs_1_), channel_id=1, source_target_pairs={{0,1},{1,0},{2,3},{3,2},{4,5},{5,4},{6,7},{7,6},{8,9},{9,8},{10,11... | collective-permute-start | bytes 442376 | tf_op jit(solution)/shard_map/ppermute | solution.py:514
  15.4 4.8 %collective-permute-start.7 = (f32[2,192,384]{2,1,0:T(8,128)S(1)}, f32[2,192,384]{2,1,0:T(8,128)S(1)}, u32[]{:S(2)}, u32[]{:S(2)}) collective-permute-start(f32[2,192,384]{2,1,0:T(8,128)S(1)} %get-tuple-element.66.mine_ref), channel_id=1, source_target_pairs={{0,1},{1,0},{2,3},{3,2},{4,5},{5,4},{6,7},{7,6},{8,9},{9,8},{10,11... | collective-permute-start | bytes 1769480 | tf_op jit(solution)/shard_map/ppermute | solution.py:514
  18.3 1.8 %copy-start.6 = (f32[384]{0:T(512)S(1)}, f32[384]{0:T(512)}, u32[]{:S(2)}) copy-start(f32[384]{0:T(512)} %param.18) | copy-start | bytes 4612
  19.0 3.3 %collective-permute-start.8 = (f32[2,192,384]{2,1,0:T(8,128)S(1)}, f32[2,192,384]{2,1,0:T(8,128)S(1)}, u32[]{:S(2)}, u32[]{:S(2)}) collective-permute-start(f32[2,192,384]{2,1,0:T(8,128)S(1)} %other_rows.1.mine_ref), channel_id=1, source_target_pairs={{0,1},{1,0},{2,3},{3,2},{4,5},{5,4},{6,7},{7,6},{8,9},{9,8},{10,11... | collective-permute-start | bytes 1769480 | tf_op jit(solution)/shard_map/ppermute | solution.py:514
  26.1 6.2 %collective-permute-start.9 = (f32[392,128]{1,0:T(8,128)S(1)}, f32[392,128]{1,0:T(8,128)S(1)}, u32[]{:S(2)}, u32[]{:S(2)}) collective-permute-start(f32[392,128]{1,0:T(8,128)S(1)} %get-tuple-element.82.total_ref), channel_id=1, source_target_pairs={{0,8},{1,9},{2,10},{3,11},{4,12},{5,13},{6,14},{7,15},{8,0},{9,1},... | collective-permute-start | bytes 602120 | tf_op jit(solution)/shard_map/ppermute | solution.py:527
  32.4 2.3 %collective-permute-start.10 = (f32[392,128]{1,0:T(8,128)S(1)}, f32[392,128]{1,0:T(8,128)S(1)}, u32[]{:S(2)}, u32[]{:S(2)}) collective-permute-start(f32[392,128]{1,0:T(8,128)S(1)} %collective-permute-done.9.refs_0_), channel_id=1, source_target_pairs={{0,1},{1,0},{2,3},{3,2},{4,5},{5,4},{6,7},{7,6},{8,9},{9,8},{10,11... | collective-permute-start | bytes 602120 | tf_op jit(solution)/shard_map/ppermute | solution.py:514
  33.6 12.9 %collective-permute-start.13 = (f32[192,384]{1,0:T(8,128)S(1)}, f32[192,384]{1,0:T(8,128)S(1)}, u32[]{:S(2)}, u32[]{:S(2)}) collective-permute-start(f32[192,384]{1,0:T(8,128)S(1)} %get-tuple-element.94), channel_id=1, source_target_pairs={{0,2},{1,3},{2,0},{3,1},{4,6},{5,7},{6,4},{7,5},{8,10},{9,11},{10,... | collective-permute-start | bytes 884744 | tf_op jit(solution)/shard_map/ppermute | solution.py:527
  35.5 11.0 %collective-permute-start.11 = (f32[392,128]{1,0:T(8,128)S(1)}, f32[392,128]{1,0:T(8,128)S(1)}, u32[]{:S(2)}, u32[]{:S(2)}) collective-permute-start(f32[392,128]{1,0:T(8,128)S(1)} %joined_covariance.1), channel_id=1, source_target_pairs={{0,2},{1,3},{2,0},{3,1},{4,6},{5,7},{6,4},{7,5},{8,16},{9,17},{10,... | collective-permute-start | bytes 602120 | tf_op jit(solution)/shard_map/ppermute | solution.py:527
  35.9 10.7 %collective-permute-start.12 = (f32[392,128]{1,0:T(8,128)S(1)}, f32[392,128]{1,0:T(8,128)S(1)}, u32[]{:S(2)}, u32[]{:S(2)}) collective-permute-start(f32[392,128]{1,0:T(8,128)S(1)} %joined_covariance.1), channel_id=1, source_target_pairs={{0,4},{1,5},{2,6},{3,7},{4,0},{5,1},{6,2},{7,3},{8,24},{9,25},{10,... | collective-permute-start | bytes 602120 | tf_op jit(solution)/shard_map/ppermute | solution.py:527
  46.6 2.6 %collective-permute-start.14 = (f32[192,384]{1,0:T(8,128)S(1)}, f32[192,384]{1,0:T(8,128)S(1)}, u32[]{:S(2)}, u32[]{:S(2)}) collective-permute-start(f32[192,384]{1,0:T(8,128)S(1)} %collective-permute-done.13.refs_0_), channel_id=1, source_target_pairs={{0,1},{1,0},{2,3},{3,2},{4,5},{5,4},{6,7},{7,6},{8,9},{9,8},{10,11... | collective-permute-start | bytes 884744 | tf_op jit(solution)/shard_map/ppermute | solution.py:514
  47.3 1.5 %collective-permute-start.15 = (f32[392,128]{1,0:T(8,128)S(1)}, f32[392,128]{1,0:T(8,128)S(1)}, u32[]{:S(2)}, u32[]{:S(2)}) collective-permute-start(f32[392,128]{1,0:T(8,128)S(1)} %collective-permute-done.11.refs_2_), channel_id=1, source_target_pairs={{0,1},{1,0},{2,3},{3,2},{4,5},{5,4},{6,7},{7,6},{8,9},{9,8},{10,11... | collective-permute-start | bytes 602120 | tf_op jit(solution)/shard_map/ppermute | solution.py:514
  47.4 1.7 %collective-permute-start.16 = (f32[392,128]{1,0:T(8,128)S(1)}, f32[392,128]{1,0:T(8,128)S(1)}, u32[]{:S(2)}, u32[]{:S(2)}) collective-permute-start(f32[392,128]{1,0:T(8,128)S(1)} %collective-permute-done.12.refs_3_), channel_id=1, source_target_pairs={{0,1},{1,0},{2,3},{3,2},{4,5},{5,4},{6,7},{7,6},{8,9},{9,8},{10,11... | collective-permute-start | bytes 602120 | tf_op jit(solution)/shard_map/ppermute | solution.py:514

commit v6 on v5

--- a/solution.py
+++ b/solution.py
@@ -237,49 +237,92 @@
             psi_half_ref[...] = dot_nn(psi_other_ref[mine, :], psi_ref[steps - 1])
 
 
-def put_packed(step_ref, covar, mean, blocks, out_ref):
+def share_rows(edge):
+    return 2 * edge + edge * 3 // 8 + 8
+
+
+def masks(edge):
+    rows = lax.broadcasted_iota(jnp.int32, (edge, edge), 0)
+    cols = lax.broadcasted_iota(jnp.int32, (edge, edge), 1)
+    return rows > cols, rows == cols
+
+
+def put_packed(step_ref, covar, mean, added, out_ref):
     states = covar.shape[0]
     edge = states // 3
+    half, part = edge // 2, edge * 3 // 8
     core = lax.rem(lax.axis_index("col"), 2)
+    whole = added if callable(added) else lambda rows, cols: 0.0
+    share = (lambda rows: 0.0) if callable(added) else (lambda rows: added[rows, :])
+
+    def put(start, block):
+        rows = slice(start, start + block.shape[0])
+        out_ref[rows, :] = block + share(rows)
+        return rows.stop
 
     @pl.when(core == 0)
     def _():
-        rows = step_ref[: 2 * edge, :]
-        low = dot_nt(dot_nn(rows, covar), rows)
-        out_ref[:edge, :] = low[:edge, :edge] + blocks(0, 0)
-        out_ref[edge : 2 * edge, :] = low[edge:, :edge] + blocks(1, 0)
-        out_ref[2 * edge : 3 * edge, :] = low[edge:, edge:] + blocks(1, 1)
-        out_ref[3 * edge :, :] = jnp.zeros((8, edge), F32)
+        rows = step_ref[: 2 * edge + part, :]
+        low = dot_nt(dot_nn(rows, covar), rows[: 2 * edge])
+        first, second = slice(0, edge), slice(edge, 2 * edge)
+        last = slice(2 * edge, 2 * edge + part)
+        below, on = masks(edge)
+        corner = low[edge : 2 * edge, edge:] + whole(second, second)
+        at = put(0, low[edge : 2 * edge, :edge] + whole(second, first))
+        at = put(at, jnp.where(below | on, low[:edge, :edge] + whole(first, first), corner))
+        at = put(at, low[2 * edge :, :edge] + whole(last, first))
+        at = put(at, jnp.broadcast_to(jnp.sum(jnp.where(on, corner, 0.0), axis=0, keepdims=True), (8, edge)))
 
     @pl.when(core == 1)
     def _():
         rows = step_ref[2 * edge :, :]
         both = dot_nt(jnp.concatenate([dot_nn(rows, covar), mean], axis=0), step_ref[...])
-        out_ref[3 * edge :, :] = jnp.zeros((8, edge), F32)
-        for j in range(3):
-            at = slice(j * edge, (j + 1) * edge)
-            out_ref[at, :] = both[:edge, at] + blocks(2, j)
-            out_ref[3 * edge + j : 3 * edge + j + 1, :] = both[edge : edge + 1, at] + blocks(3, j)
+        last, low = slice(2 * edge, states), both[:edge]
+        row = both[edge : edge + 1]
+        if callable(added):
+            low = low + added(last, slice(0, states))
+            row = row + added(None, slice(0, states))
+        corner = low[:, 2 * edge :]
+        at = put(0, low[part:, :edge])
+        at = put(at, low[:, edge : 2 * edge])
+        at = put(at, corner[half:])
+        at = put(at, jnp.concatenate([corner[: half // 2, :half], corner[half // 2 : half, :half]], axis=1))
+        rows = [row[:, j * edge : (j + 1) * edge] for j in range(3)]
+        put(at, jnp.concatenate(rows + [jnp.zeros((5, edge), F32)], axis=0))
 
 
 def unpacked(mine_ref, mate_ref, covar_ref):
     states = covar_ref.shape[0]
     edge = states // 3
+    half, part = edge // 2, edge * 3 // 8
     is_low = lax.rem(lax.axis_index("col"), 2) == 0
     low = jnp.where(is_low, mine_ref[...], mate_ref[...])
     high = jnp.where(is_low, mate_ref[...], mine_ref[...])
+    below, on = masks(edge)
 
     def put(i, j, block):
         covar_ref[i * edge : (i + 1) * edge, j * edge : (j + 1) * edge] = block
         if i != j:
             covar_ref[j * edge : (j + 1) * edge, i * edge : (i + 1) * edge] = block.T
 
-    put(0, 0, low[:edge])
-    put(1, 0, low[edge : 2 * edge])
-    put(1, 1, low[2 * edge : 3 * edge])
-    for j in range(3):
-        put(2, j, high[j * edge : (j + 1) * edge])
-    row = jnp.concatenate([high[3 * edge + j : 3 * edge + j + 1] for j in range(3)], axis=1)
+    put(1, 0, low[:edge])
+    mixed = low[edge : 2 * edge]
+    turned = mixed.T
+    put(0, 0, jnp.where(below | on, mixed, turned))
+    diagonal = low[2 * edge + part : 2 * edge + part + 1]
+    put(1, 1, jnp.where(on, diagonal, jnp.where(below, turned, mixed)))
+    at = edge - part
+    put(2, 0, jnp.concatenate([low[2 * edge : 2 * edge + part], high[:at]], axis=0))
+    put(2, 1, high[at : at + edge])
+    at += edge
+    bottom = high[at : at + half]
+    at += half
+    folded = high[at : at + half // 2]
+    at += half // 2
+    quarter = jnp.concatenate([folded[:, :half], folded[:, half:]], axis=0)
+    top = jnp.concatenate([quarter, bottom[:, :half].T], axis=1)
+    put(2, 2, jnp.concatenate([top, bottom], axis=0))
+    row = jnp.concatenate([high[at + j : at + j + 1] for j in range(3)], axis=1)
     return mean_block(row, states)
 
 
@@ -310,14 +353,12 @@
         covar_other_ref[...] = covar + noise_other_ref[at]
         mean_other_ref[...] = mean + offset_other_ref[at]
 
-    def blocks(i, j):
-        at = slice(j * edge, (j + 1) * edge)
-        if i == 3:
-            return jnp.where(is_second, mean_ref[last, :1, at], offset_other_ref[last, :1, at])
-        rows = slice(i * edge, (i + 1) * edge)
-        return jnp.where(is_second, covar_ref[last, rows, at], noise_other_ref[last, rows, at])
-
-    put_packed(step_ref, covar_other_ref[...], mean_other_ref[...], blocks, out_ref)
+    def added(rows, cols):
+        if rows is None:
+            return jnp.where(is_second, mean_ref[last, :1, cols], offset_other_ref[last, :1, cols])
+        return jnp.where(is_second, covar_ref[last, rows, cols], noise_other_ref[last, rows, cols])
+
+    put_packed(step_ref, covar_other_ref[...], mean_other_ref[...], added, out_ref)
 
 
 def pair_elements(steps, width, psi_ref, covar_ref, mean_ref, psi_other_ref, covar_other_ref, mean_other_ref, *refs):
@@ -367,19 +408,8 @@
             mean_out_ref[k] = mean_ref[k]
 
 
-def packed_blocks(ref, edge):
-    def blocks(i, j):
-        if i == 3:
-            return ref[3 * edge + j : 3 * edge + j + 1, :]
-        at = (i + j) if i < 2 else j
-        return ref[at * edge : (at + 1) * edge, :]
-
-    return blocks
-
-
-def whole_matrix(mine_ref, mate_ref):
+def whole_matrix(mine, mate):
     is_low = lax.rem(lax.axis_index("col"), 2) == 0
-    mine, mate = mine_ref[...], mate_ref[...]
     return jnp.concatenate([jnp.where(is_low, mine, mate), jnp.where(is_low, mate, mine)], axis=0)
 
 
@@ -404,20 +434,24 @@
     mines, mates = refs[:n_group], refs[n_group : 2 * n_group]
     out_ref, mine_ref, mate_ref, work_ref = refs[2 * n_group :]
 
-    @pl.when(lax.rem(lax.axis_index("seg"), 2 * bit) >= 2 * bit - 2)
+    at = lax.rem(lax.axis_index("seg"), 4 * bit)
+
+    @pl.when((at >= 2 * bit - 2) & (at < 2 * bit))
     def _():
         mine_ref[...] = chosen(mines, bit)
         mate_ref[...] = chosen(mates, bit)
         mean = unpacked(mine_ref, mate_ref, work_ref)
-        put_packed(psi_ref, work_ref[...], mean, packed_blocks(total_ref, out_ref.shape[1]), out_ref)
+        put_packed(psi_ref, work_ref[...], mean, total_ref, out_ref)
+
+
+def chosen_matrix(refs, bit):
+    n_group = bit // 2
+    mine, *mate = [chosen(refs[i * n_group : (i + 1) * n_group], bit) for i in range(3)]
+    return whole_matrix(mine, jnp.concatenate(mate, axis=0))
 
 
 def joined_matrix(bit, psi_ref, *refs):
-    n_group = bit // 2
-    psi_ref_out, mine_ref, mate_ref = refs[2 * n_group :]
-    mine_ref[...] = chosen(refs[:n_group], bit)
-    mate_ref[...] = chosen(refs[n_group : 2 * n_group], bit)
-    psi_ref_out[...] = dot_nn(psi_ref[...], whole_matrix(mine_ref, mate_ref))
+    refs[-1][...] = dot_nn(psi_ref[...], chosen_matrix(refs[:-1], bit))
 
 
 def entered(bit, psi_ref, covar_ref, mean_ref, *refs):
@@ -450,24 +484,23 @@
 
 
 def matrices_entered(bit, psi_ref, *refs):
-    n_group = bit // 2
-    psi_out_ref, mine_ref, mate_ref = refs[2 * n_group :]
-    psi_out_ref[...] = psi_ref[...]
+    psi_out_ref = refs[-1]
 
     @pl.when(takes_matrix(bit))
     def _():
-        mine_ref[...] = chosen(refs[:n_group], bit)
-        mate_ref[...] = chosen(refs[n_group : 2 * n_group], bit)
-        before = whole_matrix(mine_ref, mate_ref)
+        before = chosen_matrix(refs[:-1], bit)
         for k in range(psi_ref.shape[0]):
             psi_out_ref[k] = dot_nn(psi_ref[k], before)
 
-
-def finished(bit, n_step, psi_ref, covar_ref, mean_ref, *refs):
+    @pl.when(jnp.logical_not(takes_matrix(bit)))
+    def _():
+        psi_out_ref[...] = psi_ref[...]
+
+
+def finished(bit, psi_ref, covar_ref, mean_ref, *refs):
     n_group = bit // 2
-    step_refs, refs = refs[: 2 * n_step], refs[2 * n_step :]
     mines, mates = refs[:n_group], refs[n_group : 2 * n_group]
-    covar_out_ref, mean_out_ref, mine_ref, mate_ref, work_ref, half_ref, other_half_ref, rows_ref, enter_ref = refs[2 * n_group :]
+    covar_out_ref, mean_out_ref, mine_ref, mate_ref, work_ref = refs[2 * n_group :]
     steps, width, states = covar_ref.shape
     mine = pl.ds(pl.multiple_of(lax.axis_index("col") * width, 8), width)
 
@@ -476,30 +509,11 @@
         mine_ref[...] = chosen(mines, bit)
         mate_ref[...] = chosen(mates, bit)
         mean = unpacked(mine_ref, mate_ref, work_ref)
+        rows = jnp.concatenate([psi_ref[k, mine, :] for k in range(steps)], axis=0)
+        half = dot_nn(rows, work_ref[...])
         for k in range(steps):
-            rows_ref[k * width : (k + 1) * width, :] = psi_ref[k, mine, :]
-        n_row = steps * width
-
-        def through(rows):
-            return jnp.concatenate([dot_nn(rows, work_ref[...]), mean], axis=0)
-
-        if n_step:
-
-            @pl.when(takes_matrix(bit // 2))
-            def _():
-                half_ref[...] = chosen(step_refs[:n_step], bit // 2)
-                other_half_ref[...] = chosen(step_refs[n_step:], bit // 2)
-                before = whole_matrix(half_ref, other_half_ref)
-                enter_ref[...] = dot_nt(through(dot_nn(rows_ref[...], before)), before)
-
-            @pl.when(jnp.logical_not(takes_matrix(bit // 2)))
-            def _():
-                enter_ref[...] = through(rows_ref[...])
-        else:
-            enter_ref[...] = through(rows_ref[...])
-        for k in range(steps):
-            part = jnp.concatenate([enter_ref[k * width : (k + 1) * width, :], enter_ref[n_row:, :]], axis=0)
-            both = dot_nt(part, psi_ref[k])
+            part = half[k * width : (k + 1) * width]
+            both = dot_nt(jnp.concatenate([part, mean], axis=0), psi_ref[k])
             covar_out_ref[k] = both[:width] + covar_ref[k]
             mean_out_ref[k : k + 1, :] = both[width : width + 1] + mean_ref[k, :1, :]
 
@@ -549,7 +563,7 @@
     col = lax.axis_index("col")
     edge = states // 3
     square_shape, mean_shape = (states, states), (MEAN_ROWS, states)
-    share_shape, half_shape = (3 * edge + 8, edge), (states // 2, states)
+    share_shape, half_shape = (share_rows(edge), edge), (states // 2, states)
     far_bits = []
     bit = n_col // 2
     while bit > 1:
@@ -670,6 +684,7 @@
             scratch=[share_shape, share_shape, square_shape],
         )
         came_next = handed_up(total, 2 * bit)
+        covar, total = lax.optimization_barrier((covar, total))
         covar, mean = local_call(
             functools.partial(entered, bit),
             [(steps, width, states), (steps,) + mean_shape],
@@ -679,33 +694,28 @@
             *came,
             scratch=[share_shape, share_shape, square_shape],
         )
+        step, covar = lax.optimization_barrier((step, covar))
+        for part in (slice(0, states // 4), slice(states // 4, states // 2)):
+            step = step + [swapped(b[part], "col", 1) for b in step[: bit // 2]]
         if more:
-            step = over_core(step)
-            (psi,) = local_call(
-                functools.partial(matrices_entered, bit),
-                [(steps,) + square_shape],
-                psi,
-                *step,
-                scratch=[half_shape, half_shape],
-            )
-            (psi_all,) = local_call(
-                functools.partial(joined_matrix, bit), [square_shape], psi_all, *step, scratch=[half_shape, half_shape]
-            )
+            (psi_all,) = local_call(functools.partial(joined_matrix, bit), [square_shape], psi_all, *step)
             psi_half = lax.dynamic_slice_in_dim(psi_all, col % 2 * (states // 2), states // 2, 0)
+        (psi,) = local_call(
+            functools.partial(matrices_entered, bit), [(steps,) + square_shape], psi, *step
+        )
+        if more:
             step = handed_up(psi_half, 2 * bit, 1)
         came = came_next
         bit *= 2
-    came, covar, step = lax.optimization_barrier((came, covar, step))
+    came, covar, psi = lax.optimization_barrier((came, covar, psi))
     covars, means = local_call(
-        functools.partial(finished, bit, len(step)),
+        functools.partial(finished, bit),
         [(steps, width, states), (steps, states)],
         psi,
         covar,
         mean,
-        *over_core(step),
         *over_core(came),
-        scratch=[share_shape, share_shape, square_shape, half_shape, half_shape]
-        + [(steps * width, states), (steps * width + MEAN_ROWS, states)],
+        scratch=[share_shape, share_shape, square_shape],
     )
     return means, covars
 

time: 52.1 us -> 48 us (0.921)
  waiting for transfers between devices: 17.5 us -> 9.66 us
  starting transfers between devices: 11.8 us -> 16 us
    ppermute x4, waiting for transfers between devices: 12.5 us -> 3.23 us  [handed_up(): came.append(lax.ppermute(block, ('seg', 'col'), sorted(to.items())))]
    ppermute x13 -> x14, starting transfers between devices: 10.7 us -> 13.1 us  [swapped(): lax.ppermute(block, axis, [(i, i ^ bit) for i in range(lax.axis_size(axis...]
    ppermute x4, starting transfers between devices: 1.13 us -> 2.88 us  [handed_up(): came.append(lax.ppermute(block, ('seg', 'col'), sorted(to.items())))]
    ppermute x13 -> x14, waiting for transfers between devices: 4.91 us -> 6.43 us  [swapped(): lax.ppermute(block, axis, [(i, i ^ bit) for i in range(lax.axis_size(axis...]
    pallas_call x13 -> x14, Pallas kernels: 21.8 us -> 21.3 us  [local_call(): pl.pallas_call(body, out_shape=shapes, name=getattr(body, 'func', body)._...]
  transfers between devices with their start and end apart: 17 -> 18, of which waited for: 7 -> 10; matrix products, arithmetic and copies ran while one was open for 0% -> 0% of each run, Pallas kernels for 29% -> 33%
where the time goes in v6:
time: 48 us; the launch traced here: 47.8 us
  Pallas kernels  21.3 us (44%)
  starting transfers between devices  16 us (33%)
  waiting for transfers between devices  9.66 us (20%)
  between operations  0.82 us (2%)
    pallas_call x14, Pallas kernels, local_call(): pl.pallas_call(body, out_shape=shapes, name=getattr(body, 'func', body)._...  21.3 us
    ppermute x14, starting transfers between devices, swapped(): lax.ppermute(block, axis, [(i, i ^ bit) for i in range(lax.axis_size(axis...  13.1 us
    ppermute x14, waiting for transfers between devices, swapped(): lax.ppermute(block, axis, [(i, i ^ bit) for i in range(lax.axis_size(axis...  6.43 us
    ppermute x4, waiting for transfers between devices, handed_up(): came.append(lax.ppermute(block, ('seg', 'col'), sorted(to.items())))  3.23 us
    ppermute x4, starting transfers between devices, handed_up(): came.append(lax.ppermute(block, ('seg', 'col'), sorted(to.items())))  2.88 us
  transfers between devices with their start and end apart: 18, of which 10 were waited for; matrix products, arithmetic and copies ran while one was open for 0% of the time, Pallas kernels for 33%

profile of v6, /device:TPU:29, one launch (start us, length us, event | category | flops | bytes accessed | tf_op | source)
XLA Modules:
  0.0 47.8 jit_solution(7663680057135579076)
XLA Ops:
  0.7 1.3 %collective-permute-start = (f32[2,96,384]{2,1,0:T(8,128)}, f32[2,96,384]{2,1,0:T(8,128)S(1)}, u32[]{:S(2)}, u32[]{:S(2)}) collective-permute-start(f32[2,96,384]{2,1,0:T(8,128)} %refs_4_), channel_id=1, source_target_pairs={{0,2},{1,3},{2,0},{3,1},{4,6},{5,7},{6,4},{7,5},{8,10},{9,11},{10,... | collective-permute-start | bytes 884744 | tf_op jit(solution)/shard_map/ppermute | solution.py:528
  2.2 3.1 %correction_rows.1 = (f32[96,384]{1,0:T(8,128)}, f32[2,4,384]{2,1,0:T(4,128)}) custom-call(f32[384,1024]{1,0:T(8,128)} %gain_ref, f32[96,1024]{1,0:T(8,128)} %oper_hbm.1, f32[2,1024]{1,0:T(2,128)} %seen_hbm.1, f32[2,384]{1,0:T(2,128)} %keep_hbm.1, f32[2,384]{1,0:T(2,128)} %push_hbm.1, f32[2,384]{1,0:T(2,128)} %var_hbm.1), custom_call_target="tpu_custom_call" | custom-call | flops 2100000000 | bytes 4096 | tf_op jit(solution)/shard_map/correction_rows/pallas_call | solution.py:53
  5.7 1.2 %collective-permute-start.2 = (f32[2,4,384]{2,1,0:T(4,128)}, f32[2,4,384]{2,1,0:T(4,128)S(1)}, u32[]{:S(2)}, u32[]{:S(2)}) collective-permute-start(f32[2,4,384]{2,1,0:T(4,128)} %get-tuple-element.55.vec_ref), channel_id=1, source_target_pairs={{0,4},{4,0},{8,12},{12,8},{16,20},{20,16},{24,28},{28,24},{1,5},{5... | collective-permute-start | bytes 36872 | tf_op jit(solution)/shard_map/ppermute | solution.py:528
  6.9 1.4 %fixed_parts.1 = (f32[384,384]{1,0:T(8,128)S(1)}, f32[384,384]{1,0:T(8,128)S(1)}) custom-call(f32[384,1024]{1,0:T(8,128)S(1)} %copy-done, f32[1,1024]{1,0:T(1,128)S(1)} %bitcast.1, f32[384,384]{1,0:T(8,128)S(1)} %copy-done.1), custom_call_target="tpu_custom_call" | custom-call | bytes 4096 | tf_op jit(solution)/shard_map/fixed_parts/pallas_call | solution.py:53
  8.3 1.7 %collective-permute-done.2.vec_ref = f32[2,4,384]{2,1,0:T(4,128)S(1)} collective-permute-done((f32[2,4,384]{2,1,0:T(4,128)}, f32[2,4,384]{2,1,0:T(4,128)S(1)}, u32[]{:S(2)}, u32[]{:S(2)}) %collective-permute-start.2) | collective-permute-done | bytes 12320 | tf_op jit(solution)/shard_map/ppermute | solution.py:528
  10.2 2.3 %collective-permute-start.5 = (f32[96,384]{1,0:T(8,128)S(1)}, f32[96,384]{1,0:T(8,128)S(1)}, u32[]{:S(2)}, u32[]{:S(2)}) collective-permute-start(f32[96,384]{1,0:T(8,128)S(1)} %copy-done.3), channel_id=1, source_target_pairs={{0,1},{1,0},{2,3},{3,2},{4,5},{5,4},{6,7},{7,6},{8,9},{9,8},{10,11... | collective-permute-start | bytes 442376 | tf_op jit(solution)/shard_map/ppermute | solution.py:528
  12.6 1.0 %collective-permute-start.6 = (f32[96,384]{1,0:T(8,128)S(1)}, f32[96,384]{1,0:T(8,128)S(1)}, u32[]{:S(2)}, u32[]{:S(2)}) collective-permute-start(f32[96,384]{1,0:T(8,128)S(1)} %collective-permute-done.4.refs_1_), channel_id=1, source_target_pairs={{0,1},{1,0},{2,3},{3,2},{4,5},{5,4},{6,7},{7,6},{8,9},{9,8},{10,11... | collective-permute-start | bytes 442376 | tf_op jit(solution)/shard_map/ppermute | solution.py:528
  13.6 1.0 %collective-permute-done.6.refs_3_ = f32[96,384]{1,0:T(8,128)S(1)} collective-permute-done((f32[96,384]{1,0:T(8,128)S(1)}, f32[96,384]{1,0:T(8,128)S(1)}, u32[]{:S(2)}, u32[]{:S(2)}) %collective-permute-start.6) | collective-permute-done | bytes 147488 | tf_op jit(solution)/shard_map/ppermute | solution.py:528
  14.5 0.8 %own_rows.1 = (f32[384,384]{1,0:T(8,128)S(1)}, f32[2,192,384]{2,1,0:T(8,128)S(1)}) custom-call(f32[96,384]{1,0:T(8,128)S(1)} %copy-done.3, f32[96,384]{1,0:T(8,128)S(1)} %collective-permute-done.4.refs_1_, f32[96,384]{1,0:T(8,128)S(1)} %collective-permute-done.5.refs_2_, f32[96,384]{1,0:T(8,128)S(1)} %collective-permute-done.6.refs_3_, ...), custom_call_target="tpu_custom_call" | custom-call | bytes 4096 | tf_op jit(solution)/shard_map/own_rows/pallas_call | solution.py:53
  15.4 0.4 collective-permute-start.7
  15.8 1.3 %noises.2 = (f32[2,384,384]{2,1,0:T(8,128)S(1)}, f32[2,16,384]{2,1,0:T(8,128)S(1)}) custom-call(f32[2,4,384]{2,1,0:T(4,128)S(1)} %copy-done.4, f32[384,384]{1,0:T(8,128)S(1)} %get-tuple-element.64.fixed_ref, f32[384,384]{1,0:T(8,128)S(1)} %get-tuple-element.68.corr_ref), custom_call_target="tpu_custom_call" | custom-call | bytes 4096 | tf_op jit(solution)/shard_map/noises/pallas_call | solution.py:53
  17.1 1.3 %noises.3 = (f32[2,384,384]{2,1,0:T(8,128)S(1)}, f32[2,16,384]{2,1,0:T(8,128)S(1)}) custom-call(f32[2,4,384]{2,1,0:T(4,128)S(1)} %collective-permute-done.2.vec_ref, f32[384,384]{1,0:T(8,128)S(1)} %get-tuple-element.64.fixed_ref, f32[384,384]{1,0:T(8,128)S(1)} %get-tuple-element.68.corr_ref), custom_call_target="tpu_custom_call" | custom-call | bytes 4096 | tf_op jit(solution)/shard_map/noises/pallas_call | solution.py:53
  18.4 0.7 %other_rows.1.mine_ref = f32[2,192,384]{2,1,0:T(8,128)S(1)} custom-call(f32[384,384]{1,0:T(8,128)S(1)} %get-tuple-element.68.corr_ref, f32[2,96,384]{2,1,0:T(8,128)S(1)} %collective-permute-done.1.refs_0_, f32[2,96,384]{2,1,0:T(8,128)S(1)} %collective-permute-done.3.refs_1_), custom_call_target="tpu_custom_call" | custom-call | bytes 4096 | tf_op jit(solution)/shard_map/other_rows/pallas_call | solution.py:53
  19.0 1.1 %collective-permute-start.8 = (f32[2,192,384]{2,1,0:T(8,128)S(1)}, f32[2,192,384]{2,1,0:T(8,128)S(1)}, u32[]{:S(2)}, u32[]{:S(2)}) collective-permute-start(f32[2,192,384]{2,1,0:T(8,128)S(1)} %other_rows.1.mine_ref), channel_id=1, source_target_pairs={{0,1},{1,0},{2,3},{3,2},{4,5},{5,4},{6,7},{7,6},{8,9},{9,8},{10,11... | collective-permute-start | bytes 1769480 | tf_op jit(solution)/shard_map/ppermute | solution.py:528
  20.2 2.2 %own_segment.1 = (f32[2,384,384]{2,1,0:T(8,128)}, f32[2,384,384]{2,1,0:T(8,128)S(1)}, f32[2,384,384]{2,1,0:T(8,128)S(1)}, f32[2,16,384]{2,1,0:T(8,128)S(1)}) custom-call(f32[2,4,384]{2,1,0:T(4,128)S(1)} %copy-done.4, f32[384,384]{1,0:T(8,128)S(1)} %get-tuple-element.68.corr_ref, f32[2,192,384]{2,1,0:T(8,128)S(1)} %get-tuple-element.69.mine_ref, ...), custom_call_target="tpu_custom_call" | custom-call | flops 700000000 | bytes 4096 | tf_op jit(solution)/shard_map/own_segment/pallas_call | solution.py:53
  22.4 1.7 %other_matrices.1 = (f32[2,384,384]{2,1,0:T(8,128)S(1)}, f32[384,384]{1,0:T(8,128)S(1)}, f32[192,384]{1,0:T(8,128)S(1)}, f32[384,384]{1,0:T(8,128)S(1)}, f32[16,384]{1,0:T(8,128)S(1)}) custom-call(f32[2,4,384]{2,1,0:T(4,128)S(1)} %collective-permute-done.2.vec_ref, f32[384,384]{1,0:T(8,128)S(1)} %get-tuple-element.68.corr_ref, ...), custom_call_target="tpu_custom_call" | custom-call | bytes 4096 | tf_op jit(solution)/shard_map/other_matrices/pallas_call | solution.py:53
  24.0 2.1 %pair_covariance.1 = (f32[384,384]{1,0:T(8,128)S(1)}, f32[16,384]{1,0:T(8,128)S(1)}, f32[312,128]{1,0:T(8,128)S(1)}) custom-call(f32[2,384,384]{2,1,0:T(8,128)S(1)} %get-tuple-element.73.psi_ref, f32[2,384,384]{2,1,0:T(8,128)S(1)} %get-tuple-element.74.covar_ref, f32[2,16,384]{2,1,0:T(8,128)S(1)} %get-tuple-element.75.mean_ref, ...), custom_call_target="tpu_custom_call" | custom-call | bytes 4096 | tf_op jit(solution)/shard_map/pair_covariance/pallas_call | solution.py:53
  26.4 1.3 %collective-permute-start.13 = (f32[192,384]{1,0:T(8,128)S(1)}, f32[192,384]{1,0:T(8,128)S(1)}, u32[]{:S(2)}, u32[]{:S(2)}) collective-permute-start(f32[192,384]{1,0:T(8,128)S(1)} %get-tuple-element.93), channel_id=1, source_target_pairs={{0,2},{1,3},{2,0},{3,1},{4,6},{5,7},{6,4},{7,5},{8,10},{9,11},{10,... | collective-permute-start | bytes 884744 | tf_op jit(solution)/shard_map/ppermute | solution.py:541
  27.7 2.5 %pair_elements.1 = (f32[2,384,384]{2,1,0:T(8,128)S(1)}, f32[2,96,384]{2,1,0:T(8,128)S(1)}, f32[2,16,384]{2,1,0:T(8,128)S(1)}, f32[384,384]{1,0:T(8,128)S(1)}) custom-call(f32[2,384,384]{2,1,0:T(8,128)S(1)} %get-tuple-element.73.psi_ref, f32[2,384,384]{2,1,0:T(8,128)S(1)} %get-tuple-element.74.covar_ref, f32[2,16,384]{2,1,0:T(8,128)S(1)} %get-tuple-element.75.mean_ref, ...), custom_call_target="tpu_custom_call" | custom-call | bytes 4096 | tf_op jit(solution)/shard_map/pair_elements/pallas_call | solution.py:53
  30.2 1.2 %collective-permute-done.9.refs_0_ = f32[312,128]{1,0:T(8,128)S(1)} collective-permute-done((f32[312,128]{1,0:T(8,128)S(1)}, f32[312,128]{1,0:T(8,128)S(1)}, u32[]{:S(2)}, u32[]{:S(2)}) %collective-permute-start.9) | collective-permute-done | bytes 159776 | tf_op jit(solution)/shard_map/ppermute | solution.py:541
  31.4 2.3 %collective-permute-start.10 = (f32[312,128]{1,0:T(8,128)S(1)}, f32[312,128]{1,0:T(8,128)S(1)}, u32[]{:S(2)}, u32[]{:S(2)}) collective-permute-start(f32[312,128]{1,0:T(8,128)S(1)} %collective-permute-done.9.refs_0_), channel_id=1, source_target_pairs={{0,1},{1,0},{2,3},{3,2},{4,5},{5,4},{6,7},{7,6},{8,9},{9,8},{10,11... | collective-permute-start | bytes 479240 | tf_op jit(solution)/shard_map/ppermute | solution.py:528
  33.7 1.0 %collective-permute-done.10.refs_1_ = f32[312,128]{1,0:T(8,128)S(1)} collective-permute-done((f32[312,128]{1,0:T(8,128)S(1)}, f32[312,128]{1,0:T(8,128)S(1)}, u32[]{:S(2)}, u32[]{:S(2)}) %collective-permute-start.10) | collective-permute-done | bytes 159776 | tf_op jit(solution)/shard_map/ppermute | solution.py:528
  34.7 0.7 %collective-permute-start.11 = (f32[312,128]{1,0:T(8,128)S(1)}, f32[312,128]{1,0:T(8,128)S(1)}, u32[]{:S(2)}, u32[]{:S(2)}) collective-permute-start(f32[312,128]{1,0:T(8,128)S(1)} %joined_covariance.1), channel_id=1, source_target_pairs={{0,2},{1,3},{2,0},{3,1},{4,6},{5,7},{6,4},{7,5},{8,16},{9,17},{10,... | collective-permute-start | bytes 479240 | tf_op jit(solution)/shard_map/ppermute | solution.py:541
  35.4 0.7 %collective-permute-start.12 = (f32[312,128]{1,0:T(8,128)S(1)}, f32[312,128]{1,0:T(8,128)S(1)}, u32[]{:S(2)}, u32[]{:S(2)}) collective-permute-start(f32[312,128]{1,0:T(8,128)S(1)} %joined_covariance.1), channel_id=1, source_target_pairs={{0,4},{1,5},{2,6},{3,7},{4,0},{5,1},{6,2},{7,3},{8,24},{9,25},{10,... | collective-permute-start | bytes 479240 | tf_op jit(solution)/shard_map/ppermute | solution.py:541
  36.1 1.3 %entered.1 = (f32[2,96,384]{2,1,0:T(8,128)S(1)}, f32[2,16,384]{2,1,0:T(8,128)S(1)}) custom-call(f32[2,384,384]{2,1,0:T(8,128)S(1)} %get-tuple-element.94.psi_ref, f32[2,96,384]{2,1,0:T(8,128)S(1)} %get-tuple-element.96.covar_ref, f32[2,16,384]{2,1,0:T(8,128)S(1)} %get-tuple-element.97.mean_ref, f32[312,128]{1,0:T(8,128)S(1)} %collective-permute-done.9.refs_0_, ...), custom_call_target="tpu_custom_call" | custom-call | bytes 4096 | tf_op jit(solution)/shard_map/entered/pallas_call | solution.py:53
  37.8 1.4 %collective-permute-start.14 = (f32[96,384]{1,0:T(8,128)S(1)}, f32[96,384]{1,0:T(8,128)S(1)}, u32[]{:S(2)}, u32[]{:S(2)}) collective-permute-start(f32[96,384]{1,0:T(8,128)S(1)} %get-tuple-element.109), channel_id=1, source_target_pairs={{0,1},{1,0},{2,3},{3,2},{4,5},{5,4},{6,7},{7,6},{8,9},{9,8},{10,11... | collective-permute-start | bytes 442376 | tf_op jit(solution)/shard_map/ppermute | solution.py:528
  39.2 0.9 %collective-permute-done.14.refs_1_ = f32[96,384]{1,0:T(8,128)S(1)} collective-permute-done((f32[96,384]{1,0:T(8,128)S(1)}, f32[96,384]{1,0:T(8,128)S(1)}, u32[]{:S(2)}, u32[]{:S(2)}) %collective-permute-start.14) | collective-permute-done | bytes 147488 | tf_op jit(solution)/shard_map/ppermute | solution.py:528
  40.5 1.2 %matrices_entered.1.psi_ref = f32[2,384,384]{2,1,0:T(8,128)S(1)} custom-call(f32[2,384,384]{2,1,0:T(8,128)S(1)} %get-tuple-element.94.psi_ref, f32[192,384]{1,0:T(8,128)S(1)} %collective-permute-done.13.refs_0_, f32[96,384]{1,0:T(8,128)S(1)} %collective-permute-done.14.refs_1_, f32[96,384]{1,0:T(8,128)S(1)} %collective-permute-done.15.refs_2_), custom_call_target="tpu_custom_call" | custom-call | bytes 4096 | tf_op jit(solution)/shard_map/matrices_entered/pallas_call | solution.py:53
  41.7 1.6 %collective-permute-done.12.refs_1_ = f32[312,128]{1,0:T(8,128)S(1)} collective-permute-done((f32[312,128]{1,0:T(8,128)S(1)}, f32[312,128]{1,0:T(8,128)S(1)}, u32[]{:S(2)}, u32[]{:S(2)}) %collective-permute-start.12) | collective-permute-done | bytes 159776 | tf_op jit(solution)/shard_map/ppermute | solution.py:541
  43.4 1.2 %collective-permute-start.16 = (f32[312,128]{1,0:T(8,128)S(1)}, f32[312,128]{1,0:T(8,128)S(1)}, u32[]{:S(2)}, u32[]{:S(2)}) collective-permute-start(f32[312,128]{1,0:T(8,128)S(1)} %collective-permute-done.11.refs_0_), channel_id=1, source_target_pairs={{0,1},{1,0},{2,3},{3,2},{4,5},{5,4},{6,7},{7,6},{8,9},{9,8},{10,11... | collective-permute-start | bytes 479240 | tf_op jit(solution)/shard_map/ppermute | solution.py:528
  44.6 1.0 %collective-permute-done.16.refs_2_ = f32[312,128]{1,0:T(8,128)S(1)} collective-permute-done((f32[312,128]{1,0:T(8,128)S(1)}, f32[312,128]{1,0:T(8,128)S(1)}, u32[]{:S(2)}, u32[]{:S(2)}) %collective-permute-start.16) | collective-permute-done | bytes 159776 | tf_op jit(solution)/shard_map/ppermute | solution.py:528
  45.9 1.9 %finished.1 = (f32[2,96,384]{2,1,0:T(8,128)}, f32[2,384]{1,0:T(2,128)}) custom-call(f32[2,384,384]{2,1,0:T(8,128)S(1)} %matrices_entered.1.psi_ref, f32[2,96,384]{2,1,0:T(8,128)S(1)} %get-tuple-element.102.covar_ref, f32[2,16,384]{2,1,0:T(8,128)S(1)} %get-tuple-element.103.mean_ref, f32[312,128]{1,0:T(8,128)S(1)} %collective-permute-done.11.refs_0_, ...), custom_call_target="tpu_custom_call" | custom-call | bytes 4096 | tf_op jit(solution)/shard_map/finished/pallas_call | solution.py:53
  (34 shorter events, 2.4 us)
Async XLA Ops:
  0.6 6.2 %copy-start = (f32[384,1024]{1,0:T(8,128)S(1)}, f32[384,1024]{1,0:T(8,128)}, u32[]{:S(2)}) copy-start(f32[384,1024]{1,0:T(8,128)} %gain_ref) | copy-start | bytes 4718596
  0.6 6.2 %copy-start.5 = (f32[1024]{0:T(1024)S(1)}, f32[1024]{0:T(1024)}, u32[]{:S(2)}) copy-start(f32[1024]{0:T(1024)} %param.15) | copy-start | bytes 12292
  0.7 6.2 %copy-start.1 = (f32[384,384]{1,0:T(8,128)S(1)}, f32[384,384]{1,0:T(8,128)}, u32[]{:S(2)}) copy-start(f32[384,384]{1,0:T(8,128)} %factor_ref.1) | copy-start | bytes 1769476
  0.7 9.3 %collective-permute-start = (f32[2,96,384]{2,1,0:T(8,128)}, f32[2,96,384]{2,1,0:T(8,128)S(1)}, u32[]{:S(2)}, u32[]{:S(2)}) collective-permute-start(f32[2,96,384]{2,1,0:T(8,128)} %refs_4_), channel_id=1, source_target_pairs={{0,2},{1,3},{2,0},{3,1},{4,6},{5,7},{6,4},{7,5},{8,10},{9,11},{10,... | collective-permute-start | bytes 884744 | tf_op jit(solution)/shard_map/ppermute | solution.py:528
  1.9 8.0 %collective-permute-start.1 = (f32[2,96,384]{2,1,0:T(8,128)}, f32[2,96,384]{2,1,0:T(8,128)S(1)}, u32[]{:S(2)}, u32[]{:S(2)}) collective-permute-start(f32[2,96,384]{2,1,0:T(8,128)} %refs_4_), channel_id=1, source_target_pairs={{0,4},{4,0},{8,12},{12,8},{16,20},{20,16},{24,28},{28,24},{1,5},{5... | collective-permute-start | bytes 884744 | tf_op jit(solution)/shard_map/ppermute | solution.py:528
  5.3 5.0 %copy-start.3 = (f32[96,384]{1,0:T(8,128)S(1)}, f32[96,384]{1,0:T(8,128)}, u32[]{:S(2)}) copy-start(f32[96,384]{1,0:T(8,128)} %get-tuple-element.61.refs_0_) | copy-start | bytes 442372
  5.3 9.3 %copy-start.2 = (f32[2,96,384]{2,1,0:T(8,128)S(1)}, f32[2,96,384]{2,1,0:T(8,128)}, u32[]{:S(2)}) copy-start(f32[2,96,384]{2,1,0:T(8,128)} %refs_4_) | copy-start | bytes 884740
  5.3 7.3 %collective-permute-start.4 = (f32[96,384]{1,0:T(8,128)}, f32[96,384]{1,0:T(8,128)S(1)}, u32[]{:S(2)}, u32[]{:S(2)}) collective-permute-start(f32[96,384]{1,0:T(8,128)} %get-tuple-element.61.refs_0_), channel_id=1, source_target_pairs={{0,2},{1,3},{2,0},{3,1},{4,6},{5,7},{6,4},{7,5},{8,10},{9,11},{10,... | collective-permute-start | bytes 442376 | tf_op jit(solution)/shard_map/ppermute | solution.py:528
  5.7 4.3 %collective-permute-start.2 = (f32[2,4,384]{2,1,0:T(4,128)}, f32[2,4,384]{2,1,0:T(4,128)S(1)}, u32[]{:S(2)}, u32[]{:S(2)}) collective-permute-start(f32[2,4,384]{2,1,0:T(4,128)} %get-tuple-element.55.vec_ref), channel_id=1, source_target_pairs={{0,4},{4,0},{8,12},{12,8},{16,20},{20,16},{24,28},{28,24},{1,5},{5... | collective-permute-start | bytes 36872 | tf_op jit(solution)/shard_map/ppermute | solution.py:528
  6.9 9.0 %copy-start.4 = (f32[2,4,384]{2,1,0:T(4,128)S(1)}, f32[2,4,384]{2,1,0:T(4,128)}, u32[]{:S(2)}) copy-start(f32[2,4,384]{2,1,0:T(4,128)} %get-tuple-element.55.vec_ref) | copy-start | bytes 36868
  10.0 8.4 %collective-permute-start.3 = (f32[2,96,384]{2,1,0:T(8,128)S(1)}, f32[2,96,384]{2,1,0:T(8,128)S(1)}, u32[]{:S(2)}, u32[]{:S(2)}) collective-permute-start(f32[2,96,384]{2,1,0:T(8,128)S(1)} %collective-permute-done.refs_5_), channel_id=1, source_target_pairs={{0,4},{4,0},{8,12},{12,8},{16,20},{20,16},{24,28},{28,24},{1,5},{5... | collective-permute-start | bytes 884744 | tf_op jit(solution)/shard_map/ppermute | solution.py:528
  10.2 3.3 %collective-permute-start.5 = (f32[96,384]{1,0:T(8,128)S(1)}, f32[96,384]{1,0:T(8,128)S(1)}, u32[]{:S(2)}, u32[]{:S(2)}) collective-permute-start(f32[96,384]{1,0:T(8,128)S(1)} %copy-done.3), channel_id=1, source_target_pairs={{0,1},{1,0},{2,3},{3,2},{4,5},{5,4},{6,7},{7,6},{8,9},{9,8},{10,11... | collective-permute-start | bytes 442376 | tf_op jit(solution)/shard_map/ppermute | solution.py:528
  12.6 2.0 %collective-permute-start.6 = (f32[96,384]{1,0:T(8,128)S(1)}, f32[96,384]{1,0:T(8,128)S(1)}, u32[]{:S(2)}, u32[]{:S(2)}) collective-permute-start(f32[96,384]{1,0:T(8,128)S(1)} %collective-permute-done.4.refs_1_), channel_id=1, source_target_pairs={{0,1},{1,0},{2,3},{3,2},{4,5},{5,4},{6,7},{7,6},{8,9},{9,8},{10,11... | collective-permute-start | bytes 442376 | tf_op jit(solution)/shard_map/ppermute | solution.py:528
  15.4 4.8 %collective-permute-start.7 = (f32[2,192,384]{2,1,0:T(8,128)S(1)}, f32[2,192,384]{2,1,0:T(8,128)S(1)}, u32[]{:S(2)}, u32[]{:S(2)}) collective-permute-start(f32[2,192,384]{2,1,0:T(8,128)S(1)} %get-tuple-element.69.mine_ref), channel_id=1, source_target_pairs={{0,1},{1,0},{2,3},{3,2},{4,5},{5,4},{6,7},{7,6},{8,9},{9,8},{10,11... | collective-permute-start | bytes 1769480 | tf_op jit(solution)/shard_map/ppermute | solution.py:528
  18.3 1.8 %copy-start.6 = (f32[384]{0:T(512)S(1)}, f32[384]{0:T(512)}, u32[]{:S(2)}) copy-start(f32[384]{0:T(512)} %param.18) | copy-start | bytes 4612
  19.0 3.3 %collective-permute-start.8 = (f32[2,192,384]{2,1,0:T(8,128)S(1)}, f32[2,192,384]{2,1,0:T(8,128)S(1)}, u32[]{:S(2)}, u32[]{:S(2)}) collective-permute-start(f32[2,192,384]{2,1,0:T(8,128)S(1)} %other_rows.1.mine_ref), channel_id=1, source_target_pairs={{0,1},{1,0},{2,3},{3,2},{4,5},{5,4},{6,7},{7,6},{8,9},{9,8},{10,11... | collective-permute-start | bytes 1769480 | tf_op jit(solution)/shard_map/ppermute | solution.py:528
  26.2 5.3 %collective-permute-start.9 = (f32[312,128]{1,0:T(8,128)S(1)}, f32[312,128]{1,0:T(8,128)S(1)}, u32[]{:S(2)}, u32[]{:S(2)}) collective-permute-start(f32[312,128]{1,0:T(8,128)S(1)} %get-tuple-element.85.total_ref), channel_id=1, source_target_pairs={{0,8},{1,9},{2,10},{3,11},{4,12},{5,13},{6,14},{7,15},{8,0},{9,1},... | collective-permute-start | bytes 479240 | tf_op jit(solution)/shard_map/ppermute | solution.py:541
  26.4 11.3 %collective-permute-start.13 = (f32[192,384]{1,0:T(8,128)S(1)}, f32[192,384]{1,0:T(8,128)S(1)}, u32[]{:S(2)}, u32[]{:S(2)}) collective-permute-start(f32[192,384]{1,0:T(8,128)S(1)} %get-tuple-element.93), channel_id=1, source_target_pairs={{0,2},{1,3},{2,0},{3,1},{4,6},{5,7},{6,4},{7,5},{8,10},{9,11},{10,... | collective-permute-start | bytes 884744 | tf_op jit(solution)/shard_map/ppermute | solution.py:541
  31.4 3.3 %collective-permute-start.10 = (f32[312,128]{1,0:T(8,128)S(1)}, f32[312,128]{1,0:T(8,128)S(1)}, u32[]{:S(2)}, u32[]{:S(2)}) collective-permute-start(f32[312,128]{1,0:T(8,128)S(1)} %collective-permute-done.9.refs_0_), channel_id=1, source_target_pairs={{0,1},{1,0},{2,3},{3,2},{4,5},{5,4},{6,7},{7,6},{8,9},{9,8},{10,11... | collective-permute-start | bytes 479240 | tf_op jit(solution)/shard_map/ppermute | solution.py:528
  34.7 7.0 %collective-permute-start.11 = (f32[312,128]{1,0:T(8,128)S(1)}, f32[312,128]{1,0:T(8,128)S(1)}, u32[]{:S(2)}, u32[]{:S(2)}) collective-permute-start(f32[312,128]{1,0:T(8,128)S(1)} %joined_covariance.1), channel_id=1, source_target_pairs={{0,2},{1,3},{2,0},{3,1},{4,6},{5,7},{6,4},{7,5},{8,16},{9,17},{10,... | collective-permute-start | bytes 479240 | tf_op jit(solution)/shard_map/ppermute | solution.py:541
  35.4 7.9 %collective-permute-start.12 = (f32[312,128]{1,0:T(8,128)S(1)}, f32[312,128]{1,0:T(8,128)S(1)}, u32[]{:S(2)}, u32[]{:S(2)}) collective-permute-start(f32[312,128]{1,0:T(8,128)S(1)} %joined_covariance.1), channel_id=1, source_target_pairs={{0,4},{1,5},{2,6},{3,7},{4,0},{5,1},{6,2},{7,3},{8,24},{9,25},{10,... | collective-permute-start | bytes 479240 | tf_op jit(solution)/shard_map/ppermute | solution.py:541
  37.8 2.4 %collective-permute-start.14 = (f32[96,384]{1,0:T(8,128)S(1)}, f32[96,384]{1,0:T(8,128)S(1)}, u32[]{:S(2)}, u32[]{:S(2)}) collective-permute-start(f32[96,384]{1,0:T(8,128)S(1)} %get-tuple-element.109), channel_id=1, source_target_pairs={{0,1},{1,0},{2,3},{3,2},{4,5},{5,4},{6,7},{7,6},{8,9},{9,8},{10,11... | collective-permute-start | bytes 442376 | tf_op jit(solution)/shard_map/ppermute | solution.py:528
  39.2 1.4 %collective-permute-start.15 = (f32[96,384]{1,0:T(8,128)S(1)}, f32[96,384]{1,0:T(8,128)S(1)}, u32[]{:S(2)}, u32[]{:S(2)}) collective-permute-start(f32[96,384]{1,0:T(8,128)S(1)} %get-tuple-element.108), channel_id=1, source_target_pairs={{0,1},{1,0},{2,3},{3,2},{4,5},{5,4},{6,7},{7,6},{8,9},{9,8},{10,11... | collective-permute-start | bytes 442376 | tf_op jit(solution)/shard_map/ppermute | solution.py:528
  43.4 2.2 %collective-permute-start.16 = (f32[312,128]{1,0:T(8,128)S(1)}, f32[312,128]{1,0:T(8,128)S(1)}, u32[]{:S(2)}, u32[]{:S(2)}) collective-permute-start(f32[312,128]{1,0:T(8,128)S(1)} %collective-permute-done.11.refs_0_), channel_id=1, source_target_pairs={{0,1},{1,0},{2,3},{3,2},{4,5},{5,4},{6,7},{7,6},{8,9},{9,8},{10,11... | collective-permute-start | bytes 479240 | tf_op jit(solution)/shard_map/ppermute | solution.py:528
  44.5 1.4 %collective-permute-start.17 = (f32[312,128]{1,0:T(8,128)S(1)}, f32[312,128]{1,0:T(8,128)S(1)}, u32[]{:S(2)}, u32[]{:S(2)}) collective-permute-start(f32[312,128]{1,0:T(8,128)S(1)} %collective-permute-done.12.refs_1_), channel_id=1, source_target_pairs={{0,1},{1,0},{2,3},{3,2},{4,5},{5,4},{6,7},{7,6},{8,9},{9,8},{10,11... | collective-permute-start | bytes 479240 | tf_op jit(solution)/shard_map/ppermute | solution.py:528

commit v7 on v6

--- a/solution.py
+++ b/solution.py
@@ -131,34 +131,38 @@
         out_ref[pl.ds(at, width), :] = piece
 
 
-def noises(vec_ref, fixed_ref, corr_ref, noise_ref, offset_ref):
+def noises(vec_ref, push_ref, fixed_ref, corr_ref, noise_ref, offset_ref):
     steps, states = vec_ref.shape[0], corr_ref.shape[0]
     corr = corr_ref[...]
-    vectors = [vec_ref[k] for k in range(steps)]
-    push = [v[2:3] for v in vectors] + [jnp.zeros((MEAN_ROWS - steps, states), F32)]
-    left = jnp.concatenate([corr * v[1:2] for v in vectors] + push, axis=0)
-    both = dot_nt(left, corr)
-    base = steps * states
+    right = jnp.concatenate([corr * vec_ref[k, 1:2, :] for k in range(steps)], axis=0)
+    both = dot_nt(corr, right)
     for k in range(steps):
-        noise_ref[k] = both[k * states : (k + 1) * states] + fixed_ref[...]
-        offset_ref[k] = mean_block(both[base + k : base + k + 1] + vectors[k][3:4], states)
-
-
-def mixed_rows(out_ref, pieces, corr):
+        noise_ref[k] = both[:, k * states : (k + 1) * states] + fixed_ref[...]
+        offset_ref[k] = mean_block(push_ref[k : k + 1, :] + vec_ref[k, 3:4, :], states)
+
+
+def mixed_rows(out_ref, pieces, corr, more=()):
     steps, width = pieces[0].shape[:2]
-    rows = jnp.concatenate([piece[k] for k in range(steps) for piece in pieces], axis=0)
-    mixed = dot_nt(rows, corr)
+    rows = [piece[k] for k in range(steps) for piece in pieces] + list(more)
+    mixed = dot_nt(jnp.concatenate(rows, axis=0), corr)
     half = width * len(pieces)
     for k in range(steps):
         out_ref[k] = mixed[k * half : (k + 1) * half]
-
-
-def own_rows(offsets, *refs):
+    return mixed[steps * half :]
+
+
+def own_rows(offsets, vec_ref, vec_other_ref, *refs):
     n_piece = len(offsets)
-    pieces, own, (corr_ref, out_ref, work_ref) = refs[:n_piece], refs[n_piece:-3], refs[-3:]
+    pieces, own, (corr_ref, out_ref, push_ref, push_other_ref, work_ref) = refs[:n_piece], refs[n_piece:-5], refs[-5:]
     place([p[...] for p in pieces], offsets, work_ref, 0)
     corr_ref[...] = work_ref[...].T
-    mixed_rows(out_ref, own, corr_ref[...])
+    steps, states = vec_ref.shape[0], corr_ref.shape[0]
+    push = [ref[k, 2:3, :] for ref in (vec_ref, vec_other_ref) for k in range(steps)]
+    pushed = mixed_rows(
+        out_ref, own, corr_ref[...], push + [jnp.zeros((MEAN_ROWS - 2 * steps, states), F32)]
+    )
+    push_ref[...] = pushed[:steps]
+    push_other_ref[...] = pushed[steps : 2 * steps]
 
 
 def other_rows(corr_ref, *refs):
@@ -196,45 +200,26 @@
 
     psi_ref[0] = matrix_ref[0]
     for k in range(1, steps):
-        psi_ref[k] = dot_nn(matrix_ref[k], psi_ref[k - 1])
+
+        @pl.when(lax.axis_index("seg") > 0)
+        def _():
+            psi_ref[k] = dot_nn(matrix_ref[k], psi_ref[k - 1])
+
         covar, mean = square(matrix_ref[k], covar_ref[k - 1], mean_ref[k - 1])
         covar_ref[k] = covar + noise_ref[k]
         mean_ref[k] = mean + offset_ref[k]
 
 
 def other_matrices(
-    offsets, vec_ref, corr_ref, mine_ref, mate_ref, psi_ref, prior_ref, start_ref,
-    matrix_ref, psi_other_ref, psi_half_ref, covar_ref, mean_ref, work_ref,
+    offsets, vec_ref, corr_ref, mine_ref, mate_ref, prior_ref, start_ref, matrix_ref, covar_ref, mean_ref, work_ref
 ):
-    steps, half, states = mine_ref.shape
-    seg = lax.axis_index("seg")
-    is_second = lax.rem(seg, 2) == 1
     matrices_of(offsets, vec_ref, corr_ref[...], mine_ref, mate_ref, work_ref, matrix_ref)
-    mine = pl.ds(pl.multiple_of(lax.rem(lax.axis_index("col"), 2) * half, 8), half)
     covar_ref[...] = jnp.zeros_like(covar_ref)
     mean_ref[...] = jnp.zeros_like(mean_ref)
 
-    @pl.when(seg == 1)
+    @pl.when(lax.axis_index("seg") == 1)
     def _():
         add_prior(matrix_ref, prior_ref, start_ref, covar_ref, mean_ref)
-
-    @pl.when(seg < 2)
-    def _():
-        psi_half_ref[...] = jnp.zeros_like(psi_half_ref)
-
-    @pl.when(seg >= 2)
-    def _():
-        psi_other_ref[...] = matrix_ref[0]
-        for k in range(1, steps):
-            psi_other_ref[...] = dot_nn(matrix_ref[k], psi_other_ref[...])
-
-        @pl.when(is_second)
-        def _():
-            psi_half_ref[...] = dot_nn(psi_ref[steps - 1, mine, :], psi_other_ref[...])
-
-        @pl.when(jnp.logical_not(is_second))
-        def _():
-            psi_half_ref[...] = dot_nn(psi_other_ref[mine, :], psi_ref[steps - 1])
 
 
 def share_rows(edge):
@@ -361,8 +346,31 @@
     put_packed(step_ref, covar_other_ref[...], mean_other_ref[...], added, out_ref)
 
 
-def pair_elements(steps, width, psi_ref, covar_ref, mean_ref, psi_other_ref, covar_other_ref, mean_other_ref, *refs):
-    psi_out_ref, covar_out_ref, mean_out_ref, psi_all_ref = refs
+def pair_matrices(matrix_ref, psi_ref, psi_other_ref, psi_all_ref, half_ref):
+    steps, states = matrix_ref.shape[:2]
+    half = states // 2
+    seg = lax.axis_index("seg")
+    mine = pl.ds(pl.multiple_of(lax.rem(lax.axis_index("col"), 2) * half, 8), half)
+
+    @pl.when(seg < 2)
+    def _():
+        psi_other_ref[...] = jnp.zeros_like(psi_other_ref)
+        psi_all_ref[...] = jnp.zeros_like(psi_all_ref)
+        half_ref[...] = jnp.zeros_like(half_ref)
+
+    @pl.when(seg >= 2)
+    def _():
+        psi_other_ref[...] = matrix_ref[0]
+        for k in range(1, steps):
+            psi_other_ref[...] = dot_nn(matrix_ref[k], psi_other_ref[...])
+        own, other = psi_ref[steps - 1], psi_other_ref[...]
+        is_second = lax.rem(seg, 2) == 1
+        psi_all_ref[...] = dot_nn(jnp.where(is_second, own, other), jnp.where(is_second, other, own))
+        half_ref[...] = psi_all_ref[mine, :]
+
+
+def pair_elements(steps, width, psi_ref, covar_ref, mean_ref, psi_other_ref, psi_all_ref, covar_other_ref, mean_other_ref, *refs):
+    psi_out_ref, covar_out_ref, mean_out_ref = refs
     seg = lax.axis_index("seg")
     is_second = lax.rem(seg, 2) == 1
     mine = pl.ds(pl.multiple_of(lax.axis_index("col") * width, 8), width)
@@ -370,27 +378,16 @@
     @pl.when(seg < 2)
     def _():
         psi_out_ref[...] = jnp.zeros_like(psi_out_ref)
-        psi_all_ref[...] = jnp.zeros_like(psi_all_ref)
-
-    @pl.when(seg >= 2)
-    def _():
-        for k in range(steps):
-
-            @pl.when(is_second)
-            def _():
-                psi_out_ref[k] = dot_nn(psi_ref[k], psi_other_ref[...])
-
-            @pl.when(jnp.logical_not(is_second))
-            def _():
-                psi_out_ref[k] = psi_ref[k]
-
-        @pl.when(is_second)
-        def _():
-            psi_all_ref[...] = psi_out_ref[steps - 1]
-
-        @pl.when(jnp.logical_not(is_second))
-        def _():
-            psi_all_ref[...] = dot_nn(psi_other_ref[...], psi_ref[steps - 1])
+
+    @pl.when((seg >= 2) & is_second)
+    def _():
+        for k in range(steps - 1):
+            psi_out_ref[k] = dot_nn(psi_ref[k], psi_other_ref[...])
+        psi_out_ref[steps - 1] = psi_all_ref[...]
+
+    @pl.when((seg >= 2) & jnp.logical_not(is_second))
+    def _():
+        psi_out_ref[...] = psi_ref[...]
 
     @pl.when(is_second)
     def _():
@@ -434,9 +431,9 @@
     mines, mates = refs[:n_group], refs[n_group : 2 * n_group]
     out_ref, mine_ref, mate_ref, work_ref = refs[2 * n_group :]
 
-    at = lax.rem(lax.axis_index("seg"), 4 * bit)
-
-    @pl.when((at >= 2 * bit - 2) & (at < 2 * bit))
+    seg, last = lax.axis_index("seg"), lax.axis_size("seg") - 2
+
+    @pl.when((lax.rem(seg, 2 * bit) >= 2 * bit - 2) & (seg < last))
     def _():
         mine_ref[...] = chosen(mines, bit)
         mate_ref[...] = chosen(mates, bit)
@@ -602,16 +599,20 @@
     corr = corr + [swapped(b, "col", 1) for b in corr]
     rows_shape = (steps,) + half_shape
     noise_shapes = [(steps,) + square_shape, (steps,) + mean_shape]
-    correction, rows = local_call(
+    correction, rows, push, push_other = local_call(
         functools.partial(own_rows, offsets + [o ^ 1 for o in offsets]),
-        [square_shape, rows_shape],
+        [square_shape, rows_shape, (steps, states), (steps, states)],
+        vectors,
+        vectors_other,
         *corr,
         *own,
         scratch=[square_shape],
     )
-    noise, offset = local_call(noises, noise_shapes, vectors, fixed, correction)
+    noise, offset = local_call(noises, noise_shapes, vectors, push, fixed, correction)
     start = prior_mean[None, :]
-    noise_other, offset_other = local_call(noises, noise_shapes, vectors_other, fixed, correction)
+    noise_other, offset_other = local_call(
+        noises, noise_shapes, vectors_other, push_other, fixed, correction
+    )
     other, correction, noise, noise_other = lax.optimization_barrier((other, correction, noise, noise_other))
     (rows_other,) = local_call(other_rows, [rows_shape], correction, *other)
     matrix, psi, covar, mean = local_call(
@@ -627,13 +628,12 @@
         scratch=[square_shape],
         cost=1,
     )
-    matrix_other, psi_other, psi_half, first_other, first_mean_other = local_call(
+    matrix_other, first_other, first_mean_other = local_call(
         functools.partial(other_matrices, offsets),
-        [(steps,) + square_shape, square_shape, half_shape, square_shape, mean_shape],
+        [(steps,) + square_shape, square_shape, mean_shape],
         vectors_other,
         correction,
         *with_mate(rows_other),
-        psi,
         prior,
         start,
         scratch=[square_shape],
@@ -653,21 +653,26 @@
         first_mean_other,
         scratch=[square_shape],
     )
-    total, psi_half = lax.optimization_barrier((total, psi_half))
     came = handed_up(total, bit)
+    matrix_other, total = lax.optimization_barrier((matrix_other, total))
+    psi_other, psi_all, psi_half = local_call(
+        pair_matrices, [square_shape, square_shape, half_shape], matrix_other, psi
+    )
     step = []
     if more:
         step = handed_up(psi_half, bit, 1)
-    psi, covar, mean, psi_all = local_call(
+    psi, covar, mean = local_call(
         functools.partial(pair_elements, steps, width),
-        [(steps,) + square_shape, (steps, width, states), (steps,) + mean_shape, square_shape],
+        [(steps,) + square_shape, (steps, width, states), (steps,) + mean_shape],
         psi,
         covar,
         mean,
         psi_other,
+        psi_all,
         covar_other,
         mean_other,
     )
+
     def over_core(blocks):
         return list(blocks) + [swapped(b, "col", 1) for b in blocks]
 

time: 48 us -> 46.8 us (0.975)
  waiting for transfers between devices: 9.66 us -> 8.88 us
  Pallas kernels: 21.3 us -> 20.7 us
    ppermute x4, waiting for transfers between devices: 3.23 us -> 2.46 us  [handed_up(): came.append(lax.ppermute(block, ('seg', 'col'), sorted(to.items())))]
    pallas_call x14 -> x15, Pallas kernels: 21.3 us -> 20.7 us  [local_call(): pl.pallas_call(body, out_shape=shapes, name=getattr(body, 'func', body)._...]
    ppermute x14, starting transfers between devices: 13.1 us -> 13.6 us  [swapped(): lax.ppermute(block, axis, [(i, i ^ bit) for i in range(lax.axis_size(axis...]
  transfers between devices with their start and end apart: 18 -> 18, of which waited for: 10 -> 10; matrix products, arithmetic and copies ran while one was open for 0% -> 0% of each run, Pallas kernels for 33% -> 34%
where the time goes in v7:
time: 46.8 us; the launch traced here: 46.6 us
  Pallas kernels  20.7 us (44%)
  starting transfers between devices  16.2 us (35%)
  waiting for transfers between devices  8.88 us (19%)
  between operations  0.83 us (2%)
    pallas_call x15, Pallas kernels, local_call(): pl.pallas_call(body, out_shape=shapes, name=getattr(body, 'func', body)._...  20.7 us
    ppermute x14, starting transfers between devices, swapped(): lax.ppermute(block, axis, [(i, i ^ bit) for i in range(lax.axis_size(axis...  13.6 us
    ppermute x14, waiting for transfers between devices, swapped(): lax.ppermute(block, axis, [(i, i ^ bit) for i in range(lax.axis_size(axis...  6.42 us
    ppermute x4, starting transfers between devices, handed_up(): came.append(lax.ppermute(block, ('seg', 'col'), sorted(to.items())))  2.62 us
    ppermute x4, waiting for transfers between devices, handed_up(): came.append(lax.ppermute(block, ('seg', 'col'), sorted(to.items())))  2.46 us
  transfers between devices with their start and end apart: 18, of which 10 were waited for; matrix products, arithmetic and copies ran while one was open for 0% of the time, Pallas kernels for 34%

profile of v7, /device:TPU:29, one launch (start us, length us, event | category | flops | bytes accessed | tf_op | source)
XLA Modules:
  0.0 46.6 jit_solution(6457547774110025720)
XLA Ops:
  0.7 1.3 %collective-permute-start = (f32[2,96,384]{2,1,0:T(8,128)}, f32[2,96,384]{2,1,0:T(8,128)S(1)}, u32[]{:S(2)}, u32[]{:S(2)}) collective-permute-start(f32[2,96,384]{2,1,0:T(8,128)} %refs_4_), channel_id=1, source_target_pairs={{0,2},{1,3},{2,0},{3,1},{4,6},{5,7},{6,4},{7,5},{8,10},{9,11},{10,... | collective-permute-start | bytes 884744 | tf_op jit(solution)/shard_map/ppermute | solution.py:525
  2.2 3.1 %correction_rows.1 = (f32[96,384]{1,0:T(8,128)}, f32[2,4,384]{2,1,0:T(4,128)}) custom-call(f32[384,1024]{1,0:T(8,128)} %gain_ref, f32[96,1024]{1,0:T(8,128)} %oper_hbm.1, f32[2,1024]{1,0:T(2,128)} %seen_hbm.1, f32[2,384]{1,0:T(2,128)} %keep_hbm.1, f32[2,384]{1,0:T(2,128)} %push_hbm.1, f32[2,384]{1,0:T(2,128)} %var_hbm.1), custom_call_target="tpu_custom_call" | custom-call | flops 2100000000 | bytes 4096 | tf_op jit(solution)/shard_map/correction_rows/pallas_call | solution.py:53
  5.7 1.2 %collective-permute-start.2 = (f32[2,4,384]{2,1,0:T(4,128)}, f32[2,4,384]{2,1,0:T(4,128)S(1)}, u32[]{:S(2)}, u32[]{:S(2)}) collective-permute-start(f32[2,4,384]{2,1,0:T(4,128)} %get-tuple-element.57.vec_ref), channel_id=1, source_target_pairs={{0,4},{4,0},{8,12},{12,8},{16,20},{20,16},{24,28},{28,24},{1,5},{5... | collective-permute-start | bytes 36872 | tf_op jit(solution)/shard_map/ppermute | solution.py:525
  6.9 1.4 %fixed_parts.1 = (f32[384,384]{1,0:T(8,128)S(1)}, f32[384,384]{1,0:T(8,128)S(1)}) custom-call(f32[384,1024]{1,0:T(8,128)S(1)} %copy-done, f32[1,1024]{1,0:T(1,128)S(1)} %bitcast.1, f32[384,384]{1,0:T(8,128)S(1)} %copy-done.1), custom_call_target="tpu_custom_call" | custom-call | bytes 4096 | tf_op jit(solution)/shard_map/fixed_parts/pallas_call | solution.py:53
  8.3 1.7 %collective-permute-done.2.vec_other_ref.vec_ref = f32[2,4,384]{2,1,0:T(4,128)S(1)} collective-permute-done((f32[2,4,384]{2,1,0:T(4,128)}, f32[2,4,384]{2,1,0:T(4,128)S(1)}, u32[]{:S(2)}, u32[]{:S(2)}) %collective-permute-start.2) | collective-permute-done | bytes 12320 | tf_op jit(solution)/shard_map/ppermute | solution.py:525
  10.2 2.4 %collective-permute-start.5 = (f32[96,384]{1,0:T(8,128)S(1)}, f32[96,384]{1,0:T(8,128)S(1)}, u32[]{:S(2)}, u32[]{:S(2)}) collective-permute-start(f32[96,384]{1,0:T(8,128)S(1)} %copy-done.3), channel_id=1, source_target_pairs={{0,1},{1,0},{2,3},{3,2},{4,5},{5,4},{6,7},{7,6},{8,9},{9,8},{10,11... | collective-permute-start | bytes 442376 | tf_op jit(solution)/shard_map/ppermute | solution.py:525
  12.6 1.0 %collective-permute-start.6 = (f32[96,384]{1,0:T(8,128)S(1)}, f32[96,384]{1,0:T(8,128)S(1)}, u32[]{:S(2)}, u32[]{:S(2)}) collective-permute-start(f32[96,384]{1,0:T(8,128)S(1)} %collective-permute-done.4.refs_1_), channel_id=1, source_target_pairs={{0,1},{1,0},{2,3},{3,2},{4,5},{5,4},{6,7},{7,6},{8,9},{9,8},{10,11... | collective-permute-start | bytes 442376 | tf_op jit(solution)/shard_map/ppermute | solution.py:525
  13.6 1.0 %collective-permute-done.6.refs_3_ = f32[96,384]{1,0:T(8,128)S(1)} collective-permute-done((f32[96,384]{1,0:T(8,128)S(1)}, f32[96,384]{1,0:T(8,128)S(1)}, u32[]{:S(2)}, u32[]{:S(2)}) %collective-permute-start.6) | collective-permute-done | bytes 147488 | tf_op jit(solution)/shard_map/ppermute | solution.py:525
  14.5 0.9 %own_rows.1 = (f32[384,384]{1,0:T(8,128)S(1)}, f32[2,192,384]{2,1,0:T(8,128)S(1)}, f32[2,384]{1,0:T(2,128)S(1)}, f32[2,384]{1,0:T(2,128)S(1)}) custom-call(f32[2,4,384]{2,1,0:T(4,128)S(1)} %copy-done.4, f32[2,4,384]{2,1,0:T(4,128)S(1)} %collective-permute-done.2.vec_other_ref.vec_ref, f32[96,384]{1,0:T(8,128)S(1)} %copy-done.3, ...), custom_call_target="tpu_custom_call" | custom-call | bytes 4096 | tf_op jit(solution)/shard_map/own_rows/pallas_call | solution.py:53
  15.8 1.0 %noises.2 = (f32[2,384,384]{2,1,0:T(8,128)S(1)}, f32[2,16,384]{2,1,0:T(8,128)S(1)}) custom-call(f32[2,4,384]{2,1,0:T(4,128)S(1)} %copy-done.4, f32[2,384]{1,0:T(2,128)S(1)} %get-tuple-element.67.push_ref, f32[384,384]{1,0:T(8,128)S(1)} %get-tuple-element.68.fixed_ref, f32[384,384]{1,0:T(8,128)S(1)} %get-tuple-element.72.corr_ref), custom_call_target="tpu_custom_call" | custom-call | bytes 4096 | tf_op jit(solution)/shard_map/noises/pallas_call | solution.py:53
  16.8 1.0 %noises.3 = (f32[2,384,384]{2,1,0:T(8,128)S(1)}, f32[2,16,384]{2,1,0:T(8,128)S(1)}) custom-call(f32[2,4,384]{2,1,0:T(4,128)S(1)} %collective-permute-done.2.vec_other_ref.vec_ref, f32[2,384]{1,0:T(2,128)S(1)} %get-tuple-element.70.push_ref, f32[384,384]{1,0:T(8,128)S(1)} %get-tuple-element.68.fixed_ref, f32[384,384]{1,0:T(8,128)S(1)} %get-tuple-element.72.corr_ref), custom_call_target="tpu_custom_call" | custom-call | bytes 4096 | tf_op jit(solution)/shard_map/noises/pallas_call | solution.py:53
  17.8 0.7 %other_rows.1.mine_ref = f32[2,192,384]{2,1,0:T(8,128)S(1)} custom-call(f32[384,384]{1,0:T(8,128)S(1)} %get-tuple-element.72.corr_ref, f32[2,96,384]{2,1,0:T(8,128)S(1)} %collective-permute-done.1.refs_0_, f32[2,96,384]{2,1,0:T(8,128)S(1)} %collective-permute-done.3.refs_1_), custom_call_target="tpu_custom_call" | custom-call | bytes 4096 | tf_op jit(solution)/shard_map/other_rows/pallas_call | solution.py:53
  18.5 1.6 %collective-permute-start.8 = (f32[2,192,384]{2,1,0:T(8,128)S(1)}, f32[2,192,384]{2,1,0:T(8,128)S(1)}, u32[]{:S(2)}, u32[]{:S(2)}) collective-permute-start(f32[2,192,384]{2,1,0:T(8,128)S(1)} %other_rows.1.mine_ref), channel_id=1, source_target_pairs={{0,1},{1,0},{2,3},{3,2},{4,5},{5,4},{6,7},{7,6},{8,9},{9,8},{10,11... | collective-permute-start | bytes 1769480 | tf_op jit(solution)/shard_map/ppermute | solution.py:525
  20.2 2.4 %own_segment.1 = (f32[2,384,384]{2,1,0:T(8,128)}, f32[2,384,384]{2,1,0:T(8,128)S(1)}, f32[2,384,384]{2,1,0:T(8,128)S(1)}, f32[2,16,384]{2,1,0:T(8,128)S(1)}) custom-call(f32[2,4,384]{2,1,0:T(4,128)S(1)} %copy-done.4, f32[384,384]{1,0:T(8,128)S(1)} %get-tuple-element.72.corr_ref, f32[2,192,384]{2,1,0:T(8,128)S(1)} %get-tuple-element.73.mine_ref, ...), custom_call_target="tpu_custom_call" | custom-call | flops 700000000 | bytes 4096 | tf_op jit(solution)/shard_map/own_segment/pallas_call | solution.py:53
  22.6 0.5 other_matrices.1
  23.1 2.3 %pair_covariance.1 = (f32[384,384]{1,0:T(8,128)S(1)}, f32[16,384]{1,0:T(8,128)S(1)}, f32[312,128]{1,0:T(8,128)S(1)}) custom-call(f32[2,384,384]{2,1,0:T(8,128)S(1)} %get-tuple-element.77.psi_ref, f32[2,384,384]{2,1,0:T(8,128)S(1)} %get-tuple-element.78.covar_ref, f32[2,16,384]{2,1,0:T(8,128)S(1)} %get-tuple-element.79.mean_ref, ...), custom_call_target="tpu_custom_call" | custom-call | bytes 4096 | tf_op jit(solution)/shard_map/pair_covariance/pallas_call | solution.py:53
  25.6 1.4 %pair_matrices.1 = (f32[384,384]{1,0:T(8,128)S(1)}, f32[384,384]{1,0:T(8,128)S(1)}, f32[192,384]{1,0:T(8,128)S(1)}) custom-call(f32[2,384,384]{2,1,0:T(8,128)S(1)} %get-tuple-element.88.matrix_other_ref.matrix_ref, f32[2,384,384]{2,1,0:T(8,128)S(1)} %get-tuple-element.77.psi_ref), custom_call_target="tpu_custom_call" | custom-call | bytes 4096 | tf_op jit(solution)/shard_map/pair_matrices/pallas_call | solution.py:53
  27.0 1.4 %collective-permute-start.13 = (f32[192,384]{1,0:T(8,128)S(1)}, f32[192,384]{1,0:T(8,128)S(1)}, u32[]{:S(2)}, u32[]{:S(2)}) collective-permute-start(f32[192,384]{1,0:T(8,128)S(1)} %get-tuple-element.97), channel_id=1, source_target_pairs={{0,2},{1,3},{2,0},{3,1},{4,6},{5,7},{6,4},{7,5},{8,10},{9,11},{10,... | collective-permute-start | bytes 884744 | tf_op jit(solution)/shard_map/ppermute | solution.py:538
  28.3 1.8 %pair_elements.1 = (f32[2,384,384]{2,1,0:T(8,128)S(1)}, f32[2,96,384]{2,1,0:T(8,128)S(1)}, f32[2,16,384]{2,1,0:T(8,128)S(1)}) custom-call(f32[2,384,384]{2,1,0:T(8,128)S(1)} %get-tuple-element.77.psi_ref, f32[2,384,384]{2,1,0:T(8,128)S(1)} %get-tuple-element.78.covar_ref, f32[2,16,384]{2,1,0:T(8,128)S(1)} %get-tuple-element.79.mean_ref, ...), custom_call_target="tpu_custom_call" | custom-call | bytes 4096 | tf_op jit(solution)/shard_map/pair_elements/pallas_call | solution.py:53
  30.1 0.5 collective-permute-done.9.refs_0_
  30.6 2.3 %collective-permute-start.10 = (f32[312,128]{1,0:T(8,128)S(1)}, f32[312,128]{1,0:T(8,128)S(1)}, u32[]{:S(2)}, u32[]{:S(2)}) collective-permute-start(f32[312,128]{1,0:T(8,128)S(1)} %collective-permute-done.9.refs_0_), channel_id=1, source_target_pairs={{0,1},{1,0},{2,3},{3,2},{4,5},{5,4},{6,7},{7,6},{8,9},{9,8},{10,11... | collective-permute-start | bytes 479240 | tf_op jit(solution)/shard_map/ppermute | solution.py:525
  32.9 1.0 %collective-permute-done.10.refs_1_ = f32[312,128]{1,0:T(8,128)S(1)} collective-permute-done((f32[312,128]{1,0:T(8,128)S(1)}, f32[312,128]{1,0:T(8,128)S(1)}, u32[]{:S(2)}, u32[]{:S(2)}) %collective-permute-start.10) | collective-permute-done | bytes 159776 | tf_op jit(solution)/shard_map/ppermute | solution.py:525
  34.2 0.8 %collective-permute-start.12 = (f32[312,128]{1,0:T(8,128)S(1)}, f32[312,128]{1,0:T(8,128)S(1)}, u32[]{:S(2)}, u32[]{:S(2)}) collective-permute-start(f32[312,128]{1,0:T(8,128)S(1)} %joined_covariance.1), channel_id=1, source_target_pairs={{0,4},{1,5},{2,6},{3,7},{4,0},{5,1},{6,2},{7,3},{8,24},{9,25},{10,... | collective-permute-start | bytes 479240 | tf_op jit(solution)/shard_map/ppermute | solution.py:538
  34.9 1.3 %entered.1 = (f32[2,96,384]{2,1,0:T(8,128)S(1)}, f32[2,16,384]{2,1,0:T(8,128)S(1)}) custom-call(f32[2,384,384]{2,1,0:T(8,128)S(1)} %get-tuple-element.98.psi_ref, f32[2,96,384]{2,1,0:T(8,128)S(1)} %get-tuple-element.100.covar_ref, f32[2,16,384]{2,1,0:T(8,128)S(1)} %get-tuple-element.101.mean_ref, f32[312,128]{1,0:T(8,128)S(1)} %collective-permute-done.9.refs_0_, ...), custom_call_target="tpu_custom_call" | custom-call | bytes 4096 | tf_op jit(solution)/shard_map/entered/pallas_call | solution.py:53
  36.2 0.7 %collective-permute-done.13.refs_0_ = f32[192,384]{1,0:T(8,128)S(1)} collective-permute-done((f32[192,384]{1,0:T(8,128)S(1)}, f32[192,384]{1,0:T(8,128)S(1)}, u32[]{:S(2)}, u32[]{:S(2)}) %collective-permute-start.13) | collective-permute-done | bytes 294944 | tf_op jit(solution)/shard_map/ppermute | solution.py:538
  36.9 1.4 %collective-permute-start.14 = (f32[96,384]{1,0:T(8,128)S(1)}, f32[96,384]{1,0:T(8,128)S(1)}, u32[]{:S(2)}, u32[]{:S(2)}) collective-permute-start(f32[96,384]{1,0:T(8,128)S(1)} %get-tuple-element.113), channel_id=1, source_target_pairs={{0,1},{1,0},{2,3},{3,2},{4,5},{5,4},{6,7},{7,6},{8,9},{9,8},{10,11... | collective-permute-start | bytes 442376 | tf_op jit(solution)/shard_map/ppermute | solution.py:525
  38.4 0.9 %collective-permute-done.14.refs_1_ = f32[96,384]{1,0:T(8,128)S(1)} collective-permute-done((f32[96,384]{1,0:T(8,128)S(1)}, f32[96,384]{1,0:T(8,128)S(1)}, u32[]{:S(2)}, u32[]{:S(2)}) %collective-permute-start.14) | collective-permute-done | bytes 147488 | tf_op jit(solution)/shard_map/ppermute | solution.py:525
  39.7 1.2 %matrices_entered.1.psi_ref = f32[2,384,384]{2,1,0:T(8,128)S(1)} custom-call(f32[2,384,384]{2,1,0:T(8,128)S(1)} %get-tuple-element.98.psi_ref, f32[192,384]{1,0:T(8,128)S(1)} %collective-permute-done.13.refs_0_, f32[96,384]{1,0:T(8,128)S(1)} %collective-permute-done.14.refs_1_, f32[96,384]{1,0:T(8,128)S(1)} %collective-permute-done.15.refs_2_), custom_call_target="tpu_custom_call" | custom-call | bytes 4096 | tf_op jit(solution)/shard_map/matrices_entered/pallas_call | solution.py:53
  40.9 1.3 %collective-permute-done.12.refs_1_ = f32[312,128]{1,0:T(8,128)S(1)} collective-permute-done((f32[312,128]{1,0:T(8,128)S(1)}, f32[312,128]{1,0:T(8,128)S(1)}, u32[]{:S(2)}, u32[]{:S(2)}) %collective-permute-start.12) | collective-permute-done | bytes 159776 | tf_op jit(solution)/shard_map/ppermute | solution.py:538
  42.2 1.2 %collective-permute-start.16 = (f32[312,128]{1,0:T(8,128)S(1)}, f32[312,128]{1,0:T(8,128)S(1)}, u32[]{:S(2)}, u32[]{:S(2)}) collective-permute-start(f32[312,128]{1,0:T(8,128)S(1)} %collective-permute-done.11.refs_0_), channel_id=1, source_target_pairs={{0,1},{1,0},{2,3},{3,2},{4,5},{5,4},{6,7},{7,6},{8,9},{9,8},{10,11... | collective-permute-start | bytes 479240 | tf_op jit(solution)/shard_map/ppermute | solution.py:525
  43.4 1.0 %collective-permute-done.16.refs_2_ = f32[312,128]{1,0:T(8,128)S(1)} collective-permute-done((f32[312,128]{1,0:T(8,128)S(1)}, f32[312,128]{1,0:T(8,128)S(1)}, u32[]{:S(2)}, u32[]{:S(2)}) %collective-permute-start.16) | collective-permute-done | bytes 159776 | tf_op jit(solution)/shard_map/ppermute | solution.py:525
  44.8 1.8 %finished.1 = (f32[2,96,384]{2,1,0:T(8,128)}, f32[2,384]{1,0:T(2,128)}) custom-call(f32[2,384,384]{2,1,0:T(8,128)S(1)} %matrices_entered.1.psi_ref, f32[2,96,384]{2,1,0:T(8,128)S(1)} %get-tuple-element.106.covar_ref, f32[2,16,384]{2,1,0:T(8,128)S(1)} %get-tuple-element.107.mean_ref, f32[312,128]{1,0:T(8,128)S(1)} %collective-permute-done.11.refs_0_, ...), custom_call_target="tpu_custom_call" | custom-call | bytes 4096 | tf_op jit(solution)/shard_map/finished/pallas_call | solution.py:53
  (35 shorter events, 2.7 us)
Async XLA Ops:
  0.6 6.2 %copy-start = (f32[384,1024]{1,0:T(8,128)S(1)}, f32[384,1024]{1,0:T(8,128)}, u32[]{:S(2)}) copy-start(f32[384,1024]{1,0:T(8,128)} %gain_ref) | copy-start | bytes 4718596
  0.6 6.2 %copy-start.5 = (f32[1024]{0:T(1024)S(1)}, f32[1024]{0:T(1024)}, u32[]{:S(2)}) copy-start(f32[1024]{0:T(1024)} %param.15) | copy-start | bytes 12292
  0.7 6.2 %copy-start.1 = (f32[384,384]{1,0:T(8,128)S(1)}, f32[384,384]{1,0:T(8,128)}, u32[]{:S(2)}) copy-start(f32[384,384]{1,0:T(8,128)} %factor_ref.1) | copy-start | bytes 1769476
  0.7 9.3 %collective-permute-start = (f32[2,96,384]{2,1,0:T(8,128)}, f32[2,96,384]{2,1,0:T(8,128)S(1)}, u32[]{:S(2)}, u32[]{:S(2)}) collective-permute-start(f32[2,96,384]{2,1,0:T(8,128)} %refs_4_), channel_id=1, source_target_pairs={{0,2},{1,3},{2,0},{3,1},{4,6},{5,7},{6,4},{7,5},{8,10},{9,11},{10,... | collective-permute-start | bytes 884744 | tf_op jit(solution)/shard_map/ppermute | solution.py:525
  1.9 8.0 %collective-permute-start.1 = (f32[2,96,384]{2,1,0:T(8,128)}, f32[2,96,384]{2,1,0:T(8,128)S(1)}, u32[]{:S(2)}, u32[]{:S(2)}) collective-permute-start(f32[2,96,384]{2,1,0:T(8,128)} %refs_4_), channel_id=1, source_target_pairs={{0,4},{4,0},{8,12},{12,8},{16,20},{20,16},{24,28},{28,24},{1,5},{5... | collective-permute-start | bytes 884744 | tf_op jit(solution)/shard_map/ppermute | solution.py:525
  5.3 5.0 %copy-start.3 = (f32[96,384]{1,0:T(8,128)S(1)}, f32[96,384]{1,0:T(8,128)}, u32[]{:S(2)}) copy-start(f32[96,384]{1,0:T(8,128)} %get-tuple-element.64.refs_0_) | copy-start | bytes 442372
  5.3 9.3 %copy-start.2 = (f32[2,96,384]{2,1,0:T(8,128)S(1)}, f32[2,96,384]{2,1,0:T(8,128)}, u32[]{:S(2)}) copy-start(f32[2,96,384]{2,1,0:T(8,128)} %refs_4_) | copy-start | bytes 884740
  5.3 9.3 %copy-start.4 = (f32[2,4,384]{2,1,0:T(4,128)S(1)}, f32[2,4,384]{2,1,0:T(4,128)}, u32[]{:S(2)}) copy-start(f32[2,4,384]{2,1,0:T(4,128)} %get-tuple-element.57.vec_ref) | copy-start | bytes 36868
  5.3 7.3 %collective-permute-start.4 = (f32[96,384]{1,0:T(8,128)}, f32[96,384]{1,0:T(8,128)S(1)}, u32[]{:S(2)}, u32[]{:S(2)}) collective-permute-start(f32[96,384]{1,0:T(8,128)} %get-tuple-element.64.refs_0_), channel_id=1, source_target_pairs={{0,2},{1,3},{2,0},{3,1},{4,6},{5,7},{6,4},{7,5},{8,10},{9,11},{10,... | collective-permute-start | bytes 442376 | tf_op jit(solution)/shard_map/ppermute | solution.py:525
  5.7 4.3 %collective-permute-start.2 = (f32[2,4,384]{2,1,0:T(4,128)}, f32[2,4,384]{2,1,0:T(4,128)S(1)}, u32[]{:S(2)}, u32[]{:S(2)}) collective-permute-start(f32[2,4,384]{2,1,0:T(4,128)} %get-tuple-element.57.vec_ref), channel_id=1, source_target_pairs={{0,4},{4,0},{8,12},{12,8},{16,20},{20,16},{24,28},{28,24},{1,5},{5... | collective-permute-start | bytes 36872 | tf_op jit(solution)/shard_map/ppermute | solution.py:525
  10.0 7.8 %collective-permute-start.3 = (f32[2,96,384]{2,1,0:T(8,128)S(1)}, f32[2,96,384]{2,1,0:T(8,128)S(1)}, u32[]{:S(2)}, u32[]{:S(2)}) collective-permute-start(f32[2,96,384]{2,1,0:T(8,128)S(1)} %collective-permute-done.refs_5_), channel_id=1, source_target_pairs={{0,4},{4,0},{8,12},{12,8},{16,20},{20,16},{24,28},{28,24},{1,5},{5... | collective-permute-start | bytes 884744 | tf_op jit(solution)/shard_map/ppermute | solution.py:525
  10.2 3.4 %collective-permute-start.5 = (f32[96,384]{1,0:T(8,128)S(1)}, f32[96,384]{1,0:T(8,128)S(1)}, u32[]{:S(2)}, u32[]{:S(2)}) collective-permute-start(f32[96,384]{1,0:T(8,128)S(1)} %copy-done.3), channel_id=1, source_target_pairs={{0,1},{1,0},{2,3},{3,2},{4,5},{5,4},{6,7},{7,6},{8,9},{9,8},{10,11... | collective-permute-start | bytes 442376 | tf_op jit(solution)/shard_map/ppermute | solution.py:525
  12.6 2.0 %collective-permute-start.6 = (f32[96,384]{1,0:T(8,128)S(1)}, f32[96,384]{1,0:T(8,128)S(1)}, u32[]{:S(2)}, u32[]{:S(2)}) collective-permute-start(f32[96,384]{1,0:T(8,128)S(1)} %collective-permute-done.4.refs_1_), channel_id=1, source_target_pairs={{0,1},{1,0},{2,3},{3,2},{4,5},{5,4},{6,7},{7,6},{8,9},{9,8},{10,11... | collective-permute-start | bytes 442376 | tf_op jit(solution)/shard_map/ppermute | solution.py:525
  15.4 4.7 %collective-permute-start.7 = (f32[2,192,384]{2,1,0:T(8,128)S(1)}, f32[2,192,384]{2,1,0:T(8,128)S(1)}, u32[]{:S(2)}, u32[]{:S(2)}) collective-permute-start(f32[2,192,384]{2,1,0:T(8,128)S(1)} %get-tuple-element.73.mine_ref), channel_id=1, source_target_pairs={{0,1},{1,0},{2,3},{3,2},{4,5},{5,4},{6,7},{7,6},{8,9},{9,8},{10,11... | collective-permute-start | bytes 1769480 | tf_op jit(solution)/shard_map/ppermute | solution.py:525
  17.8 2.3 %copy-start.6 = (f32[384]{0:T(512)S(1)}, f32[384]{0:T(512)}, u32[]{:S(2)}) copy-start(f32[384]{0:T(512)} %param.18) | copy-start | bytes 4612
  18.5 4.1 %collective-permute-start.8 = (f32[2,192,384]{2,1,0:T(8,128)S(1)}, f32[2,192,384]{2,1,0:T(8,128)S(1)}, u32[]{:S(2)}, u32[]{:S(2)}) collective-permute-start(f32[2,192,384]{2,1,0:T(8,128)S(1)} %other_rows.1.mine_ref), channel_id=1, source_target_pairs={{0,1},{1,0},{2,3},{3,2},{4,5},{5,4},{6,7},{7,6},{8,9},{9,8},{10,11... | collective-permute-start | bytes 1769480 | tf_op jit(solution)/shard_map/ppermute | solution.py:525
  25.3 5.3 %collective-permute-start.9 = (f32[312,128]{1,0:T(8,128)S(1)}, f32[312,128]{1,0:T(8,128)S(1)}, u32[]{:S(2)}, u32[]{:S(2)}) collective-permute-start(f32[312,128]{1,0:T(8,128)S(1)} %get-tuple-element.95.total_ref), channel_id=1, source_target_pairs={{0,8},{1,9},{2,10},{3,11},{4,12},{5,13},{6,14},{7,15},{8,0},{9,1},... | collective-permute-start | bytes 479240 | tf_op jit(solution)/shard_map/ppermute | solution.py:538
  27.0 10.0 %collective-permute-start.13 = (f32[192,384]{1,0:T(8,128)S(1)}, f32[192,384]{1,0:T(8,128)S(1)}, u32[]{:S(2)}, u32[]{:S(2)}) collective-permute-start(f32[192,384]{1,0:T(8,128)S(1)} %get-tuple-element.97), channel_id=1, source_target_pairs={{0,2},{1,3},{2,0},{3,1},{4,6},{5,7},{6,4},{7,5},{8,10},{9,11},{10,... | collective-permute-start | bytes 884744 | tf_op jit(solution)/shard_map/ppermute | solution.py:538
  30.6 3.3 %collective-permute-start.10 = (f32[312,128]{1,0:T(8,128)S(1)}, f32[312,128]{1,0:T(8,128)S(1)}, u32[]{:S(2)}, u32[]{:S(2)}) collective-permute-start(f32[312,128]{1,0:T(8,128)S(1)} %collective-permute-done.9.refs_0_), channel_id=1, source_target_pairs={{0,1},{1,0},{2,3},{3,2},{4,5},{5,4},{6,7},{7,6},{8,9},{9,8},{10,11... | collective-permute-start | bytes 479240 | tf_op jit(solution)/shard_map/ppermute | solution.py:525
  33.9 7.0 %collective-permute-start.11 = (f32[312,128]{1,0:T(8,128)S(1)}, f32[312,128]{1,0:T(8,128)S(1)}, u32[]{:S(2)}, u32[]{:S(2)}) collective-permute-start(f32[312,128]{1,0:T(8,128)S(1)} %joined_covariance.1), channel_id=1, source_target_pairs={{0,2},{1,3},{2,0},{3,1},{4,6},{5,7},{6,4},{7,5},{8,16},{9,17},{10,... | collective-permute-start | bytes 479240 | tf_op jit(solution)/shard_map/ppermute | solution.py:538
  34.2 8.1 %collective-permute-start.12 = (f32[312,128]{1,0:T(8,128)S(1)}, f32[312,128]{1,0:T(8,128)S(1)}, u32[]{:S(2)}, u32[]{:S(2)}) collective-permute-start(f32[312,128]{1,0:T(8,128)S(1)} %joined_covariance.1), channel_id=1, source_target_pairs={{0,4},{1,5},{2,6},{3,7},{4,0},{5,1},{6,2},{7,3},{8,24},{9,25},{10,... | collective-permute-start | bytes 479240 | tf_op jit(solution)/shard_map/ppermute | solution.py:538
  36.9 2.4 %collective-permute-start.14 = (f32[96,384]{1,0:T(8,128)S(1)}, f32[96,384]{1,0:T(8,128)S(1)}, u32[]{:S(2)}, u32[]{:S(2)}) collective-permute-start(f32[96,384]{1,0:T(8,128)S(1)} %get-tuple-element.113), channel_id=1, source_target_pairs={{0,1},{1,0},{2,3},{3,2},{4,5},{5,4},{6,7},{7,6},{8,9},{9,8},{10,11... | collective-permute-start | bytes 442376 | tf_op jit(solution)/shard_map/ppermute | solution.py:525
  38.3 1.4 %collective-permute-start.15 = (f32[96,384]{1,0:T(8,128)S(1)}, f32[96,384]{1,0:T(8,128)S(1)}, u32[]{:S(2)}, u32[]{:S(2)}) collective-permute-start(f32[96,384]{1,0:T(8,128)S(1)} %get-tuple-element.112), channel_id=1, source_target_pairs={{0,1},{1,0},{2,3},{3,2},{4,5},{5,4},{6,7},{7,6},{8,9},{9,8},{10,11... | collective-permute-start | bytes 442376 | tf_op jit(solution)/shard_map/ppermute | solution.py:525
  42.2 2.2 %collective-permute-start.16 = (f32[312,128]{1,0:T(8,128)S(1)}, f32[312,128]{1,0:T(8,128)S(1)}, u32[]{:S(2)}, u32[]{:S(2)}) collective-permute-start(f32[312,128]{1,0:T(8,128)S(1)} %collective-permute-done.11.refs_0_), channel_id=1, source_target_pairs={{0,1},{1,0},{2,3},{3,2},{4,5},{5,4},{6,7},{7,6},{8,9},{9,8},{10,11... | collective-permute-start | bytes 479240 | tf_op jit(solution)/shard_map/ppermute | solution.py:525
  43.4 1.4 %collective-permute-start.17 = (f32[312,128]{1,0:T(8,128)S(1)}, f32[312,128]{1,0:T(8,128)S(1)}, u32[]{:S(2)}, u32[]{:S(2)}) collective-permute-start(f32[312,128]{1,0:T(8,128)S(1)} %collective-permute-done.12.refs_1_), channel_id=1, source_target_pairs={{0,1},{1,0},{2,3},{3,2},{4,5},{5,4},{6,7},{7,6},{8,9},{9,8},{10,11... | collective-permute-start | bytes 479240 | tf_op jit(solution)/shard_map/ppermute | solution.py:525

commit v8 on v7

--- a/solution.py
+++ b/solution.py
@@ -38,10 +38,28 @@
     return lax.dot_general(as_left(left), as_right(right, 1), NT, preferred_element_type=F32)
 
 
+def few_rows_dot(left, right, kind):
+    rows = left.shape[0]
+    left, right = parts(left), parts(right)
+    both = lax.dot_general(jnp.concatenate(left, axis=0), right[0], kind, preferred_element_type=F32)
+    return both[:rows] + (both[rows:] + lax.dot_general(left[0], right[1], kind, preferred_element_type=F32))
+
+
+def stacked(left, right):
+    return lax.dot_general(left, right, NT, preferred_element_type=F32)
+
+
 def square(step, covar, mean):
     rows = covar.shape[0]
-    both = dot_nt(jnp.concatenate([dot_nn(step, covar), mean], axis=0), step)
-    return both[:rows], both[rows:]
+    edge = rows // 3
+    half = dot_nn(step, covar)
+    right = as_right(step, 1)
+    top = stacked(as_left(half[: 2 * edge]), right[: 2 * edge])
+    low = stacked(as_left(jnp.concatenate([half[2 * edge :], mean], axis=0)), right)
+    block, last = top[edge:, :edge], low[:edge, : 2 * edge]
+    first = jnp.concatenate([top[:edge, :edge], block.T, last[:, :edge].T], axis=1)
+    second = jnp.concatenate([block, top[edge:, edge:], last[:, edge:].T], axis=1)
+    return jnp.concatenate([first, second, low[:edge]], axis=0), low[edge:]
 
 
 def mean_block(row, states):
@@ -210,18 +228,6 @@
         mean_ref[k] = mean + offset_ref[k]
 
 
-def other_matrices(
-    offsets, vec_ref, corr_ref, mine_ref, mate_ref, prior_ref, start_ref, matrix_ref, covar_ref, mean_ref, work_ref
-):
-    matrices_of(offsets, vec_ref, corr_ref[...], mine_ref, mate_ref, work_ref, matrix_ref)
-    covar_ref[...] = jnp.zeros_like(covar_ref)
-    mean_ref[...] = jnp.zeros_like(mean_ref)
-
-    @pl.when(lax.axis_index("seg") == 1)
-    def _():
-        add_prior(matrix_ref, prior_ref, start_ref, covar_ref, mean_ref)
-
-
 def share_rows(edge):
     return 2 * edge + edge * 3 // 8 + 8
 
@@ -312,19 +318,24 @@
 
 
 def pair_covariance(
-    steps, psi_ref, covar_ref, mean_ref, noise_other_ref, offset_other_ref, matrix_other_ref, first_other_ref,
-    first_mean_other_ref, covar_other_ref, mean_other_ref, out_ref, step_ref,
+    offsets, vec_ref, corr_ref, mine_ref, mate_ref, prior_ref, start_ref, psi_ref, covar_ref, mean_ref,
+    noise_other_ref, offset_other_ref, matrix_other_ref, covar_other_ref, mean_other_ref, out_ref, step_ref, work_ref,
 ):
-    states = first_other_ref.shape[0]
-    edge = states // 3
-    is_second = lax.rem(lax.axis_index("seg"), 2) == 1
+    steps, states = matrix_other_ref.shape[:2]
+    seg = lax.axis_index("seg")
+    is_second = lax.rem(seg, 2) == 1
     last = steps - 1
+    matrices_of(offsets, vec_ref, corr_ref[...], mine_ref, mate_ref, work_ref, matrix_other_ref)
 
     @pl.when(is_second)
     def _():
-        covar_other_ref[...] = noise_other_ref[0] + first_other_ref[...]
-        mean_other_ref[...] = offset_other_ref[0] + first_mean_other_ref[...]
+        covar_other_ref[...] = noise_other_ref[0]
+        mean_other_ref[...] = offset_other_ref[0]
         step_ref[...] = psi_ref[last]
+
+    @pl.when(seg == 1)
+    def _():
+        add_prior(matrix_other_ref, prior_ref, start_ref, covar_other_ref, mean_other_ref)
 
     @pl.when(jnp.logical_not(is_second))
     def _():
@@ -507,10 +518,10 @@
         mate_ref[...] = chosen(mates, bit)
         mean = unpacked(mine_ref, mate_ref, work_ref)
         rows = jnp.concatenate([psi_ref[k, mine, :] for k in range(steps)], axis=0)
-        half = dot_nn(rows, work_ref[...])
+        half = few_rows_dot(rows, work_ref[...], NN)
         for k in range(steps):
             part = half[k * width : (k + 1) * width]
-            both = dot_nt(jnp.concatenate([part, mean], axis=0), psi_ref[k])
+            both = few_rows_dot(jnp.concatenate([part, mean], axis=0), psi_ref[k], NT)
             covar_out_ref[k] = both[:width] + covar_ref[k]
             mean_out_ref[k : k + 1, :] = both[width : width + 1] + mean_ref[k, :1, :]
 
@@ -528,14 +539,14 @@
 def handed_up(block, bit, first=0):
     n_seg, n_col = lax.axis_size("seg"), lax.axis_size("col")
     came = []
-    for group in range(bit // 2):
+    for group in reversed(range(bit // 2)):
         aside = n_col // 2 if group % 2 == 0 else n_col
         to = {i: i ^ aside for i in range(n_seg * n_col)}
         for low in range(first * 2 * bit, n_seg, 2 * bit):
             for i in range((low + bit - 2) * n_col, (low + bit) * n_col):
                 j = i + (2 + 2 * group) * n_col
                 to[i], to[j] = j, i
-        came.append(lax.ppermute(block, ("seg", "col"), sorted(to.items())))
+        came.insert(0, lax.ppermute(block, ("seg", "col"), sorted(to.items())))
     return came
 
 
@@ -628,30 +639,22 @@
         scratch=[square_shape],
         cost=1,
     )
-    matrix_other, first_other, first_mean_other = local_call(
-        functools.partial(other_matrices, offsets),
-        [(steps,) + square_shape, square_shape, mean_shape],
+    bit = 2
+    more = 2 * bit < n_seg
+    matrix_other, covar_other, mean_other, total = local_call(
+        functools.partial(pair_covariance, offsets),
+        [(steps,) + square_shape, square_shape, mean_shape, share_shape],
         vectors_other,
         correction,
         *with_mate(rows_other),
         prior,
         start,
-        scratch=[square_shape],
-    )
-    bit = 2
-    more = 2 * bit < n_seg
-    covar_other, mean_other, total = local_call(
-        functools.partial(pair_covariance, steps),
-        [square_shape, mean_shape, share_shape],
         psi,
         covar,
         mean,
         noise_other,
         offset_other,
-        matrix_other,
-        first_other,
-        first_mean_other,
-        scratch=[square_shape],
+        scratch=[square_shape, square_shape],
     )
     came = handed_up(total, bit)
     matrix_other, total = lax.optimization_barrier((matrix_other, total))

time: 46.8 us -> 46.5 us (level)
    pallas_call x15 -> x14, Pallas kernels: 20.7 us -> 20.4 us  [local_call(): pl.pallas_call(body, out_shape=shapes, name=getattr(body, 'func', body)._...]
  transfers between devices with their start and end apart: 18 -> 18, of which waited for: 10 -> 10; matrix products, arithmetic and copies ran while one was open for 0% -> 0% of each run, Pallas kernels for 34% -> 35%
where the time goes in v8:
time: 46.5 us; the launch traced here: 46.3 us
  Pallas kernels  20.4 us (44%)
  starting transfers between devices  16.1 us (35%)
  waiting for transfers between devices  8.86 us (19%)
  between operations  0.82 us (2%)
    pallas_call x14, Pallas kernels, local_call(): pl.pallas_call(body, out_shape=shapes, name=getattr(body, 'func', body)._...  20.4 us
    ppermute x14, starting transfers between devices, swapped(): lax.ppermute(block, axis, [(i, i ^ bit) for i in range(lax.axis_size(axis...  13.5 us
    ppermute x14, waiting for transfers between devices, swapped(): lax.ppermute(block, axis, [(i, i ^ bit) for i in range(lax.axis_size(axis...  6.42 us
    ppermute x4, starting transfers between devices, handed_up(): came.insert(0, lax.ppermute(block, ('seg', 'col'), sorted(to.items())))  2.6 us
    ppermute x4, waiting for transfers between devices, handed_up(): came.insert(0, lax.ppermute(block, ('seg', 'col'), sorted(to.items())))  2.43 us
  transfers between devices with their start and end apart: 18, of which 10 were waited for; matrix products, arithmetic and copies ran while one was open for 0% of the time, Pallas kernels for 35%

profile of v8, /device:TPU:29, one launch (start us, length us, event | category | flops | bytes accessed | tf_op | source)
XLA Modules:
  0.0 46.3 jit_solution(3565447694680594862)
XLA Ops:
  0.7 1.3 %collective-permute-start = (f32[2,96,384]{2,1,0:T(8,128)}, f32[2,96,384]{2,1,0:T(8,128)S(1)}, u32[]{:S(2)}, u32[]{:S(2)}) collective-permute-start(f32[2,96,384]{2,1,0:T(8,128)} %refs_4_), channel_id=1, source_target_pairs={{0,2},{1,3},{2,0},{3,1},{4,6},{5,7},{6,4},{7,5},{8,10},{9,11},{10,... | collective-permute-start | bytes 884744 | tf_op jit(solution)/shard_map/ppermute | solution.py:536
  2.2 3.1 %correction_rows.1 = (f32[96,384]{1,0:T(8,128)}, f32[2,4,384]{2,1,0:T(4,128)}) custom-call(f32[384,1024]{1,0:T(8,128)} %gain_ref, f32[96,1024]{1,0:T(8,128)} %oper_hbm.1, f32[2,1024]{1,0:T(2,128)} %seen_hbm.1, f32[2,384]{1,0:T(2,128)} %keep_hbm.1, f32[2,384]{1,0:T(2,128)} %push_hbm.1, f32[2,384]{1,0:T(2,128)} %var_hbm.1), custom_call_target="tpu_custom_call" | custom-call | flops 2100000000 | bytes 4096 | tf_op jit(solution)/shard_map/correction_rows/pallas_call | solution.py:71
  5.7 1.2 %collective-permute-start.2 = (f32[2,4,384]{2,1,0:T(4,128)}, f32[2,4,384]{2,1,0:T(4,128)S(1)}, u32[]{:S(2)}, u32[]{:S(2)}) collective-permute-start(f32[2,4,384]{2,1,0:T(4,128)} %get-tuple-element.58.vec_ref), channel_id=1, source_target_pairs={{0,4},{4,0},{8,12},{12,8},{16,20},{20,16},{24,28},{28,24},{1,5},{5... | collective-permute-start | bytes 36872 | tf_op jit(solution)/shard_map/ppermute | solution.py:536
  6.9 1.4 %fixed_parts.1 = (f32[384,384]{1,0:T(8,128)S(1)}, f32[384,384]{1,0:T(8,128)S(1)}) custom-call(f32[384,1024]{1,0:T(8,128)S(1)} %copy-done, f32[1,1024]{1,0:T(1,128)S(1)} %bitcast.1, f32[384,384]{1,0:T(8,128)S(1)} %copy-done.1), custom_call_target="tpu_custom_call" | custom-call | bytes 4096 | tf_op jit(solution)/shard_map/fixed_parts/pallas_call | solution.py:71
  8.3 1.7 %collective-permute-done.2.vec_other_ref.vec_ref = f32[2,4,384]{2,1,0:T(4,128)S(1)} collective-permute-done((f32[2,4,384]{2,1,0:T(4,128)}, f32[2,4,384]{2,1,0:T(4,128)S(1)}, u32[]{:S(2)}, u32[]{:S(2)}) %collective-permute-start.2) | collective-permute-done | bytes 12320 | tf_op jit(solution)/shard_map/ppermute | solution.py:536
  10.2 2.4 %collective-permute-start.5 = (f32[96,384]{1,0:T(8,128)S(1)}, f32[96,384]{1,0:T(8,128)S(1)}, u32[]{:S(2)}, u32[]{:S(2)}) collective-permute-start(f32[96,384]{1,0:T(8,128)S(1)} %copy-done.3), channel_id=1, source_target_pairs={{0,1},{1,0},{2,3},{3,2},{4,5},{5,4},{6,7},{7,6},{8,9},{9,8},{10,11... | collective-permute-start | bytes 442376 | tf_op jit(solution)/shard_map/ppermute | solution.py:536
  12.6 1.0 %collective-permute-start.6 = (f32[96,384]{1,0:T(8,128)S(1)}, f32[96,384]{1,0:T(8,128)S(1)}, u32[]{:S(2)}, u32[]{:S(2)}) collective-permute-start(f32[96,384]{1,0:T(8,128)S(1)} %collective-permute-done.4.refs_1_), channel_id=1, source_target_pairs={{0,1},{1,0},{2,3},{3,2},{4,5},{5,4},{6,7},{7,6},{8,9},{9,8},{10,11... | collective-permute-start | bytes 442376 | tf_op jit(solution)/shard_map/ppermute | solution.py:536
  13.6 1.0 %collective-permute-done.6.refs_3_ = f32[96,384]{1,0:T(8,128)S(1)} collective-permute-done((f32[96,384]{1,0:T(8,128)S(1)}, f32[96,384]{1,0:T(8,128)S(1)}, u32[]{:S(2)}, u32[]{:S(2)}) %collective-permute-start.6) | collective-permute-done | bytes 147488 | tf_op jit(solution)/shard_map/ppermute | solution.py:536
  14.5 0.9 %own_rows.1 = (f32[384,384]{1,0:T(8,128)S(1)}, f32[2,192,384]{2,1,0:T(8,128)S(1)}, f32[2,384]{1,0:T(2,128)S(1)}, f32[2,384]{1,0:T(2,128)S(1)}) custom-call(f32[2,4,384]{2,1,0:T(4,128)S(1)} %copy-done.4, f32[2,4,384]{2,1,0:T(4,128)S(1)} %collective-permute-done.2.vec_other_ref.vec_ref, f32[96,384]{1,0:T(8,128)S(1)} %copy-done.3, ...), custom_call_target="tpu_custom_call" | custom-call | bytes 4096 | tf_op jit(solution)/shard_map/own_rows/pallas_call | solution.py:71
  15.4 0.4 collective-permute-start.8
  15.8 1.0 %noises.3 = (f32[2,384,384]{2,1,0:T(8,128)S(1)}, f32[2,16,384]{2,1,0:T(8,128)S(1)}) custom-call(f32[2,4,384]{2,1,0:T(4,128)S(1)} %collective-permute-done.2.vec_other_ref.vec_ref, f32[2,384]{1,0:T(2,128)S(1)} %get-tuple-element.68.push_ref, f32[384,384]{1,0:T(8,128)S(1)} %get-tuple-element.66.fixed_ref, f32[384,384]{1,0:T(8,128)S(1)} %get-tuple-element.70.corr_ref), custom_call_target="tpu_custom_call" | custom-call | bytes 4096 | tf_op jit(solution)/shard_map/noises/pallas_call | solution.py:71
  16.8 1.0 %noises.2 = (f32[2,384,384]{2,1,0:T(8,128)S(1)}, f32[2,16,384]{2,1,0:T(8,128)S(1)}) custom-call(f32[2,4,384]{2,1,0:T(4,128)S(1)} %copy-done.4, f32[2,384]{1,0:T(2,128)S(1)} %get-tuple-element.65.push_ref, f32[384,384]{1,0:T(8,128)S(1)} %get-tuple-element.66.fixed_ref, f32[384,384]{1,0:T(8,128)S(1)} %get-tuple-element.70.corr_ref), custom_call_target="tpu_custom_call" | custom-call | bytes 4096 | tf_op jit(solution)/shard_map/noises/pallas_call | solution.py:71
  17.9 0.7 %other_rows.1.mine_ref = f32[2,192,384]{2,1,0:T(8,128)S(1)} custom-call(f32[384,384]{1,0:T(8,128)S(1)} %get-tuple-element.70.corr_ref, f32[2,96,384]{2,1,0:T(8,128)S(1)} %collective-permute-done.1.refs_0_, f32[2,96,384]{2,1,0:T(8,128)S(1)} %collective-permute-done.3.refs_1_), custom_call_target="tpu_custom_call" | custom-call | bytes 4096 | tf_op jit(solution)/shard_map/other_rows/pallas_call | solution.py:71
  18.6 1.6 %collective-permute-start.7 = (f32[2,192,384]{2,1,0:T(8,128)S(1)}, f32[2,192,384]{2,1,0:T(8,128)S(1)}, u32[]{:S(2)}, u32[]{:S(2)}) collective-permute-start(f32[2,192,384]{2,1,0:T(8,128)S(1)} %other_rows.1.mine_ref), channel_id=1, source_target_pairs={{0,1},{1,0},{2,3},{3,2},{4,5},{5,4},{6,7},{7,6},{8,9},{9,8},{10,11... | collective-permute-start | bytes 1769480 | tf_op jit(solution)/shard_map/ppermute | solution.py:536
  20.2 2.3 %own_segment.1 = (f32[2,384,384]{2,1,0:T(8,128)}, f32[2,384,384]{2,1,0:T(8,128)S(1)}, f32[2,384,384]{2,1,0:T(8,128)S(1)}, f32[2,16,384]{2,1,0:T(8,128)S(1)}) custom-call(f32[2,4,384]{2,1,0:T(4,128)S(1)} %copy-done.4, f32[384,384]{1,0:T(8,128)S(1)} %get-tuple-element.70.corr_ref, f32[2,192,384]{2,1,0:T(8,128)S(1)} %get-tuple-element.74.mine_ref, ...), custom_call_target="tpu_custom_call" | custom-call | flops 700000000 | bytes 4096 | tf_op jit(solution)/shard_map/own_segment/pallas_call | solution.py:71
  22.5 2.6 %pair_covariance.1 = (f32[2,384,384]{2,1,0:T(8,128)S(1)}, f32[384,384]{1,0:T(8,128)S(1)}, f32[16,384]{1,0:T(8,128)S(1)}, f32[312,128]{1,0:T(8,128)S(1)}) custom-call(f32[2,4,384]{2,1,0:T(4,128)S(1)} %collective-permute-done.2.vec_other_ref.vec_ref, f32[384,384]{1,0:T(8,128)S(1)} %get-tuple-element.70.corr_ref, f32[2,192,384]{2,1,0:T(8,128)S(1)} %other_rows.1.mine_ref, ...), custom_call_target="tpu_custom_call" | custom-call | bytes 4096 | tf_op jit(solution)/shard_map/pair_covariance/pallas_call | solution.py:71
  25.3 1.4 %pair_matrices.1 = (f32[384,384]{1,0:T(8,128)S(1)}, f32[384,384]{1,0:T(8,128)S(1)}, f32[192,384]{1,0:T(8,128)S(1)}) custom-call(f32[2,384,384]{2,1,0:T(8,128)S(1)} %get-tuple-element.84.matrix_ref, f32[2,384,384]{2,1,0:T(8,128)S(1)} %get-tuple-element.77.psi_ref), custom_call_target="tpu_custom_call" | custom-call | bytes 4096 | tf_op jit(solution)/shard_map/pair_matrices/pallas_call | solution.py:71
  26.7 1.4 %collective-permute-start.13 = (f32[192,384]{1,0:T(8,128)S(1)}, f32[192,384]{1,0:T(8,128)S(1)}, u32[]{:S(2)}, u32[]{:S(2)}) collective-permute-start(f32[192,384]{1,0:T(8,128)S(1)} %get-tuple-element.93), channel_id=1, source_target_pairs={{0,2},{1,3},{2,0},{3,1},{4,6},{5,7},{6,4},{7,5},{8,10},{9,11},{10,... | collective-permute-start | bytes 884744 | tf_op jit(solution)/shard_map/ppermute | solution.py:549
  28.1 1.8 %pair_elements.1 = (f32[2,384,384]{2,1,0:T(8,128)S(1)}, f32[2,96,384]{2,1,0:T(8,128)S(1)}, f32[2,16,384]{2,1,0:T(8,128)S(1)}) custom-call(f32[2,384,384]{2,1,0:T(8,128)S(1)} %get-tuple-element.77.psi_ref, f32[2,384,384]{2,1,0:T(8,128)S(1)} %get-tuple-element.78.covar_ref, f32[2,16,384]{2,1,0:T(8,128)S(1)} %get-tuple-element.79.mean_ref, ...), custom_call_target="tpu_custom_call" | custom-call | bytes 4096 | tf_op jit(solution)/shard_map/pair_elements/pallas_call | solution.py:71
  29.9 0.4 collective-permute-done.9.refs_0_
  30.4 2.3 %collective-permute-start.10 = (f32[312,128]{1,0:T(8,128)S(1)}, f32[312,128]{1,0:T(8,128)S(1)}, u32[]{:S(2)}, u32[]{:S(2)}) collective-permute-start(f32[312,128]{1,0:T(8,128)S(1)} %collective-permute-done.9.refs_0_), channel_id=1, source_target_pairs={{0,1},{1,0},{2,3},{3,2},{4,5},{5,4},{6,7},{7,6},{8,9},{9,8},{10,11... | collective-permute-start | bytes 479240 | tf_op jit(solution)/shard_map/ppermute | solution.py:536
  32.6 1.0 %collective-permute-done.10.refs_1_ = f32[312,128]{1,0:T(8,128)S(1)} collective-permute-done((f32[312,128]{1,0:T(8,128)S(1)}, f32[312,128]{1,0:T(8,128)S(1)}, u32[]{:S(2)}, u32[]{:S(2)}) %collective-permute-start.10) | collective-permute-done | bytes 159776 | tf_op jit(solution)/shard_map/ppermute | solution.py:536
  33.9 0.8 %collective-permute-start.12 = (f32[312,128]{1,0:T(8,128)S(1)}, f32[312,128]{1,0:T(8,128)S(1)}, u32[]{:S(2)}, u32[]{:S(2)}) collective-permute-start(f32[312,128]{1,0:T(8,128)S(1)} %joined_covariance.1), channel_id=1, source_target_pairs={{0,4},{1,5},{2,6},{3,7},{4,0},{5,1},{6,2},{7,3},{8,24},{9,25},{10,... | collective-permute-start | bytes 479240 | tf_op jit(solution)/shard_map/ppermute | solution.py:549
  34.7 1.3 %entered.1 = (f32[2,96,384]{2,1,0:T(8,128)S(1)}, f32[2,16,384]{2,1,0:T(8,128)S(1)}) custom-call(f32[2,384,384]{2,1,0:T(8,128)S(1)} %get-tuple-element.94.psi_ref, f32[2,96,384]{2,1,0:T(8,128)S(1)} %get-tuple-element.96.covar_ref, f32[2,16,384]{2,1,0:T(8,128)S(1)} %get-tuple-element.97.mean_ref, f32[312,128]{1,0:T(8,128)S(1)} %collective-permute-done.9.refs_0_, ...), custom_call_target="tpu_custom_call" | custom-call | bytes 4096 | tf_op jit(solution)/shard_map/entered/pallas_call | solution.py:71
  35.9 0.7 %collective-permute-done.13.refs_0_ = f32[192,384]{1,0:T(8,128)S(1)} collective-permute-done((f32[192,384]{1,0:T(8,128)S(1)}, f32[192,384]{1,0:T(8,128)S(1)}, u32[]{:S(2)}, u32[]{:S(2)}) %collective-permute-start.13) | collective-permute-done | bytes 294944 | tf_op jit(solution)/shard_map/ppermute | solution.py:549
  36.7 1.4 %collective-permute-start.14 = (f32[96,384]{1,0:T(8,128)S(1)}, f32[96,384]{1,0:T(8,128)S(1)}, u32[]{:S(2)}, u32[]{:S(2)}) collective-permute-start(f32[96,384]{1,0:T(8,128)S(1)} %get-tuple-element.109), channel_id=1, source_target_pairs={{0,1},{1,0},{2,3},{3,2},{4,5},{5,4},{6,7},{7,6},{8,9},{9,8},{10,11... | collective-permute-start | bytes 442376 | tf_op jit(solution)/shard_map/ppermute | solution.py:536
  38.2 0.9 %collective-permute-done.14.refs_1_ = f32[96,384]{1,0:T(8,128)S(1)} collective-permute-done((f32[96,384]{1,0:T(8,128)S(1)}, f32[96,384]{1,0:T(8,128)S(1)}, u32[]{:S(2)}, u32[]{:S(2)}) %collective-permute-start.14) | collective-permute-done | bytes 147488 | tf_op jit(solution)/shard_map/ppermute | solution.py:536
  39.5 1.2 %matrices_entered.1.psi_ref = f32[2,384,384]{2,1,0:T(8,128)S(1)} custom-call(f32[2,384,384]{2,1,0:T(8,128)S(1)} %get-tuple-element.94.psi_ref, f32[192,384]{1,0:T(8,128)S(1)} %collective-permute-done.13.refs_0_, f32[96,384]{1,0:T(8,128)S(1)} %collective-permute-done.14.refs_1_, f32[96,384]{1,0:T(8,128)S(1)} %collective-permute-done.15.refs_2_), custom_call_target="tpu_custom_call" | custom-call | bytes 4096 | tf_op jit(solution)/shard_map/matrices_entered/pallas_call | solution.py:71
  40.7 1.3 %collective-permute-done.12.refs_1_ = f32[312,128]{1,0:T(8,128)S(1)} collective-permute-done((f32[312,128]{1,0:T(8,128)S(1)}, f32[312,128]{1,0:T(8,128)S(1)}, u32[]{:S(2)}, u32[]{:S(2)}) %collective-permute-start.12) | collective-permute-done | bytes 159776 | tf_op jit(solution)/shard_map/ppermute | solution.py:549
  41.9 1.2 %collective-permute-start.16 = (f32[312,128]{1,0:T(8,128)S(1)}, f32[312,128]{1,0:T(8,128)S(1)}, u32[]{:S(2)}, u32[]{:S(2)}) collective-permute-start(f32[312,128]{1,0:T(8,128)S(1)} %collective-permute-done.11.refs_0_), channel_id=1, source_target_pairs={{0,1},{1,0},{2,3},{3,2},{4,5},{5,4},{6,7},{7,6},{8,9},{9,8},{10,11... | collective-permute-start | bytes 479240 | tf_op jit(solution)/shard_map/ppermute | solution.py:536
  43.1 1.0 %collective-permute-done.16.refs_2_ = f32[312,128]{1,0:T(8,128)S(1)} collective-permute-done((f32[312,128]{1,0:T(8,128)S(1)}, f32[312,128]{1,0:T(8,128)S(1)}, u32[]{:S(2)}, u32[]{:S(2)}) %collective-permute-start.16) | collective-permute-done | bytes 159776 | tf_op jit(solution)/shard_map/ppermute | solution.py:536
  44.5 1.7 %finished.1 = (f32[2,96,384]{2,1,0:T(8,128)}, f32[2,384]{1,0:T(2,128)}) custom-call(f32[2,384,384]{2,1,0:T(8,128)S(1)} %matrices_entered.1.psi_ref, f32[2,96,384]{2,1,0:T(8,128)S(1)} %get-tuple-element.102.covar_ref, f32[2,16,384]{2,1,0:T(8,128)S(1)} %get-tuple-element.103.mean_ref, f32[312,128]{1,0:T(8,128)S(1)} %collective-permute-done.11.refs_0_, ...), custom_call_target="tpu_custom_call" | custom-call | bytes 4096 | tf_op jit(solution)/shard_map/finished/pallas_call | solution.py:71
  (34 shorter events, 2.3 us)
Async XLA Ops:
  0.6 6.2 %copy-start = (f32[384,1024]{1,0:T(8,128)S(1)}, f32[384,1024]{1,0:T(8,128)}, u32[]{:S(2)}) copy-start(f32[384,1024]{1,0:T(8,128)} %gain_ref) | copy-start | bytes 4718596
  0.6 6.2 %copy-start.5 = (f32[1024]{0:T(1024)S(1)}, f32[1024]{0:T(1024)}, u32[]{:S(2)}) copy-start(f32[1024]{0:T(1024)} %param.15) | copy-start | bytes 12292
  0.7 6.2 %copy-start.1 = (f32[384,384]{1,0:T(8,128)S(1)}, f32[384,384]{1,0:T(8,128)}, u32[]{:S(2)}) copy-start(f32[384,384]{1,0:T(8,128)} %factor_ref.1) | copy-start | bytes 1769476
  0.7 9.3 %collective-permute-start = (f32[2,96,384]{2,1,0:T(8,128)}, f32[2,96,384]{2,1,0:T(8,128)S(1)}, u32[]{:S(2)}, u32[]{:S(2)}) collective-permute-start(f32[2,96,384]{2,1,0:T(8,128)} %refs_4_), channel_id=1, source_target_pairs={{0,2},{1,3},{2,0},{3,1},{4,6},{5,7},{6,4},{7,5},{8,10},{9,11},{10,... | collective-permute-start | bytes 884744 | tf_op jit(solution)/shard_map/ppermute | solution.py:536
  1.9 8.0 %collective-permute-start.1 = (f32[2,96,384]{2,1,0:T(8,128)}, f32[2,96,384]{2,1,0:T(8,128)S(1)}, u32[]{:S(2)}, u32[]{:S(2)}) collective-permute-start(f32[2,96,384]{2,1,0:T(8,128)} %refs_4_), channel_id=1, source_target_pairs={{0,4},{4,0},{8,12},{12,8},{16,20},{20,16},{24,28},{28,24},{1,5},{5... | collective-permute-start | bytes 884744 | tf_op jit(solution)/shard_map/ppermute | solution.py:536
  5.3 5.0 %copy-start.3 = (f32[96,384]{1,0:T(8,128)S(1)}, f32[96,384]{1,0:T(8,128)}, u32[]{:S(2)}) copy-start(f32[96,384]{1,0:T(8,128)} %get-tuple-element.62.refs_0_) | copy-start | bytes 442372
  5.3 9.3 %copy-start.2 = (f32[2,96,384]{2,1,0:T(8,128)S(1)}, f32[2,96,384]{2,1,0:T(8,128)}, u32[]{:S(2)}) copy-start(f32[2,96,384]{2,1,0:T(8,128)} %refs_4_) | copy-start | bytes 884740
  5.3 9.3 %copy-start.4 = (f32[2,4,384]{2,1,0:T(4,128)S(1)}, f32[2,4,384]{2,1,0:T(4,128)}, u32[]{:S(2)}) copy-start(f32[2,4,384]{2,1,0:T(4,128)} %get-tuple-element.58.vec_ref) | copy-start | bytes 36868
  5.3 7.3 %collective-permute-start.4 = (f32[96,384]{1,0:T(8,128)}, f32[96,384]{1,0:T(8,128)S(1)}, u32[]{:S(2)}, u32[]{:S(2)}) collective-permute-start(f32[96,384]{1,0:T(8,128)} %get-tuple-element.62.refs_0_), channel_id=1, source_target_pairs={{0,2},{1,3},{2,0},{3,1},{4,6},{5,7},{6,4},{7,5},{8,10},{9,11},{10,... | collective-permute-start | bytes 442376 | tf_op jit(solution)/shard_map/ppermute | solution.py:536
  5.7 4.3 %collective-permute-start.2 = (f32[2,4,384]{2,1,0:T(4,128)}, f32[2,4,384]{2,1,0:T(4,128)S(1)}, u32[]{:S(2)}, u32[]{:S(2)}) collective-permute-start(f32[2,4,384]{2,1,0:T(4,128)} %get-tuple-element.58.vec_ref), channel_id=1, source_target_pairs={{0,4},{4,0},{8,12},{12,8},{16,20},{20,16},{24,28},{28,24},{1,5},{5... | collective-permute-start | bytes 36872 | tf_op jit(solution)/shard_map/ppermute | solution.py:536
  10.0 7.9 %collective-permute-start.3 = (f32[2,96,384]{2,1,0:T(8,128)S(1)}, f32[2,96,384]{2,1,0:T(8,128)S(1)}, u32[]{:S(2)}, u32[]{:S(2)}) collective-permute-start(f32[2,96,384]{2,1,0:T(8,128)S(1)} %collective-permute-done.refs_5_), channel_id=1, source_target_pairs={{0,4},{4,0},{8,12},{12,8},{16,20},{20,16},{24,28},{28,24},{1,5},{5... | collective-permute-start | bytes 884744 | tf_op jit(solution)/shard_map/ppermute | solution.py:536
  10.2 3.4 %collective-permute-start.5 = (f32[96,384]{1,0:T(8,128)S(1)}, f32[96,384]{1,0:T(8,128)S(1)}, u32[]{:S(2)}, u32[]{:S(2)}) collective-permute-start(f32[96,384]{1,0:T(8,128)S(1)} %copy-done.3), channel_id=1, source_target_pairs={{0,1},{1,0},{2,3},{3,2},{4,5},{5,4},{6,7},{7,6},{8,9},{9,8},{10,11... | collective-permute-start | bytes 442376 | tf_op jit(solution)/shard_map/ppermute | solution.py:536
  12.6 2.0 %collective-permute-start.6 = (f32[96,384]{1,0:T(8,128)S(1)}, f32[96,384]{1,0:T(8,128)S(1)}, u32[]{:S(2)}, u32[]{:S(2)}) collective-permute-start(f32[96,384]{1,0:T(8,128)S(1)} %collective-permute-done.4.refs_1_), channel_id=1, source_target_pairs={{0,1},{1,0},{2,3},{3,2},{4,5},{5,4},{6,7},{7,6},{8,9},{9,8},{10,11... | collective-permute-start | bytes 442376 | tf_op jit(solution)/shard_map/ppermute | solution.py:536
  15.4 4.7 %collective-permute-start.8 = (f32[2,192,384]{2,1,0:T(8,128)S(1)}, f32[2,192,384]{2,1,0:T(8,128)S(1)}, u32[]{:S(2)}, u32[]{:S(2)}) collective-permute-start(f32[2,192,384]{2,1,0:T(8,128)S(1)} %get-tuple-element.74.mine_ref), channel_id=1, source_target_pairs={{0,1},{1,0},{2,3},{3,2},{4,5},{5,4},{6,7},{7,6},{8,9},{9,8},{10,11... | collective-permute-start | bytes 1769480 | tf_op jit(solution)/shard_map/ppermute | solution.py:536
  17.9 2.3 %copy-start.6 = (f32[384]{0:T(512)S(1)}, f32[384]{0:T(512)}, u32[]{:S(2)}) copy-start(f32[384]{0:T(512)} %param.18) | copy-start | bytes 4612
  18.6 3.9 %collective-permute-start.7 = (f32[2,192,384]{2,1,0:T(8,128)S(1)}, f32[2,192,384]{2,1,0:T(8,128)S(1)}, u32[]{:S(2)}, u32[]{:S(2)}) collective-permute-start(f32[2,192,384]{2,1,0:T(8,128)S(1)} %other_rows.1.mine_ref), channel_id=1, source_target_pairs={{0,1},{1,0},{2,3},{3,2},{4,5},{5,4},{6,7},{7,6},{8,9},{9,8},{10,11... | collective-permute-start | bytes 1769480 | tf_op jit(solution)/shard_map/ppermute | solution.py:536
  25.1 5.3 %collective-permute-start.9 = (f32[312,128]{1,0:T(8,128)S(1)}, f32[312,128]{1,0:T(8,128)S(1)}, u32[]{:S(2)}, u32[]{:S(2)}) collective-permute-start(f32[312,128]{1,0:T(8,128)S(1)} %get-tuple-element.91.total_ref), channel_id=1, source_target_pairs={{0,8},{1,9},{2,10},{3,11},{4,12},{5,13},{6,14},{7,15},{8,0},{9,1},... | collective-permute-start | bytes 479240 | tf_op jit(solution)/shard_map/ppermute | solution.py:549
  26.7 10.0 %collective-permute-start.13 = (f32[192,384]{1,0:T(8,128)S(1)}, f32[192,384]{1,0:T(8,128)S(1)}, u32[]{:S(2)}, u32[]{:S(2)}) collective-permute-start(f32[192,384]{1,0:T(8,128)S(1)} %get-tuple-element.93), channel_id=1, source_target_pairs={{0,2},{1,3},{2,0},{3,1},{4,6},{5,7},{6,4},{7,5},{8,10},{9,11},{10,... | collective-permute-start | bytes 884744 | tf_op jit(solution)/shard_map/ppermute | solution.py:549
  30.4 3.3 %collective-permute-start.10 = (f32[312,128]{1,0:T(8,128)S(1)}, f32[312,128]{1,0:T(8,128)S(1)}, u32[]{:S(2)}, u32[]{:S(2)}) collective-permute-start(f32[312,128]{1,0:T(8,128)S(1)} %collective-permute-done.9.refs_0_), channel_id=1, source_target_pairs={{0,1},{1,0},{2,3},{3,2},{4,5},{5,4},{6,7},{7,6},{8,9},{9,8},{10,11... | collective-permute-start | bytes 479240 | tf_op jit(solution)/shard_map/ppermute | solution.py:536
  33.6 7.0 %collective-permute-start.11 = (f32[312,128]{1,0:T(8,128)S(1)}, f32[312,128]{1,0:T(8,128)S(1)}, u32[]{:S(2)}, u32[]{:S(2)}) collective-permute-start(f32[312,128]{1,0:T(8,128)S(1)} %joined_covariance.1), channel_id=1, source_target_pairs={{0,2},{1,3},{2,0},{3,1},{4,6},{5,7},{6,4},{7,5},{8,16},{9,17},{10,... | collective-permute-start | bytes 479240 | tf_op jit(solution)/shard_map/ppermute | solution.py:549
  33.9 8.0 %collective-permute-start.12 = (f32[312,128]{1,0:T(8,128)S(1)}, f32[312,128]{1,0:T(8,128)S(1)}, u32[]{:S(2)}, u32[]{:S(2)}) collective-permute-start(f32[312,128]{1,0:T(8,128)S(1)} %joined_covariance.1), channel_id=1, source_target_pairs={{0,4},{1,5},{2,6},{3,7},{4,0},{5,1},{6,2},{7,3},{8,24},{9,25},{10,... | collective-permute-start | bytes 479240 | tf_op jit(solution)/shard_map/ppermute | solution.py:549
  36.7 2.4 %collective-permute-start.14 = (f32[96,384]{1,0:T(8,128)S(1)}, f32[96,384]{1,0:T(8,128)S(1)}, u32[]{:S(2)}, u32[]{:S(2)}) collective-permute-start(f32[96,384]{1,0:T(8,128)S(1)} %get-tuple-element.109), channel_id=1, source_target_pairs={{0,1},{1,0},{2,3},{3,2},{4,5},{5,4},{6,7},{7,6},{8,9},{9,8},{10,11... | collective-permute-start | bytes 442376 | tf_op jit(solution)/shard_map/ppermute | solution.py:536
  38.1 1.4 %collective-permute-start.15 = (f32[96,384]{1,0:T(8,128)S(1)}, f32[96,384]{1,0:T(8,128)S(1)}, u32[]{:S(2)}, u32[]{:S(2)}) collective-permute-start(f32[96,384]{1,0:T(8,128)S(1)} %get-tuple-element.108), channel_id=1, source_target_pairs={{0,1},{1,0},{2,3},{3,2},{4,5},{5,4},{6,7},{7,6},{8,9},{9,8},{10,11... | collective-permute-start | bytes 442376 | tf_op jit(solution)/shard_map/ppermute | solution.py:536
  41.9 2.2 %collective-permute-start.16 = (f32[312,128]{1,0:T(8,128)S(1)}, f32[312,128]{1,0:T(8,128)S(1)}, u32[]{:S(2)}, u32[]{:S(2)}) collective-permute-start(f32[312,128]{1,0:T(8,128)S(1)} %collective-permute-done.11.refs_0_), channel_id=1, source_target_pairs={{0,1},{1,0},{2,3},{3,2},{4,5},{5,4},{6,7},{7,6},{8,9},{9,8},{10,11... | collective-permute-start | bytes 479240 | tf_op jit(solution)/shard_map/ppermute | solution.py:536
  43.1 1.4 %collective-permute-start.17 = (f32[312,128]{1,0:T(8,128)S(1)}, f32[312,128]{1,0:T(8,128)S(1)}, u32[]{:S(2)}, u32[]{:S(2)}) collective-permute-start(f32[312,128]{1,0:T(8,128)S(1)} %collective-permute-done.12.refs_1_), channel_id=1, source_target_pairs={{0,1},{1,0},{2,3},{3,2},{4,5},{5,4},{6,7},{7,6},{8,9},{9,8},{10,11... | collective-permute-start | bytes 479240 | tf_op jit(solution)/shard_map/ppermute | solution.py:536
